TPU v7x, 256 devices: a whole 4x4x8 slice. The times are simulated.
256 devices in a mesh: dp: 256 (over y, x, z, core).
Axes of the slice: x: 4, y: 4, z: 8, core: 2. Of those that a mesh axis runs over, the one named last changes fastest.
Arguments:
- activations: bfloat16 [262144, 512], P('dp'), may hold values from -24 to 24
- grad_key: bfloat16 [262144, 512], P('dp'), may hold values from -8 to 8
- grad_value: bfloat16 [262144, 512], P('dp'), may hold values from -6 to 6
- time_start: int32 [2048, 2], P('dp'), may hold values from 0 to 112
- time_width: int32 [2048, 2], P('dp'), may hold values from 0 to 16
- bases: bfloat16 [3, 512, 512], replicated, may hold values from -2 to 2
- old_factors: float32 [512, 3, 512], P('dp'), may hold values from -0.0004 to 0.6, as said below
Outputs:
- new_factors: float32 [512, 3, 512], P('dp')
- gradients: float32 [512, 2, 512], P('dp')
- updates: bfloat16 [2, 512, 512], P(None, 'dp')
Inputs may be any that keep to these rules, and one draw needn't show every extreme that they name: `old_factors`: symmetric within each factor, with a positive diagonal that dominates each row.
All inputs are finite; a program needn't handle non-finite values.
Results may differ from a plain program's by a relative error of at most 0.014.
Values may be sent and summed in bfloat16 or wider, within the bound.
No kernel may reach another device: no remote copies, remote signals or barrier semaphores. Data moves between devices by JAX's collectives and lax.ppermute only.
A program may use at most 64 MiB of HBM per device.

v0:
```python
import jax
import jax.numpy as jnp
from jax import lax
from jax.sharding import PartitionSpec as P

LEN = 128
NFACT = 3
NPROJ = 2


decay = 0.8
damping = 0.001
kl_clip = 0.001
learn_rate = 7e-05


def broadcast(value, axis, root):
    mine = lax.axis_index(axis) == root
    return lax.psum(jnp.where(mine, value, jnp.zeros_like(value)), axis)


def frame_keep(time_start, time_width):
    position = jnp.arange(LEN, dtype=jnp.int32)
    inside = (position[None, None, :] >= time_start[:, :, None]) & (
        position[None, None, :] < (time_start + time_width)[:, :, None]
    )
    masked = jnp.any(inside, axis=1).reshape(-1)
    return jnp.where(masked, 0.0, 1.0).astype(jnp.bfloat16)


def precondition(grad_low, basis_in, basis_out, lam_in, lam_out):
    rot_out = jnp.dot(grad_low, basis_out, preferred_element_type=jnp.float32).astype(jnp.bfloat16)
    rotated = jnp.dot(basis_in.T, rot_out, preferred_element_type=jnp.float32)
    scaled = (rotated / (lam_in[:, None] * lam_out[None, :] + damping)).astype(jnp.bfloat16)
    back_out = jnp.dot(scaled, basis_out.T, preferred_element_type=jnp.float32).astype(jnp.bfloat16)
    return jnp.dot(basis_in, back_out, preferred_element_type=jnp.float32).astype(jnp.bfloat16)


def body(activations, grad_key, grad_value, time_start, time_width, bases, old_factors):
    devices = lax.axis_size("dp")
    index = lax.axis_index("dp")
    frames = activations.shape[0]
    width = activations.shape[1]
    tokens_all = frames * devices
    local_rows = old_factors.shape[0]
    row_start = index * local_rows
    keep = frame_keep(time_start, time_width)[:, None]
    inputs = (activations * keep, grad_key * keep, grad_value * keep)

    def gradient_term():
        left = inputs[0].T
        parts = [
            jnp.dot(left, inputs[1 + p], preferred_element_type=jnp.float32) for p in range(NPROJ)
        ]
        return jnp.stack(parts, axis=1)

    parts = [jnp.dot(x.T, x, preferred_element_type=jnp.float32) for x in inputs]
    batch = lax.psum_scatter(
        jnp.stack(parts, axis=1) / tokens_all, "dp", scatter_dimension=0, tiled=True
    )
    gradients = lax.psum_scatter(gradient_term(), "dp", scatter_dimension=0, tiled=True)
    new_factors = decay * old_factors + (1.0 - decay) * batch
    partials = []
    for f in range(NFACT):
        basis = bases[f].astype(jnp.float32)
        my_rows = lax.dynamic_slice_in_dim(basis, row_start, local_rows, 0)
        image = jnp.dot(new_factors[:, f, :], basis, precision=lax.Precision.HIGHEST)
        partials.append(jnp.sum(my_rows * image, axis=0))
    lam = lax.psum(jnp.stack(partials, axis=0), "dp")
    gathered = lax.all_gather(gradients.astype(jnp.bfloat16), "dp", axis=0, tiled=True)
    owners = [(2 * p + 1) * devices // (2 * NPROJ) for p in range(NPROJ)]
    precs = []
    for p in range(NPROJ):
        grad_low = gathered[:, p, :]

        def compute_owned(grad_low=grad_low, p=p):
            return precondition(grad_low, bases[0], bases[1 + p], lam[0], lam[1 + p])

        def nothing_owned():
            return jnp.zeros((width, width), jnp.bfloat16)

        precs.append(lax.cond(index == owners[p], compute_owned, nothing_owned))
    terms = jnp.stack(
        [
            jnp.sum(precs[p].astype(jnp.float32) * gathered[:, p, :].astype(jnp.float32))
            for p in range(NPROJ)
        ]
    )
    totals = lax.psum(terms, "dp")
    factor = jnp.sqrt(kl_clip / (learn_rate * learn_rate * jnp.sum(totals)))
    payloads = [(factor * q.astype(jnp.float32)).astype(jnp.bfloat16) for q in precs]
    delivered = [broadcast(payloads[p], "dp", owners[p]) for p in range(NPROJ)]
    whole_updates = jnp.stack(delivered, axis=0)
    updates = lax.dynamic_slice_in_dim(whole_updates, row_start, local_rows, 1)
    return (new_factors, gradients, updates)


def solution(mesh):
    in_specs = (
        P("dp", None),
        P("dp", None),
        P("dp", None),
        P("dp", None),
        P("dp", None),
        P(),
        P("dp", None, None),
    )
    out_specs = (P("dp", None, None), P("dp", None, None), P(None, "dp", None))
    return jax.shard_map(body, mesh=mesh, in_specs=in_specs, out_specs=out_specs, check_vma=False)
```

profile of v0, /device:TPU:1, one launch (start us, length us, event | category | flops | bytes accessed | tf_op | source)
XLA Modules:
  0.0 749.2 jit_solution(18417237628496583930)
XLA Ops:
  7.2 0.7 add.30
  7.9 0.8 fusion.53
  8.7 2.7 convolution_bitcast_fusion.4
  11.4 1.0 convolution_bitcast_fusion.6
  12.6 1.0 convolution_bitcast_fusion.2
  13.6 0.2 copy-done.5
  13.8 1.0 convolution_bitcast_fusion.5
  14.9 1.0 convolution_bitcast_fusion.3
  15.9 1.6 pad_maximum_fusion
  17.5 2.1 maximum_multiply_fusion
  19.6 274.4 %all-reduce.7.cloned.1.call-done = (f32[512,3,512]{2,0,1:T(8,128)}, f32[512,2,512]{2,0,1:T(8,128)}) async-done(((f32[512,3,512]{2,0,1:T(8,128)}, f32[512,2,512]{2,0,1:T(8,128)}), (f32[512,3,512]{2,0,1:T(8,128)}, f32[512,2,512]{2,0,1:T(8,128)})) %all-reduce.7.cloned.1.call-update) | async-done | bytes 5242896
  294.0 0.8 fusion.56
  294.8 0.6 copy.35
  295.6 0.6 copy-done.3
  296.2 0.8 fusion.51
  297.0 0.3 fusion.32
  297.3 0.3 fusion.33
  297.7 0.3 fusion.34
  298.0 78.1 %psum.28 = f32[3,512]{1,0:T(4,128)S(1)} all-reduce(f32[3,512]{1,0:T(4,128)S(1)} %pad_maximum_fusion.1), channel_id=1, replica_groups=mesh['dp'=256] {'dp'}, use_global_device_ids=true, to_apply=%region_6.7 | all-reduce | flops 1536 | bytes 12288 | tf_op jit(solution)/shard_map/psum | solution.py:69
  376.1 25.7 %all-gather.2.cloned.1.call-done = bf16[512,2,512]{2,1,0:T(2,128)(2,1)} async-done(((bf16[2,2,512]{2,1,0:T(2,128)(2,1)}), bf16[512,2,512]{2,1,0:T(2,128)(2,1)}) %all-gather.2.cloned.1.call-update) | async-done | bytes 1048592 | tf_op jit(solution)/shard_map/all_gather | solution.py:70
  401.8 3.3 fusion.59
  405.1 0.3 copy_bitcast_fusion
  405.6 0.9 multiply_reduce_fusion.1
  406.6 0.9 multiply_reduce_fusion
  407.5 1.4 pad_maximum_fusion.2
  408.8 80.2 %psum.29 = f32[2]{0:T(128)S(1)} all-reduce(f32[2]{0:T(128)S(1)} %pad_maximum_fusion.2), channel_id=1, replica_groups=mesh['dp'=256] {'dp'}, use_global_device_ids=true, to_apply=%region_13.14 | all-reduce | flops 2 | bytes 16 | tf_op jit(solution)/shard_map/psum | solution.py:89
  489.0 0.6 reduce_sum.59
  490.4 0.9 fusion.45
  491.3 0.9 fusion.43
  492.3 0.6 copy.42
  492.9 248.5 %all-reduce.9.cloned.1.call-done = (bf16[1,512,512]{2,1,0:T(8,128)(2,1)}, bf16[1,512,512]{2,1,0:T(8,128)(2,1)}) async-done(((bf16[1,512,512]{2,1,0:T(8,128)(2,1)}, bf16[1,512,512]{2,1,0:T(8,128)(2,1)}), (bf16[1,512,512]{2,1,0:T(8,128)(2,1)}, bf16[1,512,512]{2,1,0:T(8,128)(2,1)})) %all-reduce.9.cloned.1.call-update) | async-done | bytes 1048592 | tf_op jit(solution)/shard_map/psum | solution.py:19
  741.4 1.3 fusion.54
  (23 shorter events, 1.0 us)
Async XLA Ops:
  7.2 286.8 %all-reduce.7.cloned.1.call-start = ((), (), s32[]{:S(2)}) async-start(), calls=%async_computation.1 | async-start | bytes 10485760
  8.7 2.7 copy-start.6
  11.4 1.2 copy-start.4
  12.6 1.2 copy-start.5
  19.5 275.9 %copy-start = (bf16[3,512,512]{2,1,0:T(8,128)(2,1)S(1)}, bf16[3,512,512]{2,1,0:T(8,128)(2,1)}, u32[]{:S(2)}) copy-start(bf16[3,512,512]{2,1,0:T(8,128)(2,1)} %param.16) | copy-start | bytes 4718596
  19.6 382.3 %all-gather.2.cloned.1.call-start = ((), (), s32[]{:S(2)}) async-start(), calls=%async_computation | async-start | bytes 1052672 | tf_op jit(solution)/shard_map/all_gather | solution.py:70
  295.4 446.0 %all-reduce.9.cloned.1.call-start = ((), (), s32[]{:S(2)}) async-start(), calls=%async_computation.2 | async-start | bytes 2097152 | tf_op jit(solution)/shard_map/psum | solution.py:19
  295.5 0.7 copy-start.3
  297.0 108.2 %copy-start.2 = (f32[2,3,512]{2,0,1:T(2,128)}, f32[2,3,512]{2,0,1:T(2,128)S(1)}, u32[]{:S(2)}) copy-start(f32[2,3,512]{2,0,1:T(2,128)S(1)} %fusion.51) | copy-start | bytes 36868
Sparse Core Ops, SparseCore 0:
  19.7 274.2 all-reduce.6
  298.9 102.8 all-gather.1
  492.4 248.9 all-reduce.8
where the time goes:
time: 751 us; the launch traced here: 749 us
  waiting for transfers between devices  549 us (73%)
  blocking collectives  158 us (21%)
  between operations  14.6 us (2%)
  other arithmetic  13.6 us (2%)
  matrix products  7.82 us (1%)
    unnamed x4, waiting for transfers between devices  274 us
    psum x1, waiting for transfers between devices, broadcast(): return lax.psum(jnp.where(mine, value, jnp.zeros_like(value)), axis)  249 us
    psum x1, blocking collectives, body(): totals = lax.psum(terms, 'dp')  80.2 us
    psum x1, blocking collectives, body(): lam = lax.psum(jnp.stack(partials, axis=0), 'dp')  78.1 us
    all_gather x1, waiting for transfers between devices, body(): lax.all_gather(gradients.astype(jnp.bfloat16), 'dp', axis=0, tiled=True)  25.7 us
  transfers between devices with their start and end apart: 3, of which 3 were waited for; matrix products, arithmetic and copies ran while one was open for 0% of the time, Pallas kernels for 0%

commit v1 on v0

v1 whole, which is shorter than its diff:
```python
import jax
import jax.numpy as jnp
from jax import lax
from jax.sharding import PartitionSpec as P

LEN = 128
NX, NY, NZ, NC = 4, 4, 8, 2
NXY = NX * NY
D = 512
ROWS_XY = D // NXY
ROWS_Z = ROWS_XY // NZ

decay = 0.8
damping = 0.001
kl_clip = 0.001
learn_rate = 7e-05

SWAP = [(d, d ^ 1) for d in range(NXY * NZ * NC)]
XY_GROUPS = [[(i * NZ + z) * NC + c for i in range(NXY)] for z in range(NZ) for c in range(NC)]
Z_GROUPS = [[(i * NZ + z) * NC + c for z in range(NZ)] for i in range(NXY) for c in range(NC)]


def frame_keep(time_start, time_width):
    position = jnp.arange(LEN, dtype=jnp.int32)
    inside = (position[None, None, :] >= time_start[:, :, None]) & (
        position[None, None, :] < (time_start + time_width)[:, :, None]
    )
    masked = jnp.any(inside, axis=1).reshape(-1)
    return jnp.where(masked, 0.0, 1.0).astype(jnp.bfloat16)


def split(value):
    high = value.astype(jnp.bfloat16)
    low = (value - high.astype(jnp.float32)).astype(jnp.bfloat16)
    return jnp.concatenate([high, low], axis=0)


def body(activations, grad_key, grad_value, time_start, time_width, bases, old_factors):
    f32, bf16 = jnp.float32, jnp.bfloat16
    index = lax.axis_index("dp")
    core = index % NC
    first = core == 0
    tokens = activations.shape[0] * lax.axis_size("dp")
    keep = frame_keep(time_start, time_width)[:, None]
    x = (activations * keep, grad_key * keep, grad_value * keep)

    def gram(a, b):
        return jnp.dot(a.T, b, preferred_element_type=f32).astype(bf16)

    g = [gram(x[0], x[1]), gram(x[0], x[2])]
    f = [gram(v, v) for v in x]
    whole0 = jnp.concatenate([g[0], f[0], f[2][:, : D // 2]], axis=1)
    whole1 = jnp.concatenate([g[1], f[1], f[2][:, D // 2 :]], axis=1)
    mine = jnp.where(first, whole0, whole1)
    other = jnp.where(first, whole1, whole0)
    received = lax.ppermute(other, "dp", SWAP)

    share = (1.0 - decay) / tokens
    my_rows = lax.dynamic_slice_in_dim(bases, 2 * index, 2, 1).astype(f32)
    lam = []
    for k in range(3):
        image = jnp.dot(f[k], bases[k], preferred_element_type=f32)
        part = jnp.sum(bases[k].astype(f32) * image, axis=0) * share
        old_image = jnp.dot(old_factors[:, k, :], bases[k].astype(f32), precision=lax.Precision.HIGHEST)
        lam.append(part + decay * jnp.sum(my_rows[k] * old_image, axis=0))
    lam = jnp.stack(lam)
    lam = lam + lax.ppermute(lam, "dp", SWAP)
    lam = jnp.stack([lam[0], jnp.where(first, lam[1], lam[2])])

    chip = (mine.astype(f32) + received.astype(f32)).astype(bf16)
    parts = lax.all_to_all(chip.reshape(NXY, ROWS_XY, 1280), "dp", 0, 0, axis_index_groups=XY_GROUPS, tiled=True)
    plane = jnp.sum(parts.astype(f32), axis=0).astype(bf16)

    send = jnp.concatenate(
        [
            jnp.broadcast_to(plane[None, :, :D], (NZ, ROWS_XY, D)),
            plane[:, D:].reshape(NZ, 6, D),
            jnp.broadcast_to(split(lam)[None], (NZ, 4, D)),
        ],
        axis=1,
    )
    got = lax.all_to_all(send, "dp", 0, 0, axis_index_groups=Z_GROUPS, tiled=True)
    got = jnp.sum(got.astype(f32), axis=0)
    grad = got[:ROWS_XY]
    factors = got[ROWS_XY : ROWS_XY + 6].reshape(ROWS_Z, 768) * (1.0 / tokens)
    lam = got[38:40] + got[40:42]

    basis_in = bases[0]
    basis_out = lax.dynamic_index_in_dim(bases, 1 + core, 0, keepdims=False)
    rot_out = jnp.dot(grad.astype(bf16), basis_out, preferred_element_type=f32).astype(bf16)
    send = jnp.concatenate([rot_out, split(lam)], axis=0)
    send = jnp.broadcast_to(send[None], (NXY,) + send.shape)
    got = lax.all_to_all(send, "dp", 0, 0, axis_index_groups=XY_GROUPS, tiled=True)
    rot_all = got[:, :ROWS_XY].reshape(D, D)
    lam = jnp.sum(got[:, ROWS_XY:].astype(f32), axis=0)
    lam = lam[:2] + lam[2:]
    rotated = lax.dot_general(basis_in, rot_all, (((0,), (0,)), ((), ())), preferred_element_type=f32)
    scaled = (rotated / (lam[0][:, None] * lam[1][None, :] + damping)).astype(bf16)
    curve = jnp.sum(scaled.astype(f32) * rotated)
    chip_index = index // NC
    rows_in = lax.dynamic_slice_in_dim(basis_in, chip_index * ROWS_Z, ROWS_Z, 0)
    back = jnp.dot(rows_in, scaled, preferred_element_type=f32).astype(bf16)
    prec = lax.dot_general(back, basis_out, (((1,), (1,)), ((), ())), preferred_element_type=f32)
    prec = prec.astype(bf16).astype(f32)

    def mine_theirs(rows):
        low, high = rows[:2], rows[2:4]
        return jnp.where(first, low, high), jnp.where(first, high, low)

    prec_mine, prec_theirs = mine_theirs(prec)
    extra = lax.ppermute(jnp.concatenate([prec_theirs, jnp.broadcast_to(curve, (1, D))], axis=0), "dp", SWAP)
    factor = jnp.sqrt(kl_clip / (learn_rate * learn_rate * (curve + extra[2, 0])))
    prec_other = extra[:2]
    updates = jnp.stack(
        [jnp.where(first, prec_mine, prec_other), jnp.where(first, prec_other, prec_mine)]
    )
    updates = (factor * updates).astype(bf16)

    z = (index // NC) % NZ
    grad_rows = lax.dynamic_slice_in_dim(grad, z * ROWS_Z, ROWS_Z, 0)
    rows_mine, rows_theirs = mine_theirs(jnp.concatenate([grad_rows, factors], axis=1))
    rows_other = lax.ppermute(rows_theirs, "dp", SWAP)
    rows0 = jnp.where(first, rows_mine, rows_other)
    rows1 = jnp.where(first, rows_other, rows_mine)
    gradients = jnp.stack([rows0[:, :D], rows1[:, :D]], axis=1)
    last = jnp.concatenate([rows0[:, 1024:], rows1[:, 1024:]], axis=1)
    batch = jnp.stack([rows0[:, D:1024], rows1[:, D:1024], last], axis=1)
    new_factors = decay * old_factors + (1.0 - decay) * batch
    return (new_factors, gradients, updates)


def solution(mesh):
    in_specs = (
        P("dp", None),
        P("dp", None),
        P("dp", None),
        P("dp", None),
        P("dp", None),
        P(),
        P("dp", None, None),
    )
    out_specs = (P("dp", None, None), P("dp", None, None), P(None, "dp", None))
    return jax.shard_map(body, mesh=mesh, in_specs=in_specs, out_specs=out_specs, check_vma=False)
```

time: 751 us -> 104 us (0.14)
  waiting for transfers between devices: 549 us -> 46.1 us
  blocking collectives: 158 us -> 0 us
  starting transfers between devices: 0.12 us -> 24.3 us
  between operations: 14.6 us -> 2.52 us
  matrix products: 7.82 us -> 15.9 us
    unnamed x4 -> x0, waiting for transfers between devices: 274 us -> none
    psum x1 -> x0, waiting for transfers between devices: 249 us -> none  [broadcast(): return lax.psum(jnp.where(mine, value, jnp.zeros_like(value)), axis)]
    psum x2 -> x0, blocking collectives: 158 us -> none  [the longest x1 80.2 us: body(): totals = lax.psum(terms, 'dp')]
    all_to_all x0 -> x3, waiting for transfers between devices: none -> 45 us  [the longest x1 20 us: body(): lax.all_to_all(chip.reshape(NXY, ROWS_XY, 1280), 'dp', 0, 0, axis_index_g...]
    all_gather x1 -> x0, waiting for transfers between devices: 25.7 us -> none  [body(): lax.all_gather(gradients.astype(jnp.bfloat16), 'dp', axis=0, tiled=True)]
    all_to_all x0 -> x3, starting transfers between devices: none -> 16.8 us  [the longest x1 8.18 us: body(): lax.all_to_all(send, 'dp', 0, 0, axis_index_groups=Z_GROUPS, tiled=True)]
    dot_general x8 -> x14, matrix products: 7.82 us -> 15.9 us  [the longest x5 8.45 us: gram(): return jnp.dot(a.T, b, preferred_element_type=f32).astype(bf16)]
    ppermute x0 -> x4, starting transfers between devices: none -> 7.52 us  [the longest x1 3.24 us: body(): received = lax.ppermute(other, 'dp', SWAP)]
  transfers between devices with their start and end apart: 3 -> 7, of which waited for: 3 -> 5; matrix products, arithmetic and copies ran while one was open for 0% -> 6% of each run, Pallas kernels for 0% -> 0%
where the time goes in v1:
time: 104 us
  waiting for transfers between devices  46.1 us (44%)
  starting transfers between devices  24.3 us (23%)
  matrix products  15.9 us (15%)
  other arithmetic  9.03 us (9%)
  local copies, waits for them, and re-layouts  5.87 us (6%)
  between operations  2.52 us (2%)
    all_to_all x1, waiting for transfers between devices, body(): lax.all_to_all(chip.reshape(NXY, ROWS_XY, 1280), 'dp', 0, 0, axis_index_g...  20 us
    all_to_all x1, waiting for transfers between devices, body(): lax.all_to_all(send, 'dp', 0, 0, axis_index_groups=Z_GROUPS, tiled=True)  13.2 us
    all_to_all x1, waiting for transfers between devices, body(): lax.all_to_all(send, 'dp', 0, 0, axis_index_groups=XY_GROUPS, tiled=True)  11.9 us
    dot_general x5, matrix products, gram(): return jnp.dot(a.T, b, preferred_element_type=f32).astype(bf16)  8.45 us
    all_to_all x1, starting transfers between devices, body(): lax.all_to_all(send, 'dp', 0, 0, axis_index_groups=Z_GROUPS, tiled=True)  8.18 us
    all_to_all x1, starting transfers between devices, body(): lax.all_to_all(chip.reshape(NXY, ROWS_XY, 1280), 'dp', 0, 0, axis_index_g...  5.02 us
    all_to_all x1, starting transfers between devices, body(): lax.all_to_all(send, 'dp', 0, 0, axis_index_groups=XY_GROUPS, tiled=True)  3.59 us
    ppermute x1, starting transfers between devices, body(): received = lax.ppermute(other, 'dp', SWAP)  3.24 us
  transfers between devices with their start and end apart: 7, of which 5 were waited for; matrix products, arithmetic and copies ran while one was open for 6% of the time, Pallas kernels for 0%

profile of v1, /device:TPU:1, one launch (start us, length us, event | category | flops | bytes accessed | tf_op | source)
XLA Modules:
  0.0 103.8 jit_solution(1009815413793970286)
XLA Ops:
  0.6 0.7 add.92
  1.3 0.8 fusion.39
  2.1 2.7 %convolution_convert_fusion.2 = bf16[512,512]{0,1:T(8,128)(2,1)S(1)} fusion(bf16[1024,512]{1,0:T(8,128)(2,1)} %param.9, bf16[1024]{0:T(1024)(128)(2,1)S(1)} %fusion.50), kind=kOutput, calls=%fused_computation.10 | convolution fusion | flops 537657344 | bytes 1574912 | tf_op jit(solution)/shard_map/dot_general | solution.py:48
  4.8 1.0 %convolution_convert_fusion.3 = bf16[512,512]{0,1:T(8,128)(2,1)S(1)} fusion(bf16[1024,512]{1,0:T(8,128)(2,1)S(1)} %copy-done.10, bf16[1024]{0:T(1024)(128)(2,1)S(1)} %fusion.50), kind=kOutput, calls=%fused_computation.11 | convolution fusion | flops 537657344 | bytes 1574912 | tf_op jit(solution)/shard_map/dot_general | solution.py:48
  6.2 1.0 %convolution_convert_fusion.1 = bf16[512,512]{0,1:T(8,128)(2,1)S(1)} fusion(bf16[1024,512]{1,0:T(8,128)(2,1)S(1)} %copy-done.8, bf16[1024,512]{1,0:T(8,128)(2,1)S(1)} %copy-done.10, bf16[1024]{0:T(1024)(128)(2,1)S(1)} %fusion.50), kind=kOutput, calls=%fused_computation.9 | convolution fusion | flops 538181632 | bytes 2623488 | tf_op jit(solution)/shard_map/dot_general | solution.py:48
  7.6 1.9 %convolution_convert_fusion = bf16[512,512]{0,1:T(8,128)(2,1)} fusion(bf16[1024,512]{1,0:T(8,128)(2,1)S(1)} %copy-done.9, bf16[1024]{0:T(1024)(128)(2,1)S(1)} %fusion.50), kind=kOutput, calls=%fused_computation.8 | convolution fusion | flops 537657344 | bytes 1574912 | tf_op jit(solution)/shard_map/dot_general | solution.py:48
  9.5 1.8 %convolution_convert_fusion.4 = bf16[512,512]{0,1:T(8,128)(2,1)} fusion(bf16[1024,512]{1,0:T(8,128)(2,1)S(1)} %copy-done.9, bf16[1024,512]{1,0:T(8,128)(2,1)S(1)} %copy-done.10, bf16[1024]{0:T(1024)(128)(2,1)S(1)} %fusion.50), kind=kOutput, calls=%fused_computation.12 | convolution fusion | flops 538181632 | bytes 2623488 | tf_op jit(solution)/shard_map/dot_general | solution.py:48
  11.4 2.8 %broadcast_select_fusion = bf16[512,1280]{0,1:T(8,128)(2,1)} fusion(pred[]{:T(512)S(6)} %eq.6, bf16[512,256]{0,1:T(8,128)(2,1)S(1)} %get-tuple-element.24, bf16[512,512]{0,1:T(8,128)(2,1)} %convolution_convert_fusion, bf16[512,512]{0,1:T(8,128)(2,1)S(1)} %convolution_convert_fusion.1, bf16[512,256]{0,1:T(8,128)(2,1)S(1)} %get-tuple-element.23, ...), kind=kLoop, calls=%fused_computation.7 | loop fusion | flops 8519680 | bytes 3932161 | tf_op jit(solution)/shard_map/jit(_where)/select_n | solution.py:55
  14.2 3.2 %collective-permute-start = (bf16[512,1280]{0,1:T(8,128)(2,1)}, bf16[512,1280]{0,1:T(8,128)(2,1)}, u32[]{:S(2)}, u32[]{:S(2)}) collective-permute-start(bf16[512,1280]{0,1:T(8,128)(2,1)} %broadcast_select_fusion), channel_id=1, source_target_pairs={{0,1},{1,0},{2,3},{3,2},{4,5},{5,4},{6,7},{7,6},{8,9},{9,8},{10,11... | collective-permute-start | bytes 3932168 | tf_op jit(solution)/shard_map/ppermute | solution.py:56
  18.1 1.5 %fusion.2 = f32[512]{0:T(512)S(1)} fusion(bf16[512,512]{0,1:T(8,128)(2,1)} %copy-done.6, bf16[3,512,512]{2,1,0:T(8,128)(2,1)S(1)} %copy-done), kind=kOutput, calls=%fused_computation.15 | convolution fusion | flops 269221376 | bytes 1574912 | tf_op jit(solution)/shard_map/dot_general | solution.py:62
  19.7 0.5 fusion.1
  20.7 0.5 copy-done.3
  21.4 2.0 %add_convert_fusion = bf16[512,1280]{0,1:T(8,128)(2,1)S(1)} fusion(bf16[512,1280]{0,1:T(8,128)(2,1)} %collective-permute-done, pred[]{:T(512)S(6)} %eq.6, bf16[512,256]{0,1:T(8,128)(2,1)S(1)} %get-tuple-element.24, bf16[512,512]{0,1:T(8,128)(2,1)S(1)} %copy-done.4, bf16[512,512]{0,1:T(8,128)(2,1)S(1)} %copy-done.3, bf16[512,256]{0,1:T(8,128)(2,1)S(1)} %get-tuple-element.23, ...), kind=kLoop, calls=%fused_computation | loop fusion | flops 11141120 | bytes 5242881 | tf_op jit(solution)/shard_map/convert_element_type | solution.py:70
  23.4 1.5 %copy.32 = bf16[512,1280]{1,0:T(8,128)(2,1)} copy(bf16[512,1280]{0,1:T(8,128)(2,1)S(1)} %add_convert_fusion) | data formatting | bytes 2621440 | tf_op jit(solution)/shard_map/convert_element_type | solution.py:70
  24.8 5.0 %all-to-all-start = ((bf16[16,32,1280]{2,1,0:T(8,128)(2,1)}), bf16[16,32,1280]{2,1,0:T(8,128)(2,1)S(1)}, u32[]{:S(2)}, u32[]{:S(2)}) async-start(bf16[16,32,1280]{2,1,0:T(8,128)(2,1)} %bitcast.1), calls=%async_computation | async-start | bytes 2621440 | tf_op jit(solution)/shard_map/all_to_all | solution.py:71
  30.6 0.9 collective-permute-done.1
  31.6 20.0 %all-to-all-done = bf16[16,32,1280]{2,1,0:T(8,128)(2,1)S(1)} async-done(((bf16[16,32,1280]{2,1,0:T(8,128)(2,1)}), bf16[16,32,1280]{2,1,0:T(8,128)(2,1)S(1)}, u32[]{:S(2)}, u32[]{:S(2)}) %all-to-all-start) | async-done | bytes 1310752 | tf_op jit(solution)/shard_map/all_to_all | solution.py:71
  51.8 0.8 pad_maximum_fusion.2
  52.6 8.2 %all-to-all-start.1 = ((bf16[8,42,512]{2,1,0:T(8,128)(2,1)}), bf16[8,42,512]{2,1,0:T(8,128)(2,1)S(1)}, u32[]{:S(2)}, u32[]{:S(2)}) async-start(bf16[8,42,512]{2,1,0:T(8,128)(2,1)} %pad_maximum_fusion.2), calls=%async_computation.1 | async-start | bytes 786432 | tf_op jit(solution)/shard_map/all_to_all | solution.py:82
  60.8 13.2 %all-to-all-done.1 = bf16[8,42,512]{2,1,0:T(8,128)(2,1)S(1)} async-done(((bf16[8,42,512]{2,1,0:T(8,128)(2,1)}), bf16[8,42,512]{2,1,0:T(8,128)(2,1)S(1)}, u32[]{:S(2)}, u32[]{:S(2)}) %all-to-all-start.1) | async-done | bytes 344096 | tf_op jit(solution)/shard_map/all_to_all | solution.py:82
  74.5 2.6 %collective-permute-start.2 = (f32[2,1280]{1,0:T(2,128)S(1)}, f32[2,1280]{1,0:T(2,128)S(1)}, u32[]{:S(2)}, u32[]{:S(2)}) collective-permute-start(f32[2,1280]{1,0:T(2,128)S(1)} %broadcast_select_fusion.3), channel_id=1, source_target_pairs={{0,1},{1,0},{2,3},{3,2},{4,5},{5,4},{6,7},{7,6},{8,9},{9,8},{10,11... | collective-permute-start | bytes 30728 | tf_op jit(solution)/shard_map/ppermute | solution.py:122
  77.3 0.9 broadcast_in_dim.18
  78.1 3.6 %all-to-all-start.2 = ((bf16[16,36,512]{2,1,0:T(8,128)(2,1)}), bf16[16,36,512]{2,1,0:T(8,128)(2,1)S(1)}, u32[]{:S(2)}, u32[]{:S(2)}) async-start(bf16[16,36,512]{2,1,0:T(8,128)(2,1)} %broadcast_in_dim.18), calls=%async_computation.2 | async-start | bytes 1310720 | tf_op jit(solution)/shard_map/all_to_all | solution.py:93
  81.8 0.6 fusion.35
  82.4 11.9 %all-to-all-done.2 = bf16[16,36,512]{2,1,0:T(8,128)(2,1)S(1)} async-done(((bf16[16,36,512]{2,1,0:T(8,128)(2,1)}), bf16[16,36,512]{2,1,0:T(8,128)(2,1)S(1)}, u32[]{:S(2)}, u32[]{:S(2)}) %all-to-all-start.2) | async-done | bytes 589856 | tf_op jit(solution)/shard_map/all_to_all | solution.py:93
  94.5 2.1 %multiply_reduce_fusion = (f32[]{:T(128)}, f32[512,512]{0,1:T(8,128)}) fusion(f32[512]{0:T(512)S(1)} %bitcast.88, f32[512]{0:T(512)S(1)} %bitcast.86, bf16[512,512]{1,0:T(8,128)(2,1)S(1)} %bitcast.79, bf16[3,512,512]{2,1,0:T(8,128)(2,1)S(1)} %copy-done), kind=kOutput, calls=%fused_computation.26 | convolution fusion | flops 270270464 | bytes 2101252 | tf_op jit(solution)/shard_map/dot_general | solution.py:97
  96.6 1.7 %fusion.3 = f32[4,512]{1,0:T(4,128)S(1)} fusion(bf16[3,512,512]{2,1,0:T(8,128)(2,1)S(1)} %copy-done, s32[]{:T(128)S(6)} %select_n.115, bf16[1,512,512]{2,1,0:T(8,128)(2,1)S(1)} %slice-done, s32[]{:T(128)S(6)} %select_n.117, f32[512,512]{0,1:T(8,128)} %get-tuple-element.38, f32[512]{0:T(512)S(1)} %bitcast.89, f32[512]{0:T(512)S(1)} %bitcast.87), kind=kOutput, calls=%fused_computation.18 | convolution fusion | flops 5249024 | bytes 1589256 | tf_op jit(solution)/shard_map/dot_general | solution.py:103
  98.3 0.7 concatenate.31
  99.0 1.3 %collective-permute-start.3 = (f32[3,512]{1,0:T(4,128)S(1)}, f32[3,512]{1,0:T(4,128)S(1)}, u32[]{:S(2)}, u32[]{:S(2)}) collective-permute-start(f32[3,512]{1,0:T(4,128)S(1)} %concatenate.31), channel_id=1, source_target_pairs={{0,1},{1,0},{2,3},{3,2},{4,5},{5,4},{6,7},{7,6},{8,9},{9,8},{10,11... | collective-permute-start | bytes 18440 | tf_op jit(solution)/shard_map/ppermute | solution.py:111
  100.3 0.6 copy.35
  101.2 0.6 slice.189
  103.2 0.6 fusion.37
  (71 shorter events, 4.2 us)
Async XLA Ops:
  2.1 2.7 %copy-start.10 = (bf16[1024,512]{1,0:T(8,128)(2,1)S(1)}, bf16[1024,512]{1,0:T(8,128)(2,1)}, u32[]{:S(2)}) copy-start(bf16[1024,512]{1,0:T(8,128)(2,1)} %param.7) | copy-start | bytes 3145732
  4.8 6.5 %copy-start.6 = (bf16[512,512]{0,1:T(8,128)(2,1)}, bf16[512,512]{0,1:T(8,128)(2,1)S(1)}, u32[]{:S(2)}) copy-start(bf16[512,512]{0,1:T(8,128)(2,1)S(1)} %convolution_convert_fusion.2) | copy-start | bytes 1572868
  4.8 1.4 %copy-start.8 = (bf16[1024,512]{1,0:T(8,128)(2,1)S(1)}, bf16[1024,512]{1,0:T(8,128)(2,1)}, u32[]{:S(2)}) copy-start(bf16[1024,512]{1,0:T(8,128)(2,1)} %param.9) | copy-start | bytes 3145732
  6.2 13.9 %copy-start.1 = (bf16[512,512]{0,1:T(8,128)(2,1)}, bf16[512,512]{0,1:T(8,128)(2,1)S(1)}, u32[]{:S(2)}) copy-start(bf16[512,512]{0,1:T(8,128)(2,1)S(1)} %convolution_convert_fusion.3) | copy-start | bytes 1572868
  6.2 1.4 %copy-start.9 = (bf16[1024,512]{1,0:T(8,128)(2,1)S(1)}, bf16[1024,512]{1,0:T(8,128)(2,1)}, u32[]{:S(2)}) copy-start(bf16[1024,512]{1,0:T(8,128)(2,1)} %param.8) | copy-start | bytes 3145732
  7.6 3.7 %copy-start.2 = (bf16[512,512]{0,1:T(8,128)(2,1)}, bf16[512,512]{0,1:T(8,128)(2,1)S(1)}, u32[]{:S(2)}) copy-start(bf16[512,512]{0,1:T(8,128)(2,1)S(1)} %convolution_convert_fusion.1) | copy-start | bytes 1572868
  11.4 6.0 %copy-start = (bf16[3,512,512]{2,1,0:T(8,128)(2,1)S(1)}, bf16[3,512,512]{2,1,0:T(8,128)(2,1)}, u32[]{:S(2)}) copy-start(bf16[3,512,512]{2,1,0:T(8,128)(2,1)} %param.12) | copy-start | bytes 4718596
  11.4 6.0 %copy-start.7 = (f32[2,3,512]{2,0,1:T(2,128)S(1)}, f32[2,3,512]{2,0,1:T(2,128)}, u32[]{:S(2)}) copy-start(f32[2,3,512]{2,0,1:T(2,128)} %param.13) | copy-start | bytes 36868
  14.2 6.5 %collective-permute-start = (bf16[512,1280]{0,1:T(8,128)(2,1)}, bf16[512,1280]{0,1:T(8,128)(2,1)}, u32[]{:S(2)}, u32[]{:S(2)}) collective-permute-start(bf16[512,1280]{0,1:T(8,128)(2,1)} %broadcast_select_fusion), channel_id=1, source_target_pairs={{0,1},{1,0},{2,3},{3,2},{4,5},{5,4},{6,7},{7,6},{8,9},{9,8},{10,11... | collective-permute-start | bytes 3932168 | tf_op jit(solution)/shard_map/ppermute | solution.py:56
  17.8 1.9 %copy-start.4 = (bf16[512,512]{0,1:T(8,128)(2,1)S(1)}, bf16[512,512]{0,1:T(8,128)(2,1)}, u32[]{:S(2)}) copy-start(bf16[512,512]{0,1:T(8,128)(2,1)} %convolution_convert_fusion) | copy-start | bytes 1572868
  20.2 1.0 %copy-start.3 = (bf16[512,512]{0,1:T(8,128)(2,1)S(1)}, bf16[512,512]{0,1:T(8,128)(2,1)}, u32[]{:S(2)}) copy-start(bf16[512,512]{0,1:T(8,128)(2,1)} %copy-done.2) | copy-start | bytes 1572868
  20.2 1.2 %copy-start.5 = (bf16[512,512]{0,1:T(8,128)(2,1)S(1)}, bf16[512,512]{0,1:T(8,128)(2,1)}, u32[]{:S(2)}) copy-start(bf16[512,512]{0,1:T(8,128)(2,1)} %convolution_convert_fusion.4) | copy-start | bytes 1572868
  24.8 26.7 %all-to-all-start = ((bf16[16,32,1280]{2,1,0:T(8,128)(2,1)}), bf16[16,32,1280]{2,1,0:T(8,128)(2,1)S(1)}, u32[]{:S(2)}, u32[]{:S(2)}) async-start(bf16[16,32,1280]{2,1,0:T(8,128)(2,1)} %bitcast.1), calls=%async_computation | async-start | bytes 2621440 | tf_op jit(solution)/shard_map/all_to_all | solution.py:71
  30.2 1.3 %collective-permute-start.1 = (f32[3,512]{1,0:T(4,128)S(1)}, f32[3,512]{1,0:T(4,128)S(1)}, u32[]{:S(2)}, u32[]{:S(2)}) collective-permute-start(f32[3,512]{1,0:T(4,128)S(1)} %pad_maximum_fusion.5), channel_id=1, source_target_pairs={{0,1},{1,0},{2,3},{3,2},{4,5},{5,4},{6,7},{7,6},{8,9},{9,8},{10,11... | collective-permute-start | bytes 18440 | tf_op jit(solution)/shard_map/ppermute | solution.py:67
  52.6 21.3 %all-to-all-start.1 = ((bf16[8,42,512]{2,1,0:T(8,128)(2,1)}), bf16[8,42,512]{2,1,0:T(8,128)(2,1)S(1)}, u32[]{:S(2)}, u32[]{:S(2)}) async-start(bf16[8,42,512]{2,1,0:T(8,128)(2,1)} %pad_maximum_fusion.2), calls=%async_computation.1 | async-start | bytes 786432 | tf_op jit(solution)/shard_map/all_to_all | solution.py:82
  74.5 7.3 %collective-permute-start.2 = (f32[2,1280]{1,0:T(2,128)S(1)}, f32[2,1280]{1,0:T(2,128)S(1)}, u32[]{:S(2)}, u32[]{:S(2)}) collective-permute-start(f32[2,1280]{1,0:T(2,128)S(1)} %broadcast_select_fusion.3), channel_id=1, source_target_pairs={{0,1},{1,0},{2,3},{3,2},{4,5},{5,4},{6,7},{7,6},{8,9},{9,8},{10,11... | collective-permute-start | bytes 30728 | tf_op jit(solution)/shard_map/ppermute | solution.py:122
  78.1 16.2 %all-to-all-start.2 = ((bf16[16,36,512]{2,1,0:T(8,128)(2,1)}), bf16[16,36,512]{2,1,0:T(8,128)(2,1)S(1)}, u32[]{:S(2)}, u32[]{:S(2)}) async-start(bf16[16,36,512]{2,1,0:T(8,128)(2,1)} %broadcast_in_dim.18), calls=%async_computation.2 | async-start | bytes 1310720 | tf_op jit(solution)/shard_map/all_to_all | solution.py:93
  94.5 2.1 %slice-start = ((bf16[3,512,512]{2,1,0:T(8,128)(2,1)}), bf16[1,512,512]{2,1,0:T(8,128)(2,1)S(1)}, s32[]{:S(2)}) async-start(bf16[3,512,512]{2,1,0:T(8,128)(2,1)} %param.12), calls=%async_computation.3 | async-start | bytes 1048576 | tf_op jit(solution)/shard_map/slice | solution.py:63
  99.0 2.2 %collective-permute-start.3 = (f32[3,512]{1,0:T(4,128)S(1)}, f32[3,512]{1,0:T(4,128)S(1)}, u32[]{:S(2)}, u32[]{:S(2)}) collective-permute-start(f32[3,512]{1,0:T(4,128)S(1)} %concatenate.31), channel_id=1, source_target_pairs={{0,1},{1,0},{2,3},{3,2},{4,5},{5,4},{6,7},{7,6},{8,9},{9,8},{10,11... | collective-permute-start | bytes 18440 | tf_op jit(solution)/shard_map/ppermute | solution.py:111

commit v2 on v0

v2 whole, which is shorter than its diff:
```python
import functools

import jax
import jax.numpy as jnp
from jax import lax
from jax.experimental import pallas as pl
from jax.experimental.pallas import tpu as pltpu
from jax.sharding import PartitionSpec as P

LEN = 128
NX, NY, NZ, NC = 4, 4, 8, 2
NXY = NX * NY
D = 512
HALF = D // 2
PAIR = 2
WIDE = NXY * PAIR
DEEP = NZ // PAIR
ROWS = D // WIDE
COLS = D + D + HALF
LANES = 128
FR = ROWS // DEEP
GT, FT = D // LANES, (D + HALF) // LANES
MB = 1 << 20

decay = 0.8
damping = 0.001
kl_clip = 0.001
learn_rate = 7e-05

f32, bf16 = jnp.float32, jnp.bfloat16


def device(xy, z, c):
    return (xy * NZ + z) * NC + c


SWAP = [(d, d ^ 1) for d in range(NXY * NZ * NC)]
WIDE_GROUPS = [
    [device(i, k * PAIR + l, c) for i in range(NXY) for l in range(PAIR)]
    for k in range(DEEP)
    for c in range(NC)
]
DEEP_GROUPS = [
    [device(i, k * PAIR + l, c) for k in range(DEEP)] for i in range(NXY) for l in range(PAIR) for c in range(NC)
]
HOME = [
    (device(i, k * PAIR + l, c), device(i, l * DEEP + k, c))
    for i in range(NXY)
    for k in range(DEEP)
    for l in range(PAIR)
    for c in range(NC)
]
HOME_CROSS = [(a, b ^ 1) for a, b in HOME]

VMEM = pl.BlockSpec(memory_space=pltpu.VMEM)
SMEM = pl.BlockSpec(memory_space=pltpu.SMEM)
ANY = pl.BlockSpec(memory_space=pl.ANY)


def call(kernel, outs, in_specs, scratch=(), limit=16, flops=0, moved=0):
    return pl.pallas_call(
        kernel,
        out_shape=outs,
        in_specs=in_specs,
        out_specs=jax.tree.map(lambda _: VMEM, outs),
        scratch_shapes=list(scratch),
        compiler_params=pltpu.CompilerParams(vmem_limit_bytes=limit * MB),
        cost_estimate=pl.CostEstimate(flops=flops, bytes_accessed=moved, transcendentals=0),
    )


def shape(dims, dtype):
    return jax.ShapeDtypeStruct(dims, dtype)


def dot(a, b):
    return jnp.dot(a, b, preferred_element_type=f32)


def apply_mask(buf, slot, start, width):
    position = lax.broadcasted_iota(jnp.int32, (LEN, LANES), 0)
    for u in range(start.shape[0]):
        keep = None
        for m in range(start.shape[1]):
            s = start[u, m]
            outside = (position < s) | (position >= s + width[u, m])
            keep = outside if keep is None else keep & outside
        keep = jnp.where(keep, 1.0, 0.0).astype(bf16)
        for j in range(GT):
            view = (slot, pl.ds(u * LEN, LEN), pl.ds(j * LANES, LANES))
            buf[view] = buf[view] * keep


def grams(pick, start, width, x0, xk, xv, out, buf, sem):
    first = pltpu.make_async_copy(x0, buf.at[0], sem.at[0])
    first.start()

    @pl.when(pick == 0)
    def _():
        pltpu.make_async_copy(xk, buf.at[1], sem.at[1]).start()

    @pl.when(pick != 0)
    def _():
        pltpu.make_async_copy(xv, buf.at[1], sem.at[1]).start()

    first.wait()
    apply_mask(buf, 0, start, width)
    pltpu.make_async_copy(xk, buf.at[1], sem.at[1]).wait()
    apply_mask(buf, 1, start, width)
    block = 256
    half = pl.ds(pl.multiple_of(pick * HALF, HALF), HALF)
    for r in range(D // block):
        places = pl.ds(r * (block // ROWS), block // ROWS)

        def put(value, begin):
            size = value.shape[1]
            out[places, :, pl.ds(begin, size)] = value.astype(bf16).reshape(block // ROWS, ROWS, size)

        left = buf[0, :, pl.ds(r * block, block)].T
        put(dot(left, buf[1]), 0)
        put(dot(left, buf[0, :, half]), 2 * D)
        left = buf[1, :, pl.ds(r * block, block)].T
        put(dot(left, buf[1]), D)


def theirs_kernel(core, start, width, x0, xk, xv, out, buf, sem):
    grams(1 - core[0], start, width, x0, xk, xv, out, buf, sem)


def mine_kernel(share, core, start, width, x0, xk, xv, other, bases, out, keep_lam, send_lam, buf, sem):
    c = core[0]
    grams(c, start, width, x0, xk, xv, out, buf, sem)

    def image(source, begin, size, basis):
        return dot(source[:, :, pl.ds(begin, size)].reshape(D, size), basis)

    def values(index, product):
        return jnp.sum(bases[index].astype(f32) * product, axis=0, keepdims=True) * share

    near = pl.ds(pl.multiple_of(c * HALF, HALF), HALF)
    far = pl.ds(pl.multiple_of((1 - c) * HALF, HALF), HALF)
    lam0 = values(0, image(out, 2 * D, HALF, bases[0, near, :]) + image(other, 2 * D, HALF, bases[0, far, :]))
    keep_lam[0:1, :] = lam0
    send_lam[0:1, :] = lam0
    keep_lam[1:2, :] = values(1 + c, image(out, D, D, bases[1 + c]))
    send_lam[1:2, :] = values(2 - c, image(other, D, D, bases[2 - c]))


def split(value):
    high = value.astype(bf16)
    return high.astype(f32), value - high.astype(f32)


def lam_rows(lam):
    high, low = split(lam)
    pieces = []
    for j in range(GT):
        tile = slice(j * LANES, (j + 1) * LANES)
        pieces += [high[:, tile], low[:, tile]]
    return jnp.concatenate(pieces, axis=0)


def read_lam(rows):
    tiles = [rows[4 * j : 4 * j + 2] + rows[4 * j + 2 : 4 * j + 4] for j in range(GT)]
    return jnp.concatenate(tiles, axis=1)


LAMR = 4 * GT
TAIL = ((FT * FR + LAMR + 15) // 16) * 16
DEEP_ROWS = GT * ROWS + TAIL
GATHER_ROWS = GT * ROWS + LAMR


def pack_kernel(parts, keep_lam, send_lam, out):
    total = parts[0].astype(f32)
    for i in range(1, WIDE):
        total = total + parts[i].astype(f32)
    lam = lam_rows(keep_lam[...] + send_lam[...])
    for j in range(GT):
        tile = total[:, j * LANES : (j + 1) * LANES].astype(bf16)
        for k in range(DEEP):
            out[k, pl.ds(j * ROWS, ROWS), :] = tile
    pad = jnp.zeros((TAIL - FT * FR - LAMR, LANES), f32)
    for k in range(DEEP):
        rows = total[k * FR : (k + 1) * FR]
        pieces = [rows[:, D + t * LANES : D + (t + 1) * LANES] for t in range(FT)]
        out[k, pl.ds(GT * ROWS, TAIL), :] = jnp.concatenate(pieces + [lam, pad], axis=0).astype(bf16)


def rotate_kernel(place, got, basis, out, stay, cross):
    total = got[0].astype(f32)
    for i in range(1, DEEP):
        total = total + got[i].astype(f32)
    grad = jnp.concatenate([total[j * ROWS : (j + 1) * ROWS] for j in range(GT)], axis=1)
    rot = dot(grad.astype(bf16), basis[...]).astype(bf16)
    base = GT * ROWS
    lam = lam_rows(read_lam(total[base + FT * FR : base + FT * FR + LAMR])).astype(bf16)
    for j in range(GT):
        tile = rot[:, j * LANES : (j + 1) * LANES]
        for i in range(WIDE):
            out[i, pl.ds(j * ROWS, ROWS), :] = tile
    for i in range(WIDE):
        out[i, pl.ds(base, LAMR), :] = lam
    k, c = place[0], place[1]
    rows = grad[0:FR]
    for other in range(1, DEEP):
        rows = jnp.where(k == other, grad[other * FR : (other + 1) * FR], rows)
    factors = [total[base + t * FR : base + (t + 1) * FR] for t in range(FT)]
    rows = jnp.concatenate([rows] + factors, axis=1)
    low, high = rows[0:2], rows[2:4]
    stay[...] = jnp.where(c == 0, low, high)
    cross[...] = jnp.where(c == 0, high, low)


def solve_kernel(got, basis_in_t, basis_out, rows_in, stay, cross, scaled):
    base = GT * ROWS
    lam = got[0, pl.ds(base, LAMR), :].astype(f32)
    for i in range(1, WIDE):
        lam = lam + got[i, pl.ds(base, LAMR), :].astype(f32)
    lam = read_lam(lam)
    column = jnp.broadcast_to(lam[0:1], (8, D)).T[:, 0:1]
    column = jnp.broadcast_to(column, (D, LANES))
    curve = jnp.zeros((8, LANES), f32)
    for j in range(GT):
        rot = got[:, pl.ds(j * ROWS, ROWS), :].reshape(D, LANES)
        rotated = dot(basis_in_t[...], rot)
        low = (rotated / (column * lam[1:2, j * LANES : (j + 1) * LANES] + damping)).astype(bf16)
        scaled[:, pl.ds(j * LANES, LANES)] = low
        curve = curve + jnp.sum((low.astype(f32) * rotated).reshape(D // 8, 8, LANES), axis=0)
    curve = jnp.sum(jnp.sum(curve, axis=1, keepdims=True), axis=0, keepdims=True)
    back = dot(rows_in[...], scaled[...]).astype(bf16)
    prec = lax.dot_general(back, basis_out[...], (((1,), (1,)), ((), ())), preferred_element_type=f32)
    prec = prec.astype(bf16).astype(f32)
    curve = jnp.broadcast_to(curve, (6, D))
    stay[...] = jnp.concatenate([prec[0:2], curve], axis=0)
    cross[...] = jnp.concatenate([prec[2:4], curve], axis=0)


def finish_kernel(scale, place, mine, theirs, same, cross, old, new_factors, gradients, updates):
    first = place[1] == 0
    curve = mine[2:3, :] + theirs[2:3, :]
    factor = jnp.sqrt(kl_clip / (learn_rate * learn_rate * curve))
    own = mine[0:2, :] * factor
    their = theirs[0:2, :] * factor
    updates[0] = jnp.where(first, own, their).astype(bf16)
    updates[1] = jnp.where(first, their, own).astype(bf16)
    rows0 = jnp.where(first, same[...], cross[...])
    rows1 = jnp.where(first, cross[...], same[...])
    gradients[:, 0, :] = rows0[:, :D]
    gradients[:, 1, :] = rows1[:, :D]
    batch = (
        jnp.concatenate([rows0[:, 2 * D :], rows1[:, 2 * D :]], axis=1),
        rows0[:, D : 2 * D],
        rows1[:, D : 2 * D],
    )
    for f in range(3):
        new_factors[:, f, :] = decay * old[:, f, :] + scale * batch[f]


def exchange(value, groups):
    return lax.all_to_all(value, "dp", 0, 0, axis_index_groups=groups, tiled=True)


def body(activations, grad_key, grad_value, time_start, time_width, bases, old_factors):
    index = lax.axis_index("dp").astype(jnp.int32)
    core = index % NC
    first = core == 0
    z = (index // NC) % NZ
    place = jnp.stack([z // PAIR, core])
    tokens_here = activations.shape[0]
    share = (1.0 - decay) / (tokens_here * lax.axis_size("dp"))

    inputs = (core[None], time_start, time_width, activations, grad_key, grad_value)
    specs = [SMEM, SMEM, SMEM, ANY, ANY, ANY]
    scratch = [pltpu.VMEM((2, tokens_here, D), bf16), pltpu.SemaphoreType.DMA((2,))]
    partial = shape((WIDE, ROWS, COLS), bf16)
    work = 2 * D * tokens_here * COLS
    with jax.named_scope("grams_theirs"):
        other = call(theirs_kernel, partial, specs, scratch, flops=work, moved=4 * MB)(*inputs)
    received = lax.ppermute(other, "dp", SWAP)
    lam_shape = shape((2, D), f32)
    with jax.named_scope("grams_mine"):
        mine, keep_lam, send_lam = call(
            functools.partial(mine_kernel, share),
            (partial, lam_shape, lam_shape),
            specs + [VMEM, VMEM],
            scratch,
            limit=24,
            flops=work,
            moved=6 * MB,
        )(*inputs, other, bases)
    old_lam = []
    my_rows = lax.dynamic_slice_in_dim(bases, 2 * index, 2, 1).astype(f32)
    for f in range(3):
        old_image = jnp.dot(old_factors[:, f, :], bases[f].astype(f32), precision=lax.Precision.HIGHEST)
        old_lam.append(decay * jnp.sum(my_rows[f] * old_image, axis=0))
    keep_lam = keep_lam + jnp.stack([old_lam[0], jnp.where(first, old_lam[1], old_lam[2])])
    send_lam = send_lam + jnp.stack([old_lam[0], jnp.where(first, old_lam[2], old_lam[1])])
    sent_lam = lax.ppermute(send_lam, "dp", SWAP)

    with jax.named_scope("chip_sum"):
        chip = (mine.astype(f32) + received.astype(f32)).astype(bf16)
    with jax.named_scope("wide_sum"):
        parts = exchange(chip, WIDE_GROUPS)
    with jax.named_scope("pack"):
        packed = call(pack_kernel, shape((DEEP, DEEP_ROWS, LANES), bf16), [VMEM] * 3)(parts, keep_lam, sent_lam)
    with jax.named_scope("deep_sum"):
        got = exchange(packed, DEEP_GROUPS)
    basis_out = lax.dynamic_index_in_dim(bases, 1 + core, 0, keepdims=False)
    row_shape = shape((2, COLS), f32)
    with jax.named_scope("rotate"):
        spread, stay, cross = call(
            rotate_kernel,
            (shape((WIDE, GATHER_ROWS, LANES), bf16), row_shape, row_shape),
            [SMEM, VMEM, VMEM],
        )(place, got, basis_out)
    with jax.named_scope("gather"):
        gathered = exchange(spread, WIDE_GROUPS)
    same = lax.ppermute(stay, "dp", HOME)
    cross = lax.ppermute(cross, "dp", HOME_CROSS)
    rows_in = lax.dynamic_slice_in_dim(bases[0], (index // NC) * FR, FR, 0)
    rows_in = jnp.where(first, rows_in, jnp.roll(rows_in, 2, axis=0))
    rows_in = jnp.pad(rows_in, ((0, 16 - FR), (0, 0)))
    result = shape((8, D), f32)
    with jax.named_scope("solve"):
        own, their = call(solve_kernel, (result, result), [VMEM] * 4, [pltpu.VMEM((D, D), bf16)])(
            gathered, bases[0].T, basis_out, rows_in
        )
    got_own = lax.ppermute(their, "dp", SWAP)
    with jax.named_scope("finish"):
        return call(
            functools.partial(finish_kernel, share),
            (shape((2, 3, D), f32), shape((2, 2, D), f32), shape((2, 2, D), bf16)),
            [SMEM] + [VMEM] * 5,
        )(place, own, got_own, same, cross, old_factors)


def solution(mesh):
    in_specs = (
        P("dp", None),
        P("dp", None),
        P("dp", None),
        P("dp", None),
        P("dp", None),
        P(),
        P("dp", None, None),
    )
    out_specs = (P("dp", None, None), P("dp", None, None), P(None, "dp", None))
    return jax.shard_map(body, mesh=mesh, in_specs=in_specs, out_specs=out_specs, check_vma=False)
```

time: 751 us -> 87.9 us (0.12)
  the two profiles are of different devices: /device:TPU:1 before, /device:TPU:65 now
where the time goes in v2:
time: 87.9 us; the launch traced here: 87.3 us
  waiting for transfers between devices  38.5 us (44%)
  starting transfers between devices  28.1 us (32%)
  Pallas kernels  11.2 us (13%)
  local copies, waits for them, and re-layouts  6.16 us (7%)
  other arithmetic  1.52 us (2%)
  matrix products  0.99 us (1%)
    all_to_all x3, waiting for transfers between devices, exchange(): lax.all_to_all(value, 'dp', 0, 0, axis_index_groups=groups, tiled=True)  33.2 us
    all_to_all x3, starting transfers between devices, exchange(): lax.all_to_all(value, 'dp', 0, 0, axis_index_groups=groups, tiled=True)  19.2 us
    unnamed x17, local copies, waits for them, and re-layouts  5.2 us
    ppermute x1, starting transfers between devices, body(): got_own = lax.ppermute(their, 'dp', SWAP)  3.85 us
    pallas_call x1, Pallas kernels, body(): call(functools.partial(mine_kernel, share), (partial, lam_shape, lam_shap...  3.67 us
    ppermute x1, starting transfers between devices, body(): same = lax.ppermute(stay, 'dp', HOME)  2.96 us
    pallas_call x1, Pallas kernels, body(): call(theirs_kernel, partial, specs, scratch, flops=work, moved=4 * MB)  2.83 us
    ppermute x1, waiting for transfers between devices, body(): same = lax.ppermute(stay, 'dp', HOME)  2.65 us
  transfers between devices with their start and end apart: 8, of which 6 were waited for; matrix products, arithmetic and copies ran while one was open for 2% of the time, Pallas kernels for 4%

profile of v2, /device:TPU:65, one launch (start us, length us, event | category | flops | bytes accessed | tf_op | source)
XLA Modules:
  0.0 87.3 jit_solution(7918856307324257230)
XLA Ops:
  0.6 0.8 copy.12.start
  1.4 0.8 copy.13.width
  2.1 1.2 %copy-done.1 = bf16[1024,512]{1,0:T(8,128)(2,1)S(1)} copy-done((bf16[1024,512]{1,0:T(8,128)(2,1)S(1)}, bf16[1024,512]{1,0:T(8,128)(2,1)}, u32[]{:S(2)}) %copy-start.1) | copy-done | bytes 1048600
  3.4 1.2 %copy-done.3 = bf16[1024,512]{1,0:T(8,128)(2,1)S(1)} copy-done((bf16[1024,512]{1,0:T(8,128)(2,1)S(1)}, bf16[1024,512]{1,0:T(8,128)(2,1)}, u32[]{:S(2)}) %copy-start.3) | copy-done | bytes 1048600
  4.6 1.2 %copy-done.5 = bf16[1024,512]{1,0:T(8,128)(2,1)S(1)} copy-done((bf16[1024,512]{1,0:T(8,128)(2,1)S(1)}, bf16[1024,512]{1,0:T(8,128)(2,1)}, u32[]{:S(2)}) %copy-start.5) | copy-done | bytes 1048600
  5.8 2.8 %grams_theirs.1.other = bf16[32,16,1280]{2,1,0:T(8,128)(2,1)S(1)} custom-call(s32[1]{0:T(128)} %bitcast.1.core, s32[8,2]{1,0:T(8,128)S(1)} %copy.12.start, s32[8,2]{1,0:T(8,128)S(1)} %copy.13.width, bf16[1024,512]{1,0:T(8,128)(2,1)S(1)} %copy-done.1, bf16[1024,512]{1,0:T(8,128)(2,1)S(1)} %copy-done.3, bf16[1024,512]{1,0:T(8,128)(2,1)S(1)} %copy-done.5), custom_call_target="tpu_custom_call" | custom-call | flops 1342177280 | bytes 4194304 | tf_op jit(solution)/shard_map/grams_theirs/pallas_call | solution.py:279
  8.7 0.8 collective-permute-start
  9.4 3.7 %grams_mine.1 = (bf16[32,16,1280]{2,1,0:T(8,128)(2,1)S(1)}, f32[2,512]{1,0:T(2,128)S(1)}, f32[2,512]{1,0:T(2,128)S(1)}) custom-call(s32[1]{0:T(128)} %bitcast.1.core, s32[8,2]{1,0:T(8,128)S(1)} %copy.12.start, s32[8,2]{1,0:T(8,128)S(1)} %copy.13.width, bf16[1024,512]{1,0:T(8,128)(2,1)S(1)} %copy-done.2, bf16[1024,512]{1,0:T(8,128)(2,1)S(1)} %copy-done.4, ...), custom_call_target="tpu_custom_call" | custom-call | flops 1342177280 | bytes 6291456 | tf_op jit(solution)/shard_map/grams_mine/pallas_call | solution.py:283
  13.1 1.4 %add_convert_fusion = bf16[32,16,1280]{2,1,0:T(8,128)(2,1)} fusion(bf16[32,16,1280]{2,1,0:T(8,128)(2,1)S(1)} %collective-permute-done, bf16[32,16,1280]{2,1,0:T(8,128)(2,1)S(1)} %get-tuple-element.11), kind=kLoop, calls=%fused_computation | loop fusion | flops 2621440 | bytes 3932160 | tf_op jit(solution)/shard_map/chip_sum/convert_element_type | solution.py:302
  14.5 8.5 %all-to-all-start = ((bf16[32,16,1280]{2,1,0:T(8,128)(2,1)}), bf16[32,16,1280]{2,1,0:T(8,128)(2,1)S(1)}, u32[]{:S(2)}, u32[]{:S(2)}) async-start(bf16[32,16,1280]{2,1,0:T(8,128)(2,1)} %add_convert_fusion), calls=%async_computation | async-start | bytes 2621440 | tf_op jit(solution)/shard_map/wide_sum/all_to_all | solution.py:261
  23.1 0.3 fusion
  23.4 0.3 fusion.2
  23.8 0.3 fusion.1
  24.1 0.4 collective-permute-start.1
  24.5 0.9 collective-permute-done.1.send_lam
  25.4 17.8 %all-to-all-done.parts = bf16[32,16,1280]{2,1,0:T(8,128)(2,1)S(1)} async-done(((bf16[32,16,1280]{2,1,0:T(8,128)(2,1)}), bf16[32,16,1280]{2,1,0:T(8,128)(2,1)S(1)}, u32[]{:S(2)}, u32[]{:S(2)}) %all-to-all-start) | async-done | bytes 1310752 | tf_op jit(solution)/shard_map/wide_sum/all_to_all | solution.py:261
  43.2 0.9 pack.1
  44.1 6.6 %all-to-all-start.1 = ((bf16[4,112,128]{2,1,0:T(8,128)(2,1)}), bf16[4,112,128]{2,1,0:T(8,128)(2,1)S(1)}, u32[]{:S(2)}, u32[]{:S(2)}) async-start(bf16[4,112,128]{2,1,0:T(8,128)(2,1)} %pack.1), calls=%async_computation.1 | async-start | bytes 229376 | tf_op jit(solution)/shard_map/deep_sum/all_to_all | solution.py:261
  50.7 0.1 fusion.17
  51.0 4.8 %all-to-all-done.1.got = bf16[4,112,128]{2,1,0:T(8,128)(2,1)S(1)} async-done(((bf16[4,112,128]{2,1,0:T(8,128)(2,1)}), bf16[4,112,128]{2,1,0:T(8,128)(2,1)S(1)}, u32[]{:S(2)}, u32[]{:S(2)}) %all-to-all-start.1) | async-done | bytes 114720 | tf_op jit(solution)/shard_map/deep_sum/all_to_all | solution.py:261
  55.8 1.6 %rotate.1 = (bf16[32,80,128]{2,1,0:T(8,128)(2,1)}, f32[2,1280]{1,0:T(2,128)S(1)}, f32[2,1280]{1,0:T(2,128)S(1)}) custom-call(s32[2]{0:T(128)S(1)} %pad_add_fusion.place, bf16[4,112,128]{2,1,0:T(8,128)(2,1)S(1)} %all-to-all-done.1.got, bf16[512,512]{1,0:T(8,128)(2,1)S(1)} %get-tuple-element.24.basis.basis_out), custom_call_target="tpu_custom_call" | custom-call | tf_op jit(solution)/shard_map/rotate/pallas_call | solution.py:312
  57.4 4.1 %all-to-all-start.2 = ((bf16[32,80,128]{2,1,0:T(8,128)(2,1)}), bf16[32,80,128]{2,1,0:T(8,128)(2,1)S(1)}, u32[]{:S(2)}, u32[]{:S(2)}) async-start(bf16[32,80,128]{2,1,0:T(8,128)(2,1)} %get-tuple-element.14), calls=%async_computation.2 | async-start | bytes 1310720 | tf_op jit(solution)/shard_map/gather/all_to_all | solution.py:261
  61.5 0.2 copy.14.basis_in_t
  61.8 10.6 %all-to-all-done.2.got = bf16[32,80,128]{2,1,0:T(8,128)(2,1)S(1)} async-done(((bf16[32,80,128]{2,1,0:T(8,128)(2,1)}), bf16[32,80,128]{2,1,0:T(8,128)(2,1)S(1)}, u32[]{:S(2)}, u32[]{:S(2)}) %all-to-all-start.2) | async-done | bytes 655392 | tf_op jit(solution)/shard_map/gather/all_to_all | solution.py:261
  72.3 1.1 %solve.1 = (f32[8,512]{1,0:T(8,128)S(1)}, f32[8,512]{1,0:T(8,128)S(1)}) custom-call(bf16[32,80,128]{2,1,0:T(8,128)(2,1)S(1)} %all-to-all-done.2.got, bf16[512,512]{1,0:T(8,128)(2,1)S(1)} %copy.14.basis_in_t, bf16[512,512]{1,0:T(8,128)(2,1)S(1)} %get-tuple-element.24.basis.basis_out, bf16[16,512]{1,0:T(8,128)(2,1)S(1)} %pad.4.rows_in), custom_call_target="tpu_custom_call" | custom-call | tf_op jit(solution)/shard_map/solve/pallas_call | solution.py:326
  73.4 3.9 %collective-permute-start.2 = (f32[8,512]{1,0:T(8,128)S(1)}, f32[8,512]{1,0:T(8,128)S(1)}, u32[]{:S(2)}, u32[]{:S(2)}) collective-permute-start(f32[8,512]{1,0:T(8,128)S(1)} %get-tuple-element.16), channel_id=1, source_target_pairs={{0,1},{1,0},{2,3},{3,2},{4,5},{5,4},{6,7},{7,6},{8,9},{9,8},{10,11... | collective-permute-start | bytes 49160 | tf_op jit(solution)/shard_map/ppermute | solution.py:329
  77.3 3.0 %collective-permute-start.3 = (f32[2,1280]{1,0:T(2,128)S(1)}, f32[2,1280]{1,0:T(2,128)S(1)}, u32[]{:S(2)}, u32[]{:S(2)}) collective-permute-start(f32[2,1280]{1,0:T(2,128)S(1)} %get-tuple-element.17), channel_id=1, source_target_pairs={{0,0},{1,1},{2,8},{3,9},{4,2},{5,3},{6,10},{7,11},{8,4},{9,5},{10,... | collective-permute-start | bytes 30728 | tf_op jit(solution)/shard_map/ppermute | solution.py:319
  80.2 0.9 %collective-permute-start.4 = (f32[2,1280]{1,0:T(2,128)S(1)}, f32[2,1280]{1,0:T(2,128)S(1)}, u32[]{:S(2)}, u32[]{:S(2)}) collective-permute-start(f32[2,1280]{1,0:T(2,128)S(1)} %get-tuple-element.18), channel_id=1, source_target_pairs={{0,1},{1,0},{2,9},{3,8},{4,3},{5,2},{6,11},{7,10},{8,5},{9,4},{10,... | collective-permute-start | bytes 30728 | tf_op jit(solution)/shard_map/ppermute | solution.py:320
  81.1 2.7 %collective-permute-done.3.same = f32[2,1280]{1,0:T(2,128)S(1)} collective-permute-done((f32[2,1280]{1,0:T(2,128)S(1)}, f32[2,1280]{1,0:T(2,128)S(1)}, u32[]{:S(2)}, u32[]{:S(2)}) %collective-permute-start.3) | collective-permute-done | bytes 10272 | tf_op jit(solution)/shard_map/ppermute | solution.py:319
  83.8 1.8 %collective-permute-done.4.cross = f32[2,1280]{1,0:T(2,128)S(1)} collective-permute-done((f32[2,1280]{1,0:T(2,128)S(1)}, f32[2,1280]{1,0:T(2,128)S(1)}, u32[]{:S(2)}, u32[]{:S(2)}) %collective-permute-start.4) | collective-permute-done | bytes 10272 | tf_op jit(solution)/shard_map/ppermute | solution.py:320
  85.6 1.2 %finish.1 = (f32[2,3,512]{2,1,0:T(4,128)S(1)}, f32[2,2,512]{2,1,0:T(2,128)}, bf16[2,2,512]{2,1,0:T(2,128)(2,1)}) custom-call(s32[2]{0:T(128)S(1)} %pad_add_fusion.place, f32[8,512]{1,0:T(8,128)S(1)} %get-tuple-element.15.mine, f32[8,512]{1,0:T(8,128)S(1)} %collective-permute-done.2.theirs, f32[2,1280]{1,0:T(2,128)S(1)} %collective-permute-done.3.same, ...), custom_call_target="tpu_custom_call" | custom-call | tf_op jit(solution)/shard_map/finish/pallas_call | solution.py:331
  86.7 0.6 copy.16
  (22 shorter events, 0.2 us)
Async XLA Ops:
  2.1 1.2 %copy-start.1 = (bf16[1024,512]{1,0:T(8,128)(2,1)S(1)}, bf16[1024,512]{1,0:T(8,128)(2,1)}, u32[]{:S(2)}) copy-start(bf16[1024,512]{1,0:T(8,128)(2,1)} %x0.3) | copy-start | bytes 3145732
  3.4 1.2 %copy-start.3 = (bf16[1024,512]{1,0:T(8,128)(2,1)S(1)}, bf16[1024,512]{1,0:T(8,128)(2,1)}, u32[]{:S(2)}) copy-start(bf16[1024,512]{1,0:T(8,128)(2,1)} %xk.3) | copy-start | bytes 3145732
  4.6 1.2 %copy-start.5 = (bf16[1024,512]{1,0:T(8,128)(2,1)S(1)}, bf16[1024,512]{1,0:T(8,128)(2,1)}, u32[]{:S(2)}) copy-start(bf16[1024,512]{1,0:T(8,128)(2,1)} %xv.3) | copy-start | bytes 3145732
  5.8 3.6 %copy-start = (bf16[3,512,512]{2,1,0:T(8,128)(2,1)S(1)}, bf16[3,512,512]{2,1,0:T(8,128)(2,1)}, u32[]{:S(2)}) copy-start(bf16[3,512,512]{2,1,0:T(8,128)(2,1)} %bases.1) | copy-start | bytes 4718596
  5.8 3.6 %copy-start.2 = (bf16[1024,512]{1,0:T(8,128)(2,1)S(1)}, bf16[1024,512]{1,0:T(8,128)(2,1)}, u32[]{:S(2)}) copy-start(bf16[1024,512]{1,0:T(8,128)(2,1)} %x0.3) | copy-start | bytes 3145732
  5.8 3.6 %copy-start.4 = (bf16[1024,512]{1,0:T(8,128)(2,1)S(1)}, bf16[1024,512]{1,0:T(8,128)(2,1)}, u32[]{:S(2)}) copy-start(bf16[1024,512]{1,0:T(8,128)(2,1)} %xk.3) | copy-start | bytes 3145732
  8.7 4.5 %collective-permute-start = (bf16[32,16,1280]{2,1,0:T(8,128)(2,1)S(1)}, bf16[32,16,1280]{2,1,0:T(8,128)(2,1)S(1)}, u32[]{:S(2)}, u32[]{:S(2)}) collective-permute-start(bf16[32,16,1280]{2,1,0:T(8,128)(2,1)S(1)} %grams_theirs.1.other), channel_id=1, source_target_pairs={{0,1},{1,0},{2,3},{3,2},{4,5},{5,4},{6,7},{7,6},{8,9},{9,8},{10,11... | collective-permute-start | bytes 3932168 | tf_op jit(solution)/shard_map/ppermute | solution.py:280
  14.5 8.6 %copy-start.6 = (f32[2,3,512]{2,0,1:T(2,128)S(1)}, f32[2,3,512]{2,0,1:T(2,128)}, u32[]{:S(2)}) copy-start(f32[2,3,512]{2,0,1:T(2,128)} %param.13) | copy-start | bytes 36868
  14.5 28.7 %all-to-all-start = ((bf16[32,16,1280]{2,1,0:T(8,128)(2,1)}), bf16[32,16,1280]{2,1,0:T(8,128)(2,1)S(1)}, u32[]{:S(2)}, u32[]{:S(2)}) async-start(bf16[32,16,1280]{2,1,0:T(8,128)(2,1)} %add_convert_fusion), calls=%async_computation | async-start | bytes 2621440 | tf_op jit(solution)/shard_map/wide_sum/all_to_all | solution.py:261
  24.1 1.3 %collective-permute-start.1 = (f32[2,512]{1,0:T(2,128)S(1)}, f32[2,512]{1,0:T(2,128)S(1)}, u32[]{:S(2)}, u32[]{:S(2)}) collective-permute-start(f32[2,512]{1,0:T(2,128)S(1)} %get-tuple-element.29), channel_id=1, source_target_pairs={{0,1},{1,0},{2,3},{3,2},{4,5},{5,4},{6,7},{7,6},{8,9},{9,8},{10,11... | collective-permute-start | bytes 12296 | tf_op jit(solution)/shard_map/ppermute | solution.py:299
  44.1 11.7 %all-to-all-start.1 = ((bf16[4,112,128]{2,1,0:T(8,128)(2,1)}), bf16[4,112,128]{2,1,0:T(8,128)(2,1)S(1)}, u32[]{:S(2)}, u32[]{:S(2)}) async-start(bf16[4,112,128]{2,1,0:T(8,128)(2,1)} %pack.1), calls=%async_computation.1 | async-start | bytes 229376 | tf_op jit(solution)/shard_map/deep_sum/all_to_all | solution.py:261
  57.4 14.9 %all-to-all-start.2 = ((bf16[32,80,128]{2,1,0:T(8,128)(2,1)}), bf16[32,80,128]{2,1,0:T(8,128)(2,1)S(1)}, u32[]{:S(2)}, u32[]{:S(2)}) async-start(bf16[32,80,128]{2,1,0:T(8,128)(2,1)} %get-tuple-element.14), calls=%async_computation.2 | async-start | bytes 1310720 | tf_op jit(solution)/shard_map/gather/all_to_all | solution.py:261
  73.4 12.2 %collective-permute-start.2 = (f32[8,512]{1,0:T(8,128)S(1)}, f32[8,512]{1,0:T(8,128)S(1)}, u32[]{:S(2)}, u32[]{:S(2)}) collective-permute-start(f32[8,512]{1,0:T(8,128)S(1)} %get-tuple-element.16), channel_id=1, source_target_pairs={{0,1},{1,0},{2,3},{3,2},{4,5},{5,4},{6,7},{7,6},{8,9},{9,8},{10,11... | collective-permute-start | bytes 49160 | tf_op jit(solution)/shard_map/ppermute | solution.py:329
  77.3 6.5 %collective-permute-start.3 = (f32[2,1280]{1,0:T(2,128)S(1)}, f32[2,1280]{1,0:T(2,128)S(1)}, u32[]{:S(2)}, u32[]{:S(2)}) collective-permute-start(f32[2,1280]{1,0:T(2,128)S(1)} %get-tuple-element.17), channel_id=1, source_target_pairs={{0,0},{1,1},{2,8},{3,9},{4,2},{5,3},{6,10},{7,11},{8,4},{9,5},{10,... | collective-permute-start | bytes 30728 | tf_op jit(solution)/shard_map/ppermute | solution.py:319
  80.2 5.3 %collective-permute-start.4 = (f32[2,1280]{1,0:T(2,128)S(1)}, f32[2,1280]{1,0:T(2,128)S(1)}, u32[]{:S(2)}, u32[]{:S(2)}) collective-permute-start(f32[2,1280]{1,0:T(2,128)S(1)} %get-tuple-element.18), channel_id=1, source_target_pairs={{0,1},{1,0},{2,9},{3,8},{4,3},{5,2},{6,11},{7,10},{8,5},{9,4},{10,... | collective-permute-start | bytes 30728 | tf_op jit(solution)/shard_map/ppermute | solution.py:320

commit v3 on v2

v3 whole, which is shorter than its diff:
```python
import functools

import jax
import jax.numpy as jnp
from jax import lax
from jax.experimental import pallas as pl
from jax.experimental.pallas import tpu as pltpu
from jax.sharding import PartitionSpec as P

LEN = 128
NX, NY, NZ, NC = 4, 4, 8, 2
NXY = NX * NY
D = 512
HALF = D // 2
PAIR = 2
WIDE = NXY * PAIR
DEEP = NZ // PAIR
ROWS = D // WIDE
COLS = D + D + HALF
LANES = 128
FR = ROWS // DEEP
GT, FT = D // LANES, (D + HALF) // LANES
MB = 1 << 20

decay = 0.8
damping = 0.001
kl_clip = 0.001
learn_rate = 7e-05

f32, bf16 = jnp.float32, jnp.bfloat16


def device(xy, z, c):
    return (xy * NZ + z) * NC + c


SWAP = [(d, d ^ 1) for d in range(NXY * NZ * NC)]
WIDE_GROUPS = [
    [device(i, k * PAIR + l, c) for i in range(NXY) for l in range(PAIR)]
    for k in range(DEEP)
    for c in range(NC)
]
DEEP_GROUPS = [
    [device(i, k * PAIR + l, c) for k in range(DEEP)] for i in range(NXY) for l in range(PAIR) for c in range(NC)
]
VMEM = pl.BlockSpec(memory_space=pltpu.VMEM)
SMEM = pl.BlockSpec(memory_space=pltpu.SMEM)
HBM = pl.BlockSpec(memory_space=pltpu.HBM)
CHUNKS = 4


def call(kernel, outs, in_specs, scratch=(), limit=16, flops=0, moved=0):
    return pl.pallas_call(
        kernel,
        out_shape=outs,
        in_specs=in_specs,
        out_specs=jax.tree.map(lambda _: VMEM, outs),
        scratch_shapes=list(scratch),
        compiler_params=pltpu.CompilerParams(vmem_limit_bytes=limit * MB),
        cost_estimate=pl.CostEstimate(flops=flops, bytes_accessed=moved, transcendentals=0),
    )


def shape(dims, dtype):
    return jax.ShapeDtypeStruct(dims, dtype)


def dot(a, b):
    return jnp.dot(a, b, preferred_element_type=f32)


def arrange(value):
    size = value.shape[1]
    pairs = value.reshape(value.shape[0] // 16, 2, 8, size)
    even, odd = pairs[:, 0], pairs[:, 1]
    upper = lax.broadcasted_iota(jnp.int32, even.shape, 1) < FR
    low = jnp.where(upper, even, pltpu.roll(odd, FR, 1))
    high = jnp.where(upper, pltpu.roll(even, FR, 1), odd)
    blocks = (value.shape[0] // (PAIR * ROWS), ROWS, size)
    return low.reshape(blocks), high.reshape(blocks)


def apply_mask(source, target, start, width, first, count):
    position = lax.broadcasted_iota(jnp.int32, (LEN, LANES), 0)
    for u in range(first, first + count):
        keep = None
        for m in range(start.shape[0]):
            s = start[m : m + 1, u : u + 1]
            outside = (position < s) | (position >= s + width[m : m + 1, u : u + 1])
            keep = outside if keep is None else keep & outside
        keep = jnp.where(keep, 1.0, 0.0).astype(bf16)
        for j in range(GT):
            view = (pl.ds(u * LEN, LEN), pl.ds(j * LANES, LANES))
            target[view] = source[view] * keep


def fetch(source, target, sems):
    rows = source.shape[0] // CHUNKS
    return [
        pltpu.make_async_copy(source.at[pl.ds(q * rows, rows)], target.at[pl.ds(q * rows, rows)], sems.at[q])
        for q in range(CHUNKS)
    ]


def fetch_picked(pick, xk, xv, target, sems):
    @pl.when(pick == 0)
    def _():
        for copy in fetch(xk, target, sems):
            copy.start()

    @pl.when(pick != 0)
    def _():
        for copy in fetch(xv, target, sems):
            copy.start()

    return fetch(xk, target, sems)


BLOCK = 256


def put(out, r, value, begin):
    places, cols = pl.ds(r * (BLOCK // (PAIR * ROWS)), BLOCK // (PAIR * ROWS)), pl.ds(begin, value.shape[1])
    low, high = arrange(value)
    out[places, 0, :, cols] = low.astype(bf16)
    out[places, 1, :, cols] = high.astype(bf16)


def grams(pick, x0, x1, ready, out):
    half = pl.ds(pl.multiple_of(pick * HALF, HALF), HALF)
    lefts = []
    for r in range(D // BLOCK):
        lefts.append(x0[:, pl.ds(r * BLOCK, BLOCK)].T)
        put(out, r, dot(lefts[r], x0[:, half]), 2 * D)
    ready()
    for r in range(D // BLOCK):
        put(out, r, dot(lefts[r], x1[...]), 0)
    for r in range(D // BLOCK):
        left = x1[:, pl.ds(r * BLOCK, BLOCK)].T
        put(out, r, dot(left, x1[...]), D)


def theirs_kernel(core, start, width, x0, xk, xv, out, kept, buf0, buf1, masks, sem0, sem1, sem2):
    pick = 1 - core[0]
    copies0 = fetch(x0, buf0, sem0)
    small = [pltpu.make_async_copy(v, masks.at[i], sem2.at[i]) for i, v in enumerate((start, width))]
    for copy in small + copies0:
        copy.start()
    copies1 = fetch_picked(pick, xk, xv, buf1, sem1)
    for copy in small:
        copy.wait()
    count = buf0.shape[0] // LEN // CHUNKS
    for q in range(CHUNKS):
        copies0[q].wait()
        apply_mask(buf0, kept, masks.at[0], masks.at[1], q * count, count)

    def ready():
        for q in range(CHUNKS):
            copies1[q].wait()
            apply_mask(buf1, buf1, masks.at[0], masks.at[1], q * count, count)

    grams(pick, kept, buf1, ready, out)


def mine_kernel(core, start, width, x0, xk, xv, out, buf1, masks, sem1, sem2):
    pick = core[0]
    small = [pltpu.make_async_copy(v, masks.at[i], sem2.at[i]) for i, v in enumerate((start, width))]
    for copy in small:
        copy.start()
    copies1 = fetch_picked(pick, xk, xv, buf1, sem1)
    count = buf1.shape[0] // LEN // CHUNKS

    def ready():
        for copy in small:
            copy.wait()
        for q in range(CHUNKS):
            copies1[q].wait()
            apply_mask(buf1, buf1, masks.at[0], masks.at[1], q * count, count)

    grams(pick, x0, buf1, ready, out)


def lam_kernel(share, core, mine, other, bases, keep_lam, send_lam, basis_in_t):
    c = core[0]

    def image(source, begin, size, basis):
        return dot(source[:, :, pl.ds(begin, size)].reshape(D, size), basis)

    def arranged(index):
        low, high = arrange(bases[index].astype(f32))
        return jnp.concatenate([low, high], axis=1).reshape(D, D)

    def values(basis, product):
        return jnp.sum(basis * product, axis=0, keepdims=True) * share

    near = pl.ds(pl.multiple_of(c * HALF, HALF), HALF)
    far = pl.ds(pl.multiple_of((1 - c) * HALF, HALF), HALF)
    basis = arranged(0)
    basis_in_t[...] = basis.T.astype(bf16)
    lam0 = values(basis, image(mine, 2 * D, HALF, bases[0, near, :]) + image(other, 2 * D, HALF, bases[0, far, :]))
    keep_lam[0:1, :] = lam0
    send_lam[0:1, :] = lam0
    keep_lam[1:2, :] = values(arranged(1 + c), image(mine, D, D, bases[1 + c]))
    send_lam[1:2, :] = values(arranged(2 - c), image(other, D, D, bases[2 - c]))


def split(value):
    high = value.astype(bf16)
    return high.astype(f32), value - high.astype(f32)


def lam_rows(lam):
    high, low = split(lam)
    pieces = []
    for j in range(GT):
        tile = slice(j * LANES, (j + 1) * LANES)
        pieces += [high[:, tile], low[:, tile]]
    return jnp.concatenate(pieces, axis=0)


def read_lam(rows):
    tiles = [rows[4 * j : 4 * j + 2] + rows[4 * j + 2 : 4 * j + 4] for j in range(GT)]
    return jnp.concatenate(tiles, axis=1)


LAMR = 4 * GT
TAIL = ((FT * FR + LAMR + 15) // 16) * 16
DEEP_ROWS = GT * ROWS + TAIL
GATHER_ROWS = GT * ROWS + LAMR


def pack_kernel(parts, keep_lam, send_lam, out):
    total = parts[0].astype(f32)
    for i in range(1, WIDE):
        total = total + parts[i].astype(f32)
    lam = lam_rows(keep_lam[...] + send_lam[...])
    for j in range(GT):
        tile = total[:, j * LANES : (j + 1) * LANES].astype(bf16)
        for k in range(DEEP):
            out[k, pl.ds(j * ROWS, ROWS), :] = tile
    pad = jnp.zeros((TAIL - FT * FR - LAMR, LANES), f32)
    for k in range(DEEP):
        rows = total[k * FR : (k + 1) * FR]
        pieces = [rows[:, D + t * LANES : D + (t + 1) * LANES] for t in range(FT)]
        out[k, pl.ds(GT * ROWS, TAIL), :] = jnp.concatenate(pieces + [lam, pad], axis=0).astype(bf16)


def rotate_kernel(place, got, basis, out, stay, cross):
    total = got[0].astype(f32)
    for i in range(1, DEEP):
        total = total + got[i].astype(f32)
    grad = jnp.concatenate([total[j * ROWS : (j + 1) * ROWS] for j in range(GT)], axis=1)
    rot = dot(grad.astype(bf16), basis[...]).astype(bf16)
    base = GT * ROWS
    lam = lam_rows(read_lam(total[base + FT * FR : base + FT * FR + LAMR])).astype(bf16)
    for j in range(GT):
        tile = rot[:, j * LANES : (j + 1) * LANES]
        for i in range(WIDE):
            out[i, pl.ds(j * ROWS, ROWS), :] = tile
    for i in range(WIDE):
        out[i, pl.ds(base, LAMR), :] = lam
    k, c = place[0], place[1]
    rows = grad[0:FR]
    for other in range(1, DEEP):
        rows = jnp.where(k == other, grad[other * FR : (other + 1) * FR], rows)
    factors = [total[base + t * FR : base + (t + 1) * FR] for t in range(FT)]
    full = jnp.concatenate(factors[:GT], axis=1)
    part = jnp.concatenate(factors[GT:], axis=1)

    def lines(a):
        halves = jnp.concatenate([part[a : a + 1], part[a + 1 : a + 2]], axis=1)
        return jnp.concatenate([jnp.zeros((3, D), f32), rows[a : a + 2], full[a : a + 2], halves], axis=0)

    low, high = lines(0), lines(2)
    stay[...] = jnp.where(c == 0, low, high)
    cross[...] = jnp.where(c == 0, high, low)


def solve_kernel(got, basis_in_t, basis_out, rows_in, stay, cross, own, their, scaled):
    base = GT * ROWS
    lam = got[0, pl.ds(base, LAMR), :].astype(f32)
    for i in range(1, WIDE):
        lam = lam + got[i, pl.ds(base, LAMR), :].astype(f32)
    lam = read_lam(lam)
    column = jnp.broadcast_to(lam[0:1], (8, D)).T[:, 0:1]
    column = jnp.broadcast_to(column, (D, LANES))
    curve = jnp.zeros((8, LANES), f32)
    for j in range(GT):
        rot = got[:, pl.ds(j * ROWS, ROWS), :].reshape(D, LANES)
        rotated = dot(basis_in_t[...], rot)
        low = (rotated / (column * lam[1:2, j * LANES : (j + 1) * LANES] + damping)).astype(bf16)
        scaled[:, pl.ds(j * LANES, LANES)] = low
        curve = curve + jnp.sum((low.astype(f32) * rotated).reshape(D // 8, 8, LANES), axis=0)
    curve = jnp.sum(jnp.sum(curve, axis=1, keepdims=True), axis=0, keepdims=True)
    back = dot(rows_in[...], scaled[...]).astype(bf16)
    prec = lax.dot_general(back, basis_out[...], (((1,), (1,)), ((), ())), preferred_element_type=f32)
    prec = prec.astype(bf16).astype(f32)
    curve = jnp.broadcast_to(curve, (1, D))
    own[...] = jnp.concatenate([prec[0:2], curve, stay[3:8, :]], axis=0)
    their[...] = jnp.concatenate([prec[2:4], curve, cross[3:8, :]], axis=0)


def finish_kernel(scale, core, own, got, old, new_factors, gradients, updates):
    first = core[0] == 0
    curve = own[2:3, :] + got[2:3, :]
    factor = jnp.sqrt(kl_clip / (learn_rate * learn_rate * curve))
    side0 = jnp.where(first, own[...], got[...])
    side1 = jnp.where(first, got[...], own[...])
    updates[0] = (side0[0:2] * factor).astype(bf16)
    updates[1] = (side1[0:2] * factor).astype(bf16)
    gradients[:, 0, :] = side0[3:5]
    gradients[:, 1, :] = side1[3:5]
    left, right = side0[7:8], side1[7:8]
    batch = (
        jnp.concatenate(
            [
                jnp.concatenate([left[:, :HALF], right[:, :HALF]], axis=1),
                jnp.concatenate([left[:, HALF:], right[:, HALF:]], axis=1),
            ],
            axis=0,
        ),
        side0[5:7],
        side1[5:7],
    )
    for f in range(3):
        new_factors[f] = decay * old[f] + scale * batch[f]


def exchange(value, groups):
    return lax.all_to_all(value, "dp", 0, 0, axis_index_groups=groups, tiled=True)


def body(activations, grad_key, grad_value, time_start, time_width, bases, old_factors):
    index = lax.axis_index("dp").astype(jnp.int32)
    core = index % NC
    first = core == 0
    z = (index // NC) % NZ
    place = jnp.stack([z // PAIR, core])
    tokens_here = activations.shape[0]
    share = (1.0 - decay) / (tokens_here * lax.axis_size("dp"))

    def in_hbm(value):
        return pltpu.with_memory_space_constraint(value, pltpu.HBM)

    masks = (in_hbm(time_start.T), in_hbm(time_width.T))
    frames, keys, vals = in_hbm(activations), in_hbm(grad_key), in_hbm(grad_value)
    mask_buf = pltpu.VMEM((2,) + time_start.shape[::-1], jnp.int32)
    buf = pltpu.VMEM((tokens_here, D), bf16)
    sems = pltpu.SemaphoreType.DMA((CHUNKS,))
    pair = pltpu.SemaphoreType.DMA((2,))
    partial = shape((NXY, PAIR, ROWS, COLS), bf16)
    work = 2 * D * tokens_here * COLS
    with jax.named_scope("grams_theirs"):
        other, kept = call(
            theirs_kernel,
            (partial, shape((tokens_here, D), bf16)),
            [SMEM] + [HBM] * 5,
            [buf, buf, mask_buf, sems, sems, pair],
            flops=work,
            moved=4 * MB,
        )(core[None], *masks, frames, keys, vals)
    received = lax.ppermute(other, "dp", SWAP)
    with jax.named_scope("grams_mine"):
        mine = call(
            mine_kernel,
            partial,
            [SMEM, HBM, HBM, VMEM, HBM, HBM],
            [buf, mask_buf, sems, pair],
            flops=work,
            moved=4 * MB,
        )(core[None], *masks, kept, keys, vals)
    with jax.named_scope("chip_sum"):
        chip = (mine.astype(f32) + received.astype(f32)).astype(bf16).reshape(WIDE, ROWS, COLS)
    with jax.named_scope("wide_sum"):
        parts = exchange(chip, WIDE_GROUPS)

    lam_shape = shape((2, D), f32)
    with jax.named_scope("lam"):
        keep_lam, send_lam, basis_in_t = call(
            functools.partial(lam_kernel, share),
            (lam_shape, lam_shape, shape((D, D), bf16)),
            [SMEM] + [VMEM] * 3,
            flops=6 * D * D * D,
            moved=4 * MB,
        )(core[None], mine.reshape(WIDE, ROWS, COLS), other.reshape(WIDE, ROWS, COLS), bases)
    old_lam = []
    my_rows = lax.dynamic_slice_in_dim(bases, 2 * index, 2, 1).astype(f32)
    for f in range(3):
        old_image = jnp.dot(old_factors[:, f, :], bases[f].astype(f32), precision=lax.Precision.HIGHEST)
        old_lam.append(decay * jnp.sum(my_rows[f] * old_image, axis=0))
    keep_lam = keep_lam + jnp.stack([old_lam[0], jnp.where(first, old_lam[1], old_lam[2])])
    send_lam = send_lam + jnp.stack([old_lam[0], jnp.where(first, old_lam[2], old_lam[1])])
    sent_lam = lax.ppermute(send_lam, "dp", SWAP)

    with jax.named_scope("pack"):
        packed = call(pack_kernel, shape((DEEP, DEEP_ROWS, LANES), bf16), [VMEM] * 3)(parts, keep_lam, sent_lam)
    with jax.named_scope("deep_sum"):
        got = exchange(packed, DEEP_GROUPS)
    basis_out = lax.dynamic_index_in_dim(bases, 1 + core, 0, keepdims=False)
    lines = shape((8, D), f32)
    with jax.named_scope("rotate"):
        spread, stay, cross = call(
            rotate_kernel,
            (shape((WIDE, GATHER_ROWS, LANES), bf16), lines, lines),
            [SMEM, VMEM, VMEM],
        )(place, got, basis_out)
    with jax.named_scope("gather"):
        gathered = exchange(spread, WIDE_GROUPS)
    rows_in = lax.dynamic_slice_in_dim(bases[0], (index // NC) * FR, FR, 0)
    rows_in = jnp.where(first, rows_in, jnp.roll(rows_in, 2, axis=0))
    rows_in = jnp.pad(rows_in, ((0, 16 - FR), (0, 0)))
    with jax.named_scope("solve"):
        own, their = call(solve_kernel, (lines, lines), [VMEM] * 6, [pltpu.VMEM((D, D), bf16)])(
            gathered, basis_in_t, basis_out, rows_in, stay, cross
        )
    theirs = lax.ppermute(their, "dp", SWAP)
    with jax.named_scope("finish"):
        new_factors, gradients, updates = call(
            functools.partial(finish_kernel, share),
            (shape((3, 2, D), f32), shape((2, 2, D), f32), shape((2, 2, D), bf16)),
            [SMEM] + [VMEM] * 3,
        )(core[None], own, theirs, jnp.transpose(old_factors, (1, 0, 2)))
    return (jnp.transpose(new_factors, (1, 0, 2)), gradients, updates)


def solution(mesh):
    in_specs = (
        P("dp", None),
        P("dp", None),
        P("dp", None),
        P("dp", None),
        P("dp", None),
        P(),
        P("dp", None, None),
    )
    out_specs = (P("dp", None, None), P("dp", None, None), P(None, "dp", None))
    return jax.shard_map(body, mesh=mesh, in_specs=in_specs, out_specs=out_specs, check_vma=False)
```

time: 87.9 us -> 78.5 us (0.89)
  the two profiles are of different devices: /device:TPU:65 before, /device:TPU:1 now
where the time goes in v3:
time: 78.5 us; the launch traced here: 78 us
  waiting for transfers between devices  33 us (42%)
  starting transfers between devices  26 us (33%)
  Pallas kernels  12.8 us (16%)
  local copies, waits for them, and re-layouts  2.73 us (3%)
  other arithmetic  1.58 us (2%)
  matrix products  0.99 us (1%)
  between operations  0.88 us (1%)
    all_to_all x3, waiting for transfers between devices, exchange(): lax.all_to_all(value, 'dp', 0, 0, axis_index_groups=groups, tiled=True)  31.3 us
    all_to_all x3, starting transfers between devices, exchange(): lax.all_to_all(value, 'dp', 0, 0, axis_index_groups=groups, tiled=True)  18.3 us
    pallas_call x1, Pallas kernels, body(): call(theirs_kernel, (partial, shape((tokens_here, D), bf16)), [SMEM] + [H...  4.54 us
    ppermute x1, starting transfers between devices, body(): theirs = lax.ppermute(their, 'dp', SWAP)  3.74 us
    ppermute x1, starting transfers between devices, body(): received = lax.ppermute(other, 'dp', SWAP)  3.24 us
    pallas_call x1, Pallas kernels, body(): call(mine_kernel, partial, [SMEM, HBM, HBM, VMEM, HBM, HBM], [buf, mask_b...  3.02 us
    unnamed x12, local copies, waits for them, and re-layouts  2.64 us
    pallas_call x1, Pallas kernels, body(): call(rotate_kernel, (shape((WIDE, GATHER_ROWS, LANES), bf16), lines, line...  1.6 us
  transfers between devices with their start and end apart: 6, of which 5 were waited for; matrix products, arithmetic and copies ran while one was open for 2% of the time, Pallas kernels for 5%

profile of v3, /device:TPU:1, one launch (start us, length us, event | category | flops | bytes accessed | tf_op | source)
XLA Modules:
  0.0 78.0 jit_solution(6291085295812621232)
XLA Ops:
  0.6 4.5 %grams_theirs.1 = (bf16[16,2,16,1280]{3,2,1,0:T(8,128)(2,1)S(1)}, bf16[1024,512]{1,0:T(8,128)(2,1)S(1)}) custom-call(s32[1]{0:T(128)} %bitcast.core, s32[2,8]{1,0:T(2,128)} %bitcast.58, s32[2,8]{1,0:T(2,128)} %bitcast.60, bf16[1024,512]{1,0:T(8,128)(2,1)} %x0.1, bf16[1024,512]{1,0:T(8,128)(2,1)} %xk.3, bf16[1024,512]{1,0:T(8,128)(2,1)} %xv.3), custom_call_target="tpu_custom_call" | custom-call | flops 1342177280 | bytes 4194304 | tf_op jit(solution)/shard_map/grams_theirs/pallas_call | solution.py:354
  5.2 0.0 copy-start.3
  5.2 3.2 %collective-permute-start = (bf16[16,2,16,1280]{3,2,1,0:T(8,128)(2,1)S(1)}, bf16[16,2,16,1280]{3,2,1,0:T(8,128)(2,1)S(1)}, u32[]{:S(2)}, u32[]{:S(2)}) collective-permute-start(bf16[16,2,16,1280]{3,2,1,0:T(8,128)(2,1)S(1)} %get-tuple-element.17), channel_id=1, source_target_pairs={{0,1},{1,0},{2,3},{3,2},{4,5},{5,4},{6,7},{7,6},{8,9},{9,8},{10,11... | collective-permute-start | bytes 3932168 | tf_op jit(solution)/shard_map/ppermute | solution.py:362
  8.4 3.0 %grams_mine.1 = bf16[16,2,16,1280]{3,2,1,0:T(8,128)(2,1)S(1)} custom-call(s32[1]{0:T(128)} %bitcast.core, s32[2,8]{1,0:T(2,128)} %bitcast.59, s32[2,8]{1,0:T(2,128)} %bitcast.61, bf16[1024,512]{1,0:T(8,128)(2,1)S(1)} %get-tuple-element.16.x0, bf16[1024,512]{1,0:T(8,128)(2,1)} %xk.3, bf16[1024,512]{1,0:T(8,128)(2,1)} %xv.3), custom_call_target="tpu_custom_call" | custom-call | flops 1342177280 | bytes 4194304 | tf_op jit(solution)/shard_map/grams_mine/pallas_call | solution.py:364
  11.5 0.0 copy-done.3
  11.5 0.0 copy-start.1
  11.5 0.0 collective-permute-done
  11.5 1.4 %add_convert_fusion = bf16[16,2,16,1280]{3,2,1,0:T(8,128)(2,1)} fusion(bf16[16,2,16,1280]{3,2,1,0:T(8,128)(2,1)S(1)} %collective-permute-done, bf16[16,2,16,1280]{3,2,1,0:T(8,128)(2,1)S(1)} %grams_mine.1), kind=kLoop, calls=%fused_computation | loop fusion | flops 2621440 | bytes 3932160 | tf_op jit(solution)/shard_map/chip_sum/convert_element_type | solution.py:373
  12.9 0.0 copy-done.1
  12.9 6.8 %all-to-all-start = ((bf16[32,16,1280]{2,1,0:T(8,128)(2,1)}), bf16[32,16,1280]{2,1,0:T(8,128)(2,1)S(1)}, u32[]{:S(2)}, u32[]{:S(2)}) async-start(bf16[32,16,1280]{2,1,0:T(8,128)(2,1)} %bitcast.53), calls=%async_computation | async-start | bytes 2621440 | tf_op jit(solution)/shard_map/wide_sum/all_to_all | solution.py:330
  19.7 0.0 copy-done
  19.8 1.3 %copy-done.2 = bf16[16,2,16,1280]{3,2,1,0:T(8,128)(2,1)S(1)} copy-done((bf16[16,2,16,1280]{3,2,1,0:T(8,128)(2,1)S(1)}, bf16[16,2,16,1280]{3,2,1,0:T(8,128)(2,1)}, u32[]{:S(2)}) %copy-start.2) | copy-done | bytes 1310744
  21.1 1.3 %copy-done.4 = bf16[16,2,16,1280]{3,2,1,0:T(8,128)(2,1)S(1)} copy-done((bf16[16,2,16,1280]{3,2,1,0:T(8,128)(2,1)S(1)}, bf16[16,2,16,1280]{3,2,1,0:T(8,128)(2,1)}, u32[]{:S(2)}) %copy-start.4) | copy-done | bytes 1310744
  22.4 1.1 %lam.1 = (f32[2,512]{1,0:T(2,128)S(1)}, f32[2,512]{1,0:T(2,128)S(1)}, bf16[512,512]{1,0:T(8,128)(2,1)S(1)}) custom-call(s32[1]{0:T(128)} %bitcast.core, bf16[32,16,1280]{2,1,0:T(8,128)(2,1)S(1)} %bitcast.50, bf16[32,16,1280]{2,1,0:T(8,128)(2,1)S(1)} %bitcast.51, bf16[3,512,512]{2,1,0:T(8,128)(2,1)S(1)} %copy-done), custom_call_target="tpu_custom_call" | custom-call | flops 805306368 | bytes 4194304 | tf_op jit(solution)/shard_map/lam/pallas_call | solution.py:379
  23.5 0.3 fusion.1
  23.9 0.3 fusion.2
  24.2 0.3 fusion
  24.6 0.7 collective-permute-start.1
  25.3 0.8 %collective-permute-done.1.send_lam = f32[2,512]{1,0:T(2,128)S(1)} collective-permute-done((f32[2,512]{1,0:T(2,128)S(1)}, f32[2,512]{1,0:T(2,128)S(1)}, u32[]{:S(2)}, u32[]{:S(2)}) %collective-permute-start.1) | collective-permute-done | bytes 4128 | tf_op jit(solution)/shard_map/ppermute | solution.py:393
  26.1 13.5 %all-to-all-done.parts = bf16[32,16,1280]{2,1,0:T(8,128)(2,1)S(1)} async-done(((bf16[32,16,1280]{2,1,0:T(8,128)(2,1)}), bf16[32,16,1280]{2,1,0:T(8,128)(2,1)S(1)}, u32[]{:S(2)}, u32[]{:S(2)}) %all-to-all-start) | async-done | bytes 1310752 | tf_op jit(solution)/shard_map/wide_sum/all_to_all | solution.py:330
  39.6 0.8 %pack.1 = bf16[4,112,128]{2,1,0:T(8,128)(2,1)} custom-call(bf16[32,16,1280]{2,1,0:T(8,128)(2,1)S(1)} %all-to-all-done.parts, f32[2,512]{1,0:T(2,128)S(1)} %get-tuple-element.36.keep_lam, f32[2,512]{1,0:T(2,128)S(1)} %collective-permute-done.1.send_lam), custom_call_target="tpu_custom_call" | custom-call | tf_op jit(solution)/shard_map/pack/pallas_call | solution.py:396
  40.4 7.3 %all-to-all-start.1 = ((bf16[4,112,128]{2,1,0:T(8,128)(2,1)}), bf16[4,112,128]{2,1,0:T(8,128)(2,1)S(1)}, u32[]{:S(2)}, u32[]{:S(2)}) async-start(bf16[4,112,128]{2,1,0:T(8,128)(2,1)} %pack.1), calls=%async_computation.1 | async-start | bytes 229376 | tf_op jit(solution)/shard_map/deep_sum/all_to_all | solution.py:330
  47.7 0.1 fusion.17
  47.9 0.1 pad_add_fusion.place
  47.9 6.9 %all-to-all-done.1.got = bf16[4,112,128]{2,1,0:T(8,128)(2,1)S(1)} async-done(((bf16[4,112,128]{2,1,0:T(8,128)(2,1)}), bf16[4,112,128]{2,1,0:T(8,128)(2,1)S(1)}, u32[]{:S(2)}, u32[]{:S(2)}) %all-to-all-start.1) | async-done | bytes 114720 | tf_op jit(solution)/shard_map/deep_sum/all_to_all | solution.py:330
  54.9 1.6 %rotate.1 = (bf16[32,80,128]{2,1,0:T(8,128)(2,1)}, f32[8,512]{1,0:T(8,128)S(1)}, f32[8,512]{1,0:T(8,128)S(1)}) custom-call(s32[2]{0:T(128)S(1)} %pad_add_fusion.place, bf16[4,112,128]{2,1,0:T(8,128)(2,1)S(1)} %all-to-all-done.1.got, bf16[512,512]{1,0:T(8,128)(2,1)S(1)} %get-tuple-element.30.basis.basis_out), custom_call_target="tpu_custom_call" | custom-call | tf_op jit(solution)/shard_map/rotate/pallas_call | solution.py:402
  56.5 4.2 %all-to-all-start.2 = ((bf16[32,80,128]{2,1,0:T(8,128)(2,1)}), bf16[32,80,128]{2,1,0:T(8,128)(2,1)S(1)}, u32[]{:S(2)}, u32[]{:S(2)}) async-start(bf16[32,80,128]{2,1,0:T(8,128)(2,1)} %get-tuple-element.20), calls=%async_computation.2 | async-start | bytes 1310720 | tf_op jit(solution)/shard_map/gather/all_to_all | solution.py:330
  60.8 10.9 %all-to-all-done.2.got = bf16[32,80,128]{2,1,0:T(8,128)(2,1)S(1)} async-done(((bf16[32,80,128]{2,1,0:T(8,128)(2,1)}), bf16[32,80,128]{2,1,0:T(8,128)(2,1)S(1)}, u32[]{:S(2)}, u32[]{:S(2)}) %all-to-all-start.2) | async-done | bytes 655392 | tf_op jit(solution)/shard_map/gather/all_to_all | solution.py:330
  71.7 1.1 %solve.1 = (f32[8,512]{1,0:T(8,128)S(1)}, f32[8,512]{1,0:T(8,128)S(1)}) custom-call(bf16[32,80,128]{2,1,0:T(8,128)(2,1)S(1)} %all-to-all-done.2.got, bf16[512,512]{1,0:T(8,128)(2,1)S(1)} %get-tuple-element.21.basis_in_t, bf16[512,512]{1,0:T(8,128)(2,1)S(1)} %get-tuple-element.30.basis.basis_out, bf16[16,512]{1,0:T(8,128)(2,1)S(1)} %pad.4.rows_in, ...), custom_call_target="tpu_custom_call" | custom-call | tf_op jit(solution)/shard_map/solve/pallas_call | solution.py:413
  72.8 3.7 %collective-permute-start.2 = (f32[8,512]{1,0:T(8,128)S(1)}, f32[8,512]{1,0:T(8,128)S(1)}, u32[]{:S(2)}, u32[]{:S(2)}) collective-permute-start(f32[8,512]{1,0:T(8,128)S(1)} %get-tuple-element.25), channel_id=1, source_target_pairs={{0,1},{1,0},{2,3},{3,2},{4,5},{5,4},{6,7},{7,6},{8,9},{9,8},{10,11... | collective-permute-start | bytes 49160 | tf_op jit(solution)/shard_map/ppermute | solution.py:416
  76.5 0.8 %collective-permute-done.2.got = f32[8,512]{1,0:T(8,128)S(1)} collective-permute-done((f32[8,512]{1,0:T(8,128)S(1)}, f32[8,512]{1,0:T(8,128)S(1)}, u32[]{:S(2)}, u32[]{:S(2)}) %collective-permute-start.2) | collective-permute-done | bytes 16416 | tf_op jit(solution)/shard_map/ppermute | solution.py:416
  77.4 0.6 finish.1
  (12 shorter events, 0.1 us)
Async XLA Ops:
  5.2 6.3 %copy-start.3 = (bf16[16,2,16,1280]{3,2,1,0:T(8,128)(2,1)}, bf16[16,2,16,1280]{3,2,1,0:T(8,128)(2,1)S(1)}, u32[]{:S(2)}) copy-start(bf16[16,2,16,1280]{3,2,1,0:T(8,128)(2,1)S(1)} %get-tuple-element.17) | copy-start | bytes 3932164
  5.2 6.3 %collective-permute-start = (bf16[16,2,16,1280]{3,2,1,0:T(8,128)(2,1)S(1)}, bf16[16,2,16,1280]{3,2,1,0:T(8,128)(2,1)S(1)}, u32[]{:S(2)}, u32[]{:S(2)}) collective-permute-start(bf16[16,2,16,1280]{3,2,1,0:T(8,128)(2,1)S(1)} %get-tuple-element.17), channel_id=1, source_target_pairs={{0,1},{1,0},{2,3},{3,2},{4,5},{5,4},{6,7},{7,6},{8,9},{9,8},{10,11... | collective-permute-start | bytes 3932168 | tf_op jit(solution)/shard_map/ppermute | solution.py:362
  11.5 1.5 %copy-start.1 = (bf16[16,2,16,1280]{3,2,1,0:T(8,128)(2,1)}, bf16[16,2,16,1280]{3,2,1,0:T(8,128)(2,1)S(1)}, u32[]{:S(2)}) copy-start(bf16[16,2,16,1280]{3,2,1,0:T(8,128)(2,1)S(1)} %grams_mine.1) | copy-start | bytes 3932164
  12.9 6.8 %copy-start = (bf16[3,512,512]{2,1,0:T(8,128)(2,1)S(1)}, bf16[3,512,512]{2,1,0:T(8,128)(2,1)}, u32[]{:S(2)}) copy-start(bf16[3,512,512]{2,1,0:T(8,128)(2,1)} %bases.1) | copy-start | bytes 4718596
  12.9 26.6 %all-to-all-start = ((bf16[32,16,1280]{2,1,0:T(8,128)(2,1)}), bf16[32,16,1280]{2,1,0:T(8,128)(2,1)S(1)}, u32[]{:S(2)}, u32[]{:S(2)}) async-start(bf16[32,16,1280]{2,1,0:T(8,128)(2,1)} %bitcast.53), calls=%async_computation | async-start | bytes 2621440 | tf_op jit(solution)/shard_map/wide_sum/all_to_all | solution.py:330
  19.8 1.3 %copy-start.2 = (bf16[16,2,16,1280]{3,2,1,0:T(8,128)(2,1)S(1)}, bf16[16,2,16,1280]{3,2,1,0:T(8,128)(2,1)}, u32[]{:S(2)}) copy-start(bf16[16,2,16,1280]{3,2,1,0:T(8,128)(2,1)} %copy-done.1) | copy-start | bytes 3932164
  21.1 1.3 %copy-start.4 = (bf16[16,2,16,1280]{3,2,1,0:T(8,128)(2,1)S(1)}, bf16[16,2,16,1280]{3,2,1,0:T(8,128)(2,1)}, u32[]{:S(2)}) copy-start(bf16[16,2,16,1280]{3,2,1,0:T(8,128)(2,1)} %copy-done.3) | copy-start | bytes 3932164
  22.4 1.1 %copy-start.5 = (f32[2,3,512]{2,0,1:T(2,128)S(1)}, f32[2,3,512]{2,0,1:T(2,128)}, u32[]{:S(2)}) copy-start(f32[2,3,512]{2,0,1:T(2,128)} %param.13) | copy-start | bytes 36868
  24.6 1.5 %collective-permute-start.1 = (f32[2,512]{1,0:T(2,128)S(1)}, f32[2,512]{1,0:T(2,128)S(1)}, u32[]{:S(2)}, u32[]{:S(2)}) collective-permute-start(f32[2,512]{1,0:T(2,128)S(1)} %get-tuple-element.35), channel_id=1, source_target_pairs={{0,1},{1,0},{2,3},{3,2},{4,5},{5,4},{6,7},{7,6},{8,9},{9,8},{10,11... | collective-permute-start | bytes 12296 | tf_op jit(solution)/shard_map/ppermute | solution.py:393
  40.4 14.4 %all-to-all-start.1 = ((bf16[4,112,128]{2,1,0:T(8,128)(2,1)}), bf16[4,112,128]{2,1,0:T(8,128)(2,1)S(1)}, u32[]{:S(2)}, u32[]{:S(2)}) async-start(bf16[4,112,128]{2,1,0:T(8,128)(2,1)} %pack.1), calls=%async_computation.1 | async-start | bytes 229376 | tf_op jit(solution)/shard_map/deep_sum/all_to_all | solution.py:330
  56.5 15.2 %all-to-all-start.2 = ((bf16[32,80,128]{2,1,0:T(8,128)(2,1)}), bf16[32,80,128]{2,1,0:T(8,128)(2,1)S(1)}, u32[]{:S(2)}, u32[]{:S(2)}) async-start(bf16[32,80,128]{2,1,0:T(8,128)(2,1)} %get-tuple-element.20), calls=%async_computation.2 | async-start | bytes 1310720 | tf_op jit(solution)/shard_map/gather/all_to_all | solution.py:330
  72.8 4.6 %collective-permute-start.2 = (f32[8,512]{1,0:T(8,128)S(1)}, f32[8,512]{1,0:T(8,128)S(1)}, u32[]{:S(2)}, u32[]{:S(2)}) collective-permute-start(f32[8,512]{1,0:T(8,128)S(1)} %get-tuple-element.25), channel_id=1, source_target_pairs={{0,1},{1,0},{2,3},{3,2},{4,5},{5,4},{6,7},{7,6},{8,9},{9,8},{10,11... | collective-permute-start | bytes 49160 | tf_op jit(solution)/shard_map/ppermute | solution.py:416

commit v4 on v3

--- a/solution.py
+++ b/solution.py
@@ -46,7 +46,7 @@
 VMEM = pl.BlockSpec(memory_space=pltpu.VMEM)
 SMEM = pl.BlockSpec(memory_space=pltpu.SMEM)
 HBM = pl.BlockSpec(memory_space=pltpu.HBM)
-CHUNKS = 4
+CHUNKS = 2
 
 
 def call(kernel, outs, in_specs, scratch=(), limit=16, flops=0, moved=0):
@@ -80,18 +80,22 @@
     return low.reshape(blocks), high.reshape(blocks)
 
 
-def apply_mask(source, target, start, width, first, count):
+def build_keep(start, width, keep):
     position = lax.broadcasted_iota(jnp.int32, (LEN, LANES), 0)
-    for u in range(first, first + count):
-        keep = None
+    for u in range(start.shape[1]):
+        inside = None
         for m in range(start.shape[0]):
             s = start[m : m + 1, u : u + 1]
-            outside = (position < s) | (position >= s + width[m : m + 1, u : u + 1])
-            keep = outside if keep is None else keep & outside
-        keep = jnp.where(keep, 1.0, 0.0).astype(bf16)
-        for j in range(GT):
-            view = (pl.ds(u * LEN, LEN), pl.ds(j * LANES, LANES))
-            target[view] = source[view] * keep
+            here = (position >= s) & (position < s + width[m : m + 1, u : u + 1])
+            inside = here if inside is None else inside | here
+        keep[pl.ds(u * LEN, LEN), :] = jnp.where(inside, 0.0, 1.0).astype(bf16)
+
+
+def apply_mask(source, target, keep, q):
+    rows = pl.ds(q * (source.shape[0] // CHUNKS), source.shape[0] // CHUNKS)
+    for j in range(GT):
+        view = (rows, pl.ds(j * LANES, LANES))
+        target[view] = source[view] * keep[rows, :]
 
 
 def fetch(source, target, sems):
@@ -140,44 +144,44 @@
         put(out, r, dot(left, x1[...]), D)
 
 
-def theirs_kernel(core, start, width, x0, xk, xv, out, kept, buf0, buf1, masks, sem0, sem1, sem2):
+def theirs_kernel(core, start, width, x0, xk, xv, out, kept, keep, buf0, buf1, masks, sem0, sem1, sem2):
     pick = 1 - core[0]
+    small = [pltpu.make_async_copy(v, masks.at[i], sem2.at[i]) for i, v in enumerate((start, width))]
     copies0 = fetch(x0, buf0, sem0)
-    small = [pltpu.make_async_copy(v, masks.at[i], sem2.at[i]) for i, v in enumerate((start, width))]
     for copy in small + copies0:
         copy.start()
     copies1 = fetch_picked(pick, xk, xv, buf1, sem1)
     for copy in small:
         copy.wait()
-    count = buf0.shape[0] // LEN // CHUNKS
+    build_keep(masks.at[0], masks.at[1], keep)
     for q in range(CHUNKS):
         copies0[q].wait()
-        apply_mask(buf0, kept, masks.at[0], masks.at[1], q * count, count)
+        apply_mask(buf0, kept, keep, q)
 
     def ready():
         for q in range(CHUNKS):
             copies1[q].wait()
-            apply_mask(buf1, buf1, masks.at[0], masks.at[1], q * count, count)
+            apply_mask(buf1, buf1, keep, q)
 
     grams(pick, kept, buf1, ready, out)
 
 
-def mine_kernel(core, start, width, x0, xk, xv, out, buf1, masks, sem1, sem2):
+def mine_kernel(core, keep, x0, xk, xv, out, buf1, sem1):
     pick = core[0]
-    small = [pltpu.make_async_copy(v, masks.at[i], sem2.at[i]) for i, v in enumerate((start, width))]
-    for copy in small:
-        copy.start()
     copies1 = fetch_picked(pick, xk, xv, buf1, sem1)
-    count = buf1.shape[0] // LEN // CHUNKS
 
     def ready():
-        for copy in small:
-            copy.wait()
         for q in range(CHUNKS):
             copies1[q].wait()
-            apply_mask(buf1, buf1, masks.at[0], masks.at[1], q * count, count)
+            apply_mask(buf1, buf1, keep, q)
 
     grams(pick, x0, buf1, ready, out)
+
+
+def add_kernel(mine, received, out):
+    for i in range(NXY):
+        for j in range(PAIR):
+            out[i, j] = mine[i, j] + received[i, j]
 
 
 def lam_kernel(share, core, mine, other, bases, keep_lam, send_lam, basis_in_t):
@@ -210,17 +214,15 @@
 
 
 def lam_rows(lam):
-    high, low = split(lam)
-    pieces = []
-    for j in range(GT):
-        tile = slice(j * LANES, (j + 1) * LANES)
-        pieces += [high[:, tile], low[:, tile]]
-    return jnp.concatenate(pieces, axis=0)
-
-
-def read_lam(rows):
-    tiles = [rows[4 * j : 4 * j + 2] + rows[4 * j + 2 : 4 * j + 4] for j in range(GT)]
-    return jnp.concatenate(tiles, axis=1)
+    return jnp.concatenate(split(jnp.concatenate([lam[:, j * LANES : (j + 1) * LANES] for j in range(GT)], axis=0)), axis=0)
+
+
+def add_lam(rows):
+    return rows[: 2 * GT] + rows[2 * GT :]
+
+
+def lam_row(total, index):
+    return jnp.concatenate([total[2 * j + index : 2 * j + index + 1] for j in range(GT)], axis=1)
 
 
 LAMR = 4 * GT
@@ -245,20 +247,29 @@
         out[k, pl.ds(GT * ROWS, TAIL), :] = jnp.concatenate(pieces + [lam, pad], axis=0).astype(bf16)
 
 
-def rotate_kernel(place, got, basis, out, stay, cross):
+def rotate_kernel(got, basis, out):
     total = got[0].astype(f32)
     for i in range(1, DEEP):
         total = total + got[i].astype(f32)
     grad = jnp.concatenate([total[j * ROWS : (j + 1) * ROWS] for j in range(GT)], axis=1)
     rot = dot(grad.astype(bf16), basis[...]).astype(bf16)
     base = GT * ROWS
-    lam = lam_rows(read_lam(total[base + FT * FR : base + FT * FR + LAMR])).astype(bf16)
+    lam = add_lam(total[base + FT * FR : base + FT * FR + LAMR])
+    lam = jnp.concatenate(split(lam), axis=0).astype(bf16)
+    for i in range(WIDE):
+        out[i, pl.ds(base, LAMR), :] = lam
     for j in range(GT):
         tile = rot[:, j * LANES : (j + 1) * LANES]
         for i in range(WIDE):
             out[i, pl.ds(j * ROWS, ROWS), :] = tile
-    for i in range(WIDE):
-        out[i, pl.ds(base, LAMR), :] = lam
+
+
+def rows_kernel(place, got, stay, cross):
+    total = got[0].astype(f32)
+    for i in range(1, DEEP):
+        total = total + got[i].astype(f32)
+    grad = jnp.concatenate([total[j * ROWS : (j + 1) * ROWS] for j in range(GT)], axis=1)
+    base = GT * ROWS
     k, c = place[0], place[1]
     rows = grad[0:FR]
     for other in range(1, DEEP):
@@ -281,14 +292,14 @@
     lam = got[0, pl.ds(base, LAMR), :].astype(f32)
     for i in range(1, WIDE):
         lam = lam + got[i, pl.ds(base, LAMR), :].astype(f32)
-    lam = read_lam(lam)
-    column = jnp.broadcast_to(lam[0:1], (8, D)).T[:, 0:1]
+    lam = add_lam(lam)
+    column = jnp.broadcast_to(lam_row(lam, 0), (8, D)).T[:, 0:1]
     column = jnp.broadcast_to(column, (D, LANES))
     curve = jnp.zeros((8, LANES), f32)
     for j in range(GT):
         rot = got[:, pl.ds(j * ROWS, ROWS), :].reshape(D, LANES)
         rotated = dot(basis_in_t[...], rot)
-        low = (rotated / (column * lam[1:2, j * LANES : (j + 1) * LANES] + damping)).astype(bf16)
+        low = (rotated / (column * lam[2 * j + 1 : 2 * j + 2] + damping)).astype(bf16)
         scaled[:, pl.ds(j * LANES, LANES)] = low
         curve = curve + jnp.sum((low.astype(f32) * rotated).reshape(D // 8, 8, LANES), axis=0)
     curve = jnp.sum(jnp.sum(curve, axis=1, keepdims=True), axis=0, keepdims=True)
@@ -351,9 +362,9 @@
     partial = shape((NXY, PAIR, ROWS, COLS), bf16)
     work = 2 * D * tokens_here * COLS
     with jax.named_scope("grams_theirs"):
-        other, kept = call(
+        other, kept, keep = call(
             theirs_kernel,
-            (partial, shape((tokens_here, D), bf16)),
+            (partial, shape((tokens_here, D), bf16), shape((tokens_here, LANES), bf16)),
             [SMEM] + [HBM] * 5,
             [buf, buf, mask_buf, sems, sems, pair],
             flops=work,
@@ -364,13 +375,13 @@
         mine = call(
             mine_kernel,
             partial,
-            [SMEM, HBM, HBM, VMEM, HBM, HBM],
-            [buf, mask_buf, sems, pair],
+            [SMEM, VMEM, VMEM, HBM, HBM],
+            [buf, sems],
             flops=work,
             moved=4 * MB,
-        )(core[None], *masks, kept, keys, vals)
+        )(core[None], keep, kept, keys, vals)
     with jax.named_scope("chip_sum"):
-        chip = (mine.astype(f32) + received.astype(f32)).astype(bf16).reshape(WIDE, ROWS, COLS)
+        chip = call(add_kernel, partial, [VMEM] * 2)(mine, received).reshape(WIDE, ROWS, COLS)
     with jax.named_scope("wide_sum"):
         parts = exchange(chip, WIDE_GROUPS)
 
@@ -399,13 +410,11 @@
     basis_out = lax.dynamic_index_in_dim(bases, 1 + core, 0, keepdims=False)
     lines = shape((8, D), f32)
     with jax.named_scope("rotate"):
-        spread, stay, cross = call(
-            rotate_kernel,
-            (shape((WIDE, GATHER_ROWS, LANES), bf16), lines, lines),
-            [SMEM, VMEM, VMEM],
-        )(place, got, basis_out)
+        spread = call(rotate_kernel, shape((WIDE, GATHER_ROWS, LANES), bf16), [VMEM] * 2)(got, basis_out)
     with jax.named_scope("gather"):
         gathered = exchange(spread, WIDE_GROUPS)
+    with jax.named_scope("rows"):
+        stay, cross = call(rows_kernel, (lines, lines), [SMEM, VMEM])(place, got)
     rows_in = lax.dynamic_slice_in_dim(bases[0], (index // NC) * FR, FR, 0)
     rows_in = jnp.where(first, rows_in, jnp.roll(rows_in, 2, axis=0))
     rows_in = jnp.pad(rows_in, ((0, 16 - FR), (0, 0)))

time: 78.5 us -> 77.3 us (0.985)
  local copies, waits for them, and re-layouts: 2.73 us -> 4.56 us
  other arithmetic: 1.58 us -> 0.13 us
  Pallas kernels: 12.8 us -> 11.8 us
    unnamed x12 -> x14, local copies, waits for them, and re-layouts: 2.64 us -> 4.46 us
    convert_element_type x1 -> x0, other arithmetic: 1.45 us -> none  [body(): (mine.astype(f32) + received.astype(f32)).astype(bf16)]
    pallas_call x3 -> x5, Pallas kernels: 9.16 us -> 8.12 us  [the longest x1 3.79 us: body(): call(theirs_kernel, (partial, shape((tokens_here, D), bf16), shape((token...]
  transfers between devices with their start and end apart: 6 -> 6, of which waited for: 5 -> 6; matrix products, arithmetic and copies ran while one was open for 2% -> 2% of each run, Pallas kernels for 5% -> 5%
where the time goes in v4:
time: 77.3 us; the launch traced here: 76.8 us
  waiting for transfers between devices  32.5 us (42%)
  starting transfers between devices  26 us (34%)
  Pallas kernels  11.8 us (15%)
  local copies, waits for them, and re-layouts  4.56 us (6%)
  matrix products  0.99 us (1%)
  between operations  0.89 us (1%)
    all_to_all x3, waiting for transfers between devices, exchange(): lax.all_to_all(value, 'dp', 0, 0, axis_index_groups=groups, tiled=True)  30.7 us
    all_to_all x3, starting transfers between devices, exchange(): lax.all_to_all(value, 'dp', 0, 0, axis_index_groups=groups, tiled=True)  18.3 us
    unnamed x14, local copies, waits for them, and re-layouts  4.46 us
    ppermute x1, starting transfers between devices, body(): theirs = lax.ppermute(their, 'dp', SWAP)  3.79 us
    pallas_call x1, Pallas kernels, body(): call(theirs_kernel, (partial, shape((tokens_here, D), bf16), shape((token...  3.79 us
    ppermute x1, starting transfers between devices, body(): received = lax.ppermute(other, 'dp', SWAP)  3.16 us
    pallas_call x1, Pallas kernels, body(): call(mine_kernel, partial, [SMEM, VMEM, VMEM, HBM, HBM], [buf, sems], flo...  2.51 us
  transfers between devices with their start and end apart: 6, of which 6 were waited for; matrix products, arithmetic and copies ran while one was open for 2% of the time, Pallas kernels for 5%

profile of v4, /device:TPU:1, one launch (start us, length us, event | category | flops | bytes accessed | tf_op | source)
XLA Modules:
  0.0 76.8 jit_solution(15838424843919014020)
XLA Ops:
  0.6 3.8 %grams_theirs.1 = (bf16[16,2,16,1280]{3,2,1,0:T(8,128)(2,1)S(1)}, bf16[1024,512]{1,0:T(8,128)(2,1)S(1)}, bf16[1024,128]{1,0:T(8,128)(2,1)S(1)}) custom-call(s32[1]{0:T(128)} %bitcast.core, s32[2,8]{1,0:T(2,128)} %bitcast.58, s32[2,8]{1,0:T(2,128)} %bitcast.59, bf16[1024,512]{1,0:T(8,128)(2,1)} %x0.1, bf16[1024,512]{1,0:T(8,128)(2,1)} %xk.3, bf16[1024,512]{1,0:T(8,128)(2,1)} %xv.3), custom_call_target="tpu_custom_call" | custom-call | flops 1342177280 | bytes 4194304 | tf_op jit(solution)/shard_map/grams_theirs/pallas_call | solution.py:365
  4.4 0.0 copy-start.4
  4.4 3.2 %collective-permute-start = (bf16[16,2,16,1280]{3,2,1,0:T(8,128)(2,1)S(1)}, bf16[16,2,16,1280]{3,2,1,0:T(8,128)(2,1)S(1)}, u32[]{:S(2)}, u32[]{:S(2)}) collective-permute-start(bf16[16,2,16,1280]{3,2,1,0:T(8,128)(2,1)S(1)} %get-tuple-element.18), channel_id=1, source_target_pairs={{0,1},{1,0},{2,3},{3,2},{4,5},{5,4},{6,7},{7,6},{8,9},{9,8},{10,11... | collective-permute-start | bytes 3932168 | tf_op jit(solution)/shard_map/ppermute | solution.py:373
  7.6 2.5 %grams_mine.1.mine = bf16[16,2,16,1280]{3,2,1,0:T(8,128)(2,1)S(1)} custom-call(s32[1]{0:T(128)} %bitcast.core, bf16[1024,128]{1,0:T(8,128)(2,1)S(1)} %get-tuple-element.16.keep, bf16[1024,512]{1,0:T(8,128)(2,1)S(1)} %get-tuple-element.17.x0, bf16[1024,512]{1,0:T(8,128)(2,1)} %xk.3, bf16[1024,512]{1,0:T(8,128)(2,1)} %xv.3), custom_call_target="tpu_custom_call" | custom-call | flops 1342177280 | bytes 4194304 | tf_op jit(solution)/shard_map/grams_mine/pallas_call | solution.py:375
  10.2 0.1 collective-permute-done.received
  10.3 0.2 chip_sum.1
  10.5 0.7 copy-done.2
  11.2 1.1 %copy-done.1 = bf16[16,2,16,1280]{3,2,1,0:T(8,128)(2,1)} copy-done((bf16[16,2,16,1280]{3,2,1,0:T(8,128)(2,1)}, bf16[16,2,16,1280]{3,2,1,0:T(8,128)(2,1)S(1)}, u32[]{:S(2)}) %copy-start.1) | copy-done | bytes 1310744
  12.3 6.8 %all-to-all-start = ((bf16[32,16,1280]{2,1,0:T(8,128)(2,1)}), bf16[32,16,1280]{2,1,0:T(8,128)(2,1)S(1)}, u32[]{:S(2)}, u32[]{:S(2)}) async-start(bf16[32,16,1280]{2,1,0:T(8,128)(2,1)} %bitcast.50), calls=%async_computation | async-start | bytes 2621440 | tf_op jit(solution)/shard_map/wide_sum/all_to_all | solution.py:341
  19.1 1.3 %copy-done.3 = bf16[16,2,16,1280]{3,2,1,0:T(8,128)(2,1)S(1)} copy-done((bf16[16,2,16,1280]{3,2,1,0:T(8,128)(2,1)S(1)}, bf16[16,2,16,1280]{3,2,1,0:T(8,128)(2,1)}, u32[]{:S(2)}) %copy-start.3) | copy-done | bytes 1310744
  20.4 1.3 %copy-done.5 = bf16[16,2,16,1280]{3,2,1,0:T(8,128)(2,1)S(1)} copy-done((bf16[16,2,16,1280]{3,2,1,0:T(8,128)(2,1)S(1)}, bf16[16,2,16,1280]{3,2,1,0:T(8,128)(2,1)}, u32[]{:S(2)}) %copy-start.5) | copy-done | bytes 1310744
  21.7 1.1 %lam.1 = (f32[2,512]{1,0:T(2,128)S(1)}, f32[2,512]{1,0:T(2,128)S(1)}, bf16[512,512]{1,0:T(8,128)(2,1)S(1)}) custom-call(s32[1]{0:T(128)} %bitcast.core, bf16[32,16,1280]{2,1,0:T(8,128)(2,1)S(1)} %bitcast.51, bf16[32,16,1280]{2,1,0:T(8,128)(2,1)S(1)} %bitcast.52, bf16[3,512,512]{2,1,0:T(8,128)(2,1)S(1)} %copy-done), custom_call_target="tpu_custom_call" | custom-call | flops 805306368 | bytes 4194304 | tf_op jit(solution)/shard_map/lam/pallas_call | solution.py:390
  22.8 0.0 copy-done.6
  22.9 0.3 fusion.1
  23.2 0.3 fusion.2
  23.5 0.3 fusion
  23.9 0.7 collective-permute-start.1
  24.6 0.8 %collective-permute-done.1.send_lam = f32[2,512]{1,0:T(2,128)S(1)} collective-permute-done((f32[2,512]{1,0:T(2,128)S(1)}, f32[2,512]{1,0:T(2,128)S(1)}, u32[]{:S(2)}, u32[]{:S(2)}) %collective-permute-start.1) | collective-permute-done | bytes 4128 | tf_op jit(solution)/shard_map/ppermute | solution.py:404
  25.5 13.5 %all-to-all-done.parts = bf16[32,16,1280]{2,1,0:T(8,128)(2,1)S(1)} async-done(((bf16[32,16,1280]{2,1,0:T(8,128)(2,1)}), bf16[32,16,1280]{2,1,0:T(8,128)(2,1)S(1)}, u32[]{:S(2)}, u32[]{:S(2)}) %all-to-all-start) | async-done | bytes 1310752 | tf_op jit(solution)/shard_map/wide_sum/all_to_all | solution.py:341
  38.9 0.9 %pack.1 = bf16[4,112,128]{2,1,0:T(8,128)(2,1)} custom-call(bf16[32,16,1280]{2,1,0:T(8,128)(2,1)S(1)} %all-to-all-done.parts, f32[2,512]{1,0:T(2,128)S(1)} %get-tuple-element.36.keep_lam, f32[2,512]{1,0:T(2,128)S(1)} %collective-permute-done.1.send_lam), custom_call_target="tpu_custom_call" | custom-call | tf_op jit(solution)/shard_map/pack/pallas_call | solution.py:407
  39.8 7.3 %all-to-all-start.1 = ((bf16[4,112,128]{2,1,0:T(8,128)(2,1)}), bf16[4,112,128]{2,1,0:T(8,128)(2,1)S(1)}, u32[]{:S(2)}, u32[]{:S(2)}) async-start(bf16[4,112,128]{2,1,0:T(8,128)(2,1)} %pack.1), calls=%async_computation.1 | async-start | bytes 229376 | tf_op jit(solution)/shard_map/deep_sum/all_to_all | solution.py:341
  47.1 0.1 fusion.17
  47.1 7.1 %all-to-all-done.1.got = bf16[4,112,128]{2,1,0:T(8,128)(2,1)S(1)} async-done(((bf16[4,112,128]{2,1,0:T(8,128)(2,1)}), bf16[4,112,128]{2,1,0:T(8,128)(2,1)S(1)}, u32[]{:S(2)}, u32[]{:S(2)}) %all-to-all-start.1) | async-done | bytes 114720 | tf_op jit(solution)/shard_map/deep_sum/all_to_all | solution.py:341
  54.2 1.1 %rotate.1 = bf16[32,80,128]{2,1,0:T(8,128)(2,1)} custom-call(bf16[4,112,128]{2,1,0:T(8,128)(2,1)S(1)} %all-to-all-done.1.got, bf16[512,512]{1,0:T(8,128)(2,1)S(1)} %get-tuple-element.30.basis.basis_out), custom_call_target="tpu_custom_call" | custom-call | tf_op jit(solution)/shard_map/rotate/pallas_call | solution.py:413
  55.3 4.3 %all-to-all-start.2 = ((bf16[32,80,128]{2,1,0:T(8,128)(2,1)}), bf16[32,80,128]{2,1,0:T(8,128)(2,1)S(1)}, u32[]{:S(2)}, u32[]{:S(2)}) async-start(bf16[32,80,128]{2,1,0:T(8,128)(2,1)} %rotate.1), calls=%async_computation.2 | async-start | bytes 1310720 | tf_op jit(solution)/shard_map/gather/all_to_all | solution.py:341
  59.6 0.1 pad_add_fusion.place
  59.7 0.6 rows.1
  60.3 10.2 %all-to-all-done.2.got = bf16[32,80,128]{2,1,0:T(8,128)(2,1)S(1)} async-done(((bf16[32,80,128]{2,1,0:T(8,128)(2,1)}), bf16[32,80,128]{2,1,0:T(8,128)(2,1)S(1)}, u32[]{:S(2)}, u32[]{:S(2)}) %all-to-all-start.2) | async-done | bytes 655392 | tf_op jit(solution)/shard_map/gather/all_to_all | solution.py:341
  70.5 1.1 %solve.1 = (f32[8,512]{1,0:T(8,128)S(1)}, f32[8,512]{1,0:T(8,128)S(1)}) custom-call(bf16[32,80,128]{2,1,0:T(8,128)(2,1)S(1)} %all-to-all-done.2.got, bf16[512,512]{1,0:T(8,128)(2,1)S(1)} %get-tuple-element.21.basis_in_t, bf16[512,512]{1,0:T(8,128)(2,1)S(1)} %get-tuple-element.30.basis.basis_out, bf16[16,512]{1,0:T(8,128)(2,1)S(1)} %pad.4.rows_in, ...), custom_call_target="tpu_custom_call" | custom-call | tf_op jit(solution)/shard_map/solve/pallas_call | solution.py:422
  71.5 3.8 %collective-permute-start.2 = (f32[8,512]{1,0:T(8,128)S(1)}, f32[8,512]{1,0:T(8,128)S(1)}, u32[]{:S(2)}, u32[]{:S(2)}) collective-permute-start(f32[8,512]{1,0:T(8,128)S(1)} %get-tuple-element.25), channel_id=1, source_target_pairs={{0,1},{1,0},{2,3},{3,2},{4,5},{5,4},{6,7},{7,6},{8,9},{9,8},{10,11... | collective-permute-start | bytes 49160 | tf_op jit(solution)/shard_map/ppermute | solution.py:425
  75.3 0.8 %collective-permute-done.2.got = f32[8,512]{1,0:T(8,128)S(1)} collective-permute-done((f32[8,512]{1,0:T(8,128)S(1)}, f32[8,512]{1,0:T(8,128)S(1)}, u32[]{:S(2)}, u32[]{:S(2)}) %collective-permute-start.2) | collective-permute-done | bytes 16416 | tf_op jit(solution)/shard_map/ppermute | solution.py:425
  76.2 0.6 finish.1
  (15 shorter events, 0.1 us)
Async XLA Ops:
  4.4 5.7 %copy-start.4 = (bf16[16,2,16,1280]{3,2,1,0:T(8,128)(2,1)}, bf16[16,2,16,1280]{3,2,1,0:T(8,128)(2,1)S(1)}, u32[]{:S(2)}) copy-start(bf16[16,2,16,1280]{3,2,1,0:T(8,128)(2,1)S(1)} %get-tuple-element.18) | copy-start | bytes 3932164
  4.4 5.8 %collective-permute-start = (bf16[16,2,16,1280]{3,2,1,0:T(8,128)(2,1)S(1)}, bf16[16,2,16,1280]{3,2,1,0:T(8,128)(2,1)S(1)}, u32[]{:S(2)}, u32[]{:S(2)}) collective-permute-start(bf16[16,2,16,1280]{3,2,1,0:T(8,128)(2,1)S(1)} %get-tuple-element.18), channel_id=1, source_target_pairs={{0,1},{1,0},{2,3},{3,2},{4,5},{5,4},{6,7},{7,6},{8,9},{9,8},{10,11... | collective-permute-start | bytes 3932168 | tf_op jit(solution)/shard_map/ppermute | solution.py:373
  10.1 1.1 %copy-start.2 = (bf16[16,2,16,1280]{3,2,1,0:T(8,128)(2,1)}, bf16[16,2,16,1280]{3,2,1,0:T(8,128)(2,1)S(1)}, u32[]{:S(2)}) copy-start(bf16[16,2,16,1280]{3,2,1,0:T(8,128)(2,1)S(1)} %grams_mine.1.mine) | copy-start | bytes 3932164
  11.2 1.1 %copy-start.1 = (bf16[16,2,16,1280]{3,2,1,0:T(8,128)(2,1)}, bf16[16,2,16,1280]{3,2,1,0:T(8,128)(2,1)S(1)}, u32[]{:S(2)}) copy-start(bf16[16,2,16,1280]{3,2,1,0:T(8,128)(2,1)S(1)} %chip_sum.1) | copy-start | bytes 3932164
  12.3 6.8 %copy-start = (bf16[3,512,512]{2,1,0:T(8,128)(2,1)S(1)}, bf16[3,512,512]{2,1,0:T(8,128)(2,1)}, u32[]{:S(2)}) copy-start(bf16[3,512,512]{2,1,0:T(8,128)(2,1)} %bases.1) | copy-start | bytes 4718596
  12.3 26.6 %all-to-all-start = ((bf16[32,16,1280]{2,1,0:T(8,128)(2,1)}), bf16[32,16,1280]{2,1,0:T(8,128)(2,1)S(1)}, u32[]{:S(2)}, u32[]{:S(2)}) async-start(bf16[32,16,1280]{2,1,0:T(8,128)(2,1)} %bitcast.50), calls=%async_computation | async-start | bytes 2621440 | tf_op jit(solution)/shard_map/wide_sum/all_to_all | solution.py:341
  19.1 1.3 %copy-start.3 = (bf16[16,2,16,1280]{3,2,1,0:T(8,128)(2,1)S(1)}, bf16[16,2,16,1280]{3,2,1,0:T(8,128)(2,1)}, u32[]{:S(2)}) copy-start(bf16[16,2,16,1280]{3,2,1,0:T(8,128)(2,1)} %copy-done.2) | copy-start | bytes 3932164
  20.4 1.3 %copy-start.5 = (bf16[16,2,16,1280]{3,2,1,0:T(8,128)(2,1)S(1)}, bf16[16,2,16,1280]{3,2,1,0:T(8,128)(2,1)}, u32[]{:S(2)}) copy-start(bf16[16,2,16,1280]{3,2,1,0:T(8,128)(2,1)} %copy-done.4) | copy-start | bytes 3932164
  21.7 1.1 %copy-start.6 = (f32[2,3,512]{2,0,1:T(2,128)S(1)}, f32[2,3,512]{2,0,1:T(2,128)}, u32[]{:S(2)}) copy-start(f32[2,3,512]{2,0,1:T(2,128)} %param.13) | copy-start | bytes 36868
  23.9 1.6 %collective-permute-start.1 = (f32[2,512]{1,0:T(2,128)S(1)}, f32[2,512]{1,0:T(2,128)S(1)}, u32[]{:S(2)}, u32[]{:S(2)}) collective-permute-start(f32[2,512]{1,0:T(2,128)S(1)} %get-tuple-element.35), channel_id=1, source_target_pairs={{0,1},{1,0},{2,3},{3,2},{4,5},{5,4},{6,7},{7,6},{8,9},{9,8},{10,11... | collective-permute-start | bytes 12296 | tf_op jit(solution)/shard_map/ppermute | solution.py:404
  39.8 14.4 %all-to-all-start.1 = ((bf16[4,112,128]{2,1,0:T(8,128)(2,1)}), bf16[4,112,128]{2,1,0:T(8,128)(2,1)S(1)}, u32[]{:S(2)}, u32[]{:S(2)}) async-start(bf16[4,112,128]{2,1,0:T(8,128)(2,1)} %pack.1), calls=%async_computation.1 | async-start | bytes 229376 | tf_op jit(solution)/shard_map/deep_sum/all_to_all | solution.py:341
  55.3 15.2 %all-to-all-start.2 = ((bf16[32,80,128]{2,1,0:T(8,128)(2,1)}), bf16[32,80,128]{2,1,0:T(8,128)(2,1)S(1)}, u32[]{:S(2)}, u32[]{:S(2)}) async-start(bf16[32,80,128]{2,1,0:T(8,128)(2,1)} %rotate.1), calls=%async_computation.2 | async-start | bytes 1310720 | tf_op jit(solution)/shard_map/gather/all_to_all | solution.py:341
  71.5 4.6 %collective-permute-start.2 = (f32[8,512]{1,0:T(8,128)S(1)}, f32[8,512]{1,0:T(8,128)S(1)}, u32[]{:S(2)}, u32[]{:S(2)}) collective-permute-start(f32[8,512]{1,0:T(8,128)S(1)} %get-tuple-element.25), channel_id=1, source_target_pairs={{0,1},{1,0},{2,3},{3,2},{4,5},{5,4},{6,7},{7,6},{8,9},{9,8},{10,11... | collective-permute-start | bytes 49160 | tf_op jit(solution)/shard_map/ppermute | solution.py:425

commit v5 on v4

--- a/solution.py
+++ b/solution.py
@@ -54,7 +54,7 @@
         kernel,
         out_shape=outs,
         in_specs=in_specs,
-        out_specs=jax.tree.map(lambda _: VMEM, outs),
+        out_specs=jax.tree.map(lambda out: HBM if isinstance(out, pl.MemoryRef) else VMEM, outs),
         scratch_shapes=list(scratch),
         compiler_params=pltpu.CompilerParams(vmem_limit_bytes=limit * MB),
         cost_estimate=pl.CostEstimate(flops=flops, bytes_accessed=moved, transcendentals=0),
@@ -178,17 +178,30 @@
     grams(pick, x0, buf1, ready, out)
 
 
-def add_kernel(mine, received, out):
-    for i in range(NXY):
-        for j in range(PAIR):
-            out[i, j] = mine[i, j] + received[i, j]
-
-
-def lam_kernel(share, core, mine, other, bases, keep_lam, send_lam, basis_in_t):
+PIECES = 4
+
+
+def add_kernel(mine, received, out, buf, sems):
+    size = NXY // PIECES
+    copies = []
+    for q in range(PIECES):
+        for i in range(q * size, (q + 1) * size):
+            for j in range(PAIR):
+                buf[i, j] = mine[i, j] + received[i, j]
+        part = pl.ds(q * size, size)
+        copies.append(pltpu.make_async_copy(buf.at[part], out.at[part], sems.at[q]))
+        copies[q].start()
+    for copy in copies:
+        copy.wait()
+
+
+def lam_kernel(share, core, chip, bases, keep_lam, send_lam, basis_in_t, buf, sem):
     c = core[0]
-
-    def image(source, begin, size, basis):
-        return dot(source[:, :, pl.ds(begin, size)].reshape(D, size), basis)
+    fetched = pltpu.make_async_copy(chip.at[:, :, pl.ds(D, D + HALF)], buf, sem)
+    fetched.start()
+
+    def image(begin, size, basis):
+        return dot(buf[:, :, pl.ds(begin, size)].reshape(D, size), basis)
 
     def arranged(index):
         low, high = arrange(bases[index].astype(f32))
@@ -198,14 +211,14 @@
         return jnp.sum(basis * product, axis=0, keepdims=True) * share
 
     near = pl.ds(pl.multiple_of(c * HALF, HALF), HALF)
-    far = pl.ds(pl.multiple_of((1 - c) * HALF, HALF), HALF)
     basis = arranged(0)
     basis_in_t[...] = basis.T.astype(bf16)
-    lam0 = values(basis, image(mine, 2 * D, HALF, bases[0, near, :]) + image(other, 2 * D, HALF, bases[0, far, :]))
+    fetched.wait()
+    lam0 = values(basis, image(D, HALF, bases[0, near, :]))
     keep_lam[0:1, :] = lam0
+    keep_lam[1:2, :] = values(arranged(1 + c), image(0, D, bases[1 + c]))
     send_lam[0:1, :] = lam0
-    keep_lam[1:2, :] = values(arranged(1 + c), image(mine, D, D, bases[1 + c]))
-    send_lam[1:2, :] = values(arranged(2 - c), image(other, D, D, bases[2 - c]))
+    send_lam[1:2, :] = jnp.zeros((1, D), f32)
 
 
 def split(value):
@@ -381,7 +394,12 @@
             moved=4 * MB,
         )(core[None], keep, kept, keys, vals)
     with jax.named_scope("chip_sum"):
-        chip = call(add_kernel, partial, [VMEM] * 2)(mine, received).reshape(WIDE, ROWS, COLS)
+        chip = call(
+            add_kernel,
+            pltpu.HBM(partial.shape, bf16),
+            [VMEM] * 2,
+            [pltpu.VMEM(partial.shape, bf16), pltpu.SemaphoreType.DMA((PIECES,))],
+        )(mine, received).reshape(WIDE, ROWS, COLS)
     with jax.named_scope("wide_sum"):
         parts = exchange(chip, WIDE_GROUPS)
 
@@ -390,10 +408,11 @@
         keep_lam, send_lam, basis_in_t = call(
             functools.partial(lam_kernel, share),
             (lam_shape, lam_shape, shape((D, D), bf16)),
-            [SMEM] + [VMEM] * 3,
-            flops=6 * D * D * D,
-            moved=4 * MB,
-        )(core[None], mine.reshape(WIDE, ROWS, COLS), other.reshape(WIDE, ROWS, COLS), bases)
+            [SMEM, HBM, VMEM],
+            [pltpu.VMEM((WIDE, ROWS, D + HALF), bf16), pltpu.SemaphoreType.DMA],
+            flops=3 * D * D * D,
+            moved=3 * MB,
+        )(core[None], in_hbm(chip), bases)
     old_lam = []
     my_rows = lax.dynamic_slice_in_dim(bases, 2 * index, 2, 1).astype(f32)
     for f in range(3):

time: 77.3 us -> 76.5 us (0.990)
  local copies, waits for them, and re-layouts: 4.56 us -> 0.11 us
  waiting for transfers between devices: 32.5 us -> 34.5 us
  Pallas kernels: 11.8 us -> 13.4 us
    unnamed x14 -> x4, local copies, waits for them, and re-layouts: 4.46 us -> 0.01 us
    all_to_all x3, waiting for transfers between devices: 30.7 us -> 32.7 us  [exchange(): lax.all_to_all(value, 'dp', 0, 0, axis_index_groups=groups, tiled=True)]
    pallas_call x1, Pallas kernels: 0.19 us -> 1.16 us  [body(): call(add_kernel, pltpu.HBM(partial.shape, bf16), [VMEM] * 2, [pltpu.VMEM(...]
  transfers between devices with their start and end apart: 6 -> 6, of which waited for: 6 -> 6; matrix products, arithmetic and copies ran while one was open for 2% -> 2% of each run, Pallas kernels for 5% -> 6%
where the time goes in v5:
time: 76.5 us; the launch traced here: 76 us
  waiting for transfers between devices  34.5 us (45%)
  starting transfers between devices  26 us (34%)
  Pallas kernels  13.4 us (18%)
  matrix products  0.99 us (1%)
  between operations  0.88 us (1%)
    all_to_all x3, waiting for transfers between devices, exchange(): lax.all_to_all(value, 'dp', 0, 0, axis_index_groups=groups, tiled=True)  32.7 us
    all_to_all x3, starting transfers between devices, exchange(): lax.all_to_all(value, 'dp', 0, 0, axis_index_groups=groups, tiled=True)  18.3 us
    pallas_call x1, Pallas kernels, body(): call(theirs_kernel, (partial, shape((tokens_here, D), bf16), shape((token...  3.82 us
    ppermute x1, starting transfers between devices, body(): theirs = lax.ppermute(their, 'dp', SWAP)  3.77 us
    ppermute x1, starting transfers between devices, body(): received = lax.ppermute(other, 'dp', SWAP)  3.19 us
    pallas_call x1, Pallas kernels, body(): call(mine_kernel, partial, [SMEM, VMEM, VMEM, HBM, HBM], [buf, sems], flo...  2.52 us
    pallas_call x1, Pallas kernels, body(): call(functools.partial(lam_kernel, share), (lam_shape, lam_shape, shape((...  1.75 us
  transfers between devices with their start and end apart: 6, of which 6 were waited for; matrix products, arithmetic and copies ran while one was open for 2% of the time, Pallas kernels for 6%

profile of v5, /device:TPU:1, one launch (start us, length us, event | category | flops | bytes accessed | tf_op | source)
XLA Modules:
  0.0 76.0 jit_solution(8248300777650108593)
XLA Ops:
  0.6 3.8 %grams_theirs.1 = (bf16[16,2,16,1280]{3,2,1,0:T(8,128)(2,1)S(1)}, bf16[1024,512]{1,0:T(8,128)(2,1)S(1)}, bf16[1024,128]{1,0:T(8,128)(2,1)S(1)}) custom-call(s32[1]{0:T(128)} %bitcast.core, s32[2,8]{1,0:T(2,128)} %bitcast.55, s32[2,8]{1,0:T(2,128)} %bitcast.56, bf16[1024,512]{1,0:T(8,128)(2,1)} %x0.1, bf16[1024,512]{1,0:T(8,128)(2,1)} %xk.3, bf16[1024,512]{1,0:T(8,128)(2,1)} %xv.3), custom_call_target="tpu_custom_call" | custom-call | flops 1342177280 | bytes 4194304 | tf_op jit(solution)/shard_map/grams_theirs/pallas_call | solution.py:378
  4.5 3.2 %collective-permute-start = (bf16[16,2,16,1280]{3,2,1,0:T(8,128)(2,1)S(1)}, bf16[16,2,16,1280]{3,2,1,0:T(8,128)(2,1)S(1)}, u32[]{:S(2)}, u32[]{:S(2)}) collective-permute-start(bf16[16,2,16,1280]{3,2,1,0:T(8,128)(2,1)S(1)} %get-tuple-element.18), channel_id=1, source_target_pairs={{0,1},{1,0},{2,3},{3,2},{4,5},{5,4},{6,7},{7,6},{8,9},{9,8},{10,11... | collective-permute-start | bytes 3932168 | tf_op jit(solution)/shard_map/ppermute | solution.py:386
  7.7 2.5 %grams_mine.1.mine = bf16[16,2,16,1280]{3,2,1,0:T(8,128)(2,1)S(1)} custom-call(s32[1]{0:T(128)} %bitcast.core, bf16[1024,128]{1,0:T(8,128)(2,1)S(1)} %get-tuple-element.16.keep, bf16[1024,512]{1,0:T(8,128)(2,1)S(1)} %get-tuple-element.17.x0, bf16[1024,512]{1,0:T(8,128)(2,1)} %xk.3, bf16[1024,512]{1,0:T(8,128)(2,1)} %xv.3), custom_call_target="tpu_custom_call" | custom-call | flops 1342177280 | bytes 4194304 | tf_op jit(solution)/shard_map/grams_mine/pallas_call | solution.py:388
  10.2 0.1 collective-permute-done.received
  10.3 1.2 %chip_sum.1 = bf16[16,2,16,1280]{3,2,1,0:T(8,128)(2,1)} custom-call(bf16[16,2,16,1280]{3,2,1,0:T(8,128)(2,1)S(1)} %grams_mine.1.mine, bf16[16,2,16,1280]{3,2,1,0:T(8,128)(2,1)S(1)} %collective-permute-done.received), custom_call_target="tpu_custom_call" | custom-call | tf_op jit(solution)/shard_map/chip_sum/pallas_call | solution.py:397
  11.5 0.0 copy-start
  11.5 0.0 copy-start.1
  11.5 6.8 %all-to-all-start = ((bf16[32,16,1280]{2,1,0:T(8,128)(2,1)}), bf16[32,16,1280]{2,1,0:T(8,128)(2,1)S(1)}, u32[]{:S(2)}, u32[]{:S(2)}) async-start(bf16[32,16,1280]{2,1,0:T(8,128)(2,1)} %bitcast.49), calls=%async_computation | async-start | bytes 2621440 | tf_op jit(solution)/shard_map/wide_sum/all_to_all | solution.py:354
  18.3 0.0 copy-done
  18.4 0.0 copy-done.1
  18.4 0.3 fusion.1
  18.7 0.3 fusion.2
  19.0 0.3 fusion
  19.4 1.7 %lam.1 = (f32[2,512]{1,0:T(2,128)S(1)}, f32[2,512]{1,0:T(2,128)S(1)}, bf16[512,512]{1,0:T(8,128)(2,1)S(1)}) custom-call(s32[1]{0:T(128)} %bitcast.core, bf16[32,16,1280]{2,1,0:T(8,128)(2,1)} %bitcast.50, bf16[3,512,512]{2,1,0:T(8,128)(2,1)S(1)} %copy-done), custom_call_target="tpu_custom_call" | custom-call | flops 402653184 | bytes 3145728 | tf_op jit(solution)/shard_map/lam/pallas_call | solution.py:408
  21.2 0.7 collective-permute-start.1
  21.9 0.8 %collective-permute-done.1.send_lam = f32[2,512]{1,0:T(2,128)S(1)} collective-permute-done((f32[2,512]{1,0:T(2,128)S(1)}, f32[2,512]{1,0:T(2,128)S(1)}, u32[]{:S(2)}, u32[]{:S(2)}) %collective-permute-start.1) | collective-permute-done | bytes 4128 | tf_op jit(solution)/shard_map/ppermute | solution.py:423
  22.7 15.4 %all-to-all-done.parts = bf16[32,16,1280]{2,1,0:T(8,128)(2,1)S(1)} async-done(((bf16[32,16,1280]{2,1,0:T(8,128)(2,1)}), bf16[32,16,1280]{2,1,0:T(8,128)(2,1)S(1)}, u32[]{:S(2)}, u32[]{:S(2)}) %all-to-all-start) | async-done | bytes 1310752 | tf_op jit(solution)/shard_map/wide_sum/all_to_all | solution.py:354
  38.2 0.8 %pack.1 = bf16[4,112,128]{2,1,0:T(8,128)(2,1)} custom-call(bf16[32,16,1280]{2,1,0:T(8,128)(2,1)S(1)} %all-to-all-done.parts, f32[2,512]{1,0:T(2,128)S(1)} %get-tuple-element.36.keep_lam, f32[2,512]{1,0:T(2,128)S(1)} %collective-permute-done.1.send_lam), custom_call_target="tpu_custom_call" | custom-call | tf_op jit(solution)/shard_map/pack/pallas_call | solution.py:426
  39.0 7.3 %all-to-all-start.1 = ((bf16[4,112,128]{2,1,0:T(8,128)(2,1)}), bf16[4,112,128]{2,1,0:T(8,128)(2,1)S(1)}, u32[]{:S(2)}, u32[]{:S(2)}) async-start(bf16[4,112,128]{2,1,0:T(8,128)(2,1)} %pack.1), calls=%async_computation.1 | async-start | bytes 229376 | tf_op jit(solution)/shard_map/deep_sum/all_to_all | solution.py:354
  46.3 0.1 fusion.17
  46.4 7.1 %all-to-all-done.1.got = bf16[4,112,128]{2,1,0:T(8,128)(2,1)S(1)} async-done(((bf16[4,112,128]{2,1,0:T(8,128)(2,1)}), bf16[4,112,128]{2,1,0:T(8,128)(2,1)S(1)}, u32[]{:S(2)}, u32[]{:S(2)}) %all-to-all-start.1) | async-done | bytes 114720 | tf_op jit(solution)/shard_map/deep_sum/all_to_all | solution.py:354
  53.4 1.1 %rotate.1 = bf16[32,80,128]{2,1,0:T(8,128)(2,1)} custom-call(bf16[4,112,128]{2,1,0:T(8,128)(2,1)S(1)} %all-to-all-done.1.got, bf16[512,512]{1,0:T(8,128)(2,1)S(1)} %get-tuple-element.30.basis.basis_out), custom_call_target="tpu_custom_call" | custom-call | tf_op jit(solution)/shard_map/rotate/pallas_call | solution.py:432
  54.5 4.3 %all-to-all-start.2 = ((bf16[32,80,128]{2,1,0:T(8,128)(2,1)}), bf16[32,80,128]{2,1,0:T(8,128)(2,1)S(1)}, u32[]{:S(2)}, u32[]{:S(2)}) async-start(bf16[32,80,128]{2,1,0:T(8,128)(2,1)} %rotate.1), calls=%async_computation.2 | async-start | bytes 1310720 | tf_op jit(solution)/shard_map/gather/all_to_all | solution.py:354
  58.9 0.1 pad_add_fusion.place
  58.9 0.6 rows.1
  59.5 10.2 %all-to-all-done.2.got = bf16[32,80,128]{2,1,0:T(8,128)(2,1)S(1)} async-done(((bf16[32,80,128]{2,1,0:T(8,128)(2,1)}), bf16[32,80,128]{2,1,0:T(8,128)(2,1)S(1)}, u32[]{:S(2)}, u32[]{:S(2)}) %all-to-all-start.2) | async-done | bytes 655392 | tf_op jit(solution)/shard_map/gather/all_to_all | solution.py:354
  69.7 1.1 %solve.1 = (f32[8,512]{1,0:T(8,128)S(1)}, f32[8,512]{1,0:T(8,128)S(1)}) custom-call(bf16[32,80,128]{2,1,0:T(8,128)(2,1)S(1)} %all-to-all-done.2.got, bf16[512,512]{1,0:T(8,128)(2,1)S(1)} %get-tuple-element.21.basis_in_t, bf16[512,512]{1,0:T(8,128)(2,1)S(1)} %get-tuple-element.30.basis.basis_out, bf16[16,512]{1,0:T(8,128)(2,1)S(1)} %pad.4.rows_in, ...), custom_call_target="tpu_custom_call" | custom-call | tf_op jit(solution)/shard_map/solve/pallas_call | solution.py:441
  70.8 3.8 %collective-permute-start.2 = (f32[8,512]{1,0:T(8,128)S(1)}, f32[8,512]{1,0:T(8,128)S(1)}, u32[]{:S(2)}, u32[]{:S(2)}) collective-permute-start(f32[8,512]{1,0:T(8,128)S(1)} %get-tuple-element.25), channel_id=1, source_target_pairs={{0,1},{1,0},{2,3},{3,2},{4,5},{5,4},{6,7},{7,6},{8,9},{9,8},{10,11... | collective-permute-start | bytes 49160 | tf_op jit(solution)/shard_map/ppermute | solution.py:444
  74.5 0.8 %collective-permute-done.2.got = f32[8,512]{1,0:T(8,128)S(1)} collective-permute-done((f32[8,512]{1,0:T(8,128)S(1)}, f32[8,512]{1,0:T(8,128)S(1)}, u32[]{:S(2)}, u32[]{:S(2)}) %collective-permute-start.2) | collective-permute-done | bytes 16416 | tf_op jit(solution)/shard_map/ppermute | solution.py:444
  75.4 0.6 finish.1
  (7 shorter events, 0.1 us)
Async XLA Ops:
  4.5 5.9 %collective-permute-start = (bf16[16,2,16,1280]{3,2,1,0:T(8,128)(2,1)S(1)}, bf16[16,2,16,1280]{3,2,1,0:T(8,128)(2,1)S(1)}, u32[]{:S(2)}, u32[]{:S(2)}) collective-permute-start(bf16[16,2,16,1280]{3,2,1,0:T(8,128)(2,1)S(1)} %get-tuple-element.18), channel_id=1, source_target_pairs={{0,1},{1,0},{2,3},{3,2},{4,5},{5,4},{6,7},{7,6},{8,9},{9,8},{10,11... | collective-permute-start | bytes 3932168 | tf_op jit(solution)/shard_map/ppermute | solution.py:386
  11.5 6.8 %copy-start = (bf16[3,512,512]{2,1,0:T(8,128)(2,1)S(1)}, bf16[3,512,512]{2,1,0:T(8,128)(2,1)}, u32[]{:S(2)}) copy-start(bf16[3,512,512]{2,1,0:T(8,128)(2,1)} %bases.1) | copy-start | bytes 4718596
  11.5 6.9 %copy-start.1 = (f32[2,3,512]{2,0,1:T(2,128)S(1)}, f32[2,3,512]{2,0,1:T(2,128)}, u32[]{:S(2)}) copy-start(f32[2,3,512]{2,0,1:T(2,128)} %param.13) | copy-start | bytes 36868
  11.5 26.7 %all-to-all-start = ((bf16[32,16,1280]{2,1,0:T(8,128)(2,1)}), bf16[32,16,1280]{2,1,0:T(8,128)(2,1)S(1)}, u32[]{:S(2)}, u32[]{:S(2)}) async-start(bf16[32,16,1280]{2,1,0:T(8,128)(2,1)} %bitcast.49), calls=%async_computation | async-start | bytes 2621440 | tf_op jit(solution)/shard_map/wide_sum/all_to_all | solution.py:354
  21.2 1.6 %collective-permute-start.1 = (f32[2,512]{1,0:T(2,128)S(1)}, f32[2,512]{1,0:T(2,128)S(1)}, u32[]{:S(2)}, u32[]{:S(2)}) collective-permute-start(f32[2,512]{1,0:T(2,128)S(1)} %get-tuple-element.35), channel_id=1, source_target_pairs={{0,1},{1,0},{2,3},{3,2},{4,5},{5,4},{6,7},{7,6},{8,9},{9,8},{10,11... | collective-permute-start | bytes 12296 | tf_op jit(solution)/shard_map/ppermute | solution.py:423
  39.0 14.4 %all-to-all-start.1 = ((bf16[4,112,128]{2,1,0:T(8,128)(2,1)}), bf16[4,112,128]{2,1,0:T(8,128)(2,1)S(1)}, u32[]{:S(2)}, u32[]{:S(2)}) async-start(bf16[4,112,128]{2,1,0:T(8,128)(2,1)} %pack.1), calls=%async_computation.1 | async-start | bytes 229376 | tf_op jit(solution)/shard_map/deep_sum/all_to_all | solution.py:354
  54.5 15.2 %all-to-all-start.2 = ((bf16[32,80,128]{2,1,0:T(8,128)(2,1)}), bf16[32,80,128]{2,1,0:T(8,128)(2,1)S(1)}, u32[]{:S(2)}, u32[]{:S(2)}) async-start(bf16[32,80,128]{2,1,0:T(8,128)(2,1)} %rotate.1), calls=%async_computation.2 | async-start | bytes 1310720 | tf_op jit(solution)/shard_map/gather/all_to_all | solution.py:354
  70.8 4.6 %collective-permute-start.2 = (f32[8,512]{1,0:T(8,128)S(1)}, f32[8,512]{1,0:T(8,128)S(1)}, u32[]{:S(2)}, u32[]{:S(2)}) collective-permute-start(f32[8,512]{1,0:T(8,128)S(1)} %get-tuple-element.25), channel_id=1, source_target_pairs={{0,1},{1,0},{2,3},{3,2},{4,5},{5,4},{6,7},{7,6},{8,9},{9,8},{10,11... | collective-permute-start | bytes 49160 | tf_op jit(solution)/shard_map/ppermute | solution.py:444

commit v6 on v5

--- a/solution.py
+++ b/solution.py
@@ -16,10 +16,12 @@
 WIDE = NXY * PAIR
 DEEP = NZ // PAIR
 ROWS = D // WIDE
-COLS = D + D + HALF
 LANES = 128
 FR = ROWS // DEEP
-GT, FT = D // LANES, (D + HALF) // LANES
+GT = D // LANES
+BLK = D // NXY
+FA, F0, FL = GT * ROWS, (GT + 2) * ROWS, (GT + 3) * ROWS
+WROWS = FL + ROWS // 2
 MB = 1 << 20
 
 decay = 0.8
@@ -124,24 +126,45 @@
 
 
 def put(out, r, value, begin):
-    places, cols = pl.ds(r * (BLOCK // (PAIR * ROWS)), BLOCK // (PAIR * ROWS)), pl.ds(begin, value.shape[1])
-    low, high = arrange(value)
-    out[places, 0, :, cols] = low.astype(bf16)
-    out[places, 1, :, cols] = high.astype(bf16)
+    places = pl.ds(r * (BLOCK // BLK), BLOCK // BLK)
+    for half, rows in enumerate(arrange(value)):
+        for j in range(value.shape[1] // LANES):
+            out[places, half, pl.ds(begin + j * ROWS, ROWS), :] = rows[:, :, j * LANES : (j + 1) * LANES].astype(bf16)
+
+
+def put_folded(out, r, value, begin):
+    places = pl.ds(r * (BLOCK // BLK), BLOCK // BLK)
+    for half, rows in enumerate(arrange(value)):
+        upper, lower = rows[:, : ROWS // 2], pltpu.roll(rows[:, ROWS // 2 :], LANES // 2, 2)
+        lane = lax.broadcasted_iota(jnp.int32, upper.shape, 2)
+        out[places, half, pl.ds(begin, ROWS // 2), :] = jnp.where(lane < LANES // 2, upper, lower).astype(bf16)
+
+
+def circulate(value, r):
+    rows = []
+    for b in range(BLOCK // BLK):
+        shift = (D - BLK * (r * (BLOCK // BLK) + b)) % D
+        piece = value[b * BLK : (b + 1) * BLK]
+        rows.append(pltpu.roll(piece, shift, 1) if shift else piece)
+    return [jnp.concatenate([p[:, t * LANES : (t + 1) * LANES] for p in rows], axis=0) for t in range(3)]
 
 
 def grams(pick, x0, x1, ready, out):
-    half = pl.ds(pl.multiple_of(pick * HALF, HALF), HALF)
-    lefts = []
+    lefts, rests = [], []
     for r in range(D // BLOCK):
         lefts.append(x0[:, pl.ds(r * BLOCK, BLOCK)].T)
-        put(out, r, dot(lefts[r], x0[:, half]), 2 * D)
+        tiles = circulate(dot(lefts[r], x0[...]), r)
+        put(out, r, jnp.where(pick == 0, tiles[0], tiles[1]), F0)
+        rests.append(pltpu.roll(jnp.where(pick == 0, tiles[1], tiles[2]), BLK, 1))
     ready()
     for r in range(D // BLOCK):
         put(out, r, dot(lefts[r], x1[...]), 0)
     for r in range(D // BLOCK):
         left = x1[:, pl.ds(r * BLOCK, BLOCK)].T
-        put(out, r, dot(left, x1[...]), D)
+        tiles = circulate(dot(left, x1[...]), r)
+        put(out, r, jnp.concatenate(tiles[:2], axis=1), FA)
+        lane = lax.broadcasted_iota(jnp.int32, tiles[2].shape, 1)
+        put_folded(out, r, jnp.where(lane < BLK, tiles[2], rests[r]), FL)
 
 
 def theirs_kernel(core, start, width, x0, xk, xv, out, kept, keep, buf0, buf1, masks, sem0, sem1, sem2):
@@ -195,30 +218,34 @@
         copy.wait()
 
 
-def lam_kernel(share, core, chip, bases, keep_lam, send_lam, basis_in_t, buf, sem):
+def lam_kernel(share, core, keep, x0, xk, xv, bases, keep_lam, send_lam, basis_in_t, mirror, b0, b1, b2, sem0, sem1, sem2):
     c = core[0]
-    fetched = pltpu.make_async_copy(chip.at[:, :, pl.ds(D, D + HALF)], buf, sem)
-    fetched.start()
-
-    def image(begin, size, basis):
-        return dot(buf[:, :, pl.ds(begin, size)].reshape(D, size), basis)
-
-    def arranged(index):
-        low, high = arrange(bases[index].astype(f32))
-        return jnp.concatenate([low, high], axis=1).reshape(D, D)
-
-    def values(basis, product):
-        return jnp.sum(basis * product, axis=0, keepdims=True) * share
-
-    near = pl.ds(pl.multiple_of(c * HALF, HALF), HALF)
-    basis = arranged(0)
-    basis_in_t[...] = basis.T.astype(bf16)
-    fetched.wait()
-    lam0 = values(basis, image(D, HALF, bases[0, near, :]))
-    keep_lam[0:1, :] = lam0
-    keep_lam[1:2, :] = values(arranged(1 + c), image(0, D, bases[1 + c]))
-    send_lam[0:1, :] = lam0
-    send_lam[1:2, :] = jnp.zeros((1, D), f32)
+    bufs = (b0, b1, b2)
+    copies = [fetch(x, buf, sem) for x, buf, sem in zip((x0, xk, xv), bufs, (sem0, sem1, sem2))]
+    for group in copies:
+        for copy in group:
+            copy.start()
+    low, high = arrange(bases[0].astype(f32))
+    basis_in_t[...] = jnp.concatenate([low, high], axis=1).reshape(D, D).T.astype(bf16)
+    lane = lax.broadcasted_iota(jnp.int32, (LANES, D), 0)
+    column = lax.broadcasted_iota(jnp.int32, (LANES, D), 1)
+    for half in range(PAIR):
+        home = (D - BLK * (lane >> 4) + 8 * ((lane >> 2) & 3) + FR * half + (lane & 3)) & (D - 1)
+        mirror[half] = jnp.where(column == home, 1.0, 0.0).astype(bf16)
+    lam = []
+    for f in range(3):
+        total = jnp.zeros((8, D), f32)
+        for q in range(CHUNKS):
+            copies[f][q].wait()
+            apply_mask(bufs[f], bufs[f], keep, q)
+        for q in range(bufs[f].shape[0] // BLOCK):
+            product = dot(bufs[f][pl.ds(q * BLOCK, BLOCK), :], bases[f])
+            total = total + jnp.sum((product * product).reshape(BLOCK // 8, 8, D), axis=0)
+        lam.append(jnp.sum(total, axis=0, keepdims=True) * share)
+    keep_lam[0:1, :] = lam[0]
+    send_lam[0:1, :] = lam[0]
+    keep_lam[1:2, :] = jnp.where(c == 0, lam[1], lam[2])
+    send_lam[1:2, :] = jnp.where(c == 0, lam[2], lam[1])
 
 
 def split(value):
@@ -239,72 +266,115 @@
 
 
 LAMR = 4 * GT
-TAIL = ((FT * FR + LAMR + 15) // 16) * 16
-DEEP_ROWS = GT * ROWS + TAIL
-GATHER_ROWS = GT * ROWS + LAMR
+DIRECT = GT * ROWS
+TURNED = DIRECT + 4 * FR
+DEEP_LAM = TURNED + 16
+DEEP_ROWS = DEEP_LAM + LAMR
+GATHER_LAM = GT * ROWS
+GATHER_TURNED = GATHER_LAM + LAMR
+GATHER_ROWS = GATHER_TURNED + 8
 
 
 def pack_kernel(parts, keep_lam, send_lam, out):
     total = parts[0].astype(f32)
     for i in range(1, WIDE):
         total = total + parts[i].astype(f32)
-    lam = lam_rows(keep_lam[...] + send_lam[...])
+    lam = lam_rows(keep_lam[...] + send_lam[...]).astype(bf16)
     for j in range(GT):
-        tile = total[:, j * LANES : (j + 1) * LANES].astype(bf16)
+        tile = total[j * ROWS : (j + 1) * ROWS].astype(bf16)
         for k in range(DEEP):
             out[k, pl.ds(j * ROWS, ROWS), :] = tile
-    pad = jnp.zeros((TAIL - FT * FR - LAMR, LANES), f32)
+    near, mid, zero = total[FA : FA + ROWS], total[FA + ROWS : F0], total[F0:FL]
+    last = total[FL:]
+    last = jnp.concatenate([last, pltpu.roll(last, LANES // 2, 1)], axis=0)
+    empty = jnp.zeros((LANES - ROWS, LANES), f32)
+    turned = [jnp.concatenate([v, empty], axis=0).T for v in (near, mid, zero)]
     for k in range(DEEP):
-        rows = total[k * FR : (k + 1) * FR]
-        pieces = [rows[:, D + t * LANES : D + (t + 1) * LANES] for t in range(FT)]
-        out[k, pl.ds(GT * ROWS, TAIL), :] = jnp.concatenate(pieces + [lam, pad], axis=0).astype(bf16)
-
-
-def rotate_kernel(got, basis, out):
+        rows = slice(k * FR, (k + 1) * FR)
+        direct = jnp.concatenate([v[rows] for v in (near, mid, zero, last)], axis=0)
+        out[k, pl.ds(DIRECT, 4 * FR), :] = direct.astype(bf16)
+
+        def pieces(sources):
+            result = None
+            for n in range(4 * len(sources)):
+                piece = sources[n // 4][(n % 4) * BLK + 8 * k : (n % 4) * BLK + 8 * k + 8]
+                piece = pltpu.roll(piece, ROWS * n, 1) if n else piece
+                result = piece if result is None else result + piece
+            return result
+
+        mirrored = jnp.concatenate([pieces(turned[:2]), pieces(turned[2:])], axis=0)
+        out[k, pl.ds(TURNED, 16), :] = mirrored.astype(bf16)
+        out[k, pl.ds(DEEP_LAM, LAMR), :] = lam
+
+
+def deep_total(got):
     total = got[0].astype(f32)
     for i in range(1, DEEP):
         total = total + got[i].astype(f32)
-    grad = jnp.concatenate([total[j * ROWS : (j + 1) * ROWS] for j in range(GT)], axis=1)
+    return total, jnp.concatenate([total[j * ROWS : (j + 1) * ROWS] for j in range(GT)], axis=1)
+
+
+def rotate_kernel(got, basis, out):
+    total, grad = deep_total(got)
     rot = dot(grad.astype(bf16), basis[...]).astype(bf16)
-    base = GT * ROWS
-    lam = add_lam(total[base + FT * FR : base + FT * FR + LAMR])
+    lam = add_lam(total[DEEP_LAM:])
     lam = jnp.concatenate(split(lam), axis=0).astype(bf16)
-    for i in range(WIDE):
-        out[i, pl.ds(base, LAMR), :] = lam
+    picked, zero = total[TURNED : TURNED + 8], total[TURNED + 8 : TURNED + 16]
+    for half in range(PAIR):
+        rows = slice(half * FR, (half + 1) * FR)
+        mirrored = jnp.concatenate([picked[rows], zero[rows]], axis=0).astype(bf16)
+        for i in range(half, WIDE, PAIR):
+            out[i, pl.ds(GATHER_LAM, LAMR), :] = lam
+            out[i, pl.ds(GATHER_TURNED, 8), :] = mirrored
     for j in range(GT):
         tile = rot[:, j * LANES : (j + 1) * LANES]
         for i in range(WIDE):
             out[i, pl.ds(j * ROWS, ROWS), :] = tile
 
 
-def rows_kernel(place, got, stay, cross):
-    total = got[0].astype(f32)
-    for i in range(1, DEEP):
-        total = total + got[i].astype(f32)
-    grad = jnp.concatenate([total[j * ROWS : (j + 1) * ROWS] for j in range(GT)], axis=1)
-    base = GT * ROWS
+def rows_kernel(place, got, out):
+    total, grad = deep_total(got)
     k, c = place[0], place[1]
     rows = grad[0:FR]
     for other in range(1, DEEP):
         rows = jnp.where(k == other, grad[other * FR : (other + 1) * FR], rows)
-    factors = [total[base + t * FR : base + (t + 1) * FR] for t in range(FT)]
-    full = jnp.concatenate(factors[:GT], axis=1)
-    part = jnp.concatenate(factors[GT:], axis=1)
-
-    def lines(a):
-        halves = jnp.concatenate([part[a : a + 1], part[a + 1 : a + 2]], axis=1)
-        return jnp.concatenate([jnp.zeros((3, D), f32), rows[a : a + 2], full[a : a + 2], halves], axis=0)
-
-    low, high = lines(0), lines(2)
-    stay[...] = jnp.where(c == 0, low, high)
-    cross[...] = jnp.where(c == 0, high, low)
-
-
-def solve_kernel(got, basis_in_t, basis_out, rows_in, stay, cross, own, their, scaled):
-    base = GT * ROWS
-    lam = got[0, pl.ds(base, LAMR), :].astype(f32)
+    near, mid, zero, last = [total[DIRECT + t * FR : DIRECT + (t + 1) * FR] for t in range(4)]
+    lane = lax.broadcasted_iota(jnp.int32, last.shape, 1)
+    none = jnp.zeros_like(last)
+    end = jnp.where(lane < BLK, last, none)
+    end0 = jnp.where(lane < BLK, pltpu.roll(last, LANES - BLK, 1), none)
+    picked = jnp.concatenate([near, mid, end, none], axis=1)
+    zero = jnp.where(
+        c == 0,
+        jnp.concatenate([zero, none, none, none], axis=1),
+        jnp.concatenate([none, zero, end0, none], axis=1),
+    )
+    out[...] = jnp.concatenate([rows, picked, zero, jnp.zeros_like(rows)], axis=0)
+
+
+def mirrored_rows(place, got, mirror):
+    c, block = place[1], place[2]
+    row = lax.broadcasted_iota(jnp.int32, (8, LANES), 0)
+    group = (lax.broadcasted_iota(jnp.int32, (8, LANES), 1) >> 4) + jnp.where(row >= FR, 4 * c, 0)
+    placed = None
+    for half in range(PAIR):
+        own = jnp.zeros((8, LANES), f32)
+        for i in range(NXY):
+            distance = (block - i) & (NXY - 1)
+            wanted = jnp.where((distance >= 1) & (distance < 8), distance, -1)
+            piece = got[PAIR * i + half, pl.ds(GATHER_TURNED, 8), :].astype(f32)
+            own = jnp.where(group == wanted, piece, own)
+        value = dot(own.astype(bf16), mirror[half])
+        placed = value if placed is None else placed + value
+    moved = jnp.concatenate([placed[:, LANES:], placed[:, :LANES]], axis=1)
+    row = lax.broadcasted_iota(jnp.int32, (8, D), 0)
+    return jnp.where((row >= FR) & (c != 0), moved, placed)
+
+
+def solve_kernel(place, got, basis_in_t, basis_out, rows_in, mirror, rows, own, their, scaled):
+    lam = got[0, pl.ds(GATHER_LAM, LAMR), :].astype(f32)
     for i in range(1, WIDE):
-        lam = lam + got[i, pl.ds(base, LAMR), :].astype(f32)
+        lam = lam + got[i, pl.ds(GATHER_LAM, LAMR), :].astype(f32)
     lam = add_lam(lam)
     column = jnp.broadcast_to(lam_row(lam, 0), (8, D)).T[:, 0:1]
     column = jnp.broadcast_to(column, (D, LANES))
@@ -319,9 +389,14 @@
     back = dot(rows_in[...], scaled[...]).astype(bf16)
     prec = lax.dot_general(back, basis_out[...], (((1,), (1,)), ((), ())), preferred_element_type=f32)
     prec = prec.astype(bf16).astype(f32)
-    curve = jnp.broadcast_to(curve, (1, D))
-    own[...] = jnp.concatenate([prec[0:2], curve, stay[3:8, :]], axis=0)
-    their[...] = jnp.concatenate([prec[2:4], curve, cross[3:8, :]], axis=0)
+    curve = jnp.broadcast_to(curve, (2, D))
+    factors = pltpu.roll(rows[4:12, :] + mirrored_rows(place, got, mirror), BLK * place[2], 1)
+    low = jnp.concatenate([rows[0:2, :], factors[0:2], factors[4:6]], axis=0)
+    high = jnp.concatenate([rows[2:4, :], factors[2:4], factors[6:8]], axis=0)
+    first = place[1] == 0
+    pad = jnp.zeros((6, D), f32)
+    own[...] = jnp.concatenate([prec[0:2], curve, jnp.where(first, low, high), pad], axis=0)
+    their[...] = jnp.concatenate([prec[2:4], curve, jnp.where(first, high, low), pad], axis=0)
 
 
 def finish_kernel(scale, core, own, got, old, new_factors, gradients, updates):
@@ -332,20 +407,9 @@
     side1 = jnp.where(first, got[...], own[...])
     updates[0] = (side0[0:2] * factor).astype(bf16)
     updates[1] = (side1[0:2] * factor).astype(bf16)
-    gradients[:, 0, :] = side0[3:5]
-    gradients[:, 1, :] = side1[3:5]
-    left, right = side0[7:8], side1[7:8]
-    batch = (
-        jnp.concatenate(
-            [
-                jnp.concatenate([left[:, :HALF], right[:, :HALF]], axis=1),
-                jnp.concatenate([left[:, HALF:], right[:, HALF:]], axis=1),
-            ],
-            axis=0,
-        ),
-        side0[5:7],
-        side1[5:7],
-    )
+    gradients[:, 0, :] = side0[4:6]
+    gradients[:, 1, :] = side1[4:6]
+    batch = (side0[8:10] + side1[8:10], side0[6:8], side1[6:8])
     for f in range(3):
         new_factors[f] = decay * old[f] + scale * batch[f]
 
@@ -359,7 +423,7 @@
     core = index % NC
     first = core == 0
     z = (index // NC) % NZ
-    place = jnp.stack([z // PAIR, core])
+    place = jnp.stack([z // PAIR, core, index // (NC * NZ)])
     tokens_here = activations.shape[0]
     share = (1.0 - decay) / (tokens_here * lax.axis_size("dp"))
 
@@ -372,8 +436,8 @@
     buf = pltpu.VMEM((tokens_here, D), bf16)
     sems = pltpu.SemaphoreType.DMA((CHUNKS,))
     pair = pltpu.SemaphoreType.DMA((2,))
-    partial = shape((NXY, PAIR, ROWS, COLS), bf16)
-    work = 2 * D * tokens_here * COLS
+    partial = shape((NXY, PAIR, WROWS, LANES), bf16)
+    work = 6 * D * D * tokens_here
     with jax.named_scope("grams_theirs"):
         other, kept, keep = call(
             theirs_kernel,
@@ -399,20 +463,20 @@
             pltpu.HBM(partial.shape, bf16),
             [VMEM] * 2,
             [pltpu.VMEM(partial.shape, bf16), pltpu.SemaphoreType.DMA((PIECES,))],
-        )(mine, received).reshape(WIDE, ROWS, COLS)
+        )(mine, received).reshape(WIDE, WROWS, LANES)
     with jax.named_scope("wide_sum"):
         parts = exchange(chip, WIDE_GROUPS)
 
     lam_shape = shape((2, D), f32)
     with jax.named_scope("lam"):
-        keep_lam, send_lam, basis_in_t = call(
+        keep_lam, send_lam, basis_in_t, mirror = call(
             functools.partial(lam_kernel, share),
-            (lam_shape, lam_shape, shape((D, D), bf16)),
-            [SMEM, HBM, VMEM],
-            [pltpu.VMEM((WIDE, ROWS, D + HALF), bf16), pltpu.SemaphoreType.DMA],
-            flops=3 * D * D * D,
-            moved=3 * MB,
-        )(core[None], in_hbm(chip), bases)
+            (lam_shape, lam_shape, shape((D, D), bf16), shape((PAIR, LANES, D), bf16)),
+            [SMEM, VMEM, HBM, HBM, HBM, VMEM],
+            [buf] * 3 + [sems] * 3,
+            flops=work,
+            moved=4 * MB,
+        )(core[None], keep, frames, keys, vals, bases)
     old_lam = []
     my_rows = lax.dynamic_slice_in_dim(bases, 2 * index, 2, 1).astype(f32)
     for f in range(3):
@@ -427,19 +491,19 @@
     with jax.named_scope("deep_sum"):
         got = exchange(packed, DEEP_GROUPS)
     basis_out = lax.dynamic_index_in_dim(bases, 1 + core, 0, keepdims=False)
-    lines = shape((8, D), f32)
+    lines = shape((16, D), f32)
     with jax.named_scope("rotate"):
         spread = call(rotate_kernel, shape((WIDE, GATHER_ROWS, LANES), bf16), [VMEM] * 2)(got, basis_out)
     with jax.named_scope("gather"):
         gathered = exchange(spread, WIDE_GROUPS)
     with jax.named_scope("rows"):
-        stay, cross = call(rows_kernel, (lines, lines), [SMEM, VMEM])(place, got)
+        rows = call(rows_kernel, lines, [SMEM, VMEM])(place, got)
     rows_in = lax.dynamic_slice_in_dim(bases[0], (index // NC) * FR, FR, 0)
     rows_in = jnp.where(first, rows_in, jnp.roll(rows_in, 2, axis=0))
     rows_in = jnp.pad(rows_in, ((0, 16 - FR), (0, 0)))
     with jax.named_scope("solve"):
-        own, their = call(solve_kernel, (lines, lines), [VMEM] * 6, [pltpu.VMEM((D, D), bf16)])(
-            gathered, basis_in_t, basis_out, rows_in, stay, cross
+        own, their = call(solve_kernel, (lines, lines), [SMEM] + [VMEM] * 6, [pltpu.VMEM((D, D), bf16)])(
+            place, gathered, basis_in_t, basis_out, rows_in, mirror, rows
         )
     theirs = lax.ppermute(their, "dp", SWAP)
     with jax.named_scope("finish"):

time: 76.5 us -> 75.6 us (0.988)
  waiting for transfers between devices: 34.5 us -> 29.3 us
  Pallas kernels: 13.4 us -> 17.6 us
  local copies, waits for them, and re-layouts: 0.11 us -> 0.91 us
    all_to_all x3, waiting for transfers between devices: 32.7 us -> 27.5 us  [exchange(): lax.all_to_all(value, 'dp', 0, 0, axis_index_groups=groups, tiled=True)]
    pallas_call x1, Pallas kernels: 1.75 us -> 4.06 us  [body(): call(functools.partial(lam_kernel, share), (lam_shape, lam_shape, shape((...]
    unnamed x4 -> x8, local copies, waits for them, and re-layouts: 0.01 us -> 0.82 us
  transfers between devices with their start and end apart: 6 -> 6, of which waited for: 6 -> 5; matrix products, arithmetic and copies ran while one was open for 2% -> 2% of each run, Pallas kernels for 6% -> 10%
where the time goes in v6:
time: 75.6 us; the launch traced here: 75.2 us
  waiting for transfers between devices  29.3 us (39%)
  starting transfers between devices  25.3 us (33%)
  Pallas kernels  17.6 us (23%)
  matrix products  0.99 us (1%)
  local copies, waits for them, and re-layouts  0.91 us (1%)
  between operations  0.88 us (1%)
    all_to_all x3, waiting for transfers between devices, exchange(): lax.all_to_all(value, 'dp', 0, 0, axis_index_groups=groups, tiled=True)  27.5 us
    all_to_all x3, starting transfers between devices, exchange(): lax.all_to_all(value, 'dp', 0, 0, axis_index_groups=groups, tiled=True)  18 us
    pallas_call x1, Pallas kernels, body(): call(theirs_kernel, (partial, shape((tokens_here, D), bf16), shape((token...  4.27 us
    pallas_call x1, Pallas kernels, body(): call(functools.partial(lam_kernel, share), (lam_shape, lam_shape, shape((...  4.06 us
    ppermute x1, starting transfers between devices, body(): theirs = lax.ppermute(their, 'dp', SWAP)  3.85 us
    ppermute x1, starting transfers between devices, body(): received = lax.ppermute(other, 'dp', SWAP)  3.19 us
    pallas_call x1, Pallas kernels, body(): call(mine_kernel, partial, [SMEM, VMEM, VMEM, HBM, HBM], [buf, sems], flo...  3.18 us
    pallas_call x1, Pallas kernels, body(): call(solve_kernel, (lines, lines), [SMEM] + [VMEM] * 6, [pltpu.VMEM((D, D...  1.73 us
  transfers between devices with their start and end apart: 6, of which 5 were waited for; matrix products, arithmetic and copies ran while one was open for 2% of the time, Pallas kernels for 10%

profile of v6, /device:TPU:1, one launch (start us, length us, event | category | flops | bytes accessed | tf_op | source)
XLA Modules:
  0.0 75.2 jit_solution(17822740226587402603)
XLA Ops:
  0.6 4.3 %grams_theirs.1 = (bf16[16,2,120,128]{3,2,1,0:T(8,128)(2,1)S(1)}, bf16[1024,512]{1,0:T(8,128)(2,1)S(1)}, bf16[1024,128]{1,0:T(8,128)(2,1)S(1)}) custom-call(s32[1]{0:T(128)} %bitcast.core, s32[2,8]{1,0:T(2,128)} %bitcast.55, s32[2,8]{1,0:T(2,128)} %bitcast.56, bf16[1024,512]{1,0:T(8,128)(2,1)} %x0.3, bf16[1024,512]{1,0:T(8,128)(2,1)} %xk.5, bf16[1024,512]{1,0:T(8,128)(2,1)} %xv.5), custom_call_target="tpu_custom_call" | custom-call | flops 1610612736 | bytes 4194304 | tf_op jit(solution)/shard_map/grams_theirs/pallas_call | solution.py:442
  4.9 3.2 %collective-permute-start = (bf16[16,2,120,128]{3,2,1,0:T(8,128)(2,1)S(1)}, bf16[16,2,120,128]{3,2,1,0:T(8,128)(2,1)S(1)}, u32[]{:S(2)}, u32[]{:S(2)}) collective-permute-start(bf16[16,2,120,128]{3,2,1,0:T(8,128)(2,1)S(1)} %get-tuple-element.17), channel_id=1, source_target_pairs={{0,1},{1,0},{2,3},{3,2},{4,5},{5,4},{6,7},{7,6},{8,9},{9,8},{10,11... | collective-permute-start | bytes 2949128 | tf_op jit(solution)/shard_map/ppermute | solution.py:450
  8.1 3.2 %grams_mine.1.mine = bf16[16,2,120,128]{3,2,1,0:T(8,128)(2,1)S(1)} custom-call(s32[1]{0:T(128)} %bitcast.core, bf16[1024,128]{1,0:T(8,128)(2,1)S(1)} %get-tuple-element.15.keep, bf16[1024,512]{1,0:T(8,128)(2,1)S(1)} %get-tuple-element.16.x0, bf16[1024,512]{1,0:T(8,128)(2,1)} %xk.5, bf16[1024,512]{1,0:T(8,128)(2,1)} %xv.5), custom_call_target="tpu_custom_call" | custom-call | flops 1610612736 | bytes 4194304 | tf_op jit(solution)/shard_map/grams_mine/pallas_call | solution.py:452
  11.3 0.0 collective-permute-done.received
  11.3 1.0 %chip_sum.1 = bf16[16,2,120,128]{3,2,1,0:T(8,128)(2,1)} custom-call(bf16[16,2,120,128]{3,2,1,0:T(8,128)(2,1)S(1)} %grams_mine.1.mine, bf16[16,2,120,128]{3,2,1,0:T(8,128)(2,1)S(1)} %collective-permute-done.received), custom_call_target="tpu_custom_call" | custom-call | tf_op jit(solution)/shard_map/chip_sum/pallas_call | solution.py:461
  12.4 0.0 copy-start
  12.4 0.0 copy-start.3
  12.4 6.8 %all-to-all-start = ((bf16[32,120,128]{2,1,0:T(8,128)(2,1)}), bf16[32,120,128]{2,1,0:T(8,128)(2,1)S(1)}, u32[]{:S(2)}, u32[]{:S(2)}) async-start(bf16[32,120,128]{2,1,0:T(8,128)(2,1)} %bitcast.50), calls=%async_computation | async-start | bytes 1966080 | tf_op jit(solution)/shard_map/wide_sum/all_to_all | solution.py:418
  19.2 0.0 copy-done
  19.2 0.0 copy-done.3
  19.2 0.3 fusion
  19.6 0.3 fusion.2
  19.9 0.3 fusion.1
  20.2 4.1 %lam.1 = (f32[2,512]{1,0:T(2,128)S(1)}, f32[2,512]{1,0:T(2,128)S(1)}, bf16[512,512]{1,0:T(8,128)(2,1)S(1)}, bf16[2,128,512]{2,1,0:T(8,128)(2,1)S(1)}) custom-call(s32[1]{0:T(128)} %bitcast.core, bf16[1024,128]{1,0:T(8,128)(2,1)S(1)} %get-tuple-element.15.keep, bf16[1024,512]{1,0:T(8,128)(2,1)} %x0.3, bf16[1024,512]{1,0:T(8,128)(2,1)} %xk.5, ...), custom_call_target="tpu_custom_call" | custom-call | flops 1610612736 | bytes 4194304 | tf_op jit(solution)/shard_map/lam/pallas_call | solution.py:472
  24.3 0.0 copy-start.1
  24.3 0.8 %copy-done.1 = bf16[512,512]{1,0:T(8,128)(2,1)} copy-done((bf16[512,512]{1,0:T(8,128)(2,1)}, bf16[512,512]{1,0:T(8,128)(2,1)S(1)}, u32[]{:S(2)}) %copy-start.1) | copy-done | bytes 524312
  25.2 0.3 collective-permute-start.1
  25.4 1.0 %collective-permute-done.1.send_lam = f32[2,512]{1,0:T(2,128)S(1)} collective-permute-done((f32[2,512]{1,0:T(2,128)S(1)}, f32[2,512]{1,0:T(2,128)S(1)}, u32[]{:S(2)}, u32[]{:S(2)}) %collective-permute-start.1) | collective-permute-done | bytes 4128 | tf_op jit(solution)/shard_map/ppermute | solution.py:487
  26.4 9.6 %all-to-all-done.parts = bf16[32,120,128]{2,1,0:T(8,128)(2,1)S(1)} async-done(((bf16[32,120,128]{2,1,0:T(8,128)(2,1)}), bf16[32,120,128]{2,1,0:T(8,128)(2,1)S(1)}, u32[]{:S(2)}, u32[]{:S(2)}) %all-to-all-start) | async-done | bytes 983072 | tf_op jit(solution)/shard_map/wide_sum/all_to_all | solution.py:418
  36.0 1.0 %pack.1 = bf16[4,112,128]{2,1,0:T(8,128)(2,1)} custom-call(bf16[32,120,128]{2,1,0:T(8,128)(2,1)S(1)} %all-to-all-done.parts, f32[2,512]{1,0:T(2,128)S(1)} %get-tuple-element.34.keep_lam, f32[2,512]{1,0:T(2,128)S(1)} %collective-permute-done.1.send_lam), custom_call_target="tpu_custom_call" | custom-call | tf_op jit(solution)/shard_map/pack/pallas_call | solution.py:490
  37.0 7.3 %all-to-all-start.1 = ((bf16[4,112,128]{2,1,0:T(8,128)(2,1)}), bf16[4,112,128]{2,1,0:T(8,128)(2,1)S(1)}, u32[]{:S(2)}, u32[]{:S(2)}) async-start(bf16[4,112,128]{2,1,0:T(8,128)(2,1)} %pack.1), calls=%async_computation.1 | async-start | bytes 229376 | tf_op jit(solution)/shard_map/deep_sum/all_to_all | solution.py:418
  44.3 0.1 fusion.17
  44.3 7.2 %all-to-all-done.1.got = bf16[4,112,128]{2,1,0:T(8,128)(2,1)S(1)} async-done(((bf16[4,112,128]{2,1,0:T(8,128)(2,1)}), bf16[4,112,128]{2,1,0:T(8,128)(2,1)S(1)}, u32[]{:S(2)}, u32[]{:S(2)}) %all-to-all-start.1) | async-done | bytes 114720 | tf_op jit(solution)/shard_map/deep_sum/all_to_all | solution.py:418
  51.5 1.1 %rotate.1 = bf16[32,88,128]{2,1,0:T(8,128)(2,1)} custom-call(bf16[4,112,128]{2,1,0:T(8,128)(2,1)S(1)} %all-to-all-done.1.got, bf16[512,512]{1,0:T(8,128)(2,1)S(1)} %get-tuple-element.28.basis.basis_out), custom_call_target="tpu_custom_call" | custom-call | tf_op jit(solution)/shard_map/rotate/pallas_call | solution.py:496
  52.6 3.9 %all-to-all-start.2 = ((bf16[32,88,128]{2,1,0:T(8,128)(2,1)}), bf16[32,88,128]{2,1,0:T(8,128)(2,1)S(1)}, u32[]{:S(2)}, u32[]{:S(2)}) async-start(bf16[32,88,128]{2,1,0:T(8,128)(2,1)} %rotate.1), calls=%async_computation.2 | async-start | bytes 1441792 | tf_op jit(solution)/shard_map/gather/all_to_all | solution.py:418
  56.6 0.1 pad_add_fusion.place
  56.7 0.6 rows.1
  57.3 10.8 %all-to-all-done.2.got = bf16[32,88,128]{2,1,0:T(8,128)(2,1)S(1)} async-done(((bf16[32,88,128]{2,1,0:T(8,128)(2,1)}), bf16[32,88,128]{2,1,0:T(8,128)(2,1)S(1)}, u32[]{:S(2)}, u32[]{:S(2)}) %all-to-all-start.2) | async-done | bytes 720928 | tf_op jit(solution)/shard_map/gather/all_to_all | solution.py:418
  68.1 1.7 %solve.1 = (f32[16,512]{1,0:T(8,128)S(1)}, f32[16,512]{1,0:T(8,128)S(1)}) custom-call(s32[3]{0:T(128)S(1)} %pad_add_fusion.place, bf16[32,88,128]{2,1,0:T(8,128)(2,1)S(1)} %all-to-all-done.2.got, bf16[512,512]{1,0:T(8,128)(2,1)S(1)} %copy-done.2, bf16[512,512]{1,0:T(8,128)(2,1)S(1)} %get-tuple-element.28.basis.basis_out, bf16[16,512]{1,0:T(8,128)(2,1)S(1)} %pad.4.rows_in, ...), custom_call_target="tpu_custom_call" | custom-call | tf_op jit(solution)/shard_map/solve/pallas_call | solution.py:505
  69.9 3.8 %collective-permute-start.2 = (f32[16,512]{1,0:T(8,128)S(1)}, f32[16,512]{1,0:T(8,128)S(1)}, u32[]{:S(2)}, u32[]{:S(2)}) collective-permute-start(f32[16,512]{1,0:T(8,128)S(1)} %get-tuple-element.23), channel_id=1, source_target_pairs={{0,1},{1,0},{2,3},{3,2},{4,5},{5,4},{6,7},{7,6},{8,9},{9,8},{10,11... | collective-permute-start | bytes 98312 | tf_op jit(solution)/shard_map/ppermute | solution.py:508
  73.7 0.9 %collective-permute-done.2.got = f32[16,512]{1,0:T(8,128)S(1)} collective-permute-done((f32[16,512]{1,0:T(8,128)S(1)}, f32[16,512]{1,0:T(8,128)S(1)}, u32[]{:S(2)}, u32[]{:S(2)}) %collective-permute-start.2) | collective-permute-done | bytes 32800 | tf_op jit(solution)/shard_map/ppermute | solution.py:508
  74.6 0.6 finish.1
  (9 shorter events, 0.1 us)
Async XLA Ops:
  4.9 6.4 %collective-permute-start = (bf16[16,2,120,128]{3,2,1,0:T(8,128)(2,1)S(1)}, bf16[16,2,120,128]{3,2,1,0:T(8,128)(2,1)S(1)}, u32[]{:S(2)}, u32[]{:S(2)}) collective-permute-start(bf16[16,2,120,128]{3,2,1,0:T(8,128)(2,1)S(1)} %get-tuple-element.17), channel_id=1, source_target_pairs={{0,1},{1,0},{2,3},{3,2},{4,5},{5,4},{6,7},{7,6},{8,9},{9,8},{10,11... | collective-permute-start | bytes 2949128 | tf_op jit(solution)/shard_map/ppermute | solution.py:450
  12.4 6.8 %copy-start = (bf16[3,512,512]{2,1,0:T(8,128)(2,1)S(1)}, bf16[3,512,512]{2,1,0:T(8,128)(2,1)}, u32[]{:S(2)}) copy-start(bf16[3,512,512]{2,1,0:T(8,128)(2,1)} %bases.1) | copy-start | bytes 4718596
  12.4 6.9 %copy-start.3 = (f32[2,3,512]{2,0,1:T(2,128)S(1)}, f32[2,3,512]{2,0,1:T(2,128)}, u32[]{:S(2)}) copy-start(f32[2,3,512]{2,0,1:T(2,128)} %param.13) | copy-start | bytes 36868
  12.4 23.6 %all-to-all-start = ((bf16[32,120,128]{2,1,0:T(8,128)(2,1)}), bf16[32,120,128]{2,1,0:T(8,128)(2,1)S(1)}, u32[]{:S(2)}, u32[]{:S(2)}) async-start(bf16[32,120,128]{2,1,0:T(8,128)(2,1)} %bitcast.50), calls=%async_computation | async-start | bytes 1966080 | tf_op jit(solution)/shard_map/wide_sum/all_to_all | solution.py:418
  24.3 0.8 %copy-start.1 = (bf16[512,512]{1,0:T(8,128)(2,1)}, bf16[512,512]{1,0:T(8,128)(2,1)S(1)}, u32[]{:S(2)}) copy-start(bf16[512,512]{1,0:T(8,128)(2,1)S(1)} %get-tuple-element.20.basis_in_t) | copy-start | bytes 1572868
  25.2 1.3 %collective-permute-start.1 = (f32[2,512]{1,0:T(2,128)S(1)}, f32[2,512]{1,0:T(2,128)S(1)}, u32[]{:S(2)}, u32[]{:S(2)}) collective-permute-start(f32[2,512]{1,0:T(2,128)S(1)} %get-tuple-element.33), channel_id=1, source_target_pairs={{0,1},{1,0},{2,3},{3,2},{4,5},{5,4},{6,7},{7,6},{8,9},{9,8},{10,11... | collective-permute-start | bytes 12296 | tf_op jit(solution)/shard_map/ppermute | solution.py:487
  37.0 14.5 %all-to-all-start.1 = ((bf16[4,112,128]{2,1,0:T(8,128)(2,1)}), bf16[4,112,128]{2,1,0:T(8,128)(2,1)S(1)}, u32[]{:S(2)}, u32[]{:S(2)}) async-start(bf16[4,112,128]{2,1,0:T(8,128)(2,1)} %pack.1), calls=%async_computation.1 | async-start | bytes 229376 | tf_op jit(solution)/shard_map/deep_sum/all_to_all | solution.py:418
  44.3 23.8 %copy-start.2 = (bf16[512,512]{1,0:T(8,128)(2,1)S(1)}, bf16[512,512]{1,0:T(8,128)(2,1)}, u32[]{:S(2)}) copy-start(bf16[512,512]{1,0:T(8,128)(2,1)} %copy-done.1) | copy-start | bytes 1572868
  52.6 15.5 %all-to-all-start.2 = ((bf16[32,88,128]{2,1,0:T(8,128)(2,1)}), bf16[32,88,128]{2,1,0:T(8,128)(2,1)S(1)}, u32[]{:S(2)}, u32[]{:S(2)}) async-start(bf16[32,88,128]{2,1,0:T(8,128)(2,1)} %rotate.1), calls=%async_computation.2 | async-start | bytes 1441792 | tf_op jit(solution)/shard_map/gather/all_to_all | solution.py:418
  69.9 4.7 %collective-permute-start.2 = (f32[16,512]{1,0:T(8,128)S(1)}, f32[16,512]{1,0:T(8,128)S(1)}, u32[]{:S(2)}, u32[]{:S(2)}) collective-permute-start(f32[16,512]{1,0:T(8,128)S(1)} %get-tuple-element.23), channel_id=1, source_target_pairs={{0,1},{1,0},{2,3},{3,2},{4,5},{5,4},{6,7},{7,6},{8,9},{9,8},{10,11... | collective-permute-start | bytes 98312 | tf_op jit(solution)/shard_map/ppermute | solution.py:508

commit v7 on v6

--- a/solution.py
+++ b/solution.py
@@ -140,6 +140,11 @@
         out[places, half, pl.ds(begin, ROWS // 2), :] = jnp.where(lane < LANES // 2, upper, lower).astype(bf16)
 
 
+def end_lanes(value):
+    lane = lax.broadcasted_iota(jnp.int32, value.shape, 1)
+    return jnp.where(lane < BLK, value, 0.0)
+
+
 def circulate(value, r):
     rows = []
     for b in range(BLOCK // BLK):
@@ -149,25 +154,31 @@
     return [jnp.concatenate([p[:, t * LANES : (t + 1) * LANES] for p in rows], axis=0) for t in range(3)]
 
 
-def grams(pick, x0, x1, ready, out):
+def zero_grams(pick, x0, out, spare):
     lefts, rests = [], []
     for r in range(D // BLOCK):
         lefts.append(x0[:, pl.ds(r * BLOCK, BLOCK)].T)
         tiles = circulate(dot(lefts[r], x0[...]), r)
         put(out, r, jnp.where(pick == 0, tiles[0], tiles[1]), F0)
-        rests.append(pltpu.roll(jnp.where(pick == 0, tiles[1], tiles[2]), BLK, 1))
-    ready()
+        put(spare, r, jnp.where(pick == 0, tiles[1], tiles[0]), 0)
+        last = pltpu.roll(end_lanes(tiles[2]), BLK, 1)
+        rests.append(jnp.where(pick == 0, 0.0, last))
+        put_folded(spare, r, jnp.where(pick == 0, last, 0.0), ROWS)
+    return lefts, rests
+
+
+def picked_grams(lefts, x1, rests, out, end):
     for r in range(D // BLOCK):
         put(out, r, dot(lefts[r], x1[...]), 0)
     for r in range(D // BLOCK):
         left = x1[:, pl.ds(r * BLOCK, BLOCK)].T
         tiles = circulate(dot(left, x1[...]), r)
         put(out, r, jnp.concatenate(tiles[:2], axis=1), FA)
-        lane = lax.broadcasted_iota(jnp.int32, tiles[2].shape, 1)
-        put_folded(out, r, jnp.where(lane < BLK, tiles[2], rests[r]), FL)
-
-
-def theirs_kernel(core, start, width, x0, xk, xv, out, kept, keep, buf0, buf1, masks, sem0, sem1, sem2):
+        last = end_lanes(tiles[2])
+        put_folded(out, r, last if rests is None else last + rests[r], end)
+
+
+def theirs_kernel(core, start, width, x0, xk, xv, out, spare, kept, keep, buf0, buf1, masks, sem0, sem1, sem2):
     pick = 1 - core[0]
     small = [pltpu.make_async_copy(v, masks.at[i], sem2.at[i]) for i, v in enumerate((start, width))]
     copies0 = fetch(x0, buf0, sem0)
@@ -180,37 +191,37 @@
     for q in range(CHUNKS):
         copies0[q].wait()
         apply_mask(buf0, kept, keep, q)
-
-    def ready():
-        for q in range(CHUNKS):
-            copies1[q].wait()
-            apply_mask(buf1, buf1, keep, q)
-
-    grams(pick, kept, buf1, ready, out)
+    lefts, rests = zero_grams(pick, kept, out, spare)
+    for q in range(CHUNKS):
+        copies1[q].wait()
+        apply_mask(buf1, buf1, keep, q)
+    picked_grams(lefts, buf1, rests, out, FL)
 
 
 def mine_kernel(core, keep, x0, xk, xv, out, buf1, sem1):
     pick = core[0]
     copies1 = fetch_picked(pick, xk, xv, buf1, sem1)
-
-    def ready():
-        for q in range(CHUNKS):
-            copies1[q].wait()
-            apply_mask(buf1, buf1, keep, q)
-
-    grams(pick, x0, buf1, ready, out)
+    lefts = [x0[:, pl.ds(r * BLOCK, BLOCK)].T for r in range(D // BLOCK)]
+    for q in range(CHUNKS):
+        copies1[q].wait()
+        apply_mask(buf1, buf1, keep, q)
+    picked_grams(lefts, buf1, None, out, F0)
 
 
 PIECES = 4
 
 
-def add_kernel(mine, received, out, buf, sems):
+def add_kernel(mine, spare, received, out, buf, sems):
     size = NXY // PIECES
     copies = []
+    main, zero, last = slice(0, F0), slice(F0, FL), slice(FL, WROWS)
     for q in range(PIECES):
         for i in range(q * size, (q + 1) * size):
             for j in range(PAIR):
-                buf[i, j] = mine[i, j] + received[i, j]
+                buf[i, j, main] = mine[i, j, main] + received[i, j, main]
+                buf[i, j, zero] = spare[i, j, :ROWS] + received[i, j, zero]
+                ends = mine[i, j, F0:] + spare[i, j, ROWS:]
+                buf[i, j, last] = ends + received[i, j, last]
         part = pl.ds(q * size, size)
         copies.append(pltpu.make_async_copy(buf.at[part], out.at[part], sems.at[q]))
         copies[q].start()
@@ -218,8 +229,8 @@
         copy.wait()
 
 
-def lam_kernel(share, core, keep, x0, xk, xv, bases, keep_lam, send_lam, basis_in_t, mirror, b0, b1, b2, sem0, sem1, sem2):
-    c = core[0]
+def lam_kernel(share, place, keep, x0, xk, xv, bases, keep_lam, send_lam, basis_in_t, mirror, b0, b1, b2, sem0, sem1, sem2):
+    c = place[1]
     bufs = (b0, b1, b2)
     copies = [fetch(x, buf, sem) for x, buf, sem in zip((x0, xk, xv), bufs, (sem0, sem1, sem2))]
     for group in copies:
@@ -230,8 +241,12 @@
     lane = lax.broadcasted_iota(jnp.int32, (LANES, D), 0)
     column = lax.broadcasted_iota(jnp.int32, (LANES, D), 1)
     for half in range(PAIR):
-        home = (D - BLK * (lane >> 4) + 8 * ((lane >> 2) & 3) + FR * half + (lane & 3)) & (D - 1)
-        mirror[half] = jnp.where(column == home, 1.0, 0.0).astype(bf16)
+        home = 8 * ((lane >> 2) & 3) + FR * half + (lane & 3) + 2 * D
+        for kind in range(2):
+            distance = (lane >> 4) + (4 * c if kind else 0)
+            there = (home + BLK * (place[2] - distance)) & (D - 1)
+            one = jnp.where(column == there, 1.0, 0.0).astype(bf16)
+            mirror[pl.ds((2 * half + kind) * LANES, LANES), :] = one
     lam = []
     for f in range(3):
         total = jnp.zeros((8, D), f32)
@@ -271,7 +286,7 @@
 DEEP_LAM = TURNED + 16
 DEEP_ROWS = DEEP_LAM + LAMR
 GATHER_LAM = GT * ROWS
-GATHER_TURNED = GATHER_LAM + LAMR
+GATHER_TURNED = GATHER_LAM + 2 * GT
 GATHER_ROWS = GATHER_TURNED + 8
 
 
@@ -318,14 +333,12 @@
     total, grad = deep_total(got)
     rot = dot(grad.astype(bf16), basis[...]).astype(bf16)
     lam = add_lam(total[DEEP_LAM:])
-    lam = jnp.concatenate(split(lam), axis=0).astype(bf16)
     picked, zero = total[TURNED : TURNED + 8], total[TURNED + 8 : TURNED + 16]
     for half in range(PAIR):
         rows = slice(half * FR, (half + 1) * FR)
-        mirrored = jnp.concatenate([picked[rows], zero[rows]], axis=0).astype(bf16)
+        tail = jnp.concatenate([lam, picked[rows], zero[rows]], axis=0).astype(bf16)
         for i in range(half, WIDE, PAIR):
-            out[i, pl.ds(GATHER_LAM, LAMR), :] = lam
-            out[i, pl.ds(GATHER_TURNED, 8), :] = mirrored
+            out[i, pl.ds(GATHER_LAM, ROWS), :] = tail
     for j in range(GT):
         tile = rot[:, j * LANES : (j + 1) * LANES]
         for i in range(WIDE):
@@ -349,33 +362,30 @@
         jnp.concatenate([zero, none, none, none], axis=1),
         jnp.concatenate([none, zero, end0, none], axis=1),
     )
-    out[...] = jnp.concatenate([rows, picked, zero, jnp.zeros_like(rows)], axis=0)
-
-
-def mirrored_rows(place, got, mirror):
+    factors = pltpu.roll(jnp.concatenate([picked, zero], axis=0), BLK * place[2], 1)
+    out[...] = jnp.concatenate([rows, factors, jnp.zeros_like(rows)], axis=0)
+
+
+def mirrored_rows(place, tails, mirror):
     c, block = place[1], place[2]
     row = lax.broadcasted_iota(jnp.int32, (8, LANES), 0)
     group = (lax.broadcasted_iota(jnp.int32, (8, LANES), 1) >> 4) + jnp.where(row >= FR, 4 * c, 0)
-    placed = None
+    parts = []
     for half in range(PAIR):
         own = jnp.zeros((8, LANES), f32)
         for i in range(NXY):
             distance = (block - i) & (NXY - 1)
             wanted = jnp.where((distance >= 1) & (distance < 8), distance, -1)
-            piece = got[PAIR * i + half, pl.ds(GATHER_TURNED, 8), :].astype(f32)
-            own = jnp.where(group == wanted, piece, own)
-        value = dot(own.astype(bf16), mirror[half])
-        placed = value if placed is None else placed + value
-    moved = jnp.concatenate([placed[:, LANES:], placed[:, :LANES]], axis=1)
-    row = lax.broadcasted_iota(jnp.int32, (8, D), 0)
-    return jnp.where((row >= FR) & (c != 0), moved, placed)
+            own = jnp.where(group == wanted, tails[PAIR * i + half][8:], own)
+        parts += [jnp.where(row < FR, own, 0.0), jnp.where(row < FR, 0.0, own)]
+    return dot(jnp.concatenate(parts, axis=1).astype(bf16), mirror[...])
 
 
 def solve_kernel(place, got, basis_in_t, basis_out, rows_in, mirror, rows, own, their, scaled):
-    lam = got[0, pl.ds(GATHER_LAM, LAMR), :].astype(f32)
-    for i in range(1, WIDE):
-        lam = lam + got[i, pl.ds(GATHER_LAM, LAMR), :].astype(f32)
-    lam = add_lam(lam)
+    tails = [got[i, pl.ds(GATHER_LAM, ROWS), :].astype(f32) for i in range(WIDE)]
+    lam = tails[0][:8]
+    for tail in tails[1:]:
+        lam = lam + tail[:8]
     column = jnp.broadcast_to(lam_row(lam, 0), (8, D)).T[:, 0:1]
     column = jnp.broadcast_to(column, (D, LANES))
     curve = jnp.zeros((8, LANES), f32)
@@ -390,7 +400,7 @@
     prec = lax.dot_general(back, basis_out[...], (((1,), (1,)), ((), ())), preferred_element_type=f32)
     prec = prec.astype(bf16).astype(f32)
     curve = jnp.broadcast_to(curve, (2, D))
-    factors = pltpu.roll(rows[4:12, :] + mirrored_rows(place, got, mirror), BLK * place[2], 1)
+    factors = rows[4:12, :] + mirrored_rows(place, tails, mirror)
     low = jnp.concatenate([rows[0:2, :], factors[0:2], factors[4:6]], axis=0)
     high = jnp.concatenate([rows[2:4, :], factors[2:4], factors[6:8]], axis=0)
     first = place[1] == 0
@@ -439,9 +449,9 @@
     partial = shape((NXY, PAIR, WROWS, LANES), bf16)
     work = 6 * D * D * tokens_here
     with jax.named_scope("grams_theirs"):
-        other, kept, keep = call(
+        other, spare, kept, keep = call(
             theirs_kernel,
-            (partial, shape((tokens_here, D), bf16), shape((tokens_here, LANES), bf16)),
+            (partial, shape((NXY, PAIR, ROWS + ROWS // 2, LANES), bf16), shape((tokens_here, D), bf16), shape((tokens_here, LANES), bf16)),
             [SMEM] + [HBM] * 5,
             [buf, buf, mask_buf, sems, sems, pair],
             flops=work,
@@ -451,7 +461,7 @@
     with jax.named_scope("grams_mine"):
         mine = call(
             mine_kernel,
-            partial,
+            shape((NXY, PAIR, F0 + ROWS // 2, LANES), bf16),
             [SMEM, VMEM, VMEM, HBM, HBM],
             [buf, sems],
             flops=work,
@@ -461,9 +471,9 @@
         chip = call(
             add_kernel,
             pltpu.HBM(partial.shape, bf16),
-            [VMEM] * 2,
+            [VMEM] * 3,
             [pltpu.VMEM(partial.shape, bf16), pltpu.SemaphoreType.DMA((PIECES,))],
-        )(mine, received).reshape(WIDE, WROWS, LANES)
+        )(mine, spare, received).reshape(WIDE, WROWS, LANES)
     with jax.named_scope("wide_sum"):
         parts = exchange(chip, WIDE_GROUPS)
 
@@ -471,12 +481,12 @@
     with jax.named_scope("lam"):
         keep_lam, send_lam, basis_in_t, mirror = call(
             functools.partial(lam_kernel, share),
-            (lam_shape, lam_shape, shape((D, D), bf16), shape((PAIR, LANES, D), bf16)),
+            (lam_shape, lam_shape, shape((D, D), bf16), shape((2 * PAIR * LANES, D), bf16)),
             [SMEM, VMEM, HBM, HBM, HBM, VMEM],
             [buf] * 3 + [sems] * 3,
             flops=work,
             moved=4 * MB,
-        )(core[None], keep, frames, keys, vals, bases)
+        )(place, keep, frames, keys, vals, bases)
     old_lam = []
     my_rows = lax.dynamic_slice_in_dim(bases, 2 * index, 2, 1).astype(f32)
     for f in range(3):

time: 75.6 us -> 74.3 us (0.983)
  waiting for transfers between devices: 29.3 us -> 24.2 us
  local copies, waits for them, and re-layouts: 0.91 us -> 3.3 us
    all_to_all x3, waiting for transfers between devices: 27.5 us -> 22.4 us  [exchange(): lax.all_to_all(value, 'dp', 0, 0, axis_index_groups=groups, tiled=True)]
    pallas_call x1, Pallas kernels: 4.06 us -> 4.95 us  [body(): call(functools.partial(lam_kernel, share), (lam_shape, lam_shape, shape((...]
    slice x1, local copies, waits for them, and re-layouts: 0.07 us -> 0.91 us  [body(): bases[f].astype(f32)]
    unnamed x8 -> x12, local copies, waits for them, and re-layouts: 0.82 us -> 1.6 us
    slice x1, local copies, waits for them, and re-layouts: 0.01 us -> 0.79 us  [body(): rows_in = jnp.where(first, rows_in, jnp.roll(rows_in, 2, axis=0))]
  transfers between devices with their start and end apart: 6 -> 6, of which waited for: 5 -> 5; matrix products, arithmetic and copies ran while one was open for 2% -> 5% of each run, Pallas kernels for 10% -> 11%
where the time goes in v7:
time: 74.3 us; the launch traced here: 73.8 us
  starting transfers between devices  25.6 us (34%)
  waiting for transfers between devices  24.2 us (33%)
  Pallas kernels  18.1 us (24%)
  local copies, waits for them, and re-layouts  3.3 us (4%)
  matrix products  0.99 us (1%)
  between operations  0.86 us (1%)
  other arithmetic  0.82 us (1%)
    all_to_all x3, waiting for transfers between devices, exchange(): lax.all_to_all(value, 'dp', 0, 0, axis_index_groups=groups, tiled=True)  22.4 us
    all_to_all x3, starting transfers between devices, exchange(): lax.all_to_all(value, 'dp', 0, 0, axis_index_groups=groups, tiled=True)  18 us
    pallas_call x1, Pallas kernels, body(): call(functools.partial(lam_kernel, share), (lam_shape, lam_shape, shape((...  4.95 us
    pallas_call x1, Pallas kernels, body(): call(theirs_kernel, (partial, shape((NXY, PAIR, ROWS + ROWS // 2, LANES),...  4.36 us
    ppermute x1, starting transfers between devices, body(): theirs = lax.ppermute(their, 'dp', SWAP)  4.04 us
    ppermute x1, starting transfers between devices, body(): received = lax.ppermute(other, 'dp', SWAP)  3.19 us
    pallas_call x1, Pallas kernels, body(): call(mine_kernel, shape((NXY, PAIR, F0 + ROWS // 2, LANES), bf16), [SMEM,...  2.63 us
    pallas_call x1, Pallas kernels, body(): call(solve_kernel, (lines, lines), [SMEM] + [VMEM] * 6, [pltpu.VMEM((D, D...  1.67 us
  transfers between devices with their start and end apart: 6, of which 5 were waited for; matrix products, arithmetic and copies ran while one was open for 5% of the time, Pallas kernels for 11%

profile of v7, /device:TPU:1, one launch (start us, length us, event | category | flops | bytes accessed | tf_op | source)
XLA Modules:
  0.0 73.8 jit_solution(12079563662143519232)
XLA Ops:
  0.6 4.4 %grams_theirs.1 = (bf16[16,2,120,128]{3,2,1,0:T(8,128)(2,1)S(1)}, bf16[16,2,24,128]{3,2,1,0:T(8,128)(2,1)S(1)}, bf16[1024,512]{1,0:T(8,128)(2,1)S(1)}, bf16[1024,128]{1,0:T(8,128)(2,1)S(1)}) custom-call(s32[1]{0:T(128)} %bitcast.core, s32[2,8]{1,0:T(2,128)} %bitcast.55, s32[2,8]{1,0:T(2,128)} %bitcast.56, bf16[1024,512]{1,0:T(8,128)(2,1)} %x0.3, ...), custom_call_target="tpu_custom_call" | custom-call | flops 1610612736 | bytes 4194304 | tf_op jit(solution)/shard_map/grams_theirs/pallas_call | solution.py:452
  5.0 3.2 %collective-permute-start = (bf16[16,2,120,128]{3,2,1,0:T(8,128)(2,1)S(1)}, bf16[16,2,120,128]{3,2,1,0:T(8,128)(2,1)S(1)}, u32[]{:S(2)}, u32[]{:S(2)}) collective-permute-start(bf16[16,2,120,128]{3,2,1,0:T(8,128)(2,1)S(1)} %get-tuple-element.19), channel_id=1, source_target_pairs={{0,1},{1,0},{2,3},{3,2},{4,5},{5,4},{6,7},{7,6},{8,9},{9,8},{10,11... | collective-permute-start | bytes 2949128 | tf_op jit(solution)/shard_map/ppermute | solution.py:460
  8.2 2.6 %grams_mine.1.mine = bf16[16,2,104,128]{3,2,1,0:T(8,128)(2,1)S(1)} custom-call(s32[1]{0:T(128)} %bitcast.core, bf16[1024,128]{1,0:T(8,128)(2,1)S(1)} %get-tuple-element.16.keep, bf16[1024,512]{1,0:T(8,128)(2,1)S(1)} %get-tuple-element.17.x0, bf16[1024,512]{1,0:T(8,128)(2,1)} %xk.5, bf16[1024,512]{1,0:T(8,128)(2,1)} %xv.5), custom_call_target="tpu_custom_call" | custom-call | flops 1610612736 | bytes 4194304 | tf_op jit(solution)/shard_map/grams_mine/pallas_call | solution.py:462
  10.8 0.0 collective-permute-done.received
  10.9 1.1 %chip_sum.1 = bf16[16,2,120,128]{3,2,1,0:T(8,128)(2,1)} custom-call(bf16[16,2,104,128]{3,2,1,0:T(8,128)(2,1)S(1)} %grams_mine.1.mine, bf16[16,2,24,128]{3,2,1,0:T(8,128)(2,1)S(1)} %get-tuple-element.18.spare, bf16[16,2,120,128]{3,2,1,0:T(8,128)(2,1)S(1)} %collective-permute-done.received), custom_call_target="tpu_custom_call" | custom-call | tf_op jit(solution)/shard_map/chip_sum/pallas_call | solution.py:471
  11.9 0.0 copy-start
  11.9 0.0 copy-start.5
  12.0 6.8 %all-to-all-start = ((bf16[32,120,128]{2,1,0:T(8,128)(2,1)}), bf16[32,120,128]{2,1,0:T(8,128)(2,1)S(1)}, u32[]{:S(2)}, u32[]{:S(2)}) async-start(bf16[32,120,128]{2,1,0:T(8,128)(2,1)} %bitcast.50), calls=%async_computation | async-start | bytes 1966080 | tf_op jit(solution)/shard_map/wide_sum/all_to_all | solution.py:428
  18.8 0.1 pad_add_fusion.place
  19.0 0.3 fusion
  19.3 0.3 fusion.2
  19.6 0.3 fusion.1
  20.0 4.9 %lam.1 = (f32[2,512]{1,0:T(2,128)S(1)}, f32[2,512]{1,0:T(2,128)S(1)}, bf16[512,512]{1,0:T(8,128)(2,1)S(1)}, bf16[512,512]{1,0:T(8,128)(2,1)S(1)}) custom-call(s32[3]{0:T(128)S(1)} %pad_add_fusion.place, bf16[1024,128]{1,0:T(8,128)(2,1)S(1)} %get-tuple-element.16.keep, bf16[1024,512]{1,0:T(8,128)(2,1)} %x0.3, bf16[1024,512]{1,0:T(8,128)(2,1)} %xk.5, ...), custom_call_target="tpu_custom_call" | custom-call | flops 1610612736 | bytes 4194304 | tf_op jit(solution)/shard_map/lam/pallas_call | solution.py:482
  24.9 0.8 %copy-done.1 = bf16[512,512]{1,0:T(8,128)(2,1)} copy-done((bf16[512,512]{1,0:T(8,128)(2,1)}, bf16[512,512]{1,0:T(8,128)(2,1)S(1)}, u32[]{:S(2)}) %copy-start.1) | copy-done | bytes 524312
  25.7 0.8 %copy-done.3 = bf16[512,512]{1,0:T(8,128)(2,1)} copy-done((bf16[512,512]{1,0:T(8,128)(2,1)}, bf16[512,512]{1,0:T(8,128)(2,1)S(1)}, u32[]{:S(2)}) %copy-start.3) | copy-done | bytes 524312
  26.5 0.4 collective-permute-start.1
  26.9 0.9 %collective-permute-done.1.send_lam = f32[2,512]{1,0:T(2,128)S(1)} collective-permute-done((f32[2,512]{1,0:T(2,128)S(1)}, f32[2,512]{1,0:T(2,128)S(1)}, u32[]{:S(2)}, u32[]{:S(2)}) %collective-permute-start.1) | collective-permute-done | bytes 4128 | tf_op jit(solution)/shard_map/ppermute | solution.py:497
  27.8 7.7 %all-to-all-done.parts = bf16[32,120,128]{2,1,0:T(8,128)(2,1)S(1)} async-done(((bf16[32,120,128]{2,1,0:T(8,128)(2,1)}), bf16[32,120,128]{2,1,0:T(8,128)(2,1)S(1)}, u32[]{:S(2)}, u32[]{:S(2)}) %all-to-all-start) | async-done | bytes 983072 | tf_op jit(solution)/shard_map/wide_sum/all_to_all | solution.py:428
  35.5 1.0 %pack.1 = bf16[4,112,128]{2,1,0:T(8,128)(2,1)} custom-call(bf16[32,120,128]{2,1,0:T(8,128)(2,1)S(1)} %all-to-all-done.parts, f32[2,512]{1,0:T(2,128)S(1)} %get-tuple-element.36.keep_lam, f32[2,512]{1,0:T(2,128)S(1)} %collective-permute-done.1.send_lam), custom_call_target="tpu_custom_call" | custom-call | tf_op jit(solution)/shard_map/pack/pallas_call | solution.py:500
  36.5 7.2 %all-to-all-start.1 = ((bf16[4,112,128]{2,1,0:T(8,128)(2,1)}), bf16[4,112,128]{2,1,0:T(8,128)(2,1)S(1)}, u32[]{:S(2)}, u32[]{:S(2)}) async-start(bf16[4,112,128]{2,1,0:T(8,128)(2,1)} %pack.1), calls=%async_computation.1 | async-start | bytes 229376 | tf_op jit(solution)/shard_map/deep_sum/all_to_all | solution.py:428
  43.7 0.9 %fusion.17 = (bf16[1,512,512]{2,1,0:T(8,128)(2,1)}, bf16[512,512]{1,0:T(8,128)(2,1)S(1)}) fusion(bf16[3,512,512]{2,1,0:T(8,128)(2,1)S(1)} %copy-done, s32[]{:T(128)S(6)} %select_n.83), kind=kLoop, calls=%fused_computation.34 | loop fusion | bytes 2097156 | tf_op jit(solution)/shard_map/slice | solution.py:493
  44.6 6.3 %all-to-all-done.1.got = bf16[4,112,128]{2,1,0:T(8,128)(2,1)S(1)} async-done(((bf16[4,112,128]{2,1,0:T(8,128)(2,1)}), bf16[4,112,128]{2,1,0:T(8,128)(2,1)S(1)}, u32[]{:S(2)}, u32[]{:S(2)}) %all-to-all-start.1) | async-done | bytes 114720 | tf_op jit(solution)/shard_map/deep_sum/all_to_all | solution.py:428
  50.9 1.1 %rotate.1 = bf16[32,80,128]{2,1,0:T(8,128)(2,1)} custom-call(bf16[4,112,128]{2,1,0:T(8,128)(2,1)S(1)} %all-to-all-done.1.got, bf16[512,512]{1,0:T(8,128)(2,1)S(1)} %get-tuple-element.30.basis.basis_out), custom_call_target="tpu_custom_call" | custom-call | tf_op jit(solution)/shard_map/rotate/pallas_call | solution.py:506
  51.9 3.9 %all-to-all-start.2 = ((bf16[32,80,128]{2,1,0:T(8,128)(2,1)}), bf16[32,80,128]{2,1,0:T(8,128)(2,1)S(1)}, u32[]{:S(2)}, u32[]{:S(2)}) async-start(bf16[32,80,128]{2,1,0:T(8,128)(2,1)} %rotate.1), calls=%async_computation.2 | async-start | bytes 1310720 | tf_op jit(solution)/shard_map/gather/all_to_all | solution.py:428
  55.9 0.8 %dynamic-slice_bitcast_fusion.2 = (bf16[2,512]{1,0:T(2,128)(2,1)S(1)}, bf16[2,512]{1,0:T(2,128)(2,1)S(1)}) fusion(bf16[1,512,512]{2,1,0:T(8,128)(2,1)} %get-tuple-element.29, s32[]{:T(128)S(6)} %add.39, s32[]{:T(128)S(6)} %select_n.85), kind=kLoop, calls=%fused_computation.28 | loop fusion | bytes 8200 | tf_op jit(solution)/shard_map/jit(_roll_static)/slice | solution.py:512
  56.6 0.7 maximum_select_fusion
  57.4 0.7 rows.1
  58.1 8.5 %all-to-all-done.2.got = bf16[32,80,128]{2,1,0:T(8,128)(2,1)S(1)} async-done(((bf16[32,80,128]{2,1,0:T(8,128)(2,1)}), bf16[32,80,128]{2,1,0:T(8,128)(2,1)S(1)}, u32[]{:S(2)}, u32[]{:S(2)}) %all-to-all-start.2) | async-done | bytes 655392 | tf_op jit(solution)/shard_map/gather/all_to_all | solution.py:428
  66.6 1.7 %solve.1 = (f32[16,512]{1,0:T(8,128)S(1)}, f32[16,512]{1,0:T(8,128)S(1)}) custom-call(s32[3]{0:T(128)S(1)} %pad_add_fusion.place, bf16[32,80,128]{2,1,0:T(8,128)(2,1)S(1)} %all-to-all-done.2.got, bf16[512,512]{1,0:T(8,128)(2,1)S(1)} %copy-done.2, bf16[512,512]{1,0:T(8,128)(2,1)S(1)} %get-tuple-element.30.basis.basis_out, bf16[16,512]{1,0:T(8,128)(2,1)S(1)} %pad.4.rows_in, ...), custom_call_target="tpu_custom_call" | custom-call | tf_op jit(solution)/shard_map/solve/pallas_call | solution.py:515
  68.3 4.0 %collective-permute-start.2 = (f32[16,512]{1,0:T(8,128)S(1)}, f32[16,512]{1,0:T(8,128)S(1)}, u32[]{:S(2)}, u32[]{:S(2)}) collective-permute-start(f32[16,512]{1,0:T(8,128)S(1)} %get-tuple-element.25), channel_id=1, source_target_pairs={{0,1},{1,0},{2,3},{3,2},{4,5},{5,4},{6,7},{7,6},{8,9},{9,8},{10,11... | collective-permute-start | bytes 98312 | tf_op jit(solution)/shard_map/ppermute | solution.py:518
  72.3 0.9 %collective-permute-done.2.got = f32[16,512]{1,0:T(8,128)S(1)} collective-permute-done((f32[16,512]{1,0:T(8,128)S(1)}, f32[16,512]{1,0:T(8,128)S(1)}, u32[]{:S(2)}, u32[]{:S(2)}) %collective-permute-start.2) | collective-permute-done | bytes 32800 | tf_op jit(solution)/shard_map/ppermute | solution.py:518
  73.2 0.6 finish.1
  (13 shorter events, 0.1 us)
Async XLA Ops:
  5.0 5.8 %collective-permute-start = (bf16[16,2,120,128]{3,2,1,0:T(8,128)(2,1)S(1)}, bf16[16,2,120,128]{3,2,1,0:T(8,128)(2,1)S(1)}, u32[]{:S(2)}, u32[]{:S(2)}) collective-permute-start(bf16[16,2,120,128]{3,2,1,0:T(8,128)(2,1)S(1)} %get-tuple-element.19), channel_id=1, source_target_pairs={{0,1},{1,0},{2,3},{3,2},{4,5},{5,4},{6,7},{7,6},{8,9},{9,8},{10,11... | collective-permute-start | bytes 2949128 | tf_op jit(solution)/shard_map/ppermute | solution.py:460
  11.9 7.0 %copy-start = (bf16[3,512,512]{2,1,0:T(8,128)(2,1)S(1)}, bf16[3,512,512]{2,1,0:T(8,128)(2,1)}, u32[]{:S(2)}) copy-start(bf16[3,512,512]{2,1,0:T(8,128)(2,1)} %bases.1) | copy-start | bytes 4718596
  11.9 7.0 %copy-start.5 = (f32[2,3,512]{2,0,1:T(2,128)S(1)}, f32[2,3,512]{2,0,1:T(2,128)}, u32[]{:S(2)}) copy-start(f32[2,3,512]{2,0,1:T(2,128)} %param.13) | copy-start | bytes 36868
  12.0 23.5 %all-to-all-start = ((bf16[32,120,128]{2,1,0:T(8,128)(2,1)}), bf16[32,120,128]{2,1,0:T(8,128)(2,1)S(1)}, u32[]{:S(2)}, u32[]{:S(2)}) async-start(bf16[32,120,128]{2,1,0:T(8,128)(2,1)} %bitcast.50), calls=%async_computation | async-start | bytes 1966080 | tf_op jit(solution)/shard_map/wide_sum/all_to_all | solution.py:428
  24.9 0.8 %copy-start.1 = (bf16[512,512]{1,0:T(8,128)(2,1)}, bf16[512,512]{1,0:T(8,128)(2,1)S(1)}, u32[]{:S(2)}) copy-start(bf16[512,512]{1,0:T(8,128)(2,1)S(1)} %get-tuple-element.22.basis_in_t) | copy-start | bytes 1572868
  25.7 0.8 %copy-start.3 = (bf16[512,512]{1,0:T(8,128)(2,1)}, bf16[512,512]{1,0:T(8,128)(2,1)S(1)}, u32[]{:S(2)}) copy-start(bf16[512,512]{1,0:T(8,128)(2,1)S(1)} %get-tuple-element.23.mirror) | copy-start | bytes 1572868
  26.5 1.3 %collective-permute-start.1 = (f32[2,512]{1,0:T(2,128)S(1)}, f32[2,512]{1,0:T(2,128)S(1)}, u32[]{:S(2)}, u32[]{:S(2)}) collective-permute-start(f32[2,512]{1,0:T(2,128)S(1)} %get-tuple-element.35), channel_id=1, source_target_pairs={{0,1},{1,0},{2,3},{3,2},{4,5},{5,4},{6,7},{7,6},{8,9},{9,8},{10,11... | collective-permute-start | bytes 12296 | tf_op jit(solution)/shard_map/ppermute | solution.py:497
  36.5 14.4 %all-to-all-start.1 = ((bf16[4,112,128]{2,1,0:T(8,128)(2,1)}), bf16[4,112,128]{2,1,0:T(8,128)(2,1)S(1)}, u32[]{:S(2)}, u32[]{:S(2)}) async-start(bf16[4,112,128]{2,1,0:T(8,128)(2,1)} %pack.1), calls=%async_computation.1 | async-start | bytes 229376 | tf_op jit(solution)/shard_map/deep_sum/all_to_all | solution.py:428
  44.6 22.0 %copy-start.2 = (bf16[512,512]{1,0:T(8,128)(2,1)S(1)}, bf16[512,512]{1,0:T(8,128)(2,1)}, u32[]{:S(2)}) copy-start(bf16[512,512]{1,0:T(8,128)(2,1)} %copy-done.1) | copy-start | bytes 1572868
  44.6 22.0 %copy-start.4 = (bf16[512,512]{1,0:T(8,128)(2,1)S(1)}, bf16[512,512]{1,0:T(8,128)(2,1)}, u32[]{:S(2)}) copy-start(bf16[512,512]{1,0:T(8,128)(2,1)} %copy-done.3) | copy-start | bytes 1572868
  51.9 14.6 %all-to-all-start.2 = ((bf16[32,80,128]{2,1,0:T(8,128)(2,1)}), bf16[32,80,128]{2,1,0:T(8,128)(2,1)S(1)}, u32[]{:S(2)}, u32[]{:S(2)}) async-start(bf16[32,80,128]{2,1,0:T(8,128)(2,1)} %rotate.1), calls=%async_computation.2 | async-start | bytes 1310720 | tf_op jit(solution)/shard_map/gather/all_to_all | solution.py:428
  68.3 4.9 %collective-permute-start.2 = (f32[16,512]{1,0:T(8,128)S(1)}, f32[16,512]{1,0:T(8,128)S(1)}, u32[]{:S(2)}, u32[]{:S(2)}) collective-permute-start(f32[16,512]{1,0:T(8,128)S(1)} %get-tuple-element.25), channel_id=1, source_target_pairs={{0,1},{1,0},{2,3},{3,2},{4,5},{5,4},{6,7},{7,6},{8,9},{9,8},{10,11... | collective-permute-start | bytes 98312 | tf_op jit(solution)/shard_map/ppermute | solution.py:518

commit v8 on v7

--- a/solution.py
+++ b/solution.py
@@ -184,12 +184,13 @@
     copies0 = fetch(x0, buf0, sem0)
     for copy in small + copies0:
         copy.start()
-    copies1 = fetch_picked(pick, xk, xv, buf1, sem1)
     for copy in small:
         copy.wait()
     build_keep(masks.at[0], masks.at[1], keep)
     for q in range(CHUNKS):
         copies0[q].wait()
+        if q == 0:
+            copies1 = fetch_picked(pick, xk, xv, buf1, sem1)
         apply_mask(buf0, kept, keep, q)
     lefts, rests = zero_grams(pick, kept, out, spare)
     for q in range(CHUNKS):
@@ -229,8 +230,8 @@
         copy.wait()
 
 
-def lam_kernel(share, place, keep, x0, xk, xv, bases, keep_lam, send_lam, basis_in_t, mirror, b0, b1, b2, sem0, sem1, sem2):
-    c = place[1]
+def lam_kernel(share, core, block, keep, x0, xk, xv, bases, keep_lam, send_lam, basis_in_t, mirror, b0, b1, b2, sem0, sem1, sem2):
+    c = core[0]
     bufs = (b0, b1, b2)
     copies = [fetch(x, buf, sem) for x, buf, sem in zip((x0, xk, xv), bufs, (sem0, sem1, sem2))]
     for group in copies:
@@ -244,7 +245,7 @@
         home = 8 * ((lane >> 2) & 3) + FR * half + (lane & 3) + 2 * D
         for kind in range(2):
             distance = (lane >> 4) + (4 * c if kind else 0)
-            there = (home + BLK * (place[2] - distance)) & (D - 1)
+            there = (home + BLK * (block[0] - distance)) & (D - 1)
             one = jnp.where(column == there, 1.0, 0.0).astype(bf16)
             mirror[pl.ds((2 * half + kind) * LANES, LANES), :] = one
     lam = []
@@ -345,9 +346,9 @@
             out[i, pl.ds(j * ROWS, ROWS), :] = tile
 
 
-def rows_kernel(place, got, out):
+def rows_kernel(deep, core, block, got, out):
     total, grad = deep_total(got)
-    k, c = place[0], place[1]
+    k, c = deep[0], core[0]
     rows = grad[0:FR]
     for other in range(1, DEEP):
         rows = jnp.where(k == other, grad[other * FR : (other + 1) * FR], rows)
@@ -362,12 +363,11 @@
         jnp.concatenate([zero, none, none, none], axis=1),
         jnp.concatenate([none, zero, end0, none], axis=1),
     )
-    factors = pltpu.roll(jnp.concatenate([picked, zero], axis=0), BLK * place[2], 1)
+    factors = pltpu.roll(jnp.concatenate([picked, zero], axis=0), BLK * block[0], 1)
     out[...] = jnp.concatenate([rows, factors, jnp.zeros_like(rows)], axis=0)
 
 
-def mirrored_rows(place, tails, mirror):
-    c, block = place[1], place[2]
+def mirrored_rows(c, block, tails, mirror):
     row = lax.broadcasted_iota(jnp.int32, (8, LANES), 0)
     group = (lax.broadcasted_iota(jnp.int32, (8, LANES), 1) >> 4) + jnp.where(row >= FR, 4 * c, 0)
     parts = []
@@ -381,7 +381,7 @@
     return dot(jnp.concatenate(parts, axis=1).astype(bf16), mirror[...])
 
 
-def solve_kernel(place, got, basis_in_t, basis_out, rows_in, mirror, rows, own, their, scaled):
+def solve_kernel(core, block, got, basis_in_t, basis_out, rows_in, mirror, rows, own, their, scaled):
     tails = [got[i, pl.ds(GATHER_LAM, ROWS), :].astype(f32) for i in range(WIDE)]
     lam = tails[0][:8]
     for tail in tails[1:]:
@@ -400,10 +400,10 @@
     prec = lax.dot_general(back, basis_out[...], (((1,), (1,)), ((), ())), preferred_element_type=f32)
     prec = prec.astype(bf16).astype(f32)
     curve = jnp.broadcast_to(curve, (2, D))
-    factors = rows[4:12, :] + mirrored_rows(place, tails, mirror)
+    factors = rows[4:12, :] + mirrored_rows(core[0], block[0], tails, mirror)
     low = jnp.concatenate([rows[0:2, :], factors[0:2], factors[4:6]], axis=0)
     high = jnp.concatenate([rows[2:4, :], factors[2:4], factors[6:8]], axis=0)
-    first = place[1] == 0
+    first = core[0] == 0
     pad = jnp.zeros((6, D), f32)
     own[...] = jnp.concatenate([prec[0:2], curve, jnp.where(first, low, high), pad], axis=0)
     their[...] = jnp.concatenate([prec[2:4], curve, jnp.where(first, high, low), pad], axis=0)
@@ -433,7 +433,7 @@
     core = index % NC
     first = core == 0
     z = (index // NC) % NZ
-    place = jnp.stack([z // PAIR, core, index // (NC * NZ)])
+    here = ((z // PAIR)[None], core[None], (index // (NC * NZ))[None])
     tokens_here = activations.shape[0]
     share = (1.0 - decay) / (tokens_here * lax.axis_size("dp"))
 
@@ -482,11 +482,11 @@
         keep_lam, send_lam, basis_in_t, mirror = call(
             functools.partial(lam_kernel, share),
             (lam_shape, lam_shape, shape((D, D), bf16), shape((2 * PAIR * LANES, D), bf16)),
-            [SMEM, VMEM, HBM, HBM, HBM, VMEM],
+            [SMEM, SMEM, VMEM, HBM, HBM, HBM, VMEM],
             [buf] * 3 + [sems] * 3,
             flops=work,
             moved=4 * MB,
-        )(place, keep, frames, keys, vals, bases)
+        )(*here[1:], keep, frames, keys, vals, bases)
     old_lam = []
     my_rows = lax.dynamic_slice_in_dim(bases, 2 * index, 2, 1).astype(f32)
     for f in range(3):
@@ -507,13 +507,13 @@
     with jax.named_scope("gather"):
         gathered = exchange(spread, WIDE_GROUPS)
     with jax.named_scope("rows"):
-        rows = call(rows_kernel, lines, [SMEM, VMEM])(place, got)
+        rows = call(rows_kernel, lines, [SMEM] * 3 + [VMEM])(*here, got)
     rows_in = lax.dynamic_slice_in_dim(bases[0], (index // NC) * FR, FR, 0)
     rows_in = jnp.where(first, rows_in, jnp.roll(rows_in, 2, axis=0))
     rows_in = jnp.pad(rows_in, ((0, 16 - FR), (0, 0)))
     with jax.named_scope("solve"):
-        own, their = call(solve_kernel, (lines, lines), [SMEM] + [VMEM] * 6, [pltpu.VMEM((D, D), bf16)])(
-            place, gathered, basis_in_t, basis_out, rows_in, mirror, rows
+        own, their = call(solve_kernel, (lines, lines), [SMEM] * 2 + [VMEM] * 6, [pltpu.VMEM((D, D), bf16)])(
+            *here[1:], gathered, basis_in_t, basis_out, rows_in, mirror, rows
         )
     theirs = lax.ppermute(their, "dp", SWAP)
     with jax.named_scope("finish"):

time: 74.3 us -> 73.6 us (level)
  Pallas kernels: 18.1 us -> 15.8 us
  waiting for transfers between devices: 24.2 us -> 25.7 us
    all_to_all x3, waiting for transfers between devices: 22.4 us -> 23.9 us  [exchange(): lax.all_to_all(value, 'dp', 0, 0, axis_index_groups=groups, tiled=True)]
    pallas_call x2, Pallas kernels: 2.36 us -> 1.28 us  [the longest x1 1.13 us: body(): call(solve_kernel, (lines, lines), [SMEM] * 2 + [VMEM] * 6, [pltpu.VMEM((...]
    pallas_call x1, Pallas kernels: 4.95 us -> 4.07 us  [body(): call(functools.partial(lam_kernel, share), (lam_shape, lam_shape, shape((...]
  transfers between devices with their start and end apart: 6 -> 6, of which waited for: 5 -> 5; matrix products, arithmetic and copies ran while one was open for 5% -> 5% of each run, Pallas kernels for 11% -> 9%
where the time goes in v8:
time: 73.6 us; the launch traced here: 73 us
  starting transfers between devices  25.7 us (35%)
  waiting for transfers between devices  25.7 us (35%)
  Pallas kernels  15.8 us (21%)
  local copies, waits for them, and re-layouts  3.29 us (4%)
  matrix products  0.99 us (1%)
  between operations  0.87 us (1%)
  other arithmetic  0.75 us (1%)
    all_to_all x3, waiting for transfers between devices, exchange(): lax.all_to_all(value, 'dp', 0, 0, axis_index_groups=groups, tiled=True)  23.9 us
    all_to_all x3, starting transfers between devices, exchange(): lax.all_to_all(value, 'dp', 0, 0, axis_index_groups=groups, tiled=True)  18 us
    pallas_call x1, Pallas kernels, body(): call(functools.partial(lam_kernel, share), (lam_shape, lam_shape, shape((...  4.07 us
    pallas_call x1, Pallas kernels, body(): call(theirs_kernel, (partial, shape((NXY, PAIR, ROWS + ROWS // 2, LANES),...  4.04 us
    ppermute x1, starting transfers between devices, body(): theirs = lax.ppermute(their, 'dp', SWAP)  4 us
    ppermute x1, starting transfers between devices, body(): received = lax.ppermute(other, 'dp', SWAP)  3.33 us
    pallas_call x1, Pallas kernels, body(): call(mine_kernel, shape((NXY, PAIR, F0 + ROWS // 2, LANES), bf16), [SMEM,...  2.63 us
    unnamed x12, local copies, waits for them, and re-layouts  1.6 us
  transfers between devices with their start and end apart: 6, of which 5 were waited for; matrix products, arithmetic and copies ran while one was open for 5% of the time, Pallas kernels for 9%

profile of v8, /device:TPU:1, one launch (start us, length us, event | category | flops | bytes accessed | tf_op | source)
XLA Modules:
  0.0 73.0 jit_solution(6536980045234864943)
XLA Ops:
  0.6 4.0 %grams_theirs.1 = (bf16[16,2,120,128]{3,2,1,0:T(8,128)(2,1)S(1)}, bf16[16,2,24,128]{3,2,1,0:T(8,128)(2,1)S(1)}, bf16[1024,512]{1,0:T(8,128)(2,1)S(1)}, bf16[1024,128]{1,0:T(8,128)(2,1)S(1)}) custom-call(s32[1]{0:T(128)} %bitcast.core, s32[2,8]{1,0:T(2,128)} %bitcast.55, s32[2,8]{1,0:T(2,128)} %bitcast.56, bf16[1024,512]{1,0:T(8,128)(2,1)} %x0.3, ...), custom_call_target="tpu_custom_call" | custom-call | flops 1610612736 | bytes 4194304 | tf_op jit(solution)/shard_map/grams_theirs/pallas_call | solution.py:452
  4.7 3.3 %collective-permute-start = (bf16[16,2,120,128]{3,2,1,0:T(8,128)(2,1)S(1)}, bf16[16,2,120,128]{3,2,1,0:T(8,128)(2,1)S(1)}, u32[]{:S(2)}, u32[]{:S(2)}) collective-permute-start(bf16[16,2,120,128]{3,2,1,0:T(8,128)(2,1)S(1)} %get-tuple-element.19), channel_id=1, source_target_pairs={{0,1},{1,0},{2,3},{3,2},{4,5},{5,4},{6,7},{7,6},{8,9},{9,8},{10,11... | collective-permute-start | bytes 2949128 | tf_op jit(solution)/shard_map/ppermute | solution.py:460
  8.0 2.6 %grams_mine.1.mine = bf16[16,2,104,128]{3,2,1,0:T(8,128)(2,1)S(1)} custom-call(s32[1]{0:T(128)} %bitcast.core, bf16[1024,128]{1,0:T(8,128)(2,1)S(1)} %get-tuple-element.16.keep, bf16[1024,512]{1,0:T(8,128)(2,1)S(1)} %get-tuple-element.17.x0, bf16[1024,512]{1,0:T(8,128)(2,1)} %xk.5, bf16[1024,512]{1,0:T(8,128)(2,1)} %xv.5), custom_call_target="tpu_custom_call" | custom-call | flops 1610612736 | bytes 4194304 | tf_op jit(solution)/shard_map/grams_mine/pallas_call | solution.py:462
  10.7 0.0 collective-permute-done.received
  10.7 1.1 %chip_sum.1 = bf16[16,2,120,128]{3,2,1,0:T(8,128)(2,1)} custom-call(bf16[16,2,104,128]{3,2,1,0:T(8,128)(2,1)S(1)} %grams_mine.1.mine, bf16[16,2,24,128]{3,2,1,0:T(8,128)(2,1)S(1)} %get-tuple-element.18.spare, bf16[16,2,120,128]{3,2,1,0:T(8,128)(2,1)S(1)} %collective-permute-done.received), custom_call_target="tpu_custom_call" | custom-call | tf_op jit(solution)/shard_map/chip_sum/pallas_call | solution.py:471
  11.7 0.0 copy-start
  11.8 0.0 copy-start.5
  11.8 6.8 %all-to-all-start = ((bf16[32,120,128]{2,1,0:T(8,128)(2,1)}), bf16[32,120,128]{2,1,0:T(8,128)(2,1)S(1)}, u32[]{:S(2)}, u32[]{:S(2)}) async-start(bf16[32,120,128]{2,1,0:T(8,128)(2,1)} %bitcast.50), calls=%async_computation | async-start | bytes 1966080 | tf_op jit(solution)/shard_map/wide_sum/all_to_all | solution.py:428
  18.6 0.0 copy-done.5
  18.6 0.3 fusion
  19.0 0.3 fusion.2
  19.3 0.3 fusion.1
  19.6 4.1 %lam.1 = (f32[2,512]{1,0:T(2,128)S(1)}, f32[2,512]{1,0:T(2,128)S(1)}, bf16[512,512]{1,0:T(8,128)(2,1)S(1)}, bf16[512,512]{1,0:T(8,128)(2,1)S(1)}) custom-call(s32[1]{0:T(128)} %bitcast.core, s32[1]{0:T(128)} %bitcast.1.block, bf16[1024,128]{1,0:T(8,128)(2,1)S(1)} %get-tuple-element.16.keep, bf16[1024,512]{1,0:T(8,128)(2,1)} %x0.3, bf16[1024,512]{1,0:T(8,128)(2,1)} %xk.5, ...), custom_call_target="tpu_custom_call" | custom-call | flops 1610612736 | bytes 4194304 | tf_op jit(solution)/shard_map/lam/pallas_call | solution.py:482
  23.7 0.8 %copy-done.1 = bf16[512,512]{1,0:T(8,128)(2,1)} copy-done((bf16[512,512]{1,0:T(8,128)(2,1)}, bf16[512,512]{1,0:T(8,128)(2,1)S(1)}, u32[]{:S(2)}) %copy-start.1) | copy-done | bytes 524312
  24.5 0.8 %copy-done.3 = bf16[512,512]{1,0:T(8,128)(2,1)} copy-done((bf16[512,512]{1,0:T(8,128)(2,1)}, bf16[512,512]{1,0:T(8,128)(2,1)S(1)}, u32[]{:S(2)}) %copy-start.3) | copy-done | bytes 524312
  25.3 0.4 collective-permute-start.1
  25.7 0.9 %collective-permute-done.1.send_lam = f32[2,512]{1,0:T(2,128)S(1)} collective-permute-done((f32[2,512]{1,0:T(2,128)S(1)}, f32[2,512]{1,0:T(2,128)S(1)}, u32[]{:S(2)}, u32[]{:S(2)}) %collective-permute-start.1) | collective-permute-done | bytes 4128 | tf_op jit(solution)/shard_map/ppermute | solution.py:497
  26.6 8.7 %all-to-all-done.parts = bf16[32,120,128]{2,1,0:T(8,128)(2,1)S(1)} async-done(((bf16[32,120,128]{2,1,0:T(8,128)(2,1)}), bf16[32,120,128]{2,1,0:T(8,128)(2,1)S(1)}, u32[]{:S(2)}, u32[]{:S(2)}) %all-to-all-start) | async-done | bytes 983072 | tf_op jit(solution)/shard_map/wide_sum/all_to_all | solution.py:428
  35.3 1.0 %pack.1 = bf16[4,112,128]{2,1,0:T(8,128)(2,1)} custom-call(bf16[32,120,128]{2,1,0:T(8,128)(2,1)S(1)} %all-to-all-done.parts, f32[2,512]{1,0:T(2,128)S(1)} %get-tuple-element.36.keep_lam, f32[2,512]{1,0:T(2,128)S(1)} %collective-permute-done.1.send_lam), custom_call_target="tpu_custom_call" | custom-call | tf_op jit(solution)/shard_map/pack/pallas_call | solution.py:500
  36.2 7.3 %all-to-all-start.1 = ((bf16[4,112,128]{2,1,0:T(8,128)(2,1)}), bf16[4,112,128]{2,1,0:T(8,128)(2,1)S(1)}, u32[]{:S(2)}, u32[]{:S(2)}) async-start(bf16[4,112,128]{2,1,0:T(8,128)(2,1)} %pack.1), calls=%async_computation.1 | async-start | bytes 229376 | tf_op jit(solution)/shard_map/deep_sum/all_to_all | solution.py:428
  43.5 0.9 %fusion.17 = (bf16[1,512,512]{2,1,0:T(8,128)(2,1)}, bf16[512,512]{1,0:T(8,128)(2,1)S(1)}) fusion(bf16[3,512,512]{2,1,0:T(8,128)(2,1)S(1)} %copy-done, s32[]{:T(128)S(6)} %select_n.80), kind=kLoop, calls=%fused_computation.33 | loop fusion | bytes 2097156 | tf_op jit(solution)/shard_map/slice | solution.py:493
  44.4 6.3 %all-to-all-done.1.got = bf16[4,112,128]{2,1,0:T(8,128)(2,1)S(1)} async-done(((bf16[4,112,128]{2,1,0:T(8,128)(2,1)}), bf16[4,112,128]{2,1,0:T(8,128)(2,1)S(1)}, u32[]{:S(2)}, u32[]{:S(2)}) %all-to-all-start.1) | async-done | bytes 114720 | tf_op jit(solution)/shard_map/deep_sum/all_to_all | solution.py:428
  50.7 1.1 %rotate.1 = bf16[32,80,128]{2,1,0:T(8,128)(2,1)} custom-call(bf16[4,112,128]{2,1,0:T(8,128)(2,1)S(1)} %all-to-all-done.1.got, bf16[512,512]{1,0:T(8,128)(2,1)S(1)} %get-tuple-element.30.basis.basis_out), custom_call_target="tpu_custom_call" | custom-call | tf_op jit(solution)/shard_map/rotate/pallas_call | solution.py:506
  51.8 3.9 %all-to-all-start.2 = ((bf16[32,80,128]{2,1,0:T(8,128)(2,1)}), bf16[32,80,128]{2,1,0:T(8,128)(2,1)S(1)}, u32[]{:S(2)}, u32[]{:S(2)}) async-start(bf16[32,80,128]{2,1,0:T(8,128)(2,1)} %rotate.1), calls=%async_computation.2 | async-start | bytes 1310720 | tf_op jit(solution)/shard_map/gather/all_to_all | solution.py:428
  55.7 0.8 %dynamic-slice_bitcast_fusion.2 = (bf16[2,512]{1,0:T(2,128)(2,1)S(1)}, bf16[2,512]{1,0:T(2,128)(2,1)S(1)}) fusion(bf16[1,512,512]{2,1,0:T(8,128)(2,1)} %get-tuple-element.29, s32[]{:T(128)S(6)} %add.37, s32[]{:T(128)S(6)} %select_n.83), kind=kLoop, calls=%fused_computation.28 | loop fusion | bytes 8200 | tf_op jit(solution)/shard_map/jit(_roll_static)/slice | solution.py:512
  56.5 0.7 maximum_select_fusion
  57.3 0.2 rows.1
  57.4 9.0 %all-to-all-done.2.got = bf16[32,80,128]{2,1,0:T(8,128)(2,1)S(1)} async-done(((bf16[32,80,128]{2,1,0:T(8,128)(2,1)}), bf16[32,80,128]{2,1,0:T(8,128)(2,1)S(1)}, u32[]{:S(2)}, u32[]{:S(2)}) %all-to-all-start.2) | async-done | bytes 655392 | tf_op jit(solution)/shard_map/gather/all_to_all | solution.py:428
  66.4 1.1 %solve.1 = (f32[16,512]{1,0:T(8,128)S(1)}, f32[16,512]{1,0:T(8,128)S(1)}) custom-call(s32[1]{0:T(128)} %bitcast.core, s32[1]{0:T(128)} %bitcast.1.block, bf16[32,80,128]{2,1,0:T(8,128)(2,1)S(1)} %all-to-all-done.2.got, bf16[512,512]{1,0:T(8,128)(2,1)S(1)} %copy-done.2, bf16[512,512]{1,0:T(8,128)(2,1)S(1)} %get-tuple-element.30.basis.basis_out, ...), custom_call_target="tpu_custom_call" | custom-call | tf_op jit(solution)/shard_map/solve/pallas_call | solution.py:515
  67.6 4.0 %collective-permute-start.2 = (f32[16,512]{1,0:T(8,128)S(1)}, f32[16,512]{1,0:T(8,128)S(1)}, u32[]{:S(2)}, u32[]{:S(2)}) collective-permute-start(f32[16,512]{1,0:T(8,128)S(1)} %get-tuple-element.25), channel_id=1, source_target_pairs={{0,1},{1,0},{2,3},{3,2},{4,5},{5,4},{6,7},{7,6},{8,9},{9,8},{10,11... | collective-permute-start | bytes 98312 | tf_op jit(solution)/shard_map/ppermute | solution.py:518
  71.6 0.9 %collective-permute-done.2.got = f32[16,512]{1,0:T(8,128)S(1)} collective-permute-done((f32[16,512]{1,0:T(8,128)S(1)}, f32[16,512]{1,0:T(8,128)S(1)}, u32[]{:S(2)}, u32[]{:S(2)}) %collective-permute-start.2) | collective-permute-done | bytes 32800 | tf_op jit(solution)/shard_map/ppermute | solution.py:518
  72.4 0.6 finish.1
  (12 shorter events, 0.1 us)
Async XLA Ops:
  4.7 6.0 %collective-permute-start = (bf16[16,2,120,128]{3,2,1,0:T(8,128)(2,1)S(1)}, bf16[16,2,120,128]{3,2,1,0:T(8,128)(2,1)S(1)}, u32[]{:S(2)}, u32[]{:S(2)}) collective-permute-start(bf16[16,2,120,128]{3,2,1,0:T(8,128)(2,1)S(1)} %get-tuple-element.19), channel_id=1, source_target_pairs={{0,1},{1,0},{2,3},{3,2},{4,5},{5,4},{6,7},{7,6},{8,9},{9,8},{10,11... | collective-permute-start | bytes 2949128 | tf_op jit(solution)/shard_map/ppermute | solution.py:460
  11.7 6.9 %copy-start = (bf16[3,512,512]{2,1,0:T(8,128)(2,1)S(1)}, bf16[3,512,512]{2,1,0:T(8,128)(2,1)}, u32[]{:S(2)}) copy-start(bf16[3,512,512]{2,1,0:T(8,128)(2,1)} %bases.1) | copy-start | bytes 4718596
  11.8 6.9 %copy-start.5 = (f32[2,3,512]{2,0,1:T(2,128)S(1)}, f32[2,3,512]{2,0,1:T(2,128)}, u32[]{:S(2)}) copy-start(f32[2,3,512]{2,0,1:T(2,128)} %param.13) | copy-start | bytes 36868
  11.8 23.5 %all-to-all-start = ((bf16[32,120,128]{2,1,0:T(8,128)(2,1)}), bf16[32,120,128]{2,1,0:T(8,128)(2,1)S(1)}, u32[]{:S(2)}, u32[]{:S(2)}) async-start(bf16[32,120,128]{2,1,0:T(8,128)(2,1)} %bitcast.50), calls=%async_computation | async-start | bytes 1966080 | tf_op jit(solution)/shard_map/wide_sum/all_to_all | solution.py:428
  23.7 0.8 %copy-start.1 = (bf16[512,512]{1,0:T(8,128)(2,1)}, bf16[512,512]{1,0:T(8,128)(2,1)S(1)}, u32[]{:S(2)}) copy-start(bf16[512,512]{1,0:T(8,128)(2,1)S(1)} %get-tuple-element.22.basis_in_t) | copy-start | bytes 1572868
  24.5 0.8 %copy-start.3 = (bf16[512,512]{1,0:T(8,128)(2,1)}, bf16[512,512]{1,0:T(8,128)(2,1)S(1)}, u32[]{:S(2)}) copy-start(bf16[512,512]{1,0:T(8,128)(2,1)S(1)} %get-tuple-element.23.mirror) | copy-start | bytes 1572868
  25.3 1.3 %collective-permute-start.1 = (f32[2,512]{1,0:T(2,128)S(1)}, f32[2,512]{1,0:T(2,128)S(1)}, u32[]{:S(2)}, u32[]{:S(2)}) collective-permute-start(f32[2,512]{1,0:T(2,128)S(1)} %get-tuple-element.35), channel_id=1, source_target_pairs={{0,1},{1,0},{2,3},{3,2},{4,5},{5,4},{6,7},{7,6},{8,9},{9,8},{10,11... | collective-permute-start | bytes 12296 | tf_op jit(solution)/shard_map/ppermute | solution.py:497
  36.2 14.5 %all-to-all-start.1 = ((bf16[4,112,128]{2,1,0:T(8,128)(2,1)}), bf16[4,112,128]{2,1,0:T(8,128)(2,1)S(1)}, u32[]{:S(2)}, u32[]{:S(2)}) async-start(bf16[4,112,128]{2,1,0:T(8,128)(2,1)} %pack.1), calls=%async_computation.1 | async-start | bytes 229376 | tf_op jit(solution)/shard_map/deep_sum/all_to_all | solution.py:428
  44.4 22.0 %copy-start.2 = (bf16[512,512]{1,0:T(8,128)(2,1)S(1)}, bf16[512,512]{1,0:T(8,128)(2,1)}, u32[]{:S(2)}) copy-start(bf16[512,512]{1,0:T(8,128)(2,1)} %copy-done.1) | copy-start | bytes 1572868
  44.4 22.0 %copy-start.4 = (bf16[512,512]{1,0:T(8,128)(2,1)S(1)}, bf16[512,512]{1,0:T(8,128)(2,1)}, u32[]{:S(2)}) copy-start(bf16[512,512]{1,0:T(8,128)(2,1)} %copy-done.3) | copy-start | bytes 1572868
  51.8 14.6 %all-to-all-start.2 = ((bf16[32,80,128]{2,1,0:T(8,128)(2,1)}), bf16[32,80,128]{2,1,0:T(8,128)(2,1)S(1)}, u32[]{:S(2)}, u32[]{:S(2)}) async-start(bf16[32,80,128]{2,1,0:T(8,128)(2,1)} %rotate.1), calls=%async_computation.2 | async-start | bytes 1310720 | tf_op jit(solution)/shard_map/gather/all_to_all | solution.py:428
  67.6 4.9 %collective-permute-start.2 = (f32[16,512]{1,0:T(8,128)S(1)}, f32[16,512]{1,0:T(8,128)S(1)}, u32[]{:S(2)}, u32[]{:S(2)}) collective-permute-start(f32[16,512]{1,0:T(8,128)S(1)} %get-tuple-element.25), channel_id=1, source_target_pairs={{0,1},{1,0},{2,3},{3,2},{4,5},{5,4},{6,7},{7,6},{8,9},{9,8},{10,11... | collective-permute-start | bytes 98312 | tf_op jit(solution)/shard_map/ppermute | solution.py:518

commit v9 on v8

--- a/solution.py
+++ b/solution.py
@@ -85,12 +85,12 @@
 def build_keep(start, width, keep):
     position = lax.broadcasted_iota(jnp.int32, (LEN, LANES), 0)
     for u in range(start.shape[1]):
-        inside = None
+        outside = None
         for m in range(start.shape[0]):
-            s = start[m : m + 1, u : u + 1]
-            here = (position >= s) & (position < s + width[m : m + 1, u : u + 1])
-            inside = here if inside is None else inside | here
-        keep[pl.ds(u * LEN, LEN), :] = jnp.where(inside, 0.0, 1.0).astype(bf16)
+            first = start[m, u]
+            here = (position < first) | (position >= first + width[m, u])
+            outside = here if outside is None else outside & here
+        keep[pl.ds(u * LEN, LEN), :] = jnp.where(outside, 1.0, 0.0).astype(bf16)
 
 
 def apply_mask(source, target, keep, q):
@@ -167,46 +167,46 @@
     return lefts, rests
 
 
-def picked_grams(lefts, x1, rests, out, end):
+def picked_grams(lefts, x1, keep, rests, out, end):
     for r in range(D // BLOCK):
         put(out, r, dot(lefts[r], x1[...]), 0)
+    wide = jnp.concatenate([keep[...]] * (BLOCK // LANES), axis=1)
     for r in range(D // BLOCK):
-        left = x1[:, pl.ds(r * BLOCK, BLOCK)].T
+        left = (x1[:, pl.ds(r * BLOCK, BLOCK)] * wide).T
         tiles = circulate(dot(left, x1[...]), r)
         put(out, r, jnp.concatenate(tiles[:2], axis=1), FA)
         last = end_lanes(tiles[2])
         put_folded(out, r, last if rests is None else last + rests[r], end)
 
 
-def theirs_kernel(core, start, width, x0, xk, xv, out, spare, kept, keep, buf0, buf1, masks, sem0, sem1, sem2):
+def theirs_kernel(
+    core, start, width, x0, xk, xv, out, spare, kept, keep, ahead, buf0, buf1, starts, widths, sem0, sem1, sem2, sem3
+):
     pick = 1 - core[0]
-    small = [pltpu.make_async_copy(v, masks.at[i], sem2.at[i]) for i, v in enumerate((start, width))]
+    small = [pltpu.make_async_copy(v, w, sem2.at[i]) for i, (v, w) in enumerate(((start, starts), (width, widths)))]
     copies0 = fetch(x0, buf0, sem0)
     for copy in small + copies0:
         copy.start()
     for copy in small:
         copy.wait()
-    build_keep(masks.at[0], masks.at[1], keep)
+    build_keep(starts, widths, keep)
     for q in range(CHUNKS):
         copies0[q].wait()
         if q == 0:
             copies1 = fetch_picked(pick, xk, xv, buf1, sem1)
         apply_mask(buf0, kept, keep, q)
     lefts, rests = zero_grams(pick, kept, out, spare)
-    for q in range(CHUNKS):
-        copies1[q].wait()
-        apply_mask(buf1, buf1, keep, q)
-    picked_grams(lefts, buf1, rests, out, FL)
-
-
-def mine_kernel(core, keep, x0, xk, xv, out, buf1, sem1):
-    pick = core[0]
-    copies1 = fetch_picked(pick, xk, xv, buf1, sem1)
+    for copy in copies1:
+        copy.wait()
+    copies2 = fetch_picked(core[0], xk, xv, ahead, sem3)
+    picked_grams(lefts, buf1, keep, rests, out, FL)
+    for copy in copies2:
+        copy.wait()
+
+
+def mine_kernel(keep, x0, x1, out):
     lefts = [x0[:, pl.ds(r * BLOCK, BLOCK)].T for r in range(D // BLOCK)]
-    for q in range(CHUNKS):
-        copies1[q].wait()
-        apply_mask(buf1, buf1, keep, q)
-    picked_grams(lefts, buf1, None, out, F0)
+    picked_grams(lefts, x1, keep, None, out, F0)
 
 
 PIECES = 4
@@ -230,7 +230,7 @@
         copy.wait()
 
 
-def lam_kernel(share, core, block, keep, x0, xk, xv, bases, keep_lam, send_lam, basis_in_t, mirror, b0, b1, b2, sem0, sem1, sem2):
+def lam_kernel(share, core, block, _, keep, x0, xk, xv, bases, keep_lam, send_lam, basis_in_t, mirror, b0, b1, b2, sem0, sem1, sem2):
     c = core[0]
     bufs = (b0, b1, b2)
     copies = [fetch(x, buf, sem) for x, buf, sem in zip((x0, xk, xv), bufs, (sem0, sem1, sem2))]
@@ -442,18 +442,24 @@
 
     masks = (in_hbm(time_start.T), in_hbm(time_width.T))
     frames, keys, vals = in_hbm(activations), in_hbm(grad_key), in_hbm(grad_value)
-    mask_buf = pltpu.VMEM((2,) + time_start.shape[::-1], jnp.int32)
+    mask_buf = pltpu.SMEM(time_start.shape[::-1], jnp.int32)
     buf = pltpu.VMEM((tokens_here, D), bf16)
     sems = pltpu.SemaphoreType.DMA((CHUNKS,))
     pair = pltpu.SemaphoreType.DMA((2,))
     partial = shape((NXY, PAIR, WROWS, LANES), bf16)
     work = 6 * D * D * tokens_here
     with jax.named_scope("grams_theirs"):
-        other, spare, kept, keep = call(
+        other, spare, kept, keep, ahead = call(
             theirs_kernel,
-            (partial, shape((NXY, PAIR, ROWS + ROWS // 2, LANES), bf16), shape((tokens_here, D), bf16), shape((tokens_here, LANES), bf16)),
+            (
+                partial,
+                shape((NXY, PAIR, ROWS + ROWS // 2, LANES), bf16),
+                shape((tokens_here, D), bf16),
+                shape((tokens_here, LANES), bf16),
+                shape((tokens_here, D), bf16),
+            ),
             [SMEM] + [HBM] * 5,
-            [buf, buf, mask_buf, sems, sems, pair],
+            [buf, buf, mask_buf, mask_buf, sems, sems, pair, sems],
             flops=work,
             moved=4 * MB,
         )(core[None], *masks, frames, keys, vals)
@@ -462,11 +468,10 @@
         mine = call(
             mine_kernel,
             shape((NXY, PAIR, F0 + ROWS // 2, LANES), bf16),
-            [SMEM, VMEM, VMEM, HBM, HBM],
-            [buf, sems],
+            [VMEM] * 3,
             flops=work,
             moved=4 * MB,
-        )(core[None], keep, kept, keys, vals)
+        )(keep, kept, ahead)
     with jax.named_scope("chip_sum"):
         chip = call(
             add_kernel,
@@ -482,11 +487,11 @@
         keep_lam, send_lam, basis_in_t, mirror = call(
             functools.partial(lam_kernel, share),
             (lam_shape, lam_shape, shape((D, D), bf16), shape((2 * PAIR * LANES, D), bf16)),
-            [SMEM, SMEM, VMEM, HBM, HBM, HBM, VMEM],
+            [SMEM, SMEM, HBM, VMEM, HBM, HBM, HBM, VMEM],
             [buf] * 3 + [sems] * 3,
             flops=work,
             moved=4 * MB,
-        )(*here[1:], keep, frames, keys, vals, bases)
+        )(*here[1:], in_hbm(chip), keep, frames, keys, vals, bases)
     old_lam = []
     my_rows = lax.dynamic_slice_in_dim(bases, 2 * index, 2, 1).astype(f32)
     for f in range(3):

time: 73.6 us -> 72.6 us (0.986)
  Pallas kernels: 15.8 us -> 14.4 us
  local copies, waits for them, and re-layouts: 3.29 us -> 2.46 us
  waiting for transfers between devices: 25.7 us -> 26.5 us
    pallas_call x1, Pallas kernels: 2.63 us -> 1.46 us  [body(): call(mine_kernel, shape((NXY, PAIR, F0 + ROWS // 2, LANES), bf16), [VMEM]...]
    unnamed x12 -> x8, local copies, waits for them, and re-layouts: 1.6 us -> 0.81 us
  transfers between devices with their start and end apart: 6 -> 6, of which waited for: 5 -> 6; matrix products, arithmetic and copies ran while one was open for 5% -> 5% of each run, Pallas kernels for 9% -> 8%
where the time goes in v9:
time: 72.6 us; the launch traced here: 72 us
  waiting for transfers between devices  26.5 us (37%)
  starting transfers between devices  26.2 us (36%)
  Pallas kernels  14.4 us (20%)
  local copies, waits for them, and re-layouts  2.46 us (3%)
  matrix products  0.99 us (1%)
  between operations  0.87 us (1%)
  other arithmetic  0.75 us (1%)
    all_to_all x3, waiting for transfers between devices, exchange(): lax.all_to_all(value, 'dp', 0, 0, axis_index_groups=groups, tiled=True)  24 us
    all_to_all x3, starting transfers between devices, exchange(): lax.all_to_all(value, 'dp', 0, 0, axis_index_groups=groups, tiled=True)  18 us
    ppermute x1, starting transfers between devices, body(): theirs = lax.ppermute(their, 'dp', SWAP)  4.11 us
    pallas_call x1, Pallas kernels, body(): call(functools.partial(lam_kernel, share), (lam_shape, lam_shape, shape((...  4.07 us
    pallas_call x1, Pallas kernels, body(): call(theirs_kernel, (partial, shape((NXY, PAIR, ROWS + ROWS // 2, LANES),...  3.78 us
    ppermute x1, starting transfers between devices, body(): received = lax.ppermute(other, 'dp', SWAP)  3.33 us
    pallas_call x1, Pallas kernels, body(): call(mine_kernel, shape((NXY, PAIR, F0 + ROWS // 2, LANES), bf16), [VMEM]...  1.46 us
  transfers between devices with their start and end apart: 6, of which 6 were waited for; matrix products, arithmetic and copies ran while one was open for 5% of the time, Pallas kernels for 8%

profile of v9, /device:TPU:1, one launch (start us, length us, event | category | flops | bytes accessed | tf_op | source)
XLA Modules:
  0.0 72.0 jit_solution(11275477793393104699)
XLA Ops:
  0.6 3.8 %grams_theirs.1 = (bf16[16,2,120,128]{3,2,1,0:T(8,128)(2,1)S(1)}, bf16[16,2,24,128]{3,2,1,0:T(8,128)(2,1)S(1)}, bf16[1024,512]{1,0:T(8,128)(2,1)S(1)}, bf16[1024...) custom-call(s32[1]{0:T(128)} %bitcast.core, s32[2,8]{1,0:T(2,128)} %bitcast.56, s32[2,8]{1,0:T(2,128)} %bitcast.57, ...), custom_call_target="tpu_custom_call" | custom-call | flops 1610612736 | bytes 4194304 | tf_op jit(solution)/shard_map/grams_theirs/pallas_call | solution.py:452
  4.4 3.3 %collective-permute-start = (bf16[16,2,120,128]{3,2,1,0:T(8,128)(2,1)S(1)}, bf16[16,2,120,128]{3,2,1,0:T(8,128)(2,1)S(1)}, u32[]{:S(2)}, u32[]{:S(2)}) collective-permute-start(bf16[16,2,120,128]{3,2,1,0:T(8,128)(2,1)S(1)} %get-tuple-element.21), channel_id=1, source_target_pairs={{0,1},{1,0},{2,3},{3,2},{4,5},{5,4},{6,7},{7,6},{8,9},{9,8},{10,11... | collective-permute-start | bytes 2949128 | tf_op jit(solution)/shard_map/ppermute | solution.py:466
  7.8 1.5 %grams_mine.1.mine = bf16[16,2,104,128]{3,2,1,0:T(8,128)(2,1)S(1)} custom-call(bf16[1024,128]{1,0:T(8,128)(2,1)S(1)} %get-tuple-element.17.keep, bf16[1024,512]{1,0:T(8,128)(2,1)S(1)} %get-tuple-element.18.x0, bf16[1024,512]{1,0:T(8,128)(2,1)S(1)} %get-tuple-element.19.x1), custom_call_target="tpu_custom_call" | custom-call | flops 1610612736 | bytes 4194304 | tf_op jit(solution)/shard_map/grams_mine/pallas_call | solution.py:468
  9.2 0.7 %collective-permute-done.received = bf16[16,2,120,128]{3,2,1,0:T(8,128)(2,1)S(1)} collective-permute-done((bf16[16,2,120,128]{3,2,1,0:T(8,128)(2,1)S(1)}, bf16[16,2,120,128]{3,2,1,0:T(8,128)(2,1)S(1)}, u32[]{:S(2)}, u32[]{:S(2)}) %collective-permute-start) | collective-permute-done | bytes 983072 | tf_op jit(solution)/shard_map/ppermute | solution.py:466
  10.0 1.1 %chip_sum.1 = bf16[16,2,120,128]{3,2,1,0:T(8,128)(2,1)} custom-call(bf16[16,2,104,128]{3,2,1,0:T(8,128)(2,1)S(1)} %grams_mine.1.mine, bf16[16,2,24,128]{3,2,1,0:T(8,128)(2,1)S(1)} %get-tuple-element.20.spare, bf16[16,2,120,128]{3,2,1,0:T(8,128)(2,1)S(1)} %collective-permute-done.received), custom_call_target="tpu_custom_call" | custom-call | tf_op jit(solution)/shard_map/chip_sum/pallas_call | solution.py:476
  11.0 0.0 copy-start
  11.0 0.0 copy-start.3
  11.1 6.8 %all-to-all-start = ((bf16[32,120,128]{2,1,0:T(8,128)(2,1)}), bf16[32,120,128]{2,1,0:T(8,128)(2,1)S(1)}, u32[]{:S(2)}, u32[]{:S(2)}) async-start(bf16[32,120,128]{2,1,0:T(8,128)(2,1)} %bitcast.50), calls=%async_computation | async-start | bytes 1966080 | tf_op jit(solution)/shard_map/wide_sum/all_to_all | solution.py:428
  17.9 0.0 copy-done
  17.9 0.0 copy-done.3
  17.9 0.3 fusion
  18.3 0.3 fusion.2
  18.6 0.3 fusion.1
  19.0 4.1 %lam.1 = (f32[2,512]{1,0:T(2,128)S(1)}, f32[2,512]{1,0:T(2,128)S(1)}, bf16[512,512]{1,0:T(8,128)(2,1)S(1)}, bf16[512,512]{1,0:T(8,128)(2,1)S(1)}) custom-call(s32[1]{0:T(128)} %bitcast.core, s32[1]{0:T(128)} %bitcast.1.block, bf16[32,120,128]{2,1,0:T(8,128)(2,1)} %bitcast.51, bf16[1024,128]{1,0:T(8,128)(2,1)S(1)} %get-tuple-element.17.keep, ...), custom_call_target="tpu_custom_call" | custom-call | flops 1610612736 | bytes 4194304 | tf_op jit(solution)/shard_map/lam/pallas_call | solution.py:487
  23.0 0.8 %copy-done.1 = bf16[512,512]{1,0:T(8,128)(2,1)} copy-done((bf16[512,512]{1,0:T(8,128)(2,1)}, bf16[512,512]{1,0:T(8,128)(2,1)S(1)}, u32[]{:S(2)}) %copy-start.1) | copy-done | bytes 524312
  23.8 0.7 %collective-permute-start.1 = (f32[2,512]{1,0:T(2,128)S(1)}, f32[2,512]{1,0:T(2,128)S(1)}, u32[]{:S(2)}, u32[]{:S(2)}) collective-permute-start(f32[2,512]{1,0:T(2,128)S(1)} %get-tuple-element.37), channel_id=1, source_target_pairs={{0,1},{1,0},{2,3},{3,2},{4,5},{5,4},{6,7},{7,6},{8,9},{9,8},{10,11... | collective-permute-start | bytes 12296 | tf_op jit(solution)/shard_map/ppermute | solution.py:502
  24.6 0.8 %collective-permute-done.1.send_lam = f32[2,512]{1,0:T(2,128)S(1)} collective-permute-done((f32[2,512]{1,0:T(2,128)S(1)}, f32[2,512]{1,0:T(2,128)S(1)}, u32[]{:S(2)}, u32[]{:S(2)}) %collective-permute-start.1) | collective-permute-done | bytes 4128 | tf_op jit(solution)/shard_map/ppermute | solution.py:502
  25.4 8.7 %all-to-all-done.parts = bf16[32,120,128]{2,1,0:T(8,128)(2,1)S(1)} async-done(((bf16[32,120,128]{2,1,0:T(8,128)(2,1)}), bf16[32,120,128]{2,1,0:T(8,128)(2,1)S(1)}, u32[]{:S(2)}, u32[]{:S(2)}) %all-to-all-start) | async-done | bytes 983072 | tf_op jit(solution)/shard_map/wide_sum/all_to_all | solution.py:428
  34.1 1.0 %pack.1 = bf16[4,112,128]{2,1,0:T(8,128)(2,1)} custom-call(bf16[32,120,128]{2,1,0:T(8,128)(2,1)S(1)} %all-to-all-done.parts, f32[2,512]{1,0:T(2,128)S(1)} %get-tuple-element.38.keep_lam, f32[2,512]{1,0:T(2,128)S(1)} %collective-permute-done.1.send_lam), custom_call_target="tpu_custom_call" | custom-call | tf_op jit(solution)/shard_map/pack/pallas_call | solution.py:505
  35.1 7.3 %all-to-all-start.1 = ((bf16[4,112,128]{2,1,0:T(8,128)(2,1)}), bf16[4,112,128]{2,1,0:T(8,128)(2,1)S(1)}, u32[]{:S(2)}, u32[]{:S(2)}) async-start(bf16[4,112,128]{2,1,0:T(8,128)(2,1)} %pack.1), calls=%async_computation.1 | async-start | bytes 229376 | tf_op jit(solution)/shard_map/deep_sum/all_to_all | solution.py:428
  42.4 0.9 %fusion.17 = (bf16[1,512,512]{2,1,0:T(8,128)(2,1)}, bf16[512,512]{1,0:T(8,128)(2,1)S(1)}) fusion(bf16[3,512,512]{2,1,0:T(8,128)(2,1)S(1)} %copy-done, s32[]{:T(128)S(6)} %select_n.80), kind=kLoop, calls=%fused_computation.33 | loop fusion | bytes 2097156 | tf_op jit(solution)/shard_map/slice | solution.py:498
  43.3 6.3 %all-to-all-done.1.got = bf16[4,112,128]{2,1,0:T(8,128)(2,1)S(1)} async-done(((bf16[4,112,128]{2,1,0:T(8,128)(2,1)}), bf16[4,112,128]{2,1,0:T(8,128)(2,1)S(1)}, u32[]{:S(2)}, u32[]{:S(2)}) %all-to-all-start.1) | async-done | bytes 114720 | tf_op jit(solution)/shard_map/deep_sum/all_to_all | solution.py:428
  49.6 1.1 %rotate.1 = bf16[32,80,128]{2,1,0:T(8,128)(2,1)} custom-call(bf16[4,112,128]{2,1,0:T(8,128)(2,1)S(1)} %all-to-all-done.1.got, bf16[512,512]{1,0:T(8,128)(2,1)S(1)} %get-tuple-element.32.basis.basis_out), custom_call_target="tpu_custom_call" | custom-call | tf_op jit(solution)/shard_map/rotate/pallas_call | solution.py:511
  50.6 3.9 %all-to-all-start.2 = ((bf16[32,80,128]{2,1,0:T(8,128)(2,1)}), bf16[32,80,128]{2,1,0:T(8,128)(2,1)S(1)}, u32[]{:S(2)}, u32[]{:S(2)}) async-start(bf16[32,80,128]{2,1,0:T(8,128)(2,1)} %rotate.1), calls=%async_computation.2 | async-start | bytes 1310720 | tf_op jit(solution)/shard_map/gather/all_to_all | solution.py:428
  54.6 0.8 %dynamic-slice_bitcast_fusion.2 = (bf16[2,512]{1,0:T(2,128)(2,1)S(1)}, bf16[2,512]{1,0:T(2,128)(2,1)S(1)}) fusion(bf16[1,512,512]{2,1,0:T(8,128)(2,1)} %get-tuple-element.31, s32[]{:T(128)S(6)} %add.37, s32[]{:T(128)S(6)} %select_n.83), kind=kLoop, calls=%fused_computation.28 | loop fusion | bytes 8200 | tf_op jit(solution)/shard_map/jit(_roll_static)/slice | solution.py:517
  55.4 0.7 maximum_select_fusion
  56.1 0.2 rows.1
  56.3 9.0 %all-to-all-done.2.got = bf16[32,80,128]{2,1,0:T(8,128)(2,1)S(1)} async-done(((bf16[32,80,128]{2,1,0:T(8,128)(2,1)}), bf16[32,80,128]{2,1,0:T(8,128)(2,1)S(1)}, u32[]{:S(2)}, u32[]{:S(2)}) %all-to-all-start.2) | async-done | bytes 655392 | tf_op jit(solution)/shard_map/gather/all_to_all | solution.py:428
  65.3 1.1 %solve.1 = (f32[16,512]{1,0:T(8,128)S(1)}, f32[16,512]{1,0:T(8,128)S(1)}) custom-call(s32[1]{0:T(128)} %bitcast.core, s32[1]{0:T(128)} %bitcast.1.block, bf16[32,80,128]{2,1,0:T(8,128)(2,1)S(1)} %all-to-all-done.2.got, bf16[512,512]{1,0:T(8,128)(2,1)S(1)} %get-tuple-element.24.basis_in_t, bf16[512,512]{1,0:T(8,128)(2,1)S(1)} %get-tuple-element.32.basis.basis_out, ...), custom_call_target="tpu_custom_call" | custom-call | tf_op jit(solution)/shard_map/solve/pallas_call | solution.py:520
  66.4 4.1 %collective-permute-start.2 = (f32[16,512]{1,0:T(8,128)S(1)}, f32[16,512]{1,0:T(8,128)S(1)}, u32[]{:S(2)}, u32[]{:S(2)}) collective-permute-start(f32[16,512]{1,0:T(8,128)S(1)} %get-tuple-element.27), channel_id=1, source_target_pairs={{0,1},{1,0},{2,3},{3,2},{4,5},{5,4},{6,7},{7,6},{8,9},{9,8},{10,11... | collective-permute-start | bytes 98312 | tf_op jit(solution)/shard_map/ppermute | solution.py:523
  70.6 0.9 %collective-permute-done.2.got = f32[16,512]{1,0:T(8,128)S(1)} collective-permute-done((f32[16,512]{1,0:T(8,128)S(1)}, f32[16,512]{1,0:T(8,128)S(1)}, u32[]{:S(2)}, u32[]{:S(2)}) %collective-permute-start.2) | collective-permute-done | bytes 32800 | tf_op jit(solution)/shard_map/ppermute | solution.py:523
  71.4 0.6 finish.1
  (8 shorter events, 0.0 us)
Async XLA Ops:
  4.4 5.5 %collective-permute-start = (bf16[16,2,120,128]{3,2,1,0:T(8,128)(2,1)S(1)}, bf16[16,2,120,128]{3,2,1,0:T(8,128)(2,1)S(1)}, u32[]{:S(2)}, u32[]{:S(2)}) collective-permute-start(bf16[16,2,120,128]{3,2,1,0:T(8,128)(2,1)S(1)} %get-tuple-element.21), channel_id=1, source_target_pairs={{0,1},{1,0},{2,3},{3,2},{4,5},{5,4},{6,7},{7,6},{8,9},{9,8},{10,11... | collective-permute-start | bytes 2949128 | tf_op jit(solution)/shard_map/ppermute | solution.py:466
  11.0 6.9 %copy-start = (bf16[3,512,512]{2,1,0:T(8,128)(2,1)S(1)}, bf16[3,512,512]{2,1,0:T(8,128)(2,1)}, u32[]{:S(2)}) copy-start(bf16[3,512,512]{2,1,0:T(8,128)(2,1)} %bases.1) | copy-start | bytes 4718596
  11.0 6.9 %copy-start.3 = (f32[2,3,512]{2,0,1:T(2,128)S(1)}, f32[2,3,512]{2,0,1:T(2,128)}, u32[]{:S(2)}) copy-start(f32[2,3,512]{2,0,1:T(2,128)} %param.13) | copy-start | bytes 36868
  11.1 23.1 %all-to-all-start = ((bf16[32,120,128]{2,1,0:T(8,128)(2,1)}), bf16[32,120,128]{2,1,0:T(8,128)(2,1)S(1)}, u32[]{:S(2)}, u32[]{:S(2)}) async-start(bf16[32,120,128]{2,1,0:T(8,128)(2,1)} %bitcast.50), calls=%async_computation | async-start | bytes 1966080 | tf_op jit(solution)/shard_map/wide_sum/all_to_all | solution.py:428
  23.0 0.8 %copy-start.1 = (bf16[512,512]{1,0:T(8,128)(2,1)}, bf16[512,512]{1,0:T(8,128)(2,1)S(1)}, u32[]{:S(2)}) copy-start(bf16[512,512]{1,0:T(8,128)(2,1)S(1)} %get-tuple-element.25.mirror) | copy-start | bytes 1572868
  23.8 1.6 %collective-permute-start.1 = (f32[2,512]{1,0:T(2,128)S(1)}, f32[2,512]{1,0:T(2,128)S(1)}, u32[]{:S(2)}, u32[]{:S(2)}) collective-permute-start(f32[2,512]{1,0:T(2,128)S(1)} %get-tuple-element.37), channel_id=1, source_target_pairs={{0,1},{1,0},{2,3},{3,2},{4,5},{5,4},{6,7},{7,6},{8,9},{9,8},{10,11... | collective-permute-start | bytes 12296 | tf_op jit(solution)/shard_map/ppermute | solution.py:502
  35.1 14.4 %all-to-all-start.1 = ((bf16[4,112,128]{2,1,0:T(8,128)(2,1)}), bf16[4,112,128]{2,1,0:T(8,128)(2,1)S(1)}, u32[]{:S(2)}, u32[]{:S(2)}) async-start(bf16[4,112,128]{2,1,0:T(8,128)(2,1)} %pack.1), calls=%async_computation.1 | async-start | bytes 229376 | tf_op jit(solution)/shard_map/deep_sum/all_to_all | solution.py:428
  43.3 22.0 %copy-start.2 = (bf16[512,512]{1,0:T(8,128)(2,1)S(1)}, bf16[512,512]{1,0:T(8,128)(2,1)}, u32[]{:S(2)}) copy-start(bf16[512,512]{1,0:T(8,128)(2,1)} %copy-done.1) | copy-start | bytes 1572868
  50.6 14.7 %all-to-all-start.2 = ((bf16[32,80,128]{2,1,0:T(8,128)(2,1)}), bf16[32,80,128]{2,1,0:T(8,128)(2,1)S(1)}, u32[]{:S(2)}, u32[]{:S(2)}) async-start(bf16[32,80,128]{2,1,0:T(8,128)(2,1)} %rotate.1), calls=%async_computation.2 | async-start | bytes 1310720 | tf_op jit(solution)/shard_map/gather/all_to_all | solution.py:428
  66.4 5.0 %collective-permute-start.2 = (f32[16,512]{1,0:T(8,128)S(1)}, f32[16,512]{1,0:T(8,128)S(1)}, u32[]{:S(2)}, u32[]{:S(2)}) collective-permute-start(f32[16,512]{1,0:T(8,128)S(1)} %get-tuple-element.27), channel_id=1, source_target_pairs={{0,1},{1,0},{2,3},{3,2},{4,5},{5,4},{6,7},{7,6},{8,9},{9,8},{10,11... | collective-permute-start | bytes 98312 | tf_op jit(solution)/shard_map/ppermute | solution.py:523

commit v10 on v9

--- a/solution.py
+++ b/solution.py
@@ -230,7 +230,9 @@
         copy.wait()
 
 
-def lam_kernel(share, core, block, _, keep, x0, xk, xv, bases, keep_lam, send_lam, basis_in_t, mirror, b0, b1, b2, sem0, sem1, sem2):
+def lam_kernel(
+    share, core, block, chip, _, keep, x0, xk, xv, bases, keep_lam, send_lam, basis_in_t, mirror, basis_out, rows_in, b0, b1, b2, sem0, sem1, sem2
+):
     c = core[0]
     bufs = (b0, b1, b2)
     copies = [fetch(x, buf, sem) for x, buf, sem in zip((x0, xk, xv), bufs, (sem0, sem1, sem2))]
@@ -248,6 +250,11 @@
             there = (home + BLK * (block[0] - distance)) & (D - 1)
             one = jnp.where(column == there, 1.0, 0.0).astype(bf16)
             mirror[pl.ds((2 * half + kind) * LANES, LANES), :] = one
+    basis_out[...] = bases[1 + c]
+    row = lax.broadcasted_iota(jnp.int32, (16, D), 0)
+    column = lax.broadcasted_iota(jnp.int32, (16, D), 1)
+    wanted = (row < FR) & (column == FR * chip[0] + ((row + 2 * c) & (FR - 1)))
+    rows_in[...] = dot(jnp.where(wanted, 1.0, 0.0).astype(bf16), bases[0]).astype(bf16)
     lam = []
     for f in range(3):
         total = jnp.zeros((8, D), f32)
@@ -346,9 +353,8 @@
             out[i, pl.ds(j * ROWS, ROWS), :] = tile
 
 
-def rows_kernel(deep, core, block, got, out):
+def direct_rows(k, c, block, got):
     total, grad = deep_total(got)
-    k, c = deep[0], core[0]
     rows = grad[0:FR]
     for other in range(1, DEEP):
         rows = jnp.where(k == other, grad[other * FR : (other + 1) * FR], rows)
@@ -363,8 +369,7 @@
         jnp.concatenate([zero, none, none, none], axis=1),
         jnp.concatenate([none, zero, end0, none], axis=1),
     )
-    factors = pltpu.roll(jnp.concatenate([picked, zero], axis=0), BLK * block[0], 1)
-    out[...] = jnp.concatenate([rows, factors, jnp.zeros_like(rows)], axis=0)
+    return rows, pltpu.roll(jnp.concatenate([picked, zero], axis=0), BLK * block, 1)
 
 
 def mirrored_rows(c, block, tails, mirror):
@@ -381,7 +386,7 @@
     return dot(jnp.concatenate(parts, axis=1).astype(bf16), mirror[...])
 
 
-def solve_kernel(core, block, got, basis_in_t, basis_out, rows_in, mirror, rows, own, their, scaled):
+def solve_kernel(deep, core, block, got, packed, basis_in_t, basis_out, rows_in, mirror, own, their, scaled):
     tails = [got[i, pl.ds(GATHER_LAM, ROWS), :].astype(f32) for i in range(WIDE)]
     lam = tails[0][:8]
     for tail in tails[1:]:
@@ -400,9 +405,10 @@
     prec = lax.dot_general(back, basis_out[...], (((1,), (1,)), ((), ())), preferred_element_type=f32)
     prec = prec.astype(bf16).astype(f32)
     curve = jnp.broadcast_to(curve, (2, D))
-    factors = rows[4:12, :] + mirrored_rows(core[0], block[0], tails, mirror)
-    low = jnp.concatenate([rows[0:2, :], factors[0:2], factors[4:6]], axis=0)
-    high = jnp.concatenate([rows[2:4, :], factors[2:4], factors[6:8]], axis=0)
+    rows, factors = direct_rows(deep[0], core[0], block[0], packed)
+    factors = factors + mirrored_rows(core[0], block[0], tails, mirror)
+    low = jnp.concatenate([rows[0:2], factors[0:2], factors[4:6]], axis=0)
+    high = jnp.concatenate([rows[2:4], factors[2:4], factors[6:8]], axis=0)
     first = core[0] == 0
     pad = jnp.zeros((6, D), f32)
     own[...] = jnp.concatenate([prec[0:2], curve, jnp.where(first, low, high), pad], axis=0)
@@ -430,10 +436,12 @@
 
 def body(activations, grad_key, grad_value, time_start, time_width, bases, old_factors):
     index = lax.axis_index("dp").astype(jnp.int32)
-    core = index % NC
+    core = index & (NC - 1)
     first = core == 0
-    z = (index // NC) % NZ
-    here = ((z // PAIR)[None], core[None], (index // (NC * NZ))[None])
+    chip_here = index >> 1
+    z = chip_here & (NZ - 1)
+    here = ((z >> 1)[None], core[None], (chip_here >> 3)[None])
+    chip_index = chip_here[None]
     tokens_here = activations.shape[0]
     share = (1.0 - decay) / (tokens_here * lax.axis_size("dp"))
 
@@ -482,16 +490,16 @@
     with jax.named_scope("wide_sum"):
         parts = exchange(chip, WIDE_GROUPS)
 
-    lam_shape = shape((2, D), f32)
+    lam_shape, square = shape((2, D), f32), shape((D, D), bf16)
     with jax.named_scope("lam"):
-        keep_lam, send_lam, basis_in_t, mirror = call(
+        keep_lam, send_lam, basis_in_t, mirror, basis_out, rows_in = call(
             functools.partial(lam_kernel, share),
-            (lam_shape, lam_shape, shape((D, D), bf16), shape((2 * PAIR * LANES, D), bf16)),
-            [SMEM, SMEM, HBM, VMEM, HBM, HBM, HBM, VMEM],
+            (lam_shape, lam_shape, square, square, square, shape((16, D), bf16)),
+            [SMEM, SMEM, SMEM, HBM, VMEM, HBM, HBM, HBM, VMEM],
             [buf] * 3 + [sems] * 3,
             flops=work,
             moved=4 * MB,
-        )(*here[1:], in_hbm(chip), keep, frames, keys, vals, bases)
+        )(*here[1:], chip_index, in_hbm(chip), keep, frames, keys, vals, bases)
     old_lam = []
     my_rows = lax.dynamic_slice_in_dim(bases, 2 * index, 2, 1).astype(f32)
     for f in range(3):
@@ -505,20 +513,14 @@
         packed = call(pack_kernel, shape((DEEP, DEEP_ROWS, LANES), bf16), [VMEM] * 3)(parts, keep_lam, sent_lam)
     with jax.named_scope("deep_sum"):
         got = exchange(packed, DEEP_GROUPS)
-    basis_out = lax.dynamic_index_in_dim(bases, 1 + core, 0, keepdims=False)
     lines = shape((16, D), f32)
     with jax.named_scope("rotate"):
         spread = call(rotate_kernel, shape((WIDE, GATHER_ROWS, LANES), bf16), [VMEM] * 2)(got, basis_out)
     with jax.named_scope("gather"):
         gathered = exchange(spread, WIDE_GROUPS)
-    with jax.named_scope("rows"):
-        rows = call(rows_kernel, lines, [SMEM] * 3 + [VMEM])(*here, got)
-    rows_in = lax.dynamic_slice_in_dim(bases[0], (index // NC) * FR, FR, 0)
-    rows_in = jnp.where(first, rows_in, jnp.roll(rows_in, 2, axis=0))
-    rows_in = jnp.pad(rows_in, ((0, 16 - FR), (0, 0)))
     with jax.named_scope("solve"):
-        own, their = call(solve_kernel, (lines, lines), [SMEM] * 2 + [VMEM] * 6, [pltpu.VMEM((D, D), bf16)])(
-            *here[1:], gathered, basis_in_t, basis_out, rows_in, mirror, rows
+        own, their = call(solve_kernel, (lines, lines), [SMEM] * 3 + [VMEM] * 6, [pltpu.VMEM((D, D), bf16)])(
+            *here, gathered, got, basis_in_t, basis_out, rows_in, mirror
         )
     theirs = lax.ppermute(their, "dp", SWAP)
     with jax.named_scope("finish"):

time: 72.6 us -> 71.7 us (0.988)
  blocking collectives: 0 us -> 14.4 us
  starting transfers between devices: 26.2 us -> 18.9 us
  waiting for transfers between devices: 26.5 us -> 21.4 us
  Pallas kernels: 14.4 us -> 13.2 us
  local copies, waits for them, and re-layouts: 2.46 us -> 1.62 us
    all_to_all x0 -> x1, blocking collectives: none -> 14.4 us  [exchange(): lax.all_to_all(value, 'dp', 0, 0, axis_index_groups=groups, tiled=True)]
    all_to_all x3 -> x2, starting transfers between devices: 18 us -> 10.7 us  [exchange(): lax.all_to_all(value, 'dp', 0, 0, axis_index_groups=groups, tiled=True)]
    all_to_all x3 -> x2, waiting for transfers between devices: 24 us -> 19 us  [exchange(): lax.all_to_all(value, 'dp', 0, 0, axis_index_groups=groups, tiled=True)]
    slice x2 -> x0, local copies, waits for them, and re-layouts: 1.64 us -> none  [the longest x1 0.86 us: body(): bases[f].astype(f32)]
    unnamed x8 -> x12, local copies, waits for them, and re-layouts: 0.81 us -> 1.62 us
    pallas_call x3 -> x2, Pallas kernels: 5.35 us -> 4.92 us  [the longest x1 3.79 us: body(): call(functools.partial(lam_kernel, share), (lam_shape, lam_shape, square,...]
  transfers between devices with their start and end apart: 6 -> 5, of which waited for: 6 -> 5; matrix products, arithmetic and copies ran while one was open for 5% -> 1% of each run, Pallas kernels for 8% -> 7%
where the time goes in v10:
time: 71.7 us; the launch traced here: 71.3 us
  waiting for transfers between devices  21.4 us (30%)
  starting transfers between devices  18.9 us (26%)
  blocking collectives  14.4 us (20%)
  Pallas kernels  13.2 us (18%)
  local copies, waits for them, and re-layouts  1.62 us (2%)
  matrix products  0.99 us (1%)
  between operations  0.79 us (1%)
    all_to_all x2, waiting for transfers between devices, exchange(): lax.all_to_all(value, 'dp', 0, 0, axis_index_groups=groups, tiled=True)  19 us
    all_to_all x1, blocking collectives, exchange(): lax.all_to_all(value, 'dp', 0, 0, axis_index_groups=groups, tiled=True)  14.4 us
    all_to_all x2, starting transfers between devices, exchange(): lax.all_to_all(value, 'dp', 0, 0, axis_index_groups=groups, tiled=True)  10.7 us
    ppermute x1, starting transfers between devices, body(): theirs = lax.ppermute(their, 'dp', SWAP)  4.11 us
    pallas_call x1, Pallas kernels, body(): call(functools.partial(lam_kernel, share), (lam_shape, lam_shape, square,...  3.79 us
    pallas_call x1, Pallas kernels, body(): call(theirs_kernel, (partial, shape((NXY, PAIR, ROWS + ROWS // 2, LANES),...  3.78 us
    ppermute x1, starting transfers between devices, body(): received = lax.ppermute(other, 'dp', SWAP)  3.33 us
    unnamed x12, local copies, waits for them, and re-layouts  1.62 us
  transfers between devices with their start and end apart: 5, of which 5 were waited for; matrix products, arithmetic and copies ran while one was open for 1% of the time, Pallas kernels for 7%

profile of v10, /device:TPU:1, one launch (start us, length us, event | category | flops | bytes accessed | tf_op | source)
XLA Modules:
  0.0 71.3 jit_solution(13915731134153894882)
XLA Ops:
  0.6 3.8 %grams_theirs.1 = (bf16[16,2,120,128]{3,2,1,0:T(8,128)(2,1)S(1)}, bf16[16,2,24,128]{3,2,1,0:T(8,128)(2,1)S(1)}, bf16[1024,512]{1,0:T(8,128)(2,1)S(1)}, bf16[1024...) custom-call(s32[1]{0:T(128)} %bitcast.core, s32[2,8]{1,0:T(2,128)} %bitcast.49, s32[2,8]{1,0:T(2,128)} %bitcast.50, ...), custom_call_target="tpu_custom_call" | custom-call | flops 1610612736 | bytes 4194304 | tf_op jit(solution)/shard_map/grams_theirs/pallas_call | solution.py:460
  4.4 3.3 %collective-permute-start = (bf16[16,2,120,128]{3,2,1,0:T(8,128)(2,1)S(1)}, bf16[16,2,120,128]{3,2,1,0:T(8,128)(2,1)S(1)}, u32[]{:S(2)}, u32[]{:S(2)}) collective-permute-start(bf16[16,2,120,128]{3,2,1,0:T(8,128)(2,1)S(1)} %get-tuple-element.23), channel_id=1, source_target_pairs={{0,1},{1,0},{2,3},{3,2},{4,5},{5,4},{6,7},{7,6},{8,9},{9,8},{10,11... | collective-permute-start | bytes 2949128 | tf_op jit(solution)/shard_map/ppermute | solution.py:474
  7.8 1.4 %grams_mine.1.mine = bf16[16,2,104,128]{3,2,1,0:T(8,128)(2,1)S(1)} custom-call(bf16[1024,128]{1,0:T(8,128)(2,1)S(1)} %get-tuple-element.19.keep, bf16[1024,512]{1,0:T(8,128)(2,1)S(1)} %get-tuple-element.20.x0, bf16[1024,512]{1,0:T(8,128)(2,1)S(1)} %get-tuple-element.21.x1), custom_call_target="tpu_custom_call" | custom-call | flops 1610612736 | bytes 4194304 | tf_op jit(solution)/shard_map/grams_mine/pallas_call | solution.py:476
  9.2 0.8 %collective-permute-done.received = bf16[16,2,120,128]{3,2,1,0:T(8,128)(2,1)S(1)} collective-permute-done((bf16[16,2,120,128]{3,2,1,0:T(8,128)(2,1)S(1)}, bf16[16,2,120,128]{3,2,1,0:T(8,128)(2,1)S(1)}, u32[]{:S(2)}, u32[]{:S(2)}) %collective-permute-start) | collective-permute-done | bytes 983072 | tf_op jit(solution)/shard_map/ppermute | solution.py:474
  9.9 1.0 %chip_sum.1 = bf16[16,2,120,128]{3,2,1,0:T(8,128)(2,1)} custom-call(bf16[16,2,104,128]{3,2,1,0:T(8,128)(2,1)S(1)} %grams_mine.1.mine, bf16[16,2,24,128]{3,2,1,0:T(8,128)(2,1)S(1)} %get-tuple-element.22.spare, bf16[16,2,120,128]{3,2,1,0:T(8,128)(2,1)S(1)} %collective-permute-done.received), custom_call_target="tpu_custom_call" | custom-call | tf_op jit(solution)/shard_map/chip_sum/pallas_call | solution.py:484
  11.0 0.0 copy-start
  11.0 0.0 copy-start.5
  11.0 6.8 %all-to-all-start = ((bf16[32,120,128]{2,1,0:T(8,128)(2,1)}), bf16[32,120,128]{2,1,0:T(8,128)(2,1)S(1)}, u32[]{:S(2)}, u32[]{:S(2)}) async-start(bf16[32,120,128]{2,1,0:T(8,128)(2,1)} %bitcast.43), calls=%async_computation | async-start | bytes 1966080 | tf_op jit(solution)/shard_map/wide_sum/all_to_all | solution.py:434
  17.8 0.0 copy-done
  17.9 0.0 copy-done.5
  17.9 0.3 fusion.1
  18.2 0.3 fusion.2
  18.6 0.3 fusion
  18.9 3.8 %lam.1 = (f32[2,512]{1,0:T(2,128)S(1)}, f32[2,512]{1,0:T(2,128)S(1)}, bf16[512,512]{1,0:T(8,128)(2,1)S(1)}, bf16[512,512]{1,0:T(8,128)(2,1)S(1)}, bf16[512,512]{...) custom-call(s32[1]{0:T(128)} %bitcast.core, s32[1]{0:T(128)} %bitcast.2.block, s32[1]{0:T(128)} %bitcast.6.chip, ...), custom_call_target="tpu_custom_call" | custom-call | flops 1610612736 | bytes 4194304 | tf_op jit(solution)/shard_map/lam/pallas_call | solution.py:495
  22.7 0.0 copy-start.1
  22.7 0.8 %copy-done.1 = bf16[512,512]{1,0:T(8,128)(2,1)} copy-done((bf16[512,512]{1,0:T(8,128)(2,1)}, bf16[512,512]{1,0:T(8,128)(2,1)S(1)}, u32[]{:S(2)}) %copy-start.1) | copy-done | bytes 524312
  23.5 0.8 %copy-done.3 = bf16[512,512]{1,0:T(8,128)(2,1)} copy-done((bf16[512,512]{1,0:T(8,128)(2,1)}, bf16[512,512]{1,0:T(8,128)(2,1)S(1)}, u32[]{:S(2)}) %copy-start.3) | copy-done | bytes 524312
  24.3 0.7 %collective-permute-start.1 = (f32[2,512]{1,0:T(2,128)S(1)}, f32[2,512]{1,0:T(2,128)S(1)}, u32[]{:S(2)}, u32[]{:S(2)}) collective-permute-start(f32[2,512]{1,0:T(2,128)S(1)} %get-tuple-element.37), channel_id=1, source_target_pairs={{0,1},{1,0},{2,3},{3,2},{4,5},{5,4},{6,7},{7,6},{8,9},{9,8},{10,11... | collective-permute-start | bytes 12296 | tf_op jit(solution)/shard_map/ppermute | solution.py:510
  25.1 0.8 %collective-permute-done.1.send_lam = f32[2,512]{1,0:T(2,128)S(1)} collective-permute-done((f32[2,512]{1,0:T(2,128)S(1)}, f32[2,512]{1,0:T(2,128)S(1)}, u32[]{:S(2)}, u32[]{:S(2)}) %collective-permute-start.1) | collective-permute-done | bytes 4128 | tf_op jit(solution)/shard_map/ppermute | solution.py:510
  25.9 8.2 %all-to-all-done.parts = bf16[32,120,128]{2,1,0:T(8,128)(2,1)S(1)} async-done(((bf16[32,120,128]{2,1,0:T(8,128)(2,1)}), bf16[32,120,128]{2,1,0:T(8,128)(2,1)S(1)}, u32[]{:S(2)}, u32[]{:S(2)}) %all-to-all-start) | async-done | bytes 983072 | tf_op jit(solution)/shard_map/wide_sum/all_to_all | solution.py:434
  34.1 0.3 pack.1
  34.5 0.0 copy-start.2
  34.5 0.0 copy-start.4
  34.5 14.4 %all_to_all.15.got.packed = bf16[4,112,128]{2,1,0:T(8,128)(2,1)S(1)} all-to-all(bf16[4,112,128]{2,1,0:T(8,128)(2,1)S(1)} %pack.1), channel_id=1, replica_groups={{0,4,8,12},{1,5,9,13},{2,6,10,14},{3,7,11,15},{16,20,24,28},{17,21,25,2..., dimensions={0} | all-to-all | bytes 229376 | tf_op jit(solution)/shard_map/deep_sum/all_to_all | solution.py:434
  48.8 1.1 %rotate.1 = bf16[32,80,128]{2,1,0:T(8,128)(2,1)} custom-call(bf16[4,112,128]{2,1,0:T(8,128)(2,1)S(1)} %all_to_all.15.got.packed, bf16[512,512]{1,0:T(8,128)(2,1)S(1)} %get-tuple-element.26.basis.basis_out), custom_call_target="tpu_custom_call" | custom-call | tf_op jit(solution)/shard_map/rotate/pallas_call | solution.py:518
  49.9 3.9 %all-to-all-start.2 = ((bf16[32,80,128]{2,1,0:T(8,128)(2,1)}), bf16[32,80,128]{2,1,0:T(8,128)(2,1)S(1)}, u32[]{:S(2)}, u32[]{:S(2)}) async-start(bf16[32,80,128]{2,1,0:T(8,128)(2,1)} %rotate.1), calls=%async_computation.2 | async-start | bytes 1310720 | tf_op jit(solution)/shard_map/gather/all_to_all | solution.py:434
  53.8 10.7 %all-to-all-done.2.got = bf16[32,80,128]{2,1,0:T(8,128)(2,1)S(1)} async-done(((bf16[32,80,128]{2,1,0:T(8,128)(2,1)}), bf16[32,80,128]{2,1,0:T(8,128)(2,1)S(1)}, u32[]{:S(2)}, u32[]{:S(2)}) %all-to-all-start.2) | async-done | bytes 655392 | tf_op jit(solution)/shard_map/gather/all_to_all | solution.py:434
  64.6 0.0 copy-done.2
  64.6 1.1 %solve.1 = (f32[16,512]{1,0:T(8,128)S(1)}, f32[16,512]{1,0:T(8,128)S(1)}) custom-call(s32[1]{0:T(128)} %bitcast.1.deep, s32[1]{0:T(128)} %bitcast.core, s32[1]{0:T(128)} %bitcast.2.block, bf16[32,80,128]{2,1,0:T(8,128)(2,1)S(1)} %all-to-all-done.2.got, bf16[4,112,128]{2,1,0:T(8,128)(2,1)S(1)} %all_to_all.15.got.packed, bf16[512,512]{1,0:T(8,128)(2,1)S(1)} %copy-done.2, ...), custom_call_target="tpu_custom_call" | custom-call | tf_op jit(solution)/shard_map/solve/pallas_call | solution.py:522
  65.7 4.1 %collective-permute-start.2 = (f32[16,512]{1,0:T(8,128)S(1)}, f32[16,512]{1,0:T(8,128)S(1)}, u32[]{:S(2)}, u32[]{:S(2)}) collective-permute-start(f32[16,512]{1,0:T(8,128)S(1)} %get-tuple-element.31), channel_id=1, source_target_pairs={{0,1},{1,0},{2,3},{3,2},{4,5},{5,4},{6,7},{7,6},{8,9},{9,8},{10,11... | collective-permute-start | bytes 98312 | tf_op jit(solution)/shard_map/ppermute | solution.py:525
  69.8 0.9 %collective-permute-done.2.got = f32[16,512]{1,0:T(8,128)S(1)} collective-permute-done((f32[16,512]{1,0:T(8,128)S(1)}, f32[16,512]{1,0:T(8,128)S(1)}, u32[]{:S(2)}, u32[]{:S(2)}) %collective-permute-start.2) | collective-permute-done | bytes 32800 | tf_op jit(solution)/shard_map/ppermute | solution.py:525
  70.7 0.6 finish.1
  (6 shorter events, 0.0 us)
Async XLA Ops:
  4.4 5.5 %collective-permute-start = (bf16[16,2,120,128]{3,2,1,0:T(8,128)(2,1)S(1)}, bf16[16,2,120,128]{3,2,1,0:T(8,128)(2,1)S(1)}, u32[]{:S(2)}, u32[]{:S(2)}) collective-permute-start(bf16[16,2,120,128]{3,2,1,0:T(8,128)(2,1)S(1)} %get-tuple-element.23), channel_id=1, source_target_pairs={{0,1},{1,0},{2,3},{3,2},{4,5},{5,4},{6,7},{7,6},{8,9},{9,8},{10,11... | collective-permute-start | bytes 2949128 | tf_op jit(solution)/shard_map/ppermute | solution.py:474
  11.0 6.8 %copy-start = (bf16[3,512,512]{2,1,0:T(8,128)(2,1)S(1)}, bf16[3,512,512]{2,1,0:T(8,128)(2,1)}, u32[]{:S(2)}) copy-start(bf16[3,512,512]{2,1,0:T(8,128)(2,1)} %bases.1) | copy-start | bytes 4718596
  11.0 6.9 %copy-start.5 = (f32[2,3,512]{2,0,1:T(2,128)S(1)}, f32[2,3,512]{2,0,1:T(2,128)}, u32[]{:S(2)}) copy-start(f32[2,3,512]{2,0,1:T(2,128)} %param.13) | copy-start | bytes 36868
  11.0 23.1 %all-to-all-start = ((bf16[32,120,128]{2,1,0:T(8,128)(2,1)}), bf16[32,120,128]{2,1,0:T(8,128)(2,1)S(1)}, u32[]{:S(2)}, u32[]{:S(2)}) async-start(bf16[32,120,128]{2,1,0:T(8,128)(2,1)} %bitcast.43), calls=%async_computation | async-start | bytes 1966080 | tf_op jit(solution)/shard_map/wide_sum/all_to_all | solution.py:434
  22.7 0.8 %copy-start.1 = (bf16[512,512]{1,0:T(8,128)(2,1)}, bf16[512,512]{1,0:T(8,128)(2,1)S(1)}, u32[]{:S(2)}) copy-start(bf16[512,512]{1,0:T(8,128)(2,1)S(1)} %get-tuple-element.27.basis_in_t) | copy-start | bytes 1572868
  23.5 0.8 %copy-start.3 = (bf16[512,512]{1,0:T(8,128)(2,1)}, bf16[512,512]{1,0:T(8,128)(2,1)S(1)}, u32[]{:S(2)}) copy-start(bf16[512,512]{1,0:T(8,128)(2,1)S(1)} %get-tuple-element.29.mirror) | copy-start | bytes 1572868
  24.3 1.6 %collective-permute-start.1 = (f32[2,512]{1,0:T(2,128)S(1)}, f32[2,512]{1,0:T(2,128)S(1)}, u32[]{:S(2)}, u32[]{:S(2)}) collective-permute-start(f32[2,512]{1,0:T(2,128)S(1)} %get-tuple-element.37), channel_id=1, source_target_pairs={{0,1},{1,0},{2,3},{3,2},{4,5},{5,4},{6,7},{7,6},{8,9},{9,8},{10,11... | collective-permute-start | bytes 12296 | tf_op jit(solution)/shard_map/ppermute | solution.py:510
  34.5 30.1 %copy-start.2 = (bf16[512,512]{1,0:T(8,128)(2,1)S(1)}, bf16[512,512]{1,0:T(8,128)(2,1)}, u32[]{:S(2)}) copy-start(bf16[512,512]{1,0:T(8,128)(2,1)} %copy-done.1) | copy-start | bytes 1572868
  34.5 30.1 %copy-start.4 = (bf16[512,512]{1,0:T(8,128)(2,1)S(1)}, bf16[512,512]{1,0:T(8,128)(2,1)}, u32[]{:S(2)}) copy-start(bf16[512,512]{1,0:T(8,128)(2,1)} %copy-done.3) | copy-start | bytes 1572868
  49.9 14.7 %all-to-all-start.2 = ((bf16[32,80,128]{2,1,0:T(8,128)(2,1)}), bf16[32,80,128]{2,1,0:T(8,128)(2,1)S(1)}, u32[]{:S(2)}, u32[]{:S(2)}) async-start(bf16[32,80,128]{2,1,0:T(8,128)(2,1)} %rotate.1), calls=%async_computation.2 | async-start | bytes 1310720 | tf_op jit(solution)/shard_map/gather/all_to_all | solution.py:434
  65.7 5.0 %collective-permute-start.2 = (f32[16,512]{1,0:T(8,128)S(1)}, f32[16,512]{1,0:T(8,128)S(1)}, u32[]{:S(2)}, u32[]{:S(2)}) collective-permute-start(f32[16,512]{1,0:T(8,128)S(1)} %get-tuple-element.31), channel_id=1, source_target_pairs={{0,1},{1,0},{2,3},{3,2},{4,5},{5,4},{6,7},{7,6},{8,9},{9,8},{10,11... | collective-permute-start | bytes 98312 | tf_op jit(solution)/shard_map/ppermute | solution.py:525

commit v11 on v10

--- a/solution.py
+++ b/solution.py
@@ -231,7 +231,7 @@
 
 
 def lam_kernel(
-    share, core, block, chip, _, keep, x0, xk, xv, bases, keep_lam, send_lam, basis_in_t, mirror, basis_out, rows_in, b0, b1, b2, sem0, sem1, sem2
+    share, core, chip, _, keep, x0, xk, xv, bases, keep_lam, send_lam, basis_in_t, mirror, basis_out, rows_in, b0, b1, b2, sem0, sem1, sem2
 ):
     c = core[0]
     bufs = (b0, b1, b2)
@@ -247,7 +247,7 @@
         home = 8 * ((lane >> 2) & 3) + FR * half + (lane & 3) + 2 * D
         for kind in range(2):
             distance = (lane >> 4) + (4 * c if kind else 0)
-            there = (home + BLK * (block[0] - distance)) & (D - 1)
+            there = (home + BLK * ((chip[0] >> 3) - distance)) & (D - 1)
             one = jnp.where(column == there, 1.0, 0.0).astype(bf16)
             mirror[pl.ds((2 * half + kind) * LANES, LANES), :] = one
     basis_out[...] = bases[1 + c]
@@ -386,7 +386,7 @@
     return dot(jnp.concatenate(parts, axis=1).astype(bf16), mirror[...])
 
 
-def solve_kernel(deep, core, block, got, packed, basis_in_t, basis_out, rows_in, mirror, own, their, scaled):
+def solve_kernel(core, chip, got, packed, basis_in_t, basis_out, rows_in, mirror, own, their, scaled):
     tails = [got[i, pl.ds(GATHER_LAM, ROWS), :].astype(f32) for i in range(WIDE)]
     lam = tails[0][:8]
     for tail in tails[1:]:
@@ -405,8 +405,8 @@
     prec = lax.dot_general(back, basis_out[...], (((1,), (1,)), ((), ())), preferred_element_type=f32)
     prec = prec.astype(bf16).astype(f32)
     curve = jnp.broadcast_to(curve, (2, D))
-    rows, factors = direct_rows(deep[0], core[0], block[0], packed)
-    factors = factors + mirrored_rows(core[0], block[0], tails, mirror)
+    rows, factors = direct_rows((chip[0] & (NZ - 1)) >> 1, core[0], chip[0] >> 3, packed)
+    factors = factors + mirrored_rows(core[0], chip[0] >> 3, tails, mirror)
     low = jnp.concatenate([rows[0:2], factors[0:2], factors[4:6]], axis=0)
     high = jnp.concatenate([rows[2:4], factors[2:4], factors[6:8]], axis=0)
     first = core[0] == 0
@@ -438,10 +438,7 @@
     index = lax.axis_index("dp").astype(jnp.int32)
     core = index & (NC - 1)
     first = core == 0
-    chip_here = index >> 1
-    z = chip_here & (NZ - 1)
-    here = ((z >> 1)[None], core[None], (chip_here >> 3)[None])
-    chip_index = chip_here[None]
+    here = (core[None], (index >> 1)[None])
     tokens_here = activations.shape[0]
     share = (1.0 - decay) / (tokens_here * lax.axis_size("dp"))
 
@@ -495,11 +492,11 @@
         keep_lam, send_lam, basis_in_t, mirror, basis_out, rows_in = call(
             functools.partial(lam_kernel, share),
             (lam_shape, lam_shape, square, square, square, shape((16, D), bf16)),
-            [SMEM, SMEM, SMEM, HBM, VMEM, HBM, HBM, HBM, VMEM],
+            [SMEM, SMEM, HBM, VMEM, HBM, HBM, HBM, VMEM],
             [buf] * 3 + [sems] * 3,
             flops=work,
             moved=4 * MB,
-        )(*here[1:], chip_index, in_hbm(chip), keep, frames, keys, vals, bases)
+        )(*here, in_hbm(chip), keep, frames, keys, vals, bases)
     old_lam = []
     my_rows = lax.dynamic_slice_in_dim(bases, 2 * index, 2, 1).astype(f32)
     for f in range(3):
@@ -519,7 +516,7 @@
     with jax.named_scope("gather"):
         gathered = exchange(spread, WIDE_GROUPS)
     with jax.named_scope("solve"):
-        own, their = call(solve_kernel, (lines, lines), [SMEM] * 3 + [VMEM] * 6, [pltpu.VMEM((D, D), bf16)])(
+        own, their = call(solve_kernel, (lines, lines), [SMEM] * 2 + [VMEM] * 6, [pltpu.VMEM((D, D), bf16)])(
             *here, gathered, got, basis_in_t, basis_out, rows_in, mirror
         )
     theirs = lax.ppermute(their, "dp", SWAP)

time: 71.7 us -> 70.4 us (0.982)
  blocking collectives: 14.4 us -> 28.7 us
  waiting for transfers between devices: 21.4 us -> 10.7 us
  starting transfers between devices: 18.9 us -> 14.9 us
  Pallas kernels: 13.2 us -> 12.3 us
    all_to_all x1 -> x2, blocking collectives: 14.4 us -> 28.7 us  [exchange(): lax.all_to_all(value, 'dp', 0, 0, axis_index_groups=groups, tiled=True)]
    all_to_all x2 -> x1, waiting for transfers between devices: 19 us -> 8.26 us  [exchange(): lax.all_to_all(value, 'dp', 0, 0, axis_index_groups=groups, tiled=True)]
    all_to_all x2 -> x1, starting transfers between devices: 10.7 us -> 6.8 us  [exchange(): lax.all_to_all(value, 'dp', 0, 0, axis_index_groups=groups, tiled=True)]
    pallas_call x1, Pallas kernels: 1.06 us -> 0.21 us  [body(): call(rotate_kernel, shape((WIDE, GATHER_ROWS, LANES), bf16), [VMEM] * 2)]
  transfers between devices with their start and end apart: 5 -> 4, of which waited for: 5 -> 4; matrix products, arithmetic and copies ran while one was open for 1% -> 1% of each run, Pallas kernels for 7% -> 7%
where the time goes in v11:
time: 70.4 us; the launch traced here: 70 us
  blocking collectives  28.7 us (41%)
  starting transfers between devices  14.9 us (21%)
  Pallas kernels  12.3 us (17%)
  waiting for transfers between devices  10.7 us (15%)
  local copies, waits for them, and re-layouts  1.61 us (2%)
  matrix products  0.99 us (1%)
  between operations  0.79 us (1%)
    all_to_all x2, blocking collectives, exchange(): lax.all_to_all(value, 'dp', 0, 0, axis_index_groups=groups, tiled=True)  28.7 us
    all_to_all x1, waiting for transfers between devices, exchange(): lax.all_to_all(value, 'dp', 0, 0, axis_index_groups=groups, tiled=True)  8.26 us
    all_to_all x1, starting transfers between devices, exchange(): lax.all_to_all(value, 'dp', 0, 0, axis_index_groups=groups, tiled=True)  6.8 us
    ppermute x1, starting transfers between devices, body(): theirs = lax.ppermute(their, 'dp', SWAP)  4.04 us
    pallas_call x1, Pallas kernels, body(): call(theirs_kernel, (partial, shape((NXY, PAIR, ROWS + ROWS // 2, LANES),...  3.78 us
    pallas_call x1, Pallas kernels, body(): call(functools.partial(lam_kernel, share), (lam_shape, lam_shape, square,...  3.75 us
    ppermute x1, starting transfers between devices, body(): received = lax.ppermute(other, 'dp', SWAP)  3.33 us
    unnamed x12, local copies, waits for them, and re-layouts  1.61 us
  transfers between devices with their start and end apart: 4, of which 4 were waited for; matrix products, arithmetic and copies ran while one was open for 1% of the time, Pallas kernels for 7%

profile of v11, /device:TPU:1, one launch (start us, length us, event | category | flops | bytes accessed | tf_op | source)
XLA Modules:
  0.0 70.0 jit_solution(14612295253359910905)
XLA Ops:
  0.6 3.8 %grams_theirs.1 = (bf16[16,2,120,128]{3,2,1,0:T(8,128)(2,1)S(1)}, bf16[16,2,24,128]{3,2,1,0:T(8,128)(2,1)S(1)}, bf16[1024,512]{1,0:T(8,128)(2,1)S(1)}, bf16[1024...) custom-call(s32[1]{0:T(128)} %bitcast.core, s32[2,8]{1,0:T(2,128)} %bitcast.47, s32[2,8]{1,0:T(2,128)} %bitcast.48, ...), custom_call_target="tpu_custom_call" | custom-call | flops 1610612736 | bytes 4194304 | tf_op jit(solution)/shard_map/grams_theirs/pallas_call | solution.py:457
  4.4 3.3 %collective-permute-start = (bf16[16,2,120,128]{3,2,1,0:T(8,128)(2,1)S(1)}, bf16[16,2,120,128]{3,2,1,0:T(8,128)(2,1)S(1)}, u32[]{:S(2)}, u32[]{:S(2)}) collective-permute-start(bf16[16,2,120,128]{3,2,1,0:T(8,128)(2,1)S(1)} %get-tuple-element.23), channel_id=1, source_target_pairs={{0,1},{1,0},{2,3},{3,2},{4,5},{5,4},{6,7},{7,6},{8,9},{9,8},{10,11... | collective-permute-start | bytes 2949128 | tf_op jit(solution)/shard_map/ppermute | solution.py:471
  7.8 1.4 %grams_mine.1.mine = bf16[16,2,104,128]{3,2,1,0:T(8,128)(2,1)S(1)} custom-call(bf16[1024,128]{1,0:T(8,128)(2,1)S(1)} %get-tuple-element.19.keep, bf16[1024,512]{1,0:T(8,128)(2,1)S(1)} %get-tuple-element.20.x0, bf16[1024,512]{1,0:T(8,128)(2,1)S(1)} %get-tuple-element.21.x1), custom_call_target="tpu_custom_call" | custom-call | flops 1610612736 | bytes 4194304 | tf_op jit(solution)/shard_map/grams_mine/pallas_call | solution.py:473
  9.2 0.8 %collective-permute-done.received = bf16[16,2,120,128]{3,2,1,0:T(8,128)(2,1)S(1)} collective-permute-done((bf16[16,2,120,128]{3,2,1,0:T(8,128)(2,1)S(1)}, bf16[16,2,120,128]{3,2,1,0:T(8,128)(2,1)S(1)}, u32[]{:S(2)}, u32[]{:S(2)}) %collective-permute-start) | collective-permute-done | bytes 983072 | tf_op jit(solution)/shard_map/ppermute | solution.py:471
  9.9 1.0 %chip_sum.1 = bf16[16,2,120,128]{3,2,1,0:T(8,128)(2,1)} custom-call(bf16[16,2,104,128]{3,2,1,0:T(8,128)(2,1)S(1)} %grams_mine.1.mine, bf16[16,2,24,128]{3,2,1,0:T(8,128)(2,1)S(1)} %get-tuple-element.22.spare, bf16[16,2,120,128]{3,2,1,0:T(8,128)(2,1)S(1)} %collective-permute-done.received), custom_call_target="tpu_custom_call" | custom-call | tf_op jit(solution)/shard_map/chip_sum/pallas_call | solution.py:481
  11.0 0.0 copy-start
  11.0 0.0 copy-start.5
  11.0 6.8 %all-to-all-start = ((bf16[32,120,128]{2,1,0:T(8,128)(2,1)}), bf16[32,120,128]{2,1,0:T(8,128)(2,1)S(1)}, u32[]{:S(2)}, u32[]{:S(2)}) async-start(bf16[32,120,128]{2,1,0:T(8,128)(2,1)} %bitcast.41), calls=%async_computation | async-start | bytes 1966080 | tf_op jit(solution)/shard_map/wide_sum/all_to_all | solution.py:434
  17.8 0.0 copy-done
  17.9 0.0 copy-done.5
  17.9 0.3 fusion.1
  18.2 0.3 fusion.2
  18.5 0.3 fusion
  18.9 3.8 %lam.1 = (f32[2,512]{1,0:T(2,128)S(1)}, f32[2,512]{1,0:T(2,128)S(1)}, bf16[512,512]{1,0:T(8,128)(2,1)S(1)}, bf16[512,512]{1,0:T(8,128)(2,1)S(1)}, bf16[512,512]{...) custom-call(s32[1]{0:T(128)} %bitcast.core, s32[1]{0:T(128)} %bitcast.1.chip, bf16[32,120,128]{2,1,0:T(8,128)(2,1)} %bitcast.42, ...), custom_call_target="tpu_custom_call" | custom-call | flops 1610612736 | bytes 4194304 | tf_op jit(solution)/shard_map/lam/pallas_call | solution.py:492
  22.7 0.0 copy-start.1
  22.7 0.8 %copy-done.1 = bf16[512,512]{1,0:T(8,128)(2,1)} copy-done((bf16[512,512]{1,0:T(8,128)(2,1)}, bf16[512,512]{1,0:T(8,128)(2,1)S(1)}, u32[]{:S(2)}) %copy-start.1) | copy-done | bytes 524312
  23.5 0.8 %copy-done.3 = bf16[512,512]{1,0:T(8,128)(2,1)} copy-done((bf16[512,512]{1,0:T(8,128)(2,1)}, bf16[512,512]{1,0:T(8,128)(2,1)S(1)}, u32[]{:S(2)}) %copy-start.3) | copy-done | bytes 524312
  24.3 0.7 %collective-permute-start.1 = (f32[2,512]{1,0:T(2,128)S(1)}, f32[2,512]{1,0:T(2,128)S(1)}, u32[]{:S(2)}, u32[]{:S(2)}) collective-permute-start(f32[2,512]{1,0:T(2,128)S(1)} %get-tuple-element.37), channel_id=1, source_target_pairs={{0,1},{1,0},{2,3},{3,2},{4,5},{5,4},{6,7},{7,6},{8,9},{9,8},{10,11... | collective-permute-start | bytes 12296 | tf_op jit(solution)/shard_map/ppermute | solution.py:507
  25.0 0.8 %collective-permute-done.1.send_lam = f32[2,512]{1,0:T(2,128)S(1)} collective-permute-done((f32[2,512]{1,0:T(2,128)S(1)}, f32[2,512]{1,0:T(2,128)S(1)}, u32[]{:S(2)}, u32[]{:S(2)}) %collective-permute-start.1) | collective-permute-done | bytes 4128 | tf_op jit(solution)/shard_map/ppermute | solution.py:507
  25.8 8.3 %all-to-all-done.parts = bf16[32,120,128]{2,1,0:T(8,128)(2,1)S(1)} async-done(((bf16[32,120,128]{2,1,0:T(8,128)(2,1)}), bf16[32,120,128]{2,1,0:T(8,128)(2,1)S(1)}, u32[]{:S(2)}, u32[]{:S(2)}) %all-to-all-start) | async-done | bytes 983072 | tf_op jit(solution)/shard_map/wide_sum/all_to_all | solution.py:434
  34.1 0.3 pack.1
  34.4 0.0 copy-start.2
  34.5 0.0 copy-start.4
  34.5 14.4 %all_to_all.15.got.packed = bf16[4,112,128]{2,1,0:T(8,128)(2,1)S(1)} all-to-all(bf16[4,112,128]{2,1,0:T(8,128)(2,1)S(1)} %pack.1), channel_id=1, replica_groups={{0,4,8,12},{1,5,9,13},{2,6,10,14},{3,7,11,15},{16,20,24,28},{17,21,25,2..., dimensions={0} | all-to-all | bytes 229376 | tf_op jit(solution)/shard_map/deep_sum/all_to_all | solution.py:434
  48.8 0.2 rotate.1
  49.0 14.3 %all_to_all.16.got = bf16[32,80,128]{2,1,0:T(8,128)(2,1)S(1)} all-to-all(bf16[32,80,128]{2,1,0:T(8,128)(2,1)S(1)} %rotate.1), channel_id=1, replica_groups={{0,2,16,18,32,34,48,50,64,66,80,82,96,98,112,114,128,130,144,146,160,16..., dimensions={0} | all-to-all | bytes 1310720 | tf_op jit(solution)/shard_map/gather/all_to_all | solution.py:434
  63.4 0.0 copy-done.2
  63.4 0.0 copy-done.4
  63.4 1.1 %solve.1 = (f32[16,512]{1,0:T(8,128)S(1)}, f32[16,512]{1,0:T(8,128)S(1)}) custom-call(s32[1]{0:T(128)} %bitcast.core, s32[1]{0:T(128)} %bitcast.1.chip, bf16[32,80,128]{2,1,0:T(8,128)(2,1)S(1)} %all_to_all.16.got, bf16[4,112,128]{2,1,0:T(8,128)(2,1)S(1)} %all_to_all.15.got.packed, bf16[512,512]{1,0:T(8,128)(2,1)S(1)} %copy-done.2, ...), custom_call_target="tpu_custom_call" | custom-call | tf_op jit(solution)/shard_map/solve/pallas_call | solution.py:519
  64.5 4.0 %collective-permute-start.2 = (f32[16,512]{1,0:T(8,128)S(1)}, f32[16,512]{1,0:T(8,128)S(1)}, u32[]{:S(2)}, u32[]{:S(2)}) collective-permute-start(f32[16,512]{1,0:T(8,128)S(1)} %get-tuple-element.31), channel_id=1, source_target_pairs={{0,1},{1,0},{2,3},{3,2},{4,5},{5,4},{6,7},{7,6},{8,9},{9,8},{10,11... | collective-permute-start | bytes 98312 | tf_op jit(solution)/shard_map/ppermute | solution.py:522
  68.6 0.9 %collective-permute-done.2.got = f32[16,512]{1,0:T(8,128)S(1)} collective-permute-done((f32[16,512]{1,0:T(8,128)S(1)}, f32[16,512]{1,0:T(8,128)S(1)}, u32[]{:S(2)}, u32[]{:S(2)}) %collective-permute-start.2) | collective-permute-done | bytes 32800 | tf_op jit(solution)/shard_map/ppermute | solution.py:522
  69.4 0.6 finish.1
  (5 shorter events, 0.0 us)
Async XLA Ops:
  4.4 5.5 %collective-permute-start = (bf16[16,2,120,128]{3,2,1,0:T(8,128)(2,1)S(1)}, bf16[16,2,120,128]{3,2,1,0:T(8,128)(2,1)S(1)}, u32[]{:S(2)}, u32[]{:S(2)}) collective-permute-start(bf16[16,2,120,128]{3,2,1,0:T(8,128)(2,1)S(1)} %get-tuple-element.23), channel_id=1, source_target_pairs={{0,1},{1,0},{2,3},{3,2},{4,5},{5,4},{6,7},{7,6},{8,9},{9,8},{10,11... | collective-permute-start | bytes 2949128 | tf_op jit(solution)/shard_map/ppermute | solution.py:471
  11.0 6.8 %copy-start = (bf16[3,512,512]{2,1,0:T(8,128)(2,1)S(1)}, bf16[3,512,512]{2,1,0:T(8,128)(2,1)}, u32[]{:S(2)}) copy-start(bf16[3,512,512]{2,1,0:T(8,128)(2,1)} %bases.1) | copy-start | bytes 4718596
  11.0 6.9 %copy-start.5 = (f32[2,3,512]{2,0,1:T(2,128)S(1)}, f32[2,3,512]{2,0,1:T(2,128)}, u32[]{:S(2)}) copy-start(f32[2,3,512]{2,0,1:T(2,128)} %param.13) | copy-start | bytes 36868
  11.0 23.1 %all-to-all-start = ((bf16[32,120,128]{2,1,0:T(8,128)(2,1)}), bf16[32,120,128]{2,1,0:T(8,128)(2,1)S(1)}, u32[]{:S(2)}, u32[]{:S(2)}) async-start(bf16[32,120,128]{2,1,0:T(8,128)(2,1)} %bitcast.41), calls=%async_computation | async-start | bytes 1966080 | tf_op jit(solution)/shard_map/wide_sum/all_to_all | solution.py:434
  22.7 0.8 %copy-start.1 = (bf16[512,512]{1,0:T(8,128)(2,1)}, bf16[512,512]{1,0:T(8,128)(2,1)S(1)}, u32[]{:S(2)}) copy-start(bf16[512,512]{1,0:T(8,128)(2,1)S(1)} %get-tuple-element.27.basis_in_t) | copy-start | bytes 1572868
  23.5 0.8 %copy-start.3 = (bf16[512,512]{1,0:T(8,128)(2,1)}, bf16[512,512]{1,0:T(8,128)(2,1)S(1)}, u32[]{:S(2)}) copy-start(bf16[512,512]{1,0:T(8,128)(2,1)S(1)} %get-tuple-element.29.mirror) | copy-start | bytes 1572868
  24.3 1.6 %collective-permute-start.1 = (f32[2,512]{1,0:T(2,128)S(1)}, f32[2,512]{1,0:T(2,128)S(1)}, u32[]{:S(2)}, u32[]{:S(2)}) collective-permute-start(f32[2,512]{1,0:T(2,128)S(1)} %get-tuple-element.37), channel_id=1, source_target_pairs={{0,1},{1,0},{2,3},{3,2},{4,5},{5,4},{6,7},{7,6},{8,9},{9,8},{10,11... | collective-permute-start | bytes 12296 | tf_op jit(solution)/shard_map/ppermute | solution.py:507
  34.4 28.9 %copy-start.2 = (bf16[512,512]{1,0:T(8,128)(2,1)S(1)}, bf16[512,512]{1,0:T(8,128)(2,1)}, u32[]{:S(2)}) copy-start(bf16[512,512]{1,0:T(8,128)(2,1)} %copy-done.1) | copy-start | bytes 1572868
  34.5 28.9 %copy-start.4 = (bf16[512,512]{1,0:T(8,128)(2,1)S(1)}, bf16[512,512]{1,0:T(8,128)(2,1)}, u32[]{:S(2)}) copy-start(bf16[512,512]{1,0:T(8,128)(2,1)} %copy-done.3) | copy-start | bytes 1572868
  64.5 4.9 %collective-permute-start.2 = (f32[16,512]{1,0:T(8,128)S(1)}, f32[16,512]{1,0:T(8,128)S(1)}, u32[]{:S(2)}, u32[]{:S(2)}) collective-permute-start(f32[16,512]{1,0:T(8,128)S(1)} %get-tuple-element.31), channel_id=1, source_target_pairs={{0,1},{1,0},{2,3},{3,2},{4,5},{5,4},{6,7},{7,6},{8,9},{9,8},{10,11... | collective-permute-start | bytes 98312 | tf_op jit(solution)/shard_map/ppermute | solution.py:522

commit v12 on v11

--- a/solution.py
+++ b/solution.py
@@ -154,11 +154,13 @@
     return [jnp.concatenate([p[:, t * LANES : (t + 1) * LANES] for p in rows], axis=0) for t in range(3)]
 
 
-def zero_grams(pick, x0, out, spare):
+def zero_grams(pick, x0, out, spare, full):
     lefts, rests = [], []
     for r in range(D // BLOCK):
         lefts.append(x0[:, pl.ds(r * BLOCK, BLOCK)].T)
-        tiles = circulate(dot(lefts[r], x0[...]), r)
+        value = dot(lefts[r], x0[...])
+        full[pl.ds(r * BLOCK, BLOCK), :] = value.astype(bf16)
+        tiles = circulate(value, r)
         put(out, r, jnp.where(pick == 0, tiles[0], tiles[1]), F0)
         put(spare, r, jnp.where(pick == 0, tiles[1], tiles[0]), 0)
         last = pltpu.roll(end_lanes(tiles[2]), BLK, 1)
@@ -167,26 +169,42 @@
     return lefts, rests
 
 
-def picked_grams(lefts, x1, keep, rests, out, end):
+def picked_grams(lefts, x1, keep, rests, out, end, full):
     for r in range(D // BLOCK):
         put(out, r, dot(lefts[r], x1[...]), 0)
     wide = jnp.concatenate([keep[...]] * (BLOCK // LANES), axis=1)
     for r in range(D // BLOCK):
         left = (x1[:, pl.ds(r * BLOCK, BLOCK)] * wide).T
-        tiles = circulate(dot(left, x1[...]), r)
+        value = dot(left, x1[...])
+        full[pl.ds(r * BLOCK, BLOCK), :] = value.astype(bf16)
+        tiles = circulate(value, r)
         put(out, r, jnp.concatenate(tiles[:2], axis=1), FA)
         last = end_lanes(tiles[2])
         put_folded(out, r, last if rests is None else last + rests[r], end)
 
 
+def make_mirror(c, chip, mirror):
+    lane = lax.broadcasted_iota(jnp.int32, (LANES, D), 0)
+    column = lax.broadcasted_iota(jnp.int32, (LANES, D), 1)
+    for half in range(PAIR):
+        home = 8 * ((lane >> 2) & 3) + FR * half + (lane & 3) + 2 * D
+        for kind in range(2):
+            distance = (lane >> 4) + (4 * c if kind else 0)
+            there = (home + BLK * ((chip >> 3) - distance)) & (D - 1)
+            one = jnp.where(column == there, 1.0, 0.0).astype(bf16)
+            mirror[pl.ds((2 * half + kind) * LANES, LANES), :] = one
+
+
 def theirs_kernel(
-    core, start, width, x0, xk, xv, out, spare, kept, keep, ahead, buf0, buf1, starts, widths, sem0, sem1, sem2, sem3
+    core, chip, start, width, x0, xk, xv, bases, out, spare, kept, keep, ahead, full0, full1, mirror, bases_here,
+    buf0, buf1, starts, widths, sem0, sem1, sem2, sem3, sem4
 ):
     pick = 1 - core[0]
     small = [pltpu.make_async_copy(v, w, sem2.at[i]) for i, (v, w) in enumerate(((start, starts), (width, widths)))]
     copies0 = fetch(x0, buf0, sem0)
     for copy in small + copies0:
         copy.start()
+    make_mirror(core[0], chip[0], mirror)
     for copy in small:
         copy.wait()
     build_keep(starts, widths, keep)
@@ -195,80 +213,59 @@
         if q == 0:
             copies1 = fetch_picked(pick, xk, xv, buf1, sem1)
         apply_mask(buf0, kept, keep, q)
-    lefts, rests = zero_grams(pick, kept, out, spare)
+    lefts, rests = zero_grams(pick, kept, out, spare, full0)
     for copy in copies1:
         copy.wait()
     copies2 = fetch_picked(core[0], xk, xv, ahead, sem3)
-    picked_grams(lefts, buf1, keep, rests, out, FL)
+    fetched = pltpu.make_async_copy(bases, bases_here, sem4)
+    fetched.start()
+    picked_grams(lefts, buf1, keep, rests, out, FL, full1)
     for copy in copies2:
         copy.wait()
-
-
-def mine_kernel(keep, x0, x1, out):
+    fetched.wait()
+
+
+def basis_values(share, full, basis, old, picked):
+    high = old.astype(bf16).astype(f32)
+    mid = (old - high).astype(bf16).astype(f32)
+    row = lax.broadcasted_iota(jnp.int32, (8, D), 0)
+    column = lax.broadcasted_iota(jnp.int32, (8, D), 1)
+    chosen = jnp.zeros((8, D), f32)
+    for r, index in enumerate(picked):
+        chosen = jnp.where((row == r) & (column == index), 1.0, chosen)
+    extra = jnp.concatenate([high, mid, old - high - mid, jnp.zeros((2, D), f32), chosen], axis=0).astype(bf16)
+    image = dot(full[...], basis)
+    more = dot(extra, basis)
+    batch = jnp.sum(basis.astype(f32) * image, axis=0, keepdims=True)
+    old_image = more[0:2] + more[2:4] + more[4:6]
+    return batch * share + decay * jnp.sum(more[8:10] * old_image, axis=0, keepdims=True), more[8:]
+
+
+def mine_kernel(
+    share, core, chip, keep, x0, x1, full0, full1, bases, old, out, keep_lam, send_lam, basis_in_t, rows_in, full
+):
+    c, first_row = core[0], FR * chip[0]
     lefts = [x0[:, pl.ds(r * BLOCK, BLOCK)].T for r in range(D // BLOCK)]
-    picked_grams(lefts, x1, keep, None, out, F0)
-
-
-PIECES = 4
-
-
-def add_kernel(mine, spare, received, out, buf, sems):
-    size = NXY // PIECES
-    copies = []
-    main, zero, last = slice(0, F0), slice(F0, FL), slice(FL, WROWS)
-    for q in range(PIECES):
-        for i in range(q * size, (q + 1) * size):
-            for j in range(PAIR):
-                buf[i, j, main] = mine[i, j, main] + received[i, j, main]
-                buf[i, j, zero] = spare[i, j, :ROWS] + received[i, j, zero]
-                ends = mine[i, j, F0:] + spare[i, j, ROWS:]
-                buf[i, j, last] = ends + received[i, j, last]
-        part = pl.ds(q * size, size)
-        copies.append(pltpu.make_async_copy(buf.at[part], out.at[part], sems.at[q]))
-        copies[q].start()
-    for copy in copies:
-        copy.wait()
-
-
-def lam_kernel(
-    share, core, chip, _, keep, x0, xk, xv, bases, keep_lam, send_lam, basis_in_t, mirror, basis_out, rows_in, b0, b1, b2, sem0, sem1, sem2
-):
-    c = core[0]
-    bufs = (b0, b1, b2)
-    copies = [fetch(x, buf, sem) for x, buf, sem in zip((x0, xk, xv), bufs, (sem0, sem1, sem2))]
-    for group in copies:
-        for copy in group:
-            copy.start()
+    picked_grams(lefts, x1, keep, None, out, F0, full)
     low, high = arrange(bases[0].astype(f32))
     basis_in_t[...] = jnp.concatenate([low, high], axis=1).reshape(D, D).T.astype(bf16)
-    lane = lax.broadcasted_iota(jnp.int32, (LANES, D), 0)
-    column = lax.broadcasted_iota(jnp.int32, (LANES, D), 1)
-    for half in range(PAIR):
-        home = 8 * ((lane >> 2) & 3) + FR * half + (lane & 3) + 2 * D
-        for kind in range(2):
-            distance = (lane >> 4) + (4 * c if kind else 0)
-            there = (home + BLK * ((chip[0] >> 3) - distance)) & (D - 1)
-            one = jnp.where(column == there, 1.0, 0.0).astype(bf16)
-            mirror[pl.ds((2 * half + kind) * LANES, LANES), :] = one
-    basis_out[...] = bases[1 + c]
-    row = lax.broadcasted_iota(jnp.int32, (16, D), 0)
-    column = lax.broadcasted_iota(jnp.int32, (16, D), 1)
-    wanted = (row < FR) & (column == FR * chip[0] + ((row + 2 * c) & (FR - 1)))
-    rows_in[...] = dot(jnp.where(wanted, 1.0, 0.0).astype(bf16), bases[0]).astype(bf16)
-    lam = []
-    for f in range(3):
-        total = jnp.zeros((8, D), f32)
-        for q in range(CHUNKS):
-            copies[f][q].wait()
-            apply_mask(bufs[f], bufs[f], keep, q)
-        for q in range(bufs[f].shape[0] // BLOCK):
-            product = dot(bufs[f][pl.ds(q * BLOCK, BLOCK), :], bases[f])
-            total = total + jnp.sum((product * product).reshape(BLOCK // 8, 8, D), axis=0)
-        lam.append(jnp.sum(total, axis=0, keepdims=True) * share)
-    keep_lam[0:1, :] = lam[0]
-    send_lam[0:1, :] = lam[0]
-    keep_lam[1:2, :] = jnp.where(c == 0, lam[1], lam[2])
-    send_lam[1:2, :] = jnp.where(c == 0, lam[2], lam[1])
+    own = [first_row + 2 * c, first_row + 2 * c + 1]
+    rest = [first_row + 2 * (1 - c), first_row + 2 * (1 - c) + 1]
+    lam0, rows = basis_values(share, full0, bases[0], old[0], own + rest)
+    rows_in[...] = jnp.concatenate([rows, jnp.zeros((8, D), f32)], axis=0).astype(bf16)
+    keep_lam[0:1, :] = lam0
+    send_lam[0:1, :] = lam0
+    keep_lam[1:2, :] = basis_values(share, full, bases[1 + c], old[1 + c], own)[0]
+    send_lam[1:2, :] = basis_values(share, full1, bases[2 - c], old[2 - c], own)[0]
+
+
+def add_kernel(mine, spare, received, out):
+    main, zero, last = slice(0, F0), slice(F0, FL), slice(FL, WROWS)
+    for i in range(NXY):
+        for j in range(PAIR):
+            out[i, j, main] = mine[i, j, main] + received[i, j, main]
+            out[i, j, zero] = spare[i, j, :ROWS] + received[i, j, zero]
+            out[i, j, last] = mine[i, j, F0:] + spare[i, j, ROWS:] + received[i, j, last]
 
 
 def split(value):
@@ -337,9 +334,9 @@
     return total, jnp.concatenate([total[j * ROWS : (j + 1) * ROWS] for j in range(GT)], axis=1)
 
 
-def rotate_kernel(got, basis, out):
+def rotate_kernel(core, got, bases, out):
     total, grad = deep_total(got)
-    rot = dot(grad.astype(bf16), basis[...]).astype(bf16)
+    rot = dot(grad.astype(bf16), bases[1 + core[0]]).astype(bf16)
     lam = add_lam(total[DEEP_LAM:])
     picked, zero = total[TURNED : TURNED + 8], total[TURNED + 8 : TURNED + 16]
     for half in range(PAIR):
@@ -386,7 +383,7 @@
     return dot(jnp.concatenate(parts, axis=1).astype(bf16), mirror[...])
 
 
-def solve_kernel(core, chip, got, packed, basis_in_t, basis_out, rows_in, mirror, own, their, scaled):
+def solve_kernel(core, chip, got, packed, basis_in_t, bases, rows_in, mirror, own, their, scaled):
     tails = [got[i, pl.ds(GATHER_LAM, ROWS), :].astype(f32) for i in range(WIDE)]
     lam = tails[0][:8]
     for tail in tails[1:]:
@@ -402,7 +399,7 @@
         curve = curve + jnp.sum((low.astype(f32) * rotated).reshape(D // 8, 8, LANES), axis=0)
     curve = jnp.sum(jnp.sum(curve, axis=1, keepdims=True), axis=0, keepdims=True)
     back = dot(rows_in[...], scaled[...]).astype(bf16)
-    prec = lax.dot_general(back, basis_out[...], (((1,), (1,)), ((), ())), preferred_element_type=f32)
+    prec = lax.dot_general(back, bases[1 + core[0]], (((1,), (1,)), ((), ())), preferred_element_type=f32)
     prec = prec.astype(bf16).astype(f32)
     curve = jnp.broadcast_to(curve, (2, D))
     rows, factors = direct_rows((chip[0] & (NZ - 1)) >> 1, core[0], chip[0] >> 3, packed)
@@ -437,7 +434,6 @@
 def body(activations, grad_key, grad_value, time_start, time_width, bases, old_factors):
     index = lax.axis_index("dp").astype(jnp.int32)
     core = index & (NC - 1)
-    first = core == 0
     here = (core[None], (index >> 1)[None])
     tokens_here = activations.shape[0]
     share = (1.0 - decay) / (tokens_here * lax.axis_size("dp"))
@@ -453,71 +449,65 @@
     pair = pltpu.SemaphoreType.DMA((2,))
     partial = shape((NXY, PAIR, WROWS, LANES), bf16)
     work = 6 * D * D * tokens_here
+    square, lam_shape = shape((D, D), bf16), shape((2, D), f32)
+    frames_shape = shape((tokens_here, D), bf16)
+    old = jnp.transpose(old_factors, (1, 0, 2))
     with jax.named_scope("grams_theirs"):
-        other, spare, kept, keep, ahead = call(
+        other, spare, kept, keep, ahead, full0, full1, mirror, bases_here = call(
             theirs_kernel,
             (
                 partial,
                 shape((NXY, PAIR, ROWS + ROWS // 2, LANES), bf16),
-                shape((tokens_here, D), bf16),
+                frames_shape,
                 shape((tokens_here, LANES), bf16),
-                shape((tokens_here, D), bf16),
+                frames_shape,
+                square,
+                square,
+                square,
+                shape(bases.shape, bf16),
             ),
-            [SMEM] + [HBM] * 5,
-            [buf, buf, mask_buf, mask_buf, sems, sems, pair, sems],
+            [SMEM] * 2 + [HBM] * 6,
+            [buf, buf, mask_buf, mask_buf, sems, sems, pair, sems, pltpu.SemaphoreType.DMA],
+            limit=20,
+            flops=work,
+            moved=5 * MB,
+        )(*here, *masks, frames, keys, vals, in_hbm(bases))
+    received = lax.ppermute(other, "dp", SWAP)
+    with jax.named_scope("grams_mine"):
+        mine, keep_lam, send_lam, basis_in_t, rows_in = call(
+            functools.partial(mine_kernel, share),
+            (
+                shape((NXY, PAIR, F0 + ROWS // 2, LANES), bf16),
+                lam_shape,
+                lam_shape,
+                square,
+                shape((16, D), bf16),
+            ),
+            [SMEM] * 2 + [VMEM] * 7,
+            [pltpu.VMEM((D, D), bf16)],
+            limit=20,
             flops=work,
             moved=4 * MB,
-        )(core[None], *masks, frames, keys, vals)
-    received = lax.ppermute(other, "dp", SWAP)
-    with jax.named_scope("grams_mine"):
-        mine = call(
-            mine_kernel,
-            shape((NXY, PAIR, F0 + ROWS // 2, LANES), bf16),
-            [VMEM] * 3,
-            flops=work,
-            moved=4 * MB,
-        )(keep, kept, ahead)
+        )(*here, keep, kept, ahead, full0, full1, bases_here, old)
+    sent_lam = lax.ppermute(send_lam, "dp", SWAP)
     with jax.named_scope("chip_sum"):
-        chip = call(
-            add_kernel,
-            pltpu.HBM(partial.shape, bf16),
-            [VMEM] * 3,
-            [pltpu.VMEM(partial.shape, bf16), pltpu.SemaphoreType.DMA((PIECES,))],
-        )(mine, spare, received).reshape(WIDE, WROWS, LANES)
+        chip = call(add_kernel, partial, [VMEM] * 3)(mine, spare, received).reshape(WIDE, WROWS, LANES)
     with jax.named_scope("wide_sum"):
         parts = exchange(chip, WIDE_GROUPS)
-
-    lam_shape, square = shape((2, D), f32), shape((D, D), bf16)
-    with jax.named_scope("lam"):
-        keep_lam, send_lam, basis_in_t, mirror, basis_out, rows_in = call(
-            functools.partial(lam_kernel, share),
-            (lam_shape, lam_shape, square, square, square, shape((16, D), bf16)),
-            [SMEM, SMEM, HBM, VMEM, HBM, HBM, HBM, VMEM],
-            [buf] * 3 + [sems] * 3,
-            flops=work,
-            moved=4 * MB,
-        )(*here, in_hbm(chip), keep, frames, keys, vals, bases)
-    old_lam = []
-    my_rows = lax.dynamic_slice_in_dim(bases, 2 * index, 2, 1).astype(f32)
-    for f in range(3):
-        old_image = jnp.dot(old_factors[:, f, :], bases[f].astype(f32), precision=lax.Precision.HIGHEST)
-        old_lam.append(decay * jnp.sum(my_rows[f] * old_image, axis=0))
-    keep_lam = keep_lam + jnp.stack([old_lam[0], jnp.where(first, old_lam[1], old_lam[2])])
-    send_lam = send_lam + jnp.stack([old_lam[0], jnp.where(first, old_lam[2], old_lam[1])])
-    sent_lam = lax.ppermute(send_lam, "dp", SWAP)
-
     with jax.named_scope("pack"):
         packed = call(pack_kernel, shape((DEEP, DEEP_ROWS, LANES), bf16), [VMEM] * 3)(parts, keep_lam, sent_lam)
     with jax.named_scope("deep_sum"):
         got = exchange(packed, DEEP_GROUPS)
     lines = shape((16, D), f32)
     with jax.named_scope("rotate"):
-        spread = call(rotate_kernel, shape((WIDE, GATHER_ROWS, LANES), bf16), [VMEM] * 2)(got, basis_out)
+        spread = call(rotate_kernel, shape((WIDE, GATHER_ROWS, LANES), bf16), [SMEM] + [VMEM] * 2)(
+            here[0], got, bases_here
+        )
     with jax.named_scope("gather"):
         gathered = exchange(spread, WIDE_GROUPS)
     with jax.named_scope("solve"):
         own, their = call(solve_kernel, (lines, lines), [SMEM] * 2 + [VMEM] * 6, [pltpu.VMEM((D, D), bf16)])(
-            *here, gathered, got, basis_in_t, basis_out, rows_in, mirror
+            *here, gathered, got, basis_in_t, bases_here, rows_in, mirror
         )
     theirs = lax.ppermute(their, "dp", SWAP)
     with jax.named_scope("finish"):
@@ -525,7 +515,7 @@
             functools.partial(finish_kernel, share),
             (shape((3, 2, D), f32), shape((2, 2, D), f32), shape((2, 2, D), bf16)),
             [SMEM] + [VMEM] * 3,
-        )(core[None], own, theirs, jnp.transpose(old_factors, (1, 0, 2)))
+        )(core[None], own, theirs, old)
     return (jnp.transpose(new_factors, (1, 0, 2)), gradients, updates)
 
 

time: 70.4 us -> 72.2 us (1.026)
  waiting for transfers between devices: 10.7 us -> 17 us
  local copies, waits for them, and re-layouts: 1.61 us -> 0.01 us
  Pallas kernels: 12.3 us -> 11 us
  matrix products: 0.99 us -> 0 us
    all_to_all x1, waiting for transfers between devices: 8.26 us -> 15.4 us  [exchange(): lax.all_to_all(value, 'dp', 0, 0, axis_index_groups=groups, tiled=True)]
    pallas_call x4 -> x3, Pallas kernels: 6.44 us -> 3.88 us  [the longest x1 2.45 us: body(): call(functools.partial(mine_kernel, share), (shape((NXY, PAIR, F0 + ROWS...]
    unnamed x12 -> x6, local copies, waits for them, and re-layouts: 1.61 us -> 0.01 us
    pallas_call x1, Pallas kernels: 3.78 us -> 5.05 us  [body(): call(theirs_kernel, (partial, shape((NXY, PAIR, ROWS + ROWS // 2, LANES),...]
    dot_general x3 -> x0, matrix products: 0.99 us -> none  [body(): jnp.dot(old_factors[:, f, :], bases[f].astype(f32), precision=lax.Precisi...]
    ppermute x1, waiting for transfers between devices: 0.75 us -> 0.01 us  [body(): received = lax.ppermute(other, 'dp', SWAP)]
  transfers between devices with their start and end apart: 4 -> 4, of which waited for: 4 -> 3; matrix products, arithmetic and copies ran while one was open for 1% -> 0% of each run, Pallas kernels for 7% -> 3%
where the time goes in v12:
time: 72.2 us; the launch traced here: 71.8 us
  blocking collectives  28.4 us (39%)
  waiting for transfers between devices  17 us (24%)
  starting transfers between devices  14.7 us (20%)
  Pallas kernels  11 us (15%)
    all_to_all x2, blocking collectives, exchange(): lax.all_to_all(value, 'dp', 0, 0, axis_index_groups=groups, tiled=True)  28.4 us
    all_to_all x1, waiting for transfers between devices, exchange(): lax.all_to_all(value, 'dp', 0, 0, axis_index_groups=groups, tiled=True)  15.4 us
    all_to_all x1, starting transfers between devices, exchange(): lax.all_to_all(value, 'dp', 0, 0, axis_index_groups=groups, tiled=True)  6.68 us
    pallas_call x1, Pallas kernels, body(): call(theirs_kernel, (partial, shape((NXY, PAIR, ROWS + ROWS // 2, LANES),...  5.05 us
    ppermute x1, starting transfers between devices, body(): theirs = lax.ppermute(their, 'dp', SWAP)  4.24 us
    ppermute x1, starting transfers between devices, body(): received = lax.ppermute(other, 'dp', SWAP)  3.33 us
    pallas_call x1, Pallas kernels, body(): call(functools.partial(mine_kernel, share), (shape((NXY, PAIR, F0 + ROWS...  2.45 us
  transfers between devices with their start and end apart: 4, of which 3 were waited for; matrix products, arithmetic and copies ran while one was open for 0% of the time, Pallas kernels for 3%

profile of v12, /device:TPU:1, one launch (start us, length us, event | category | flops | bytes accessed | tf_op | source)
XLA Modules:
  0.0 71.8 jit_solution(6046631764856872405)
XLA Ops:
  0.6 0.0 copy-start.2
  0.6 5.0 %grams_theirs.1 = (bf16[16,2,120,128]{3,2,1,0:T(8,128)(2,1)S(1)}, bf16[16,2,24,128]{3,2,1,0:T(8,128)(2,1)S(1)}, bf16[1024,512]{1,0:T(8,128)(2,1)S(1)}, bf16[1024...) custom-call(s32[1]{0:T(128)} %bitcast.core, ...), custom_call_target="tpu_custom_call" | custom-call | flops 1610612736 | bytes 5242880 | tf_op jit(solution)/shard_map/grams_theirs/pallas_call | solution.py:456
  5.7 3.3 %collective-permute-start = (bf16[16,2,120,128]{3,2,1,0:T(8,128)(2,1)S(1)}, bf16[16,2,120,128]{3,2,1,0:T(8,128)(2,1)S(1)}, u32[]{:S(2)}, u32[]{:S(2)}) collective-permute-start(bf16[16,2,120,128]{3,2,1,0:T(8,128)(2,1)S(1)} %get-tuple-element.30), channel_id=1, source_target_pairs={{0,1},{1,0},{2,3},{3,2},{4,5},{5,4},{6,7},{7,6},{8,9},{9,8},{10,11... | collective-permute-start | bytes 2949128 | tf_op jit(solution)/shard_map/ppermute | solution.py:475
  9.0 0.0 copy-done.2
  9.0 2.4 %grams_mine.1 = (bf16[16,2,104,128]{3,2,1,0:T(8,128)(2,1)S(1)}, f32[2,512]{1,0:T(2,128)S(1)}, f32[2,512]{1,0:T(2,128)S(1)}, bf16[512,512]{1,0:T(8,128)(2,1)S(1)}, bf16[16,512]{1,0:T(8,128)(2,1)S(1)}) custom-call(s32[1]{0:T(128)} %bitcast.core, s32[1]{0:T(128)} %bitcast.1.chip, bf16[1024,128]{1,0:T(8,128)(2,1)S(1)} %get-tuple-element.22.keep, ...), custom_call_target="tpu_custom_call" | custom-call | flops 1610612736 | bytes 4194304 | tf_op jit(solution)/shard_map/grams_mine/pallas_call | solution.py:477
  11.5 0.0 copy-start
  11.5 0.0 collective-permute-done.received
  11.5 1.2 %chip_sum.1 = bf16[16,2,120,128]{3,2,1,0:T(8,128)(2,1)} custom-call(bf16[16,2,104,128]{3,2,1,0:T(8,128)(2,1)S(1)} %get-tuple-element.28.mine, bf16[16,2,24,128]{3,2,1,0:T(8,128)(2,1)S(1)} %get-tuple-element.29.spare, bf16[16,2,120,128]{3,2,1,0:T(8,128)(2,1)S(1)} %collective-permute-done.received), custom_call_target="tpu_custom_call" | custom-call | tf_op jit(solution)/shard_map/chip_sum/pallas_call | solution.py:494
  12.7 0.0 copy-done
  12.7 6.7 %all-to-all-start = ((bf16[32,120,128]{2,1,0:T(8,128)(2,1)}), bf16[32,120,128]{2,1,0:T(8,128)(2,1)S(1)}, u32[]{:S(2)}, u32[]{:S(2)}) async-start(bf16[32,120,128]{2,1,0:T(8,128)(2,1)} %bitcast.5), calls=%async_computation | async-start | bytes 1966080 | tf_op jit(solution)/shard_map/wide_sum/all_to_all | solution.py:431
  19.4 0.4 collective-permute-start.1
  19.8 0.8 %collective-permute-done.1.send_lam = f32[2,512]{1,0:T(2,128)S(1)} collective-permute-done((f32[2,512]{1,0:T(2,128)S(1)}, f32[2,512]{1,0:T(2,128)S(1)}, u32[]{:S(2)}, u32[]{:S(2)}) %collective-permute-start.1) | collective-permute-done | bytes 4128 | tf_op jit(solution)/shard_map/ppermute | solution.py:492
  20.7 15.4 %all-to-all-done.parts = bf16[32,120,128]{2,1,0:T(8,128)(2,1)S(1)} async-done(((bf16[32,120,128]{2,1,0:T(8,128)(2,1)}), bf16[32,120,128]{2,1,0:T(8,128)(2,1)S(1)}, u32[]{:S(2)}, u32[]{:S(2)}) %all-to-all-start) | async-done | bytes 983072 | tf_op jit(solution)/shard_map/wide_sum/all_to_all | solution.py:431
  36.0 0.3 pack.1
  36.4 14.2 %all_to_all.15.got.packed = bf16[4,112,128]{2,1,0:T(8,128)(2,1)S(1)} all-to-all(bf16[4,112,128]{2,1,0:T(8,128)(2,1)S(1)} %pack.1), channel_id=1, replica_groups={{0,4,8,12},{1,5,9,13},{2,6,10,14},{3,7,11,15},{16,20,24,28},{17,21,25,2..., dimensions={0} | all-to-all | bytes 229376 | tf_op jit(solution)/shard_map/deep_sum/all_to_all | solution.py:431
  50.6 0.0 copy-start.1
  50.6 0.2 rotate.1
  50.8 14.1 %all_to_all.16.got = bf16[32,80,128]{2,1,0:T(8,128)(2,1)S(1)} all-to-all(bf16[32,80,128]{2,1,0:T(8,128)(2,1)S(1)} %rotate.1), channel_id=1, replica_groups={{0,2,16,18,32,34,48,50,64,66,80,82,96,98,112,114,128,130,144,146,160,16..., dimensions={0} | all-to-all | bytes 1310720 | tf_op jit(solution)/shard_map/gather/all_to_all | solution.py:431
  65.0 0.0 copy-done.1
  65.0 1.1 %solve.1 = (f32[16,512]{1,0:T(8,128)S(1)}, f32[16,512]{1,0:T(8,128)S(1)}) custom-call(s32[1]{0:T(128)} %bitcast.core, s32[1]{0:T(128)} %bitcast.1.chip, bf16[32,80,128]{2,1,0:T(8,128)(2,1)S(1)} %all_to_all.16.got, bf16[4,112,128]{2,1,0:T(8,128)(2,1)S(1)} %all_to_all.15.got.packed, bf16[512,512]{1,0:T(8,128)(2,1)S(1)} %copy-done.1, ...), custom_call_target="tpu_custom_call" | custom-call | tf_op jit(solution)/shard_map/solve/pallas_call | solution.py:509
  66.1 4.2 %collective-permute-start.2 = (f32[16,512]{1,0:T(8,128)S(1)}, f32[16,512]{1,0:T(8,128)S(1)}, u32[]{:S(2)}, u32[]{:S(2)}) collective-permute-start(f32[16,512]{1,0:T(8,128)S(1)} %get-tuple-element.37), channel_id=1, source_target_pairs={{0,1},{1,0},{2,3},{3,2},{4,5},{5,4},{6,7},{7,6},{8,9},{9,8},{10,11... | collective-permute-start | bytes 98312 | tf_op jit(solution)/shard_map/ppermute | solution.py:512
  70.4 0.9 %collective-permute-done.2.got = f32[16,512]{1,0:T(8,128)S(1)} collective-permute-done((f32[16,512]{1,0:T(8,128)S(1)}, f32[16,512]{1,0:T(8,128)S(1)}, u32[]{:S(2)}, u32[]{:S(2)}) %collective-permute-start.2) | collective-permute-done | bytes 32800 | tf_op jit(solution)/shard_map/ppermute | solution.py:512
  71.2 0.6 finish.1
Async XLA Ops:
  0.6 8.4 %copy-start.2 = (f32[2,3,512]{2,0,1:T(2,128)S(1)}, f32[2,3,512]{2,0,1:T(2,128)}, u32[]{:S(2)}) copy-start(f32[2,3,512]{2,0,1:T(2,128)} %param.13) | copy-start | bytes 36868
  5.7 5.8 %collective-permute-start = (bf16[16,2,120,128]{3,2,1,0:T(8,128)(2,1)S(1)}, bf16[16,2,120,128]{3,2,1,0:T(8,128)(2,1)S(1)}, u32[]{:S(2)}, u32[]{:S(2)}) collective-permute-start(bf16[16,2,120,128]{3,2,1,0:T(8,128)(2,1)S(1)} %get-tuple-element.30), channel_id=1, source_target_pairs={{0,1},{1,0},{2,3},{3,2},{4,5},{5,4},{6,7},{7,6},{8,9},{9,8},{10,11... | collective-permute-start | bytes 2949128 | tf_op jit(solution)/shard_map/ppermute | solution.py:475
  11.5 1.2 %copy-start = (bf16[512,512]{1,0:T(8,128)(2,1)}, bf16[512,512]{1,0:T(8,128)(2,1)S(1)}, u32[]{:S(2)}) copy-start(bf16[512,512]{1,0:T(8,128)(2,1)S(1)} %get-tuple-element.33.basis_in_t) | copy-start | bytes 1572868
  12.7 23.3 %all-to-all-start = ((bf16[32,120,128]{2,1,0:T(8,128)(2,1)}), bf16[32,120,128]{2,1,0:T(8,128)(2,1)S(1)}, u32[]{:S(2)}, u32[]{:S(2)}) async-start(bf16[32,120,128]{2,1,0:T(8,128)(2,1)} %bitcast.5), calls=%async_computation | async-start | bytes 1966080 | tf_op jit(solution)/shard_map/wide_sum/all_to_all | solution.py:431
  19.4 1.3 %collective-permute-start.1 = (f32[2,512]{1,0:T(2,128)S(1)}, f32[2,512]{1,0:T(2,128)S(1)}, u32[]{:S(2)}, u32[]{:S(2)}) collective-permute-start(f32[2,512]{1,0:T(2,128)S(1)} %get-tuple-element.32), channel_id=1, source_target_pairs={{0,1},{1,0},{2,3},{3,2},{4,5},{5,4},{6,7},{7,6},{8,9},{9,8},{10,11... | collective-permute-start | bytes 12296 | tf_op jit(solution)/shard_map/ppermute | solution.py:492
  50.6 14.3 %copy-start.1 = (bf16[512,512]{1,0:T(8,128)(2,1)S(1)}, bf16[512,512]{1,0:T(8,128)(2,1)}, u32[]{:S(2)}) copy-start(bf16[512,512]{1,0:T(8,128)(2,1)} %copy-done) | copy-start | bytes 1572868
  66.1 5.1 %collective-permute-start.2 = (f32[16,512]{1,0:T(8,128)S(1)}, f32[16,512]{1,0:T(8,128)S(1)}, u32[]{:S(2)}, u32[]{:S(2)}) collective-permute-start(f32[16,512]{1,0:T(8,128)S(1)} %get-tuple-element.37), channel_id=1, source_target_pairs={{0,1},{1,0},{2,3},{3,2},{4,5},{5,4},{6,7},{7,6},{8,9},{9,8},{10,11... | collective-permute-start | bytes 98312 | tf_op jit(solution)/shard_map/ppermute | solution.py:512

commit v13 on v12

--- a/solution.py
+++ b/solution.py
@@ -169,16 +169,19 @@
     return lefts, rests
 
 
-def picked_grams(lefts, x1, keep, rests, out, end, full):
+def gradient_grams(lefts, x1, out):
     for r in range(D // BLOCK):
         put(out, r, dot(lefts[r], x1[...]), 0)
+
+
+def picked_grams(x1, keep, rests, out, begin, end, full):
     wide = jnp.concatenate([keep[...]] * (BLOCK // LANES), axis=1)
     for r in range(D // BLOCK):
         left = (x1[:, pl.ds(r * BLOCK, BLOCK)] * wide).T
         value = dot(left, x1[...])
         full[pl.ds(r * BLOCK, BLOCK), :] = value.astype(bf16)
         tiles = circulate(value, r)
-        put(out, r, jnp.concatenate(tiles[:2], axis=1), FA)
+        put(out, r, jnp.concatenate(tiles[:2], axis=1), begin)
         last = end_lanes(tiles[2])
         put_folded(out, r, last if rests is None else last + rests[r], end)
 
@@ -196,8 +199,8 @@
 
 
 def theirs_kernel(
-    core, chip, start, width, x0, xk, xv, bases, out, spare, kept, keep, ahead, full0, full1, mirror, bases_here,
-    buf0, buf1, starts, widths, sem0, sem1, sem2, sem3, sem4
+    core, chip, start, width, x0, xk, xv, out, spare, kept, keep, ahead, full0, full1, mirror,
+    buf0, buf1, starts, widths, sem0, sem1, sem2, sem3
 ):
     pick = 1 - core[0]
     small = [pltpu.make_async_copy(v, w, sem2.at[i]) for i, (v, w) in enumerate(((start, starts), (width, widths)))]
@@ -217,12 +220,10 @@
     for copy in copies1:
         copy.wait()
     copies2 = fetch_picked(core[0], xk, xv, ahead, sem3)
-    fetched = pltpu.make_async_copy(bases, bases_here, sem4)
-    fetched.start()
-    picked_grams(lefts, buf1, keep, rests, out, FL, full1)
+    gradient_grams(lefts, buf1, out)
+    picked_grams(buf1, keep, rests, out, FA, FL, full1)
     for copy in copies2:
         copy.wait()
-    fetched.wait()
 
 
 def basis_values(share, full, basis, old, picked):
@@ -242,11 +243,13 @@
 
 
 def mine_kernel(
-    share, core, chip, keep, x0, x1, full0, full1, bases, old, out, keep_lam, send_lam, basis_in_t, rows_in, full
+    share, core, chip, keep, x1, full0, full1, old, bases_far, out, keep_lam, send_lam, basis_in_t, rows_in, bases, full, sem
 ):
+    fetched = pltpu.make_async_copy(bases_far, bases, sem)
+    fetched.start()
     c, first_row = core[0], FR * chip[0]
-    lefts = [x0[:, pl.ds(r * BLOCK, BLOCK)].T for r in range(D // BLOCK)]
-    picked_grams(lefts, x1, keep, None, out, F0, full)
+    picked_grams(x1, keep, None, out, 0, F0 - FA, full)
+    fetched.wait()
     low, high = arrange(bases[0].astype(f32))
     basis_in_t[...] = jnp.concatenate([low, high], axis=1).reshape(D, D).T.astype(bf16)
     own = [first_row + 2 * c, first_row + 2 * c + 1]
@@ -259,13 +262,19 @@
     send_lam[1:2, :] = basis_values(share, full1, bases[2 - c], old[2 - c], own)[0]
 
 
-def add_kernel(mine, spare, received, out):
-    main, zero, last = slice(0, F0), slice(F0, FL), slice(FL, WROWS)
+def gradient_kernel(x0, x1, out):
+    gradient_grams([x0[:, pl.ds(r * BLOCK, BLOCK)].T for r in range(D // BLOCK)], x1, out)
+
+
+def add_kernel(gradient, picked, spare, received, keep_lam, sent_lam, out, lam):
+    first, second, zero, last = slice(0, FA), slice(FA, F0), slice(F0, FL), slice(FL, WROWS)
     for i in range(NXY):
         for j in range(PAIR):
-            out[i, j, main] = mine[i, j, main] + received[i, j, main]
+            out[i, j, first] = gradient[i, j] + received[i, j, first]
+            out[i, j, second] = picked[i, j, : F0 - FA] + received[i, j, second]
             out[i, j, zero] = spare[i, j, :ROWS] + received[i, j, zero]
-            out[i, j, last] = mine[i, j, F0:] + spare[i, j, ROWS:] + received[i, j, last]
+            out[i, j, last] = picked[i, j, F0 - FA :] + spare[i, j, ROWS:] + received[i, j, last]
+    lam[...] = keep_lam[...] + sent_lam[...]
 
 
 def split(value):
@@ -295,11 +304,11 @@
 GATHER_ROWS = GATHER_TURNED + 8
 
 
-def pack_kernel(parts, keep_lam, send_lam, out):
+def pack_kernel(parts, lam, out):
     total = parts[0].astype(f32)
     for i in range(1, WIDE):
         total = total + parts[i].astype(f32)
-    lam = lam_rows(keep_lam[...] + send_lam[...]).astype(bf16)
+    lam = lam_rows(lam[...]).astype(bf16)
     for j in range(GT):
         tile = total[j * ROWS : (j + 1) * ROWS].astype(bf16)
         for k in range(DEEP):
@@ -453,7 +462,7 @@
     frames_shape = shape((tokens_here, D), bf16)
     old = jnp.transpose(old_factors, (1, 0, 2))
     with jax.named_scope("grams_theirs"):
-        other, spare, kept, keep, ahead, full0, full1, mirror, bases_here = call(
+        other, spare, kept, keep, ahead, full0, full1, mirror = call(
             theirs_kernel,
             (
                 partial,
@@ -464,38 +473,49 @@
                 square,
                 square,
                 square,
-                shape(bases.shape, bf16),
             ),
-            [SMEM] * 2 + [HBM] * 6,
-            [buf, buf, mask_buf, mask_buf, sems, sems, pair, sems, pltpu.SemaphoreType.DMA],
+            [SMEM] * 2 + [HBM] * 5,
+            [buf, buf, mask_buf, mask_buf, sems, sems, pair, sems],
             limit=20,
             flops=work,
             moved=5 * MB,
-        )(*here, *masks, frames, keys, vals, in_hbm(bases))
+        )(*here, *masks, frames, keys, vals)
     received = lax.ppermute(other, "dp", SWAP)
-    with jax.named_scope("grams_mine"):
-        mine, keep_lam, send_lam, basis_in_t, rows_in = call(
+    with jax.named_scope("factors_mine"):
+        picked, keep_lam, send_lam, basis_in_t, rows_in, bases_here = call(
             functools.partial(mine_kernel, share),
             (
-                shape((NXY, PAIR, F0 + ROWS // 2, LANES), bf16),
+                shape((NXY, PAIR, F0 - FA + ROWS // 2, LANES), bf16),
                 lam_shape,
                 lam_shape,
                 square,
                 shape((16, D), bf16),
+                shape(bases.shape, bf16),
             ),
-            [SMEM] * 2 + [VMEM] * 7,
-            [pltpu.VMEM((D, D), bf16)],
+            [SMEM] * 2 + [VMEM] * 5 + [HBM],
+            [pltpu.VMEM((D, D), bf16), pltpu.SemaphoreType.DMA],
             limit=20,
             flops=work,
             moved=4 * MB,
-        )(*here, keep, kept, ahead, full0, full1, bases_here, old)
+        )(*here, keep, ahead, full0, full1, old, in_hbm(bases))
     sent_lam = lax.ppermute(send_lam, "dp", SWAP)
+    with jax.named_scope("gradient_mine"):
+        gradient = call(
+            gradient_kernel,
+            shape((NXY, PAIR, FA, LANES), bf16),
+            [VMEM] * 2,
+            flops=work // 3,
+            moved=4 * MB,
+        )(kept, ahead)
     with jax.named_scope("chip_sum"):
-        chip = call(add_kernel, partial, [VMEM] * 3)(mine, spare, received).reshape(WIDE, WROWS, LANES)
+        chip, lam = call(add_kernel, (partial, lam_shape), [VMEM] * 6)(
+            gradient, picked, spare, received, keep_lam, sent_lam
+        )
+        chip = chip.reshape(WIDE, WROWS, LANES)
     with jax.named_scope("wide_sum"):
         parts = exchange(chip, WIDE_GROUPS)
     with jax.named_scope("pack"):
-        packed = call(pack_kernel, shape((DEEP, DEEP_ROWS, LANES), bf16), [VMEM] * 3)(parts, keep_lam, sent_lam)
+        packed = call(pack_kernel, shape((DEEP, DEEP_ROWS, LANES), bf16), [VMEM] * 2)(parts, lam)
     with jax.named_scope("deep_sum"):
         got = exchange(packed, DEEP_GROUPS)
     lines = shape((16, D), f32)

time: 72.2 us -> 71.9 us (level)
  blocking collectives: 28.4 us -> 51.3 us
  waiting for transfers between devices: 17 us -> 1.27 us
  starting transfers between devices: 14.7 us -> 7.47 us
    all_to_all x2 -> x3, blocking collectives: 28.4 us -> 51.3 us  [exchange(): lax.all_to_all(value, 'dp', 0, 0, axis_index_groups=groups, tiled=True)]
    all_to_all x1 -> x0, waiting for transfers between devices: 15.4 us -> none  [exchange(): lax.all_to_all(value, 'dp', 0, 0, axis_index_groups=groups, tiled=True)]
    all_to_all x1 -> x0, starting transfers between devices: 6.68 us -> none  [exchange(): lax.all_to_all(value, 'dp', 0, 0, axis_index_groups=groups, tiled=True)]
    pallas_call x3 -> x4, Pallas kernels: 4.02 us -> 4.07 us  [the longest x1 2.72 us: body(): call(functools.partial(mine_kernel, share), (shape((NXY, PAIR, F0 - FA +...]
  transfers between devices with their start and end apart: 4 -> 3, of which waited for: 3 -> 2; matrix products, arithmetic and copies ran while one was open for 0% -> 0% of each run, Pallas kernels for 3% -> 5%
where the time goes in v13:
time: 71.9 us; the launch traced here: 71.6 us
  blocking collectives  51.3 us (71%)
  Pallas kernels  10.9 us (15%)
  starting transfers between devices  7.47 us (10%)
  waiting for transfers between devices  1.27 us (2%)
    all_to_all x3, blocking collectives, exchange(): lax.all_to_all(value, 'dp', 0, 0, axis_index_groups=groups, tiled=True)  51.3 us
    pallas_call x1, Pallas kernels, body(): call(theirs_kernel, (partial, shape((NXY, PAIR, ROWS + ROWS // 2, LANES),...  4.83 us
    ppermute x1, starting transfers between devices, body(): theirs = lax.ppermute(their, 'dp', SWAP)  4.03 us
    ppermute x1, starting transfers between devices, body(): received = lax.ppermute(other, 'dp', SWAP)  3.33 us
    pallas_call x1, Pallas kernels, body(): call(functools.partial(mine_kernel, share), (shape((NXY, PAIR, F0 - FA +...  2.72 us
  transfers between devices with their start and end apart: 3, of which 2 were waited for; matrix products, arithmetic and copies ran while one was open for 0% of the time, Pallas kernels for 5%

profile of v13, /device:TPU:1, one launch (start us, length us, event | category | flops | bytes accessed | tf_op | source)
XLA Modules:
  0.0 71.6 jit_solution(3020318614429236239)
XLA Ops:
  0.6 0.0 copy-start
  0.6 4.8 %grams_theirs.1 = (bf16[16,2,120,128]{3,2,1,0:T(8,128)(2,1)S(1)}, bf16[16,2,24,128]{3,2,1,0:T(8,128)(2,1)S(1)}, bf16[1024,512]{1,0:T(8,128)(2,1)S(1)}, bf16[1024...) custom-call(s32[1]{0:T(128)} %bitcast.core, ...), custom_call_target="tpu_custom_call" | custom-call | flops 1610612736 | bytes 5242880 | tf_op jit(solution)/shard_map/grams_theirs/pallas_call | solution.py:465
  5.5 3.3 %collective-permute-start = (bf16[16,2,120,128]{3,2,1,0:T(8,128)(2,1)S(1)}, bf16[16,2,120,128]{3,2,1,0:T(8,128)(2,1)S(1)}, u32[]{:S(2)}, u32[]{:S(2)}) collective-permute-start(bf16[16,2,120,128]{3,2,1,0:T(8,128)(2,1)S(1)} %get-tuple-element.31), channel_id=1, source_target_pairs={{0,1},{1,0},{2,3},{3,2},{4,5},{5,4},{6,7},{7,6},{8,9},{9,8},{10,11... | collective-permute-start | bytes 2949128 | tf_op jit(solution)/shard_map/ppermute | solution.py:483
  8.8 0.0 copy-done
  8.8 2.7 %factors_mine.1 = (bf16[16,2,40,128]{3,2,1,0:T(8,128)(2,1)S(1)}, f32[2,512]{1,0:T(2,128)S(1)}, f32[2,512]{1,0:T(2,128)S(1)}, bf16[512,512]{1,0:T(8,128)(2,1)S(1)...) custom-call(s32[1]{0:T(128)} %bitcast.core, s32[1]{0:T(128)} %bitcast.1.chip, ...), custom_call_target="tpu_custom_call" | custom-call | flops 1610612736 | bytes 4194304 | tf_op jit(solution)/shard_map/factors_mine/pallas_call | solution.py:485
  11.5 0.1 collective-permute-start.1
  11.7 0.7 %gradient_mine.1.gradient = bf16[16,2,64,128]{3,2,1,0:T(8,128)(2,1)S(1)} custom-call(bf16[1024,512]{1,0:T(8,128)(2,1)S(1)} %get-tuple-element.24.x0, bf16[1024,512]{1,0:T(8,128)(2,1)S(1)} %get-tuple-element.25.x1), custom_call_target="tpu_custom_call" | custom-call | flops 536870912 | bytes 4194304 | tf_op jit(solution)/shard_map/gradient_mine/pallas_call | solution.py:503
  12.4 0.4 collective-permute-done.1.sent_lam
  12.8 0.0 collective-permute-done.received
  12.8 0.3 chip_sum.1
  13.1 23.0 %all_to_all.15.parts = bf16[32,120,128]{2,1,0:T(8,128)(2,1)S(1)} all-to-all(bf16[32,120,128]{2,1,0:T(8,128)(2,1)S(1)} %bitcast.7), channel_id=1, replica_groups={{0,2,16,18,32,34,48,50,64,66,80,82,96,98,112,114,128,130,144,146,160,16..., dimensions={0} | all-to-all | bytes 1966080 | tf_op jit(solution)/shard_map/wide_sum/all_to_all | solution.py:440
  36.0 0.3 pack.1
  36.4 14.2 %all_to_all.16.got.packed = bf16[4,112,128]{2,1,0:T(8,128)(2,1)S(1)} all-to-all(bf16[4,112,128]{2,1,0:T(8,128)(2,1)S(1)} %pack.1), channel_id=1, replica_groups={{0,4,8,12},{1,5,9,13},{2,6,10,14},{3,7,11,15},{16,20,24,28},{17,21,25,2..., dimensions={0} | all-to-all | bytes 229376 | tf_op jit(solution)/shard_map/deep_sum/all_to_all | solution.py:440
  50.6 0.2 rotate.1
  50.8 14.1 %all_to_all.17.got = bf16[32,80,128]{2,1,0:T(8,128)(2,1)S(1)} all-to-all(bf16[32,80,128]{2,1,0:T(8,128)(2,1)S(1)} %rotate.1), channel_id=1, replica_groups={{0,2,16,18,32,34,48,50,64,66,80,82,96,98,112,114,128,130,144,146,160,16..., dimensions={0} | all-to-all | bytes 1310720 | tf_op jit(solution)/shard_map/gather/all_to_all | solution.py:440
  64.9 1.2 %solve.1 = (f32[16,512]{1,0:T(8,128)S(1)}, f32[16,512]{1,0:T(8,128)S(1)}) custom-call(s32[1]{0:T(128)} %bitcast.core, s32[1]{0:T(128)} %bitcast.1.chip, bf16[32,80,128]{2,1,0:T(8,128)(2,1)S(1)} %all_to_all.17.got, bf16[4,112,128]{2,1,0:T(8,128)(2,1)S(1)} %all_to_all.16.got.packed, bf16[512,512]{1,0:T(8,128)(2,1)S(1)} %get-tuple-element.37.basis_in_t, ...), custom_call_target="tpu_custom_call" | custom-call | tf_op jit(solution)/shard_map/solve/pallas_call | solution.py:529
  66.1 4.0 %collective-permute-start.2 = (f32[16,512]{1,0:T(8,128)S(1)}, f32[16,512]{1,0:T(8,128)S(1)}, u32[]{:S(2)}, u32[]{:S(2)}) collective-permute-start(f32[16,512]{1,0:T(8,128)S(1)} %get-tuple-element.41), channel_id=1, source_target_pairs={{0,1},{1,0},{2,3},{3,2},{4,5},{5,4},{6,7},{7,6},{8,9},{9,8},{10,11... | collective-permute-start | bytes 98312 | tf_op jit(solution)/shard_map/ppermute | solution.py:532
  70.1 0.9 %collective-permute-done.2.got = f32[16,512]{1,0:T(8,128)S(1)} collective-permute-done((f32[16,512]{1,0:T(8,128)S(1)}, f32[16,512]{1,0:T(8,128)S(1)}, u32[]{:S(2)}, u32[]{:S(2)}) %collective-permute-start.2) | collective-permute-done | bytes 32800 | tf_op jit(solution)/shard_map/ppermute | solution.py:532
  71.0 0.6 finish.1
Async XLA Ops:
  0.6 8.2 %copy-start = (f32[2,3,512]{2,0,1:T(2,128)S(1)}, f32[2,3,512]{2,0,1:T(2,128)}, u32[]{:S(2)}) copy-start(f32[2,3,512]{2,0,1:T(2,128)} %param.13) | copy-start | bytes 36868
  5.5 7.3 %collective-permute-start = (bf16[16,2,120,128]{3,2,1,0:T(8,128)(2,1)S(1)}, bf16[16,2,120,128]{3,2,1,0:T(8,128)(2,1)S(1)}, u32[]{:S(2)}, u32[]{:S(2)}) collective-permute-start(bf16[16,2,120,128]{3,2,1,0:T(8,128)(2,1)S(1)} %get-tuple-element.31), channel_id=1, source_target_pairs={{0,1},{1,0},{2,3},{3,2},{4,5},{5,4},{6,7},{7,6},{8,9},{9,8},{10,11... | collective-permute-start | bytes 2949128 | tf_op jit(solution)/shard_map/ppermute | solution.py:483
  11.5 1.3 %collective-permute-start.1 = (f32[2,512]{1,0:T(2,128)S(1)}, f32[2,512]{1,0:T(2,128)S(1)}, u32[]{:S(2)}, u32[]{:S(2)}) collective-permute-start(f32[2,512]{1,0:T(2,128)S(1)} %get-tuple-element.33), channel_id=1, source_target_pairs={{0,1},{1,0},{2,3},{3,2},{4,5},{5,4},{6,7},{7,6},{8,9},{9,8},{10,11... | collective-permute-start | bytes 12296 | tf_op jit(solution)/shard_map/ppermute | solution.py:501
  66.1 4.9 %collective-permute-start.2 = (f32[16,512]{1,0:T(8,128)S(1)}, f32[16,512]{1,0:T(8,128)S(1)}, u32[]{:S(2)}, u32[]{:S(2)}) collective-permute-start(f32[16,512]{1,0:T(8,128)S(1)} %get-tuple-element.41), channel_id=1, source_target_pairs={{0,1},{1,0},{2,3},{3,2},{4,5},{5,4},{6,7},{7,6},{8,9},{9,8},{10,11... | collective-permute-start | bytes 98312 | tf_op jit(solution)/shard_map/ppermute | solution.py:532

commit v14 on v11

--- a/solution.py
+++ b/solution.py
@@ -51,13 +51,14 @@
 CHUNKS = 2
 
 
-def call(kernel, outs, in_specs, scratch=(), limit=16, flops=0, moved=0):
+def call(kernel, outs, in_specs, scratch=(), limit=16, flops=0, moved=0, aliases=None):
     return pl.pallas_call(
         kernel,
         out_shape=outs,
         in_specs=in_specs,
         out_specs=jax.tree.map(lambda out: HBM if isinstance(out, pl.MemoryRef) else VMEM, outs),
         scratch_shapes=list(scratch),
+        input_output_aliases=aliases or {},
         compiler_params=pltpu.CompilerParams(vmem_limit_bytes=limit * MB),
         cost_estimate=pl.CostEstimate(flops=flops, bytes_accessed=moved, transcendentals=0),
     )
@@ -126,18 +127,16 @@
 
 
 def put(out, r, value, begin):
-    places = pl.ds(r * (BLOCK // BLK), BLOCK // BLK)
     for half, rows in enumerate(arrange(value)):
         for j in range(value.shape[1] // LANES):
-            out[places, half, pl.ds(begin + j * ROWS, ROWS), :] = rows[:, :, j * LANES : (j + 1) * LANES].astype(bf16)
+            out[r][:, half, pl.ds(begin + j * ROWS, ROWS), :] = rows[:, :, j * LANES : (j + 1) * LANES].astype(bf16)
 
 
 def put_folded(out, r, value, begin):
-    places = pl.ds(r * (BLOCK // BLK), BLOCK // BLK)
     for half, rows in enumerate(arrange(value)):
         upper, lower = rows[:, : ROWS // 2], pltpu.roll(rows[:, ROWS // 2 :], LANES // 2, 2)
         lane = lax.broadcasted_iota(jnp.int32, upper.shape, 2)
-        out[places, half, pl.ds(begin, ROWS // 2), :] = jnp.where(lane < LANES // 2, upper, lower).astype(bf16)
+        out[r][:, half, pl.ds(begin, ROWS // 2), :] = jnp.where(lane < LANES // 2, upper, lower).astype(bf16)
 
 
 def end_lanes(value):
@@ -180,7 +179,7 @@
 
 
 def theirs_kernel(
-    core, start, width, x0, xk, xv, out, spare, kept, keep, ahead, buf0, buf1, starts, widths, sem0, sem1, sem2, sem3
+    core, start, width, x0, xk, xv, out0, out1, spare0, spare1, kept, keep, ahead, buf0, buf1, starts, widths, sem0, sem1, sem2, sem3
 ):
     pick = 1 - core[0]
     small = [pltpu.make_async_copy(v, w, sem2.at[i]) for i, (v, w) in enumerate(((start, starts), (width, widths)))]
@@ -195,6 +194,7 @@
         if q == 0:
             copies1 = fetch_picked(pick, xk, xv, buf1, sem1)
         apply_mask(buf0, kept, keep, q)
+    out, spare = (out0, out1), (spare0, spare1)
     lefts, rests = zero_grams(pick, kept, out, spare)
     for copy in copies1:
         copy.wait()
@@ -204,16 +204,18 @@
         copy.wait()
 
 
-def mine_kernel(keep, x0, x1, out):
+def mine_kernel(keep, x0, x1, out0, out1):
     lefts = [x0[:, pl.ds(r * BLOCK, BLOCK)].T for r in range(D // BLOCK)]
-    picked_grams(lefts, x1, keep, None, out, F0)
-
-
-PIECES = 4
-
-
-def add_kernel(mine, spare, received, out, buf, sems):
-    size = NXY // PIECES
+    picked_grams(lefts, x1, keep, None, (out0, out1), F0)
+
+
+SIDES = D // BLOCK
+PIECES = 2
+
+
+def add_kernel(side, mine, spare, received, *rest):
+    out, buf, sems = rest[-3:]
+    size = NXY // SIDES // PIECES
     copies = []
     main, zero, last = slice(0, F0), slice(F0, FL), slice(FL, WROWS)
     for q in range(PIECES):
@@ -223,8 +225,8 @@
                 buf[i, j, zero] = spare[i, j, :ROWS] + received[i, j, zero]
                 ends = mine[i, j, F0:] + spare[i, j, ROWS:]
                 buf[i, j, last] = ends + received[i, j, last]
-        part = pl.ds(q * size, size)
-        copies.append(pltpu.make_async_copy(buf.at[part], out.at[part], sems.at[q]))
+        target = out.at[pl.ds(side * (NXY // SIDES) + q * size, size)]
+        copies.append(pltpu.make_async_copy(buf.at[pl.ds(q * size, size)], target, sems.at[q]))
         copies[q].start()
     for copy in copies:
         copy.wait()
@@ -451,14 +453,19 @@
     buf = pltpu.VMEM((tokens_here, D), bf16)
     sems = pltpu.SemaphoreType.DMA((CHUNKS,))
     pair = pltpu.SemaphoreType.DMA((2,))
-    partial = shape((NXY, PAIR, WROWS, LANES), bf16)
+    side_rows = NXY // SIDES
+    partial = shape((side_rows, PAIR, WROWS, LANES), bf16)
+    spare_shape = shape((side_rows, PAIR, ROWS + ROWS // 2, LANES), bf16)
+    mine_shape = shape((side_rows, PAIR, F0 + ROWS // 2, LANES), bf16)
     work = 6 * D * D * tokens_here
     with jax.named_scope("grams_theirs"):
-        other, spare, kept, keep, ahead = call(
+        *sent, spare0, spare1, kept, keep, ahead = call(
             theirs_kernel,
             (
                 partial,
-                shape((NXY, PAIR, ROWS + ROWS // 2, LANES), bf16),
+                partial,
+                spare_shape,
+                spare_shape,
                 shape((tokens_here, D), bf16),
                 shape((tokens_here, LANES), bf16),
                 shape((tokens_here, D), bf16),
@@ -468,22 +475,24 @@
             flops=work,
             moved=4 * MB,
         )(core[None], *masks, frames, keys, vals)
-    received = lax.ppermute(other, "dp", SWAP)
+    received = [lax.ppermute(part, "dp", SWAP) for part in sent]
     with jax.named_scope("grams_mine"):
         mine = call(
             mine_kernel,
-            shape((NXY, PAIR, F0 + ROWS // 2, LANES), bf16),
+            (mine_shape, mine_shape),
             [VMEM] * 3,
             flops=work,
             moved=4 * MB,
         )(keep, kept, ahead)
-    with jax.named_scope("chip_sum"):
+    whole = pltpu.HBM((NXY, PAIR, WROWS, LANES), bf16)
+    room = [pltpu.VMEM(partial.shape, bf16), pltpu.SemaphoreType.DMA((PIECES,))]
+    with jax.named_scope("chip_sum0"):
+        chip = call(functools.partial(add_kernel, 0), whole, [VMEM] * 3, room, moved=MB)(mine[0], spare0, received[0])
+    with jax.named_scope("chip_sum1"):
         chip = call(
-            add_kernel,
-            pltpu.HBM(partial.shape, bf16),
-            [VMEM] * 3,
-            [pltpu.VMEM(partial.shape, bf16), pltpu.SemaphoreType.DMA((PIECES,))],
-        )(mine, spare, received).reshape(WIDE, WROWS, LANES)
+            functools.partial(add_kernel, 1), whole, [VMEM] * 3 + [HBM], room, moved=MB, aliases={3: 0}
+        )(mine[1], spare1, received[1], chip)
+        chip = chip.reshape(WIDE, WROWS, LANES)
     with jax.named_scope("wide_sum"):
         parts = exchange(chip, WIDE_GROUPS)
 

time: 70.4 us -> 70.4 us (level)
  waiting for transfers between devices: 10.7 us -> 9.86 us
    ppermute x1 -> x2, waiting for transfers between devices: 0.75 us -> 0.01 us  [body(): received = [lax.ppermute(part, 'dp', SWAP) for part in sent]]
    pallas_call x3 -> x4, Pallas kernels: 6.25 us -> 6.96 us  [the longest x1 3.78 us: body(): call(theirs_kernel, (partial, partial, spare_shape, spare_shape, shape((t...]
    ppermute x1 -> x2, starting transfers between devices: 3.33 us -> 3.43 us  [body(): received = [lax.ppermute(part, 'dp', SWAP) for part in sent]]
  transfers between devices with their start and end apart: 4 -> 5, of which waited for: 4 -> 3; matrix products, arithmetic and copies ran while one was open for 1% -> 1% of each run, Pallas kernels for 7% -> 9%
where the time goes in v14:
time: 70.4 us; the launch traced here: 70.1 us
  blocking collectives  28.7 us (41%)
  starting transfers between devices  15 us (21%)
  Pallas kernels  13 us (18%)
  waiting for transfers between devices  9.86 us (14%)
  local copies, waits for them, and re-layouts  1.62 us (2%)
  matrix products  0.99 us (1%)
  between operations  0.8 us (1%)
    all_to_all x2, blocking collectives, exchange(): lax.all_to_all(value, 'dp', 0, 0, axis_index_groups=groups, tiled=True)  28.7 us
    all_to_all x1, waiting for transfers between devices, exchange(): lax.all_to_all(value, 'dp', 0, 0, axis_index_groups=groups, tiled=True)  8.17 us
    all_to_all x1, starting transfers between devices, exchange(): lax.all_to_all(value, 'dp', 0, 0, axis_index_groups=groups, tiled=True)  6.8 us
    ppermute x1, starting transfers between devices, body(): theirs = lax.ppermute(their, 'dp', SWAP)  4.04 us
    pallas_call x1, Pallas kernels, body(): call(theirs_kernel, (partial, partial, spare_shape, spare_shape, shape((t...  3.78 us
    pallas_call x1, Pallas kernels, body(): call(functools.partial(lam_kernel, share), (lam_shape, lam_shape, square,...  3.75 us
    ppermute x2, starting transfers between devices, body(): received = [lax.ppermute(part, 'dp', SWAP) for part in sent]  3.43 us
    unnamed x12, local copies, waits for them, and re-layouts  1.62 us
  transfers between devices with their start and end apart: 5, of which 3 were waited for; matrix products, arithmetic and copies ran while one was open for 1% of the time, Pallas kernels for 9%

profile of v14, /device:TPU:1, one launch (start us, length us, event | category | flops | bytes accessed | tf_op | source)
XLA Modules:
  0.0 70.1 jit_solution(4937175239074090129)
XLA Ops:
  0.6 3.8 %grams_theirs.1 = (bf16[8,2,120,128]{3,2,1,0:T(8,128)(2,1)S(1)}, bf16[8,2,120,128]{3,2,1,0:T(8,128)(2,1)S(1)}, bf16[8,2,24,128]{3,2,1,0:T(8,128)(2,1)S(1)}, bf16...) custom-call(s32[1]{0:T(128)} %bitcast.core, ...), custom_call_target="tpu_custom_call" | custom-call | flops 1610612736 | bytes 4194304 | tf_op jit(solution)/shard_map/grams_theirs/pallas_call | solution.py:462
  4.4 3.3 %collective-permute-start.1 = (bf16[8,2,120,128]{3,2,1,0:T(8,128)(2,1)S(1)}, bf16[8,2,120,128]{3,2,1,0:T(8,128)(2,1)S(1)}, u32[]{:S(2)}, u32[]{:S(2)}) collective-permute-start(bf16[8,2,120,128]{3,2,1,0:T(8,128)(2,1)S(1)} %get-tuple-element.31), channel_id=1, source_target_pairs={{0,1},{1,0},{2,3},{3,2},{4,5},{5,4},{6,7},{7,6},{8,9},{9,8},{10,11... | collective-permute-start | bytes 1474568 | tf_op jit(solution)/shard_map/ppermute | solution.py:478
  7.8 0.1 collective-permute-start
  7.9 1.4 %grams_mine.1 = (bf16[8,2,104,128]{3,2,1,0:T(8,128)(2,1)S(1)}, bf16[8,2,104,128]{3,2,1,0:T(8,128)(2,1)S(1)}) custom-call(bf16[1024,128]{1,0:T(8,128)(2,1)S(1)} %get-tuple-element.23.keep, bf16[1024,512]{1,0:T(8,128)(2,1)S(1)} %get-tuple-element.24.x0, bf16[1024,512]{1,0:T(8,128)(2,1)S(1)} %get-tuple-element.25.x1), custom_call_target="tpu_custom_call" | custom-call | flops 1610612736 | bytes 4194304 | tf_op jit(solution)/shard_map/grams_mine/pallas_call | solution.py:480
  9.3 0.0 collective-permute-done.1.received
  9.3 0.9 %chip_sum0.1.rest_0_ = bf16[16,2,120,128]{3,2,1,0:T(8,128)(2,1)} custom-call(bf16[8,2,104,128]{3,2,1,0:T(8,128)(2,1)S(1)} %get-tuple-element.29.mine, bf16[8,2,24,128]{3,2,1,0:T(8,128)(2,1)S(1)} %get-tuple-element.30.spare, bf16[8,2,120,128]{3,2,1,0:T(8,128)(2,1)S(1)} %collective-permute-done.1.received), custom_call_target="tpu_custom_call" | custom-call | bytes 1048576 | tf_op jit(solution)/shard_map/chip_sum0/pallas_call | solution.py:490
  10.2 0.0 collective-permute-done.received
  10.2 0.9 %chip_sum1.1 = bf16[16,2,120,128]{3,2,1,0:T(8,128)(2,1)} custom-call(bf16[8,2,104,128]{3,2,1,0:T(8,128)(2,1)S(1)} %get-tuple-element.26.mine, bf16[8,2,24,128]{3,2,1,0:T(8,128)(2,1)S(1)} %get-tuple-element.27.spare, bf16[8,2,120,128]{3,2,1,0:T(8,128)(2,1)S(1)} %collective-permute-done.received, ...), custom_call_target="tpu_custom_call", output_to_operand_aliasing={{}: (3, {})} | custom-call | bytes 1048576 | tf_op jit(solution)/shard_map/chip_sum1/pallas_call | solution.py:492
  11.1 0.0 copy-start
  11.1 0.0 copy-start.5
  11.1 6.8 %all-to-all-start = ((bf16[32,120,128]{2,1,0:T(8,128)(2,1)}), bf16[32,120,128]{2,1,0:T(8,128)(2,1)S(1)}, u32[]{:S(2)}, u32[]{:S(2)}) async-start(bf16[32,120,128]{2,1,0:T(8,128)(2,1)} %bitcast.41), calls=%async_computation | async-start | bytes 1966080 | tf_op jit(solution)/shard_map/wide_sum/all_to_all | solution.py:436
  17.9 0.0 copy-done
  17.9 0.0 copy-done.5
  17.9 0.3 fusion.1
  18.3 0.3 fusion.2
  18.6 0.3 fusion
  19.0 3.8 %lam.1 = (f32[2,512]{1,0:T(2,128)S(1)}, f32[2,512]{1,0:T(2,128)S(1)}, bf16[512,512]{1,0:T(8,128)(2,1)S(1)}, bf16[512,512]{1,0:T(8,128)(2,1)S(1)}, bf16[512,512]{...) custom-call(s32[1]{0:T(128)} %bitcast.core, s32[1]{0:T(128)} %bitcast.1.chip, bf16[32,120,128]{2,1,0:T(8,128)(2,1)} %bitcast.42, ...), custom_call_target="tpu_custom_call" | custom-call | flops 1610612736 | bytes 4194304 | tf_op jit(solution)/shard_map/lam/pallas_call | solution.py:501
  22.7 0.8 %copy-done.1 = bf16[512,512]{1,0:T(8,128)(2,1)} copy-done((bf16[512,512]{1,0:T(8,128)(2,1)}, bf16[512,512]{1,0:T(8,128)(2,1)S(1)}, u32[]{:S(2)}) %copy-start.1) | copy-done | bytes 524312
  23.5 0.8 %copy-done.3 = bf16[512,512]{1,0:T(8,128)(2,1)} copy-done((bf16[512,512]{1,0:T(8,128)(2,1)}, bf16[512,512]{1,0:T(8,128)(2,1)S(1)}, u32[]{:S(2)}) %copy-start.3) | copy-done | bytes 524312
  24.3 0.8 %collective-permute-start.2 = (f32[2,512]{1,0:T(2,128)S(1)}, f32[2,512]{1,0:T(2,128)S(1)}, u32[]{:S(2)}, u32[]{:S(2)}) collective-permute-start(f32[2,512]{1,0:T(2,128)S(1)} %get-tuple-element.45), channel_id=1, source_target_pairs={{0,1},{1,0},{2,3},{3,2},{4,5},{5,4},{6,7},{7,6},{8,9},{9,8},{10,11... | collective-permute-start | bytes 12296 | tf_op jit(solution)/shard_map/ppermute | solution.py:516
  25.1 0.8 %collective-permute-done.2.send_lam = f32[2,512]{1,0:T(2,128)S(1)} collective-permute-done((f32[2,512]{1,0:T(2,128)S(1)}, f32[2,512]{1,0:T(2,128)S(1)}, u32[]{:S(2)}, u32[]{:S(2)}) %collective-permute-start.2) | collective-permute-done | bytes 4128 | tf_op jit(solution)/shard_map/ppermute | solution.py:516
  25.9 8.2 %all-to-all-done.parts = bf16[32,120,128]{2,1,0:T(8,128)(2,1)S(1)} async-done(((bf16[32,120,128]{2,1,0:T(8,128)(2,1)}), bf16[32,120,128]{2,1,0:T(8,128)(2,1)S(1)}, u32[]{:S(2)}, u32[]{:S(2)}) %all-to-all-start) | async-done | bytes 983072 | tf_op jit(solution)/shard_map/wide_sum/all_to_all | solution.py:436
  34.1 0.3 pack.1
  34.5 0.0 copy-start.2
  34.5 0.0 copy-start.4
  34.5 14.3 %all_to_all.15.got.packed = bf16[4,112,128]{2,1,0:T(8,128)(2,1)S(1)} all-to-all(bf16[4,112,128]{2,1,0:T(8,128)(2,1)S(1)} %pack.1), channel_id=1, replica_groups={{0,4,8,12},{1,5,9,13},{2,6,10,14},{3,7,11,15},{16,20,24,28},{17,21,25,2..., dimensions={0} | all-to-all | bytes 229376 | tf_op jit(solution)/shard_map/deep_sum/all_to_all | solution.py:436
  48.8 0.2 rotate.1
  49.1 14.4 %all_to_all.16.got = bf16[32,80,128]{2,1,0:T(8,128)(2,1)S(1)} all-to-all(bf16[32,80,128]{2,1,0:T(8,128)(2,1)S(1)} %rotate.1), channel_id=1, replica_groups={{0,2,16,18,32,34,48,50,64,66,80,82,96,98,112,114,128,130,144,146,160,16..., dimensions={0} | all-to-all | bytes 1310720 | tf_op jit(solution)/shard_map/gather/all_to_all | solution.py:436
  63.4 1.1 %solve.1 = (f32[16,512]{1,0:T(8,128)S(1)}, f32[16,512]{1,0:T(8,128)S(1)}) custom-call(s32[1]{0:T(128)} %bitcast.core, s32[1]{0:T(128)} %bitcast.1.chip, bf16[32,80,128]{2,1,0:T(8,128)(2,1)S(1)} %all_to_all.16.got, bf16[4,112,128]{2,1,0:T(8,128)(2,1)S(1)} %all_to_all.15.got.packed, bf16[512,512]{1,0:T(8,128)(2,1)S(1)} %copy-done.2, ...), custom_call_target="tpu_custom_call" | custom-call | tf_op jit(solution)/shard_map/solve/pallas_call | solution.py:528
  64.6 4.0 %collective-permute-start.3 = (f32[16,512]{1,0:T(8,128)S(1)}, f32[16,512]{1,0:T(8,128)S(1)}, u32[]{:S(2)}, u32[]{:S(2)}) collective-permute-start(f32[16,512]{1,0:T(8,128)S(1)} %get-tuple-element.39), channel_id=1, source_target_pairs={{0,1},{1,0},{2,3},{3,2},{4,5},{5,4},{6,7},{7,6},{8,9},{9,8},{10,11... | collective-permute-start | bytes 98312 | tf_op jit(solution)/shard_map/ppermute | solution.py:531
  68.6 0.9 %collective-permute-done.3.got = f32[16,512]{1,0:T(8,128)S(1)} collective-permute-done((f32[16,512]{1,0:T(8,128)S(1)}, f32[16,512]{1,0:T(8,128)S(1)}, u32[]{:S(2)}, u32[]{:S(2)}) %collective-permute-start.3) | collective-permute-done | bytes 32800 | tf_op jit(solution)/shard_map/ppermute | solution.py:531
  69.5 0.6 finish.1
  (8 shorter events, 0.0 us)
Async XLA Ops:
  4.4 4.9 %collective-permute-start.1 = (bf16[8,2,120,128]{3,2,1,0:T(8,128)(2,1)S(1)}, bf16[8,2,120,128]{3,2,1,0:T(8,128)(2,1)S(1)}, u32[]{:S(2)}, u32[]{:S(2)}) collective-permute-start(bf16[8,2,120,128]{3,2,1,0:T(8,128)(2,1)S(1)} %get-tuple-element.31), channel_id=1, source_target_pairs={{0,1},{1,0},{2,3},{3,2},{4,5},{5,4},{6,7},{7,6},{8,9},{9,8},{10,11... | collective-permute-start | bytes 1474568 | tf_op jit(solution)/shard_map/ppermute | solution.py:478
  7.8 2.4 %collective-permute-start = (bf16[8,2,120,128]{3,2,1,0:T(8,128)(2,1)S(1)}, bf16[8,2,120,128]{3,2,1,0:T(8,128)(2,1)S(1)}, u32[]{:S(2)}, u32[]{:S(2)}) collective-permute-start(bf16[8,2,120,128]{3,2,1,0:T(8,128)(2,1)S(1)} %get-tuple-element.28), channel_id=1, source_target_pairs={{0,1},{1,0},{2,3},{3,2},{4,5},{5,4},{6,7},{7,6},{8,9},{9,8},{10,11... | collective-permute-start | bytes 1474568 | tf_op jit(solution)/shard_map/ppermute | solution.py:478
  11.1 6.8 %copy-start = (bf16[3,512,512]{2,1,0:T(8,128)(2,1)S(1)}, bf16[3,512,512]{2,1,0:T(8,128)(2,1)}, u32[]{:S(2)}) copy-start(bf16[3,512,512]{2,1,0:T(8,128)(2,1)} %bases.1) | copy-start | bytes 4718596
  11.1 6.9 %copy-start.5 = (f32[2,3,512]{2,0,1:T(2,128)S(1)}, f32[2,3,512]{2,0,1:T(2,128)}, u32[]{:S(2)}) copy-start(f32[2,3,512]{2,0,1:T(2,128)} %param.13) | copy-start | bytes 36868
  11.1 23.0 %all-to-all-start = ((bf16[32,120,128]{2,1,0:T(8,128)(2,1)}), bf16[32,120,128]{2,1,0:T(8,128)(2,1)S(1)}, u32[]{:S(2)}, u32[]{:S(2)}) async-start(bf16[32,120,128]{2,1,0:T(8,128)(2,1)} %bitcast.41), calls=%async_computation | async-start | bytes 1966080 | tf_op jit(solution)/shard_map/wide_sum/all_to_all | solution.py:436
  22.7 0.8 %copy-start.1 = (bf16[512,512]{1,0:T(8,128)(2,1)}, bf16[512,512]{1,0:T(8,128)(2,1)S(1)}, u32[]{:S(2)}) copy-start(bf16[512,512]{1,0:T(8,128)(2,1)S(1)} %get-tuple-element.35.basis_in_t) | copy-start | bytes 1572868
  23.5 0.8 %copy-start.3 = (bf16[512,512]{1,0:T(8,128)(2,1)}, bf16[512,512]{1,0:T(8,128)(2,1)S(1)}, u32[]{:S(2)}) copy-start(bf16[512,512]{1,0:T(8,128)(2,1)S(1)} %get-tuple-element.37.mirror) | copy-start | bytes 1572868
  24.3 1.6 %collective-permute-start.2 = (f32[2,512]{1,0:T(2,128)S(1)}, f32[2,512]{1,0:T(2,128)S(1)}, u32[]{:S(2)}, u32[]{:S(2)}) collective-permute-start(f32[2,512]{1,0:T(2,128)S(1)} %get-tuple-element.45), channel_id=1, source_target_pairs={{0,1},{1,0},{2,3},{3,2},{4,5},{5,4},{6,7},{7,6},{8,9},{9,8},{10,11... | collective-permute-start | bytes 12296 | tf_op jit(solution)/shard_map/ppermute | solution.py:516
  34.5 29.0 %copy-start.2 = (bf16[512,512]{1,0:T(8,128)(2,1)S(1)}, bf16[512,512]{1,0:T(8,128)(2,1)}, u32[]{:S(2)}) copy-start(bf16[512,512]{1,0:T(8,128)(2,1)} %copy-done.1) | copy-start | bytes 1572868
  34.5 29.0 %copy-start.4 = (bf16[512,512]{1,0:T(8,128)(2,1)S(1)}, bf16[512,512]{1,0:T(8,128)(2,1)}, u32[]{:S(2)}) copy-start(bf16[512,512]{1,0:T(8,128)(2,1)} %copy-done.3) | copy-start | bytes 1572868
  64.6 4.9 %collective-permute-start.3 = (f32[16,512]{1,0:T(8,128)S(1)}, f32[16,512]{1,0:T(8,128)S(1)}, u32[]{:S(2)}, u32[]{:S(2)}) collective-permute-start(f32[16,512]{1,0:T(8,128)S(1)} %get-tuple-element.39), channel_id=1, source_target_pairs={{0,1},{1,0},{2,3},{3,2},{4,5},{5,4},{6,7},{7,6},{8,9},{9,8},{10,11... | collective-permute-start | bytes 98312 | tf_op jit(solution)/shard_map/ppermute | solution.py:531

commit v15 on v14

--- a/solution.py
+++ b/solution.py
@@ -51,14 +51,13 @@
 CHUNKS = 2
 
 
-def call(kernel, outs, in_specs, scratch=(), limit=16, flops=0, moved=0, aliases=None):
+def call(kernel, outs, in_specs, scratch=(), limit=16, flops=0, moved=0):
     return pl.pallas_call(
         kernel,
         out_shape=outs,
         in_specs=in_specs,
         out_specs=jax.tree.map(lambda out: HBM if isinstance(out, pl.MemoryRef) else VMEM, outs),
         scratch_shapes=list(scratch),
-        input_output_aliases=aliases or {},
         compiler_params=pltpu.CompilerParams(vmem_limit_bytes=limit * MB),
         cost_estimate=pl.CostEstimate(flops=flops, bytes_accessed=moved, transcendentals=0),
     )
@@ -213,21 +212,30 @@
 PIECES = 2
 
 
-def add_kernel(side, mine, spare, received, *rest):
-    out, buf, sems = rest[-3:]
-    size = NXY // SIDES // PIECES
-    copies = []
+def add_rows(mine, spare, received, out, blocks):
     main, zero, last = slice(0, F0), slice(F0, FL), slice(FL, WROWS)
+    for i in blocks:
+        for j in range(PAIR):
+            out[i, j, main] = mine[i, j, main] + received[i, j, main]
+            out[i, j, zero] = spare[i, j, :ROWS] + received[i, j, zero]
+            ends = mine[i, j, F0:] + spare[i, j, ROWS:]
+            out[i, j, last] = ends + received[i, j, last]
+
+
+def add_first_kernel(mine, spare, received, out):
+    add_rows(mine, spare, received, out, range(NXY // SIDES))
+
+
+def add_second_kernel(first, mine, spare, received, out, buf, sems):
+    count = NXY // SIDES
+    size = count // PIECES
+    copies = [pltpu.make_async_copy(first, out.at[pl.ds(0, count)], sems.at[PIECES])]
+    copies[0].start()
     for q in range(PIECES):
-        for i in range(q * size, (q + 1) * size):
-            for j in range(PAIR):
-                buf[i, j, main] = mine[i, j, main] + received[i, j, main]
-                buf[i, j, zero] = spare[i, j, :ROWS] + received[i, j, zero]
-                ends = mine[i, j, F0:] + spare[i, j, ROWS:]
-                buf[i, j, last] = ends + received[i, j, last]
-        target = out.at[pl.ds(side * (NXY // SIDES) + q * size, size)]
+        add_rows(mine, spare, received, buf, range(q * size, (q + 1) * size))
+        target = out.at[pl.ds(count + q * size, size)]
         copies.append(pltpu.make_async_copy(buf.at[pl.ds(q * size, size)], target, sems.at[q]))
-        copies[q].start()
+        copies[-1].start()
     for copy in copies:
         copy.wait()
 
@@ -484,14 +492,16 @@
             flops=work,
             moved=4 * MB,
         )(keep, kept, ahead)
-    whole = pltpu.HBM((NXY, PAIR, WROWS, LANES), bf16)
-    room = [pltpu.VMEM(partial.shape, bf16), pltpu.SemaphoreType.DMA((PIECES,))]
     with jax.named_scope("chip_sum0"):
-        chip = call(functools.partial(add_kernel, 0), whole, [VMEM] * 3, room, moved=MB)(mine[0], spare0, received[0])
+        half = call(add_first_kernel, partial, [VMEM] * 3, moved=MB)(mine[0], spare0, received[0])
     with jax.named_scope("chip_sum1"):
         chip = call(
-            functools.partial(add_kernel, 1), whole, [VMEM] * 3 + [HBM], room, moved=MB, aliases={3: 0}
-        )(mine[1], spare1, received[1], chip)
+            add_second_kernel,
+            pltpu.HBM((NXY, PAIR, WROWS, LANES), bf16),
+            [VMEM] * 4,
+            [pltpu.VMEM(partial.shape, bf16), pltpu.SemaphoreType.DMA((PIECES + 1,))],
+            moved=MB,
+        )(half, mine[1], spare1, received[1])
         chip = chip.reshape(WIDE, WROWS, LANES)
     with jax.named_scope("wide_sum"):
         parts = exchange(chip, WIDE_GROUPS)

time: 70.4 us -> 70.3 us (level)
  transfers between devices with their start and end apart: 5 -> 5, of which waited for: 3 -> 4; matrix products, arithmetic and copies ran while one was open for 1% -> 1% of each run, Pallas kernels for 9% -> 8%
where the time goes in v15:
time: 70.3 us; the launch traced here: 70 us
  blocking collectives  28.7 us (41%)
  starting transfers between devices  15 us (21%)
  Pallas kernels  12.4 us (18%)
  waiting for transfers between devices  10.5 us (15%)
  local copies, waits for them, and re-layouts  1.62 us (2%)
  matrix products  0.99 us (1%)
  between operations  0.8 us (1%)
    all_to_all x2, blocking collectives, exchange(): lax.all_to_all(value, 'dp', 0, 0, axis_index_groups=groups, tiled=True)  28.7 us
    all_to_all x1, waiting for transfers between devices, exchange(): lax.all_to_all(value, 'dp', 0, 0, axis_index_groups=groups, tiled=True)  8.25 us
    all_to_all x1, starting transfers between devices, exchange(): lax.all_to_all(value, 'dp', 0, 0, axis_index_groups=groups, tiled=True)  6.8 us
    ppermute x1, starting transfers between devices, body(): theirs = lax.ppermute(their, 'dp', SWAP)  4.04 us
    pallas_call x1, Pallas kernels, body(): call(theirs_kernel, (partial, partial, spare_shape, spare_shape, shape((t...  3.78 us
    pallas_call x1, Pallas kernels, body(): call(functools.partial(lam_kernel, share), (lam_shape, lam_shape, square,...  3.75 us
    ppermute x2, starting transfers between devices, body(): received = [lax.ppermute(part, 'dp', SWAP) for part in sent]  3.43 us
    unnamed x12, local copies, waits for them, and re-layouts  1.62 us
  transfers between devices with their start and end apart: 5, of which 4 were waited for; matrix products, arithmetic and copies ran while one was open for 1% of the time, Pallas kernels for 8%

profile of v15, /device:TPU:1, one launch (start us, length us, event | category | flops | bytes accessed | tf_op | source)
XLA Modules:
  0.0 70.0 jit_solution(2518775984727706025)
XLA Ops:
  0.6 3.8 %grams_theirs.1 = (bf16[8,2,120,128]{3,2,1,0:T(8,128)(2,1)S(1)}, bf16[8,2,120,128]{3,2,1,0:T(8,128)(2,1)S(1)}, bf16[8,2,24,128]{3,2,1,0:T(8,128)(2,1)S(1)}, bf16...) custom-call(s32[1]{0:T(128)} %bitcast.core, ...), custom_call_target="tpu_custom_call" | custom-call | flops 1610612736 | bytes 4194304 | tf_op jit(solution)/shard_map/grams_theirs/pallas_call | solution.py:470
  4.4 3.3 %collective-permute-start = (bf16[8,2,120,128]{3,2,1,0:T(8,128)(2,1)S(1)}, bf16[8,2,120,128]{3,2,1,0:T(8,128)(2,1)S(1)}, u32[]{:S(2)}, u32[]{:S(2)}) collective-permute-start(bf16[8,2,120,128]{3,2,1,0:T(8,128)(2,1)S(1)} %get-tuple-element.28), channel_id=1, source_target_pairs={{0,1},{1,0},{2,3},{3,2},{4,5},{5,4},{6,7},{7,6},{8,9},{9,8},{10,11... | collective-permute-start | bytes 1474568 | tf_op jit(solution)/shard_map/ppermute | solution.py:486
  7.8 0.1 collective-permute-start.1
  7.9 1.4 %grams_mine.1 = (bf16[8,2,104,128]{3,2,1,0:T(8,128)(2,1)S(1)}, bf16[8,2,104,128]{3,2,1,0:T(8,128)(2,1)S(1)}) custom-call(bf16[1024,128]{1,0:T(8,128)(2,1)S(1)} %get-tuple-element.23.keep, bf16[1024,512]{1,0:T(8,128)(2,1)S(1)} %get-tuple-element.24.x0, bf16[1024,512]{1,0:T(8,128)(2,1)S(1)} %get-tuple-element.25.x1), custom_call_target="tpu_custom_call" | custom-call | flops 1610612736 | bytes 4194304 | tf_op jit(solution)/shard_map/grams_mine/pallas_call | solution.py:488
  9.3 0.0 collective-permute-done.received
  9.3 0.1 chip_sum0.1.first
  9.4 0.5 collective-permute-done.1.received
  9.9 1.0 %chip_sum1.1 = bf16[16,2,120,128]{3,2,1,0:T(8,128)(2,1)} custom-call(bf16[8,2,120,128]{3,2,1,0:T(8,128)(2,1)S(1)} %chip_sum0.1.first, bf16[8,2,104,128]{3,2,1,0:T(8,128)(2,1)S(1)} %get-tuple-element.29.mine, bf16[8,2,24,128]{3,2,1,0:T(8,128)(2,1)S(1)} %get-tuple-element.30.spare, bf16[8,2,120,128]{3,2,1,0:T(8,128)(2,1)S(1)} %collective-permute-done.1.received), custom_call_target="tpu_custom_call" | custom-call | bytes 1048576 | tf_op jit(solution)/shard_map/chip_sum1/pallas_call | solution.py:498
  10.9 0.0 copy-start
  10.9 0.0 copy-start.5
  11.0 6.8 %all-to-all-start = ((bf16[32,120,128]{2,1,0:T(8,128)(2,1)}), bf16[32,120,128]{2,1,0:T(8,128)(2,1)S(1)}, u32[]{:S(2)}, u32[]{:S(2)}) async-start(bf16[32,120,128]{2,1,0:T(8,128)(2,1)} %bitcast.41), calls=%async_computation | async-start | bytes 1966080 | tf_op jit(solution)/shard_map/wide_sum/all_to_all | solution.py:444
  17.8 0.0 copy-done
  17.8 0.0 copy-done.5
  17.8 0.3 fusion.1
  18.1 0.3 fusion.2
  18.5 0.3 fusion
  18.8 3.8 %lam.1 = (f32[2,512]{1,0:T(2,128)S(1)}, f32[2,512]{1,0:T(2,128)S(1)}, bf16[512,512]{1,0:T(8,128)(2,1)S(1)}, bf16[512,512]{1,0:T(8,128)(2,1)S(1)}, bf16[512,512]{...) custom-call(s32[1]{0:T(128)} %bitcast.core, s32[1]{0:T(128)} %bitcast.1.chip, bf16[32,120,128]{2,1,0:T(8,128)(2,1)} %bitcast.42, ...), custom_call_target="tpu_custom_call" | custom-call | flops 1610612736 | bytes 4194304 | tf_op jit(solution)/shard_map/lam/pallas_call | solution.py:511
  22.6 0.0 copy-start.1
  22.6 0.8 %copy-done.1 = bf16[512,512]{1,0:T(8,128)(2,1)} copy-done((bf16[512,512]{1,0:T(8,128)(2,1)}, bf16[512,512]{1,0:T(8,128)(2,1)S(1)}, u32[]{:S(2)}) %copy-start.1) | copy-done | bytes 524312
  23.4 0.8 %copy-done.3 = bf16[512,512]{1,0:T(8,128)(2,1)} copy-done((bf16[512,512]{1,0:T(8,128)(2,1)}, bf16[512,512]{1,0:T(8,128)(2,1)S(1)}, u32[]{:S(2)}) %copy-start.3) | copy-done | bytes 524312
  24.2 0.7 %collective-permute-start.2 = (f32[2,512]{1,0:T(2,128)S(1)}, f32[2,512]{1,0:T(2,128)S(1)}, u32[]{:S(2)}, u32[]{:S(2)}) collective-permute-start(f32[2,512]{1,0:T(2,128)S(1)} %get-tuple-element.45), channel_id=1, source_target_pairs={{0,1},{1,0},{2,3},{3,2},{4,5},{5,4},{6,7},{7,6},{8,9},{9,8},{10,11... | collective-permute-start | bytes 12296 | tf_op jit(solution)/shard_map/ppermute | solution.py:526
  25.0 0.8 %collective-permute-done.2.send_lam = f32[2,512]{1,0:T(2,128)S(1)} collective-permute-done((f32[2,512]{1,0:T(2,128)S(1)}, f32[2,512]{1,0:T(2,128)S(1)}, u32[]{:S(2)}, u32[]{:S(2)}) %collective-permute-start.2) | collective-permute-done | bytes 4128 | tf_op jit(solution)/shard_map/ppermute | solution.py:526
  25.8 8.2 %all-to-all-done.parts = bf16[32,120,128]{2,1,0:T(8,128)(2,1)S(1)} async-done(((bf16[32,120,128]{2,1,0:T(8,128)(2,1)}), bf16[32,120,128]{2,1,0:T(8,128)(2,1)S(1)}, u32[]{:S(2)}, u32[]{:S(2)}) %all-to-all-start) | async-done | bytes 983072 | tf_op jit(solution)/shard_map/wide_sum/all_to_all | solution.py:444
  34.0 0.3 pack.1
  34.4 0.0 copy-start.2
  34.4 14.4 %all_to_all.15.got.packed = bf16[4,112,128]{2,1,0:T(8,128)(2,1)S(1)} all-to-all(bf16[4,112,128]{2,1,0:T(8,128)(2,1)S(1)} %pack.1), channel_id=1, replica_groups={{0,4,8,12},{1,5,9,13},{2,6,10,14},{3,7,11,15},{16,20,24,28},{17,21,25,2..., dimensions={0} | all-to-all | bytes 229376 | tf_op jit(solution)/shard_map/deep_sum/all_to_all | solution.py:444
  48.8 0.2 rotate.1
  49.0 14.3 %all_to_all.16.got = bf16[32,80,128]{2,1,0:T(8,128)(2,1)S(1)} all-to-all(bf16[32,80,128]{2,1,0:T(8,128)(2,1)S(1)} %rotate.1), channel_id=1, replica_groups={{0,2,16,18,32,34,48,50,64,66,80,82,96,98,112,114,128,130,144,146,160,16..., dimensions={0} | all-to-all | bytes 1310720 | tf_op jit(solution)/shard_map/gather/all_to_all | solution.py:444
  63.3 1.1 %solve.1 = (f32[16,512]{1,0:T(8,128)S(1)}, f32[16,512]{1,0:T(8,128)S(1)}) custom-call(s32[1]{0:T(128)} %bitcast.core, s32[1]{0:T(128)} %bitcast.1.chip, bf16[32,80,128]{2,1,0:T(8,128)(2,1)S(1)} %all_to_all.16.got, bf16[4,112,128]{2,1,0:T(8,128)(2,1)S(1)} %all_to_all.15.got.packed, bf16[512,512]{1,0:T(8,128)(2,1)S(1)} %copy-done.2, ...), custom_call_target="tpu_custom_call" | custom-call | tf_op jit(solution)/shard_map/solve/pallas_call | solution.py:538
  64.5 4.0 %collective-permute-start.3 = (f32[16,512]{1,0:T(8,128)S(1)}, f32[16,512]{1,0:T(8,128)S(1)}, u32[]{:S(2)}, u32[]{:S(2)}) collective-permute-start(f32[16,512]{1,0:T(8,128)S(1)} %get-tuple-element.39), channel_id=1, source_target_pairs={{0,1},{1,0},{2,3},{3,2},{4,5},{5,4},{6,7},{7,6},{8,9},{9,8},{10,11... | collective-permute-start | bytes 98312 | tf_op jit(solution)/shard_map/ppermute | solution.py:541
  68.5 0.9 %collective-permute-done.3.got = f32[16,512]{1,0:T(8,128)S(1)} collective-permute-done((f32[16,512]{1,0:T(8,128)S(1)}, f32[16,512]{1,0:T(8,128)S(1)}, u32[]{:S(2)}, u32[]{:S(2)}) %collective-permute-start.3) | collective-permute-done | bytes 32800 | tf_op jit(solution)/shard_map/ppermute | solution.py:541
  69.4 0.6 finish.1
  (8 shorter events, 0.0 us)
Async XLA Ops:
  4.4 4.9 %collective-permute-start = (bf16[8,2,120,128]{3,2,1,0:T(8,128)(2,1)S(1)}, bf16[8,2,120,128]{3,2,1,0:T(8,128)(2,1)S(1)}, u32[]{:S(2)}, u32[]{:S(2)}) collective-permute-start(bf16[8,2,120,128]{3,2,1,0:T(8,128)(2,1)S(1)} %get-tuple-element.28), channel_id=1, source_target_pairs={{0,1},{1,0},{2,3},{3,2},{4,5},{5,4},{6,7},{7,6},{8,9},{9,8},{10,11... | collective-permute-start | bytes 1474568 | tf_op jit(solution)/shard_map/ppermute | solution.py:486
  7.8 2.2 %collective-permute-start.1 = (bf16[8,2,120,128]{3,2,1,0:T(8,128)(2,1)S(1)}, bf16[8,2,120,128]{3,2,1,0:T(8,128)(2,1)S(1)}, u32[]{:S(2)}, u32[]{:S(2)}) collective-permute-start(bf16[8,2,120,128]{3,2,1,0:T(8,128)(2,1)S(1)} %get-tuple-element.31), channel_id=1, source_target_pairs={{0,1},{1,0},{2,3},{3,2},{4,5},{5,4},{6,7},{7,6},{8,9},{9,8},{10,11... | collective-permute-start | bytes 1474568 | tf_op jit(solution)/shard_map/ppermute | solution.py:486
  10.9 6.8 %copy-start = (bf16[3,512,512]{2,1,0:T(8,128)(2,1)S(1)}, bf16[3,512,512]{2,1,0:T(8,128)(2,1)}, u32[]{:S(2)}) copy-start(bf16[3,512,512]{2,1,0:T(8,128)(2,1)} %bases.1) | copy-start | bytes 4718596
  10.9 6.9 %copy-start.5 = (f32[2,3,512]{2,0,1:T(2,128)S(1)}, f32[2,3,512]{2,0,1:T(2,128)}, u32[]{:S(2)}) copy-start(f32[2,3,512]{2,0,1:T(2,128)} %param.13) | copy-start | bytes 36868
  11.0 23.1 %all-to-all-start = ((bf16[32,120,128]{2,1,0:T(8,128)(2,1)}), bf16[32,120,128]{2,1,0:T(8,128)(2,1)S(1)}, u32[]{:S(2)}, u32[]{:S(2)}) async-start(bf16[32,120,128]{2,1,0:T(8,128)(2,1)} %bitcast.41), calls=%async_computation | async-start | bytes 1966080 | tf_op jit(solution)/shard_map/wide_sum/all_to_all | solution.py:444
  22.6 0.8 %copy-start.1 = (bf16[512,512]{1,0:T(8,128)(2,1)}, bf16[512,512]{1,0:T(8,128)(2,1)S(1)}, u32[]{:S(2)}) copy-start(bf16[512,512]{1,0:T(8,128)(2,1)S(1)} %get-tuple-element.35.basis_in_t) | copy-start | bytes 1572868
  23.4 0.8 %copy-start.3 = (bf16[512,512]{1,0:T(8,128)(2,1)}, bf16[512,512]{1,0:T(8,128)(2,1)S(1)}, u32[]{:S(2)}) copy-start(bf16[512,512]{1,0:T(8,128)(2,1)S(1)} %get-tuple-element.37.mirror) | copy-start | bytes 1572868
  24.2 1.6 %collective-permute-start.2 = (f32[2,512]{1,0:T(2,128)S(1)}, f32[2,512]{1,0:T(2,128)S(1)}, u32[]{:S(2)}, u32[]{:S(2)}) collective-permute-start(f32[2,512]{1,0:T(2,128)S(1)} %get-tuple-element.45), channel_id=1, source_target_pairs={{0,1},{1,0},{2,3},{3,2},{4,5},{5,4},{6,7},{7,6},{8,9},{9,8},{10,11... | collective-permute-start | bytes 12296 | tf_op jit(solution)/shard_map/ppermute | solution.py:526
  34.4 28.9 %copy-start.2 = (bf16[512,512]{1,0:T(8,128)(2,1)S(1)}, bf16[512,512]{1,0:T(8,128)(2,1)}, u32[]{:S(2)}) copy-start(bf16[512,512]{1,0:T(8,128)(2,1)} %copy-done.1) | copy-start | bytes 1572868
  34.4 28.9 %copy-start.4 = (bf16[512,512]{1,0:T(8,128)(2,1)S(1)}, bf16[512,512]{1,0:T(8,128)(2,1)}, u32[]{:S(2)}) copy-start(bf16[512,512]{1,0:T(8,128)(2,1)} %copy-done.3) | copy-start | bytes 1572868
  64.5 4.9 %collective-permute-start.3 = (f32[16,512]{1,0:T(8,128)S(1)}, f32[16,512]{1,0:T(8,128)S(1)}, u32[]{:S(2)}, u32[]{:S(2)}) collective-permute-start(f32[16,512]{1,0:T(8,128)S(1)} %get-tuple-element.39), channel_id=1, source_target_pairs={{0,1},{1,0},{2,3},{3,2},{4,5},{5,4},{6,7},{7,6},{8,9},{9,8},{10,11... | collective-permute-start | bytes 98312 | tf_op jit(solution)/shard_map/ppermute | solution.py:541

commit v16 on v15

--- a/solution.py
+++ b/solution.py
@@ -404,12 +404,15 @@
     column = jnp.broadcast_to(lam_row(lam, 0), (8, D)).T[:, 0:1]
     column = jnp.broadcast_to(column, (D, LANES))
     curve = jnp.zeros((8, LANES), f32)
-    for j in range(GT):
-        rot = got[:, pl.ds(j * ROWS, ROWS), :].reshape(D, LANES)
-        rotated = dot(basis_in_t[...], rot)
-        low = (rotated / (column * lam[2 * j + 1 : 2 * j + 2] + damping)).astype(bf16)
-        scaled[:, pl.ds(j * LANES, LANES)] = low
-        curve = curve + jnp.sum((low.astype(f32) * rotated).reshape(D // 8, 8, LANES), axis=0)
+    for pair in range(0, GT, 2):
+        tiles = (pair, pair + 1)
+        rot = jnp.concatenate([got[:, pl.ds(j * ROWS, ROWS), :].reshape(D, LANES) for j in tiles], axis=1)
+        both = dot(basis_in_t[...], rot)
+        for j in tiles:
+            rotated = both[:, (j - pair) * LANES : (j - pair + 1) * LANES]
+            low = (rotated / (column * lam[2 * j + 1 : 2 * j + 2] + damping)).astype(bf16)
+            scaled[:, pl.ds(j * LANES, LANES)] = low
+            curve = curve + jnp.sum((low.astype(f32) * rotated).reshape(D // 8, 8, LANES), axis=0)
     curve = jnp.sum(jnp.sum(curve, axis=1, keepdims=True), axis=0, keepdims=True)
     back = dot(rows_in[...], scaled[...]).astype(bf16)
     prec = lax.dot_general(back, basis_out[...], (((1,), (1,)), ((), ())), preferred_element_type=f32)

time: 70.3 us -> 70.2 us (level)
  no operation moved by 1% of the time
where the time goes in v16:
time: 70.2 us; the launch traced here: 69.9 us
  blocking collectives  28.7 us (41%)
  starting transfers between devices  15 us (21%)
  Pallas kernels  12.3 us (18%)
  waiting for transfers between devices  10.5 us (15%)
  local copies, waits for them, and re-layouts  1.62 us (2%)
  matrix products  0.99 us (1%)
  between operations  0.8 us (1%)
    all_to_all x2, blocking collectives, exchange(): lax.all_to_all(value, 'dp', 0, 0, axis_index_groups=groups, tiled=True)  28.7 us
    all_to_all x1, waiting for transfers between devices, exchange(): lax.all_to_all(value, 'dp', 0, 0, axis_index_groups=groups, tiled=True)  8.25 us
    all_to_all x1, starting transfers between devices, exchange(): lax.all_to_all(value, 'dp', 0, 0, axis_index_groups=groups, tiled=True)  6.8 us
    ppermute x1, starting transfers between devices, body(): theirs = lax.ppermute(their, 'dp', SWAP)  4.04 us
    pallas_call x1, Pallas kernels, body(): call(theirs_kernel, (partial, partial, spare_shape, spare_shape, shape((t...  3.78 us
    pallas_call x1, Pallas kernels, body(): call(functools.partial(lam_kernel, share), (lam_shape, lam_shape, square,...  3.75 us
    ppermute x2, starting transfers between devices, body(): received = [lax.ppermute(part, 'dp', SWAP) for part in sent]  3.43 us
    unnamed x12, local copies, waits for them, and re-layouts  1.62 us
  transfers between devices with their start and end apart: 5, of which 4 were waited for; matrix products, arithmetic and copies ran while one was open for 1% of the time, Pallas kernels for 8%

profile of v16, /device:TPU:1, one launch (start us, length us, event | category | flops | bytes accessed | tf_op | source)
XLA Modules:
  0.0 69.9 jit_solution(8180178371362709273)
XLA Ops:
  0.6 3.8 %grams_theirs.1 = (bf16[8,2,120,128]{3,2,1,0:T(8,128)(2,1)S(1)}, bf16[8,2,120,128]{3,2,1,0:T(8,128)(2,1)S(1)}, bf16[8,2,24,128]{3,2,1,0:T(8,128)(2,1)S(1)}, bf16...) custom-call(s32[1]{0:T(128)} %bitcast.core, ...), custom_call_target="tpu_custom_call" | custom-call | flops 1610612736 | bytes 4194304 | tf_op jit(solution)/shard_map/grams_theirs/pallas_call | solution.py:473
  4.4 3.3 %collective-permute-start = (bf16[8,2,120,128]{3,2,1,0:T(8,128)(2,1)S(1)}, bf16[8,2,120,128]{3,2,1,0:T(8,128)(2,1)S(1)}, u32[]{:S(2)}, u32[]{:S(2)}) collective-permute-start(bf16[8,2,120,128]{3,2,1,0:T(8,128)(2,1)S(1)} %get-tuple-element.28), channel_id=1, source_target_pairs={{0,1},{1,0},{2,3},{3,2},{4,5},{5,4},{6,7},{7,6},{8,9},{9,8},{10,11... | collective-permute-start | bytes 1474568 | tf_op jit(solution)/shard_map/ppermute | solution.py:489
  7.8 0.1 collective-permute-start.1
  7.9 1.4 %grams_mine.1 = (bf16[8,2,104,128]{3,2,1,0:T(8,128)(2,1)S(1)}, bf16[8,2,104,128]{3,2,1,0:T(8,128)(2,1)S(1)}) custom-call(bf16[1024,128]{1,0:T(8,128)(2,1)S(1)} %get-tuple-element.23.keep, bf16[1024,512]{1,0:T(8,128)(2,1)S(1)} %get-tuple-element.24.x0, bf16[1024,512]{1,0:T(8,128)(2,1)S(1)} %get-tuple-element.25.x1), custom_call_target="tpu_custom_call" | custom-call | flops 1610612736 | bytes 4194304 | tf_op jit(solution)/shard_map/grams_mine/pallas_call | solution.py:491
  9.3 0.0 collective-permute-done.received
  9.3 0.1 chip_sum0.1.first
  9.4 0.5 collective-permute-done.1.received
  9.9 1.0 %chip_sum1.1 = bf16[16,2,120,128]{3,2,1,0:T(8,128)(2,1)} custom-call(bf16[8,2,120,128]{3,2,1,0:T(8,128)(2,1)S(1)} %chip_sum0.1.first, bf16[8,2,104,128]{3,2,1,0:T(8,128)(2,1)S(1)} %get-tuple-element.29.mine, bf16[8,2,24,128]{3,2,1,0:T(8,128)(2,1)S(1)} %get-tuple-element.30.spare, bf16[8,2,120,128]{3,2,1,0:T(8,128)(2,1)S(1)} %collective-permute-done.1.received), custom_call_target="tpu_custom_call" | custom-call | bytes 1048576 | tf_op jit(solution)/shard_map/chip_sum1/pallas_call | solution.py:501
  10.9 0.0 copy-start
  10.9 0.0 copy-start.5
  11.0 6.8 %all-to-all-start = ((bf16[32,120,128]{2,1,0:T(8,128)(2,1)}), bf16[32,120,128]{2,1,0:T(8,128)(2,1)S(1)}, u32[]{:S(2)}, u32[]{:S(2)}) async-start(bf16[32,120,128]{2,1,0:T(8,128)(2,1)} %bitcast.41), calls=%async_computation | async-start | bytes 1966080 | tf_op jit(solution)/shard_map/wide_sum/all_to_all | solution.py:447
  17.8 0.0 copy-done
  17.8 0.0 copy-done.5
  17.8 0.3 fusion.1
  18.1 0.3 fusion.2
  18.5 0.3 fusion
  18.8 3.8 %lam.1 = (f32[2,512]{1,0:T(2,128)S(1)}, f32[2,512]{1,0:T(2,128)S(1)}, bf16[512,512]{1,0:T(8,128)(2,1)S(1)}, bf16[512,512]{1,0:T(8,128)(2,1)S(1)}, bf16[512,512]{...) custom-call(s32[1]{0:T(128)} %bitcast.core, s32[1]{0:T(128)} %bitcast.1.chip, bf16[32,120,128]{2,1,0:T(8,128)(2,1)} %bitcast.42, ...), custom_call_target="tpu_custom_call" | custom-call | flops 1610612736 | bytes 4194304 | tf_op jit(solution)/shard_map/lam/pallas_call | solution.py:514
  22.6 0.0 copy-start.1
  22.6 0.8 %copy-done.1 = bf16[512,512]{1,0:T(8,128)(2,1)} copy-done((bf16[512,512]{1,0:T(8,128)(2,1)}, bf16[512,512]{1,0:T(8,128)(2,1)S(1)}, u32[]{:S(2)}) %copy-start.1) | copy-done | bytes 524312
  23.4 0.8 %copy-done.3 = bf16[512,512]{1,0:T(8,128)(2,1)} copy-done((bf16[512,512]{1,0:T(8,128)(2,1)}, bf16[512,512]{1,0:T(8,128)(2,1)S(1)}, u32[]{:S(2)}) %copy-start.3) | copy-done | bytes 524312
  24.2 0.7 %collective-permute-start.2 = (f32[2,512]{1,0:T(2,128)S(1)}, f32[2,512]{1,0:T(2,128)S(1)}, u32[]{:S(2)}, u32[]{:S(2)}) collective-permute-start(f32[2,512]{1,0:T(2,128)S(1)} %get-tuple-element.45), channel_id=1, source_target_pairs={{0,1},{1,0},{2,3},{3,2},{4,5},{5,4},{6,7},{7,6},{8,9},{9,8},{10,11... | collective-permute-start | bytes 12296 | tf_op jit(solution)/shard_map/ppermute | solution.py:529
  25.0 0.8 %collective-permute-done.2.send_lam = f32[2,512]{1,0:T(2,128)S(1)} collective-permute-done((f32[2,512]{1,0:T(2,128)S(1)}, f32[2,512]{1,0:T(2,128)S(1)}, u32[]{:S(2)}, u32[]{:S(2)}) %collective-permute-start.2) | collective-permute-done | bytes 4128 | tf_op jit(solution)/shard_map/ppermute | solution.py:529
  25.8 8.2 %all-to-all-done.parts = bf16[32,120,128]{2,1,0:T(8,128)(2,1)S(1)} async-done(((bf16[32,120,128]{2,1,0:T(8,128)(2,1)}), bf16[32,120,128]{2,1,0:T(8,128)(2,1)S(1)}, u32[]{:S(2)}, u32[]{:S(2)}) %all-to-all-start) | async-done | bytes 983072 | tf_op jit(solution)/shard_map/wide_sum/all_to_all | solution.py:447
  34.0 0.3 pack.1
  34.4 0.0 copy-start.2
  34.4 14.4 %all_to_all.15.got.packed = bf16[4,112,128]{2,1,0:T(8,128)(2,1)S(1)} all-to-all(bf16[4,112,128]{2,1,0:T(8,128)(2,1)S(1)} %pack.1), channel_id=1, replica_groups={{0,4,8,12},{1,5,9,13},{2,6,10,14},{3,7,11,15},{16,20,24,28},{17,21,25,2..., dimensions={0} | all-to-all | bytes 229376 | tf_op jit(solution)/shard_map/deep_sum/all_to_all | solution.py:447
  48.8 0.2 rotate.1
  49.0 14.3 %all_to_all.16.got = bf16[32,80,128]{2,1,0:T(8,128)(2,1)S(1)} all-to-all(bf16[32,80,128]{2,1,0:T(8,128)(2,1)S(1)} %rotate.1), channel_id=1, replica_groups={{0,2,16,18,32,34,48,50,64,66,80,82,96,98,112,114,128,130,144,146,160,16..., dimensions={0} | all-to-all | bytes 1310720 | tf_op jit(solution)/shard_map/gather/all_to_all | solution.py:447
  63.3 1.0 %solve.1 = (f32[16,512]{1,0:T(8,128)S(1)}, f32[16,512]{1,0:T(8,128)S(1)}) custom-call(s32[1]{0:T(128)} %bitcast.core, s32[1]{0:T(128)} %bitcast.1.chip, bf16[32,80,128]{2,1,0:T(8,128)(2,1)S(1)} %all_to_all.16.got, bf16[4,112,128]{2,1,0:T(8,128)(2,1)S(1)} %all_to_all.15.got.packed, bf16[512,512]{1,0:T(8,128)(2,1)S(1)} %copy-done.2, ...), custom_call_target="tpu_custom_call" | custom-call | tf_op jit(solution)/shard_map/solve/pallas_call | solution.py:541
  64.4 4.0 %collective-permute-start.3 = (f32[16,512]{1,0:T(8,128)S(1)}, f32[16,512]{1,0:T(8,128)S(1)}, u32[]{:S(2)}, u32[]{:S(2)}) collective-permute-start(f32[16,512]{1,0:T(8,128)S(1)} %get-tuple-element.39), channel_id=1, source_target_pairs={{0,1},{1,0},{2,3},{3,2},{4,5},{5,4},{6,7},{7,6},{8,9},{9,8},{10,11... | collective-permute-start | bytes 98312 | tf_op jit(solution)/shard_map/ppermute | solution.py:544
  68.4 0.9 %collective-permute-done.3.got = f32[16,512]{1,0:T(8,128)S(1)} collective-permute-done((f32[16,512]{1,0:T(8,128)S(1)}, f32[16,512]{1,0:T(8,128)S(1)}, u32[]{:S(2)}, u32[]{:S(2)}) %collective-permute-start.3) | collective-permute-done | bytes 32800 | tf_op jit(solution)/shard_map/ppermute | solution.py:544
  69.3 0.6 finish.1
  (8 shorter events, 0.0 us)
Async XLA Ops:
  4.4 4.9 %collective-permute-start = (bf16[8,2,120,128]{3,2,1,0:T(8,128)(2,1)S(1)}, bf16[8,2,120,128]{3,2,1,0:T(8,128)(2,1)S(1)}, u32[]{:S(2)}, u32[]{:S(2)}) collective-permute-start(bf16[8,2,120,128]{3,2,1,0:T(8,128)(2,1)S(1)} %get-tuple-element.28), channel_id=1, source_target_pairs={{0,1},{1,0},{2,3},{3,2},{4,5},{5,4},{6,7},{7,6},{8,9},{9,8},{10,11... | collective-permute-start | bytes 1474568 | tf_op jit(solution)/shard_map/ppermute | solution.py:489
  7.8 2.2 %collective-permute-start.1 = (bf16[8,2,120,128]{3,2,1,0:T(8,128)(2,1)S(1)}, bf16[8,2,120,128]{3,2,1,0:T(8,128)(2,1)S(1)}, u32[]{:S(2)}, u32[]{:S(2)}) collective-permute-start(bf16[8,2,120,128]{3,2,1,0:T(8,128)(2,1)S(1)} %get-tuple-element.31), channel_id=1, source_target_pairs={{0,1},{1,0},{2,3},{3,2},{4,5},{5,4},{6,7},{7,6},{8,9},{9,8},{10,11... | collective-permute-start | bytes 1474568 | tf_op jit(solution)/shard_map/ppermute | solution.py:489
  10.9 6.8 %copy-start = (bf16[3,512,512]{2,1,0:T(8,128)(2,1)S(1)}, bf16[3,512,512]{2,1,0:T(8,128)(2,1)}, u32[]{:S(2)}) copy-start(bf16[3,512,512]{2,1,0:T(8,128)(2,1)} %bases.1) | copy-start | bytes 4718596
  10.9 6.9 %copy-start.5 = (f32[2,3,512]{2,0,1:T(2,128)S(1)}, f32[2,3,512]{2,0,1:T(2,128)}, u32[]{:S(2)}) copy-start(f32[2,3,512]{2,0,1:T(2,128)} %param.13) | copy-start | bytes 36868
  11.0 23.1 %all-to-all-start = ((bf16[32,120,128]{2,1,0:T(8,128)(2,1)}), bf16[32,120,128]{2,1,0:T(8,128)(2,1)S(1)}, u32[]{:S(2)}, u32[]{:S(2)}) async-start(bf16[32,120,128]{2,1,0:T(8,128)(2,1)} %bitcast.41), calls=%async_computation | async-start | bytes 1966080 | tf_op jit(solution)/shard_map/wide_sum/all_to_all | solution.py:447
  22.6 0.8 %copy-start.1 = (bf16[512,512]{1,0:T(8,128)(2,1)}, bf16[512,512]{1,0:T(8,128)(2,1)S(1)}, u32[]{:S(2)}) copy-start(bf16[512,512]{1,0:T(8,128)(2,1)S(1)} %get-tuple-element.35.basis_in_t) | copy-start | bytes 1572868
  23.4 0.8 %copy-start.3 = (bf16[512,512]{1,0:T(8,128)(2,1)}, bf16[512,512]{1,0:T(8,128)(2,1)S(1)}, u32[]{:S(2)}) copy-start(bf16[512,512]{1,0:T(8,128)(2,1)S(1)} %get-tuple-element.37.mirror) | copy-start | bytes 1572868
  24.2 1.6 %collective-permute-start.2 = (f32[2,512]{1,0:T(2,128)S(1)}, f32[2,512]{1,0:T(2,128)S(1)}, u32[]{:S(2)}, u32[]{:S(2)}) collective-permute-start(f32[2,512]{1,0:T(2,128)S(1)} %get-tuple-element.45), channel_id=1, source_target_pairs={{0,1},{1,0},{2,3},{3,2},{4,5},{5,4},{6,7},{7,6},{8,9},{9,8},{10,11... | collective-permute-start | bytes 12296 | tf_op jit(solution)/shard_map/ppermute | solution.py:529
  34.4 28.9 %copy-start.2 = (bf16[512,512]{1,0:T(8,128)(2,1)S(1)}, bf16[512,512]{1,0:T(8,128)(2,1)}, u32[]{:S(2)}) copy-start(bf16[512,512]{1,0:T(8,128)(2,1)} %copy-done.1) | copy-start | bytes 1572868
  34.4 28.9 %copy-start.4 = (bf16[512,512]{1,0:T(8,128)(2,1)S(1)}, bf16[512,512]{1,0:T(8,128)(2,1)}, u32[]{:S(2)}) copy-start(bf16[512,512]{1,0:T(8,128)(2,1)} %copy-done.3) | copy-start | bytes 1572868
  64.4 4.9 %collective-permute-start.3 = (f32[16,512]{1,0:T(8,128)S(1)}, f32[16,512]{1,0:T(8,128)S(1)}, u32[]{:S(2)}, u32[]{:S(2)}) collective-permute-start(f32[16,512]{1,0:T(8,128)S(1)} %get-tuple-element.39), channel_id=1, source_target_pairs={{0,1},{1,0},{2,3},{3,2},{4,5},{5,4},{6,7},{7,6},{8,9},{9,8},{10,11... | collective-permute-start | bytes 98312 | tf_op jit(solution)/shard_map/ppermute | solution.py:544

commit v17 on v16

--- a/solution.py
+++ b/solution.py
@@ -209,7 +209,7 @@
 
 
 SIDES = D // BLOCK
-PIECES = 2
+PIECES = 4
 
 
 def add_rows(mine, spare, received, out, blocks):
@@ -229,8 +229,11 @@
 def add_second_kernel(first, mine, spare, received, out, buf, sems):
     count = NXY // SIDES
     size = count // PIECES
-    copies = [pltpu.make_async_copy(first, out.at[pl.ds(0, count)], sems.at[PIECES])]
-    copies[0].start()
+    copies = []
+    for q in range(2):
+        part = pl.ds(q * (count // 2), count // 2)
+        copies.append(pltpu.make_async_copy(first.at[part], out.at[part], sems.at[PIECES + q]))
+        copies[-1].start()
     for q in range(PIECES):
         add_rows(mine, spare, received, buf, range(q * size, (q + 1) * size))
         target = out.at[pl.ds(count + q * size, size)]
@@ -502,7 +505,7 @@
             add_second_kernel,
             pltpu.HBM((NXY, PAIR, WROWS, LANES), bf16),
             [VMEM] * 4,
-            [pltpu.VMEM(partial.shape, bf16), pltpu.SemaphoreType.DMA((PIECES + 1,))],
+            [pltpu.VMEM(partial.shape, bf16), pltpu.SemaphoreType.DMA((PIECES + 2,))],
             moved=MB,
         )(half, mine[1], spare1, received[1])
         chip = chip.reshape(WIDE, WROWS, LANES)

time: 70.2 us -> 70.2 us (level)
  no operation moved by 1% of the time
where the time goes in v17:
time: 70.2 us; the launch traced here: 69.9 us
  blocking collectives  28.7 us (41%)
  starting transfers between devices  15 us (21%)
  Pallas kernels  12.3 us (18%)
  waiting for transfers between devices  10.5 us (15%)
  local copies, waits for them, and re-layouts  1.62 us (2%)
  matrix products  0.99 us (1%)
  between operations  0.8 us (1%)
    all_to_all x2, blocking collectives, exchange(): lax.all_to_all(value, 'dp', 0, 0, axis_index_groups=groups, tiled=True)  28.7 us
    all_to_all x1, waiting for transfers between devices, exchange(): lax.all_to_all(value, 'dp', 0, 0, axis_index_groups=groups, tiled=True)  8.25 us
    all_to_all x1, starting transfers between devices, exchange(): lax.all_to_all(value, 'dp', 0, 0, axis_index_groups=groups, tiled=True)  6.8 us
    ppermute x1, starting transfers between devices, body(): theirs = lax.ppermute(their, 'dp', SWAP)  4.03 us
    pallas_call x1, Pallas kernels, body(): call(theirs_kernel, (partial, partial, spare_shape, spare_shape, shape((t...  3.78 us
    pallas_call x1, Pallas kernels, body(): call(functools.partial(lam_kernel, share), (lam_shape, lam_shape, square,...  3.75 us
    ppermute x2, starting transfers between devices, body(): received = [lax.ppermute(part, 'dp', SWAP) for part in sent]  3.43 us
    unnamed x12, local copies, waits for them, and re-layouts  1.62 us
  transfers between devices with their start and end apart: 5, of which 4 were waited for; matrix products, arithmetic and copies ran while one was open for 1% of the time, Pallas kernels for 8%

profile of v17, /device:TPU:1, one launch (start us, length us, event | category | flops | bytes accessed | tf_op | source)
XLA Modules:
  0.0 69.9 jit_solution(7237101801193500914)
XLA Ops:
  0.6 3.8 %grams_theirs.1 = (bf16[8,2,120,128]{3,2,1,0:T(8,128)(2,1)S(1)}, bf16[8,2,120,128]{3,2,1,0:T(8,128)(2,1)S(1)}, bf16[8,2,24,128]{3,2,1,0:T(8,128)(2,1)S(1)}, bf16...) custom-call(s32[1]{0:T(128)} %bitcast.core, ...), custom_call_target="tpu_custom_call" | custom-call | flops 1610612736 | bytes 4194304 | tf_op jit(solution)/shard_map/grams_theirs/pallas_call | solution.py:476
  4.4 3.3 %collective-permute-start = (bf16[8,2,120,128]{3,2,1,0:T(8,128)(2,1)S(1)}, bf16[8,2,120,128]{3,2,1,0:T(8,128)(2,1)S(1)}, u32[]{:S(2)}, u32[]{:S(2)}) collective-permute-start(bf16[8,2,120,128]{3,2,1,0:T(8,128)(2,1)S(1)} %get-tuple-element.28), channel_id=1, source_target_pairs={{0,1},{1,0},{2,3},{3,2},{4,5},{5,4},{6,7},{7,6},{8,9},{9,8},{10,11... | collective-permute-start | bytes 1474568 | tf_op jit(solution)/shard_map/ppermute | solution.py:492
  7.8 0.1 collective-permute-start.1
  7.9 1.4 %grams_mine.1 = (bf16[8,2,104,128]{3,2,1,0:T(8,128)(2,1)S(1)}, bf16[8,2,104,128]{3,2,1,0:T(8,128)(2,1)S(1)}) custom-call(bf16[1024,128]{1,0:T(8,128)(2,1)S(1)} %get-tuple-element.23.keep, bf16[1024,512]{1,0:T(8,128)(2,1)S(1)} %get-tuple-element.24.x0, bf16[1024,512]{1,0:T(8,128)(2,1)S(1)} %get-tuple-element.25.x1), custom_call_target="tpu_custom_call" | custom-call | flops 1610612736 | bytes 4194304 | tf_op jit(solution)/shard_map/grams_mine/pallas_call | solution.py:494
  9.3 0.0 collective-permute-done.received
  9.3 0.1 chip_sum0.1.first
  9.4 0.5 collective-permute-done.1.received
  9.9 1.0 %chip_sum1.1 = bf16[16,2,120,128]{3,2,1,0:T(8,128)(2,1)} custom-call(bf16[8,2,120,128]{3,2,1,0:T(8,128)(2,1)S(1)} %chip_sum0.1.first, bf16[8,2,104,128]{3,2,1,0:T(8,128)(2,1)S(1)} %get-tuple-element.29.mine, bf16[8,2,24,128]{3,2,1,0:T(8,128)(2,1)S(1)} %get-tuple-element.30.spare, bf16[8,2,120,128]{3,2,1,0:T(8,128)(2,1)S(1)} %collective-permute-done.1.received), custom_call_target="tpu_custom_call" | custom-call | bytes 1048576 | tf_op jit(solution)/shard_map/chip_sum1/pallas_call | solution.py:504
  11.0 0.0 copy-start
  11.0 0.0 copy-start.5
  11.0 6.8 %all-to-all-start = ((bf16[32,120,128]{2,1,0:T(8,128)(2,1)}), bf16[32,120,128]{2,1,0:T(8,128)(2,1)S(1)}, u32[]{:S(2)}, u32[]{:S(2)}) async-start(bf16[32,120,128]{2,1,0:T(8,128)(2,1)} %bitcast.41), calls=%async_computation | async-start | bytes 1966080 | tf_op jit(solution)/shard_map/wide_sum/all_to_all | solution.py:450
  17.8 0.0 copy-done
  17.8 0.0 copy-done.5
  17.8 0.3 fusion.1
  18.2 0.3 fusion.2
  18.5 0.3 fusion
  18.9 3.8 %lam.1 = (f32[2,512]{1,0:T(2,128)S(1)}, f32[2,512]{1,0:T(2,128)S(1)}, bf16[512,512]{1,0:T(8,128)(2,1)S(1)}, bf16[512,512]{1,0:T(8,128)(2,1)S(1)}, bf16[512,512]{...) custom-call(s32[1]{0:T(128)} %bitcast.core, s32[1]{0:T(128)} %bitcast.1.chip, bf16[32,120,128]{2,1,0:T(8,128)(2,1)} %bitcast.42, ...), custom_call_target="tpu_custom_call" | custom-call | flops 1610612736 | bytes 4194304 | tf_op jit(solution)/shard_map/lam/pallas_call | solution.py:517
  22.6 0.0 copy-start.1
  22.6 0.8 %copy-done.1 = bf16[512,512]{1,0:T(8,128)(2,1)} copy-done((bf16[512,512]{1,0:T(8,128)(2,1)}, bf16[512,512]{1,0:T(8,128)(2,1)S(1)}, u32[]{:S(2)}) %copy-start.1) | copy-done | bytes 524312
  23.4 0.8 %copy-done.3 = bf16[512,512]{1,0:T(8,128)(2,1)} copy-done((bf16[512,512]{1,0:T(8,128)(2,1)}, bf16[512,512]{1,0:T(8,128)(2,1)S(1)}, u32[]{:S(2)}) %copy-start.3) | copy-done | bytes 524312
  24.2 0.7 %collective-permute-start.2 = (f32[2,512]{1,0:T(2,128)S(1)}, f32[2,512]{1,0:T(2,128)S(1)}, u32[]{:S(2)}, u32[]{:S(2)}) collective-permute-start(f32[2,512]{1,0:T(2,128)S(1)} %get-tuple-element.45), channel_id=1, source_target_pairs={{0,1},{1,0},{2,3},{3,2},{4,5},{5,4},{6,7},{7,6},{8,9},{9,8},{10,11... | collective-permute-start | bytes 12296 | tf_op jit(solution)/shard_map/ppermute | solution.py:532
  25.0 0.8 %collective-permute-done.2.send_lam = f32[2,512]{1,0:T(2,128)S(1)} collective-permute-done((f32[2,512]{1,0:T(2,128)S(1)}, f32[2,512]{1,0:T(2,128)S(1)}, u32[]{:S(2)}, u32[]{:S(2)}) %collective-permute-start.2) | collective-permute-done | bytes 4128 | tf_op jit(solution)/shard_map/ppermute | solution.py:532
  25.8 8.2 %all-to-all-done.parts = bf16[32,120,128]{2,1,0:T(8,128)(2,1)S(1)} async-done(((bf16[32,120,128]{2,1,0:T(8,128)(2,1)}), bf16[32,120,128]{2,1,0:T(8,128)(2,1)S(1)}, u32[]{:S(2)}, u32[]{:S(2)}) %all-to-all-start) | async-done | bytes 983072 | tf_op jit(solution)/shard_map/wide_sum/all_to_all | solution.py:450
  34.1 0.3 pack.1
  34.4 0.0 copy-start.2
  34.4 14.4 %all_to_all.15.got.packed = bf16[4,112,128]{2,1,0:T(8,128)(2,1)S(1)} all-to-all(bf16[4,112,128]{2,1,0:T(8,128)(2,1)S(1)} %pack.1), channel_id=1, replica_groups={{0,4,8,12},{1,5,9,13},{2,6,10,14},{3,7,11,15},{16,20,24,28},{17,21,25,2..., dimensions={0} | all-to-all | bytes 229376 | tf_op jit(solution)/shard_map/deep_sum/all_to_all | solution.py:450
  48.8 0.2 rotate.1
  49.0 14.3 %all_to_all.16.got = bf16[32,80,128]{2,1,0:T(8,128)(2,1)S(1)} all-to-all(bf16[32,80,128]{2,1,0:T(8,128)(2,1)S(1)} %rotate.1), channel_id=1, replica_groups={{0,2,16,18,32,34,48,50,64,66,80,82,96,98,112,114,128,130,144,146,160,16..., dimensions={0} | all-to-all | bytes 1310720 | tf_op jit(solution)/shard_map/gather/all_to_all | solution.py:450
  63.4 1.0 %solve.1 = (f32[16,512]{1,0:T(8,128)S(1)}, f32[16,512]{1,0:T(8,128)S(1)}) custom-call(s32[1]{0:T(128)} %bitcast.core, s32[1]{0:T(128)} %bitcast.1.chip, bf16[32,80,128]{2,1,0:T(8,128)(2,1)S(1)} %all_to_all.16.got, bf16[4,112,128]{2,1,0:T(8,128)(2,1)S(1)} %all_to_all.15.got.packed, bf16[512,512]{1,0:T(8,128)(2,1)S(1)} %copy-done.2, ...), custom_call_target="tpu_custom_call" | custom-call | tf_op jit(solution)/shard_map/solve/pallas_call | solution.py:544
  64.4 4.0 %collective-permute-start.3 = (f32[16,512]{1,0:T(8,128)S(1)}, f32[16,512]{1,0:T(8,128)S(1)}, u32[]{:S(2)}, u32[]{:S(2)}) collective-permute-start(f32[16,512]{1,0:T(8,128)S(1)} %get-tuple-element.39), channel_id=1, source_target_pairs={{0,1},{1,0},{2,3},{3,2},{4,5},{5,4},{6,7},{7,6},{8,9},{9,8},{10,11... | collective-permute-start | bytes 98312 | tf_op jit(solution)/shard_map/ppermute | solution.py:547
  68.4 0.9 %collective-permute-done.3.got = f32[16,512]{1,0:T(8,128)S(1)} collective-permute-done((f32[16,512]{1,0:T(8,128)S(1)}, f32[16,512]{1,0:T(8,128)S(1)}, u32[]{:S(2)}, u32[]{:S(2)}) %collective-permute-start.3) | collective-permute-done | bytes 32800 | tf_op jit(solution)/shard_map/ppermute | solution.py:547
  69.3 0.6 finish.1
  (8 shorter events, 0.0 us)
Async XLA Ops:
  4.4 4.9 %collective-permute-start = (bf16[8,2,120,128]{3,2,1,0:T(8,128)(2,1)S(1)}, bf16[8,2,120,128]{3,2,1,0:T(8,128)(2,1)S(1)}, u32[]{:S(2)}, u32[]{:S(2)}) collective-permute-start(bf16[8,2,120,128]{3,2,1,0:T(8,128)(2,1)S(1)} %get-tuple-element.28), channel_id=1, source_target_pairs={{0,1},{1,0},{2,3},{3,2},{4,5},{5,4},{6,7},{7,6},{8,9},{9,8},{10,11... | collective-permute-start | bytes 1474568 | tf_op jit(solution)/shard_map/ppermute | solution.py:492
  7.8 2.2 %collective-permute-start.1 = (bf16[8,2,120,128]{3,2,1,0:T(8,128)(2,1)S(1)}, bf16[8,2,120,128]{3,2,1,0:T(8,128)(2,1)S(1)}, u32[]{:S(2)}, u32[]{:S(2)}) collective-permute-start(bf16[8,2,120,128]{3,2,1,0:T(8,128)(2,1)S(1)} %get-tuple-element.31), channel_id=1, source_target_pairs={{0,1},{1,0},{2,3},{3,2},{4,5},{5,4},{6,7},{7,6},{8,9},{9,8},{10,11... | collective-permute-start | bytes 1474568 | tf_op jit(solution)/shard_map/ppermute | solution.py:492
  11.0 6.8 %copy-start = (bf16[3,512,512]{2,1,0:T(8,128)(2,1)S(1)}, bf16[3,512,512]{2,1,0:T(8,128)(2,1)}, u32[]{:S(2)}) copy-start(bf16[3,512,512]{2,1,0:T(8,128)(2,1)} %bases.1) | copy-start | bytes 4718596
  11.0 6.9 %copy-start.5 = (f32[2,3,512]{2,0,1:T(2,128)S(1)}, f32[2,3,512]{2,0,1:T(2,128)}, u32[]{:S(2)}) copy-start(f32[2,3,512]{2,0,1:T(2,128)} %param.13) | copy-start | bytes 36868
  11.0 23.1 %all-to-all-start = ((bf16[32,120,128]{2,1,0:T(8,128)(2,1)}), bf16[32,120,128]{2,1,0:T(8,128)(2,1)S(1)}, u32[]{:S(2)}, u32[]{:S(2)}) async-start(bf16[32,120,128]{2,1,0:T(8,128)(2,1)} %bitcast.41), calls=%async_computation | async-start | bytes 1966080 | tf_op jit(solution)/shard_map/wide_sum/all_to_all | solution.py:450
  22.6 0.8 %copy-start.1 = (bf16[512,512]{1,0:T(8,128)(2,1)}, bf16[512,512]{1,0:T(8,128)(2,1)S(1)}, u32[]{:S(2)}) copy-start(bf16[512,512]{1,0:T(8,128)(2,1)S(1)} %get-tuple-element.35.basis_in_t) | copy-start | bytes 1572868
  23.4 0.8 %copy-start.3 = (bf16[512,512]{1,0:T(8,128)(2,1)}, bf16[512,512]{1,0:T(8,128)(2,1)S(1)}, u32[]{:S(2)}) copy-start(bf16[512,512]{1,0:T(8,128)(2,1)S(1)} %get-tuple-element.37.mirror) | copy-start | bytes 1572868
  24.2 1.6 %collective-permute-start.2 = (f32[2,512]{1,0:T(2,128)S(1)}, f32[2,512]{1,0:T(2,128)S(1)}, u32[]{:S(2)}, u32[]{:S(2)}) collective-permute-start(f32[2,512]{1,0:T(2,128)S(1)} %get-tuple-element.45), channel_id=1, source_target_pairs={{0,1},{1,0},{2,3},{3,2},{4,5},{5,4},{6,7},{7,6},{8,9},{9,8},{10,11... | collective-permute-start | bytes 12296 | tf_op jit(solution)/shard_map/ppermute | solution.py:532
  34.4 28.9 %copy-start.2 = (bf16[512,512]{1,0:T(8,128)(2,1)S(1)}, bf16[512,512]{1,0:T(8,128)(2,1)}, u32[]{:S(2)}) copy-start(bf16[512,512]{1,0:T(8,128)(2,1)} %copy-done.1) | copy-start | bytes 1572868
  34.4 28.9 %copy-start.4 = (bf16[512,512]{1,0:T(8,128)(2,1)S(1)}, bf16[512,512]{1,0:T(8,128)(2,1)}, u32[]{:S(2)}) copy-start(bf16[512,512]{1,0:T(8,128)(2,1)} %copy-done.3) | copy-start | bytes 1572868
  64.4 4.9 %collective-permute-start.3 = (f32[16,512]{1,0:T(8,128)S(1)}, f32[16,512]{1,0:T(8,128)S(1)}, u32[]{:S(2)}, u32[]{:S(2)}) collective-permute-start(f32[16,512]{1,0:T(8,128)S(1)} %get-tuple-element.39), channel_id=1, source_target_pairs={{0,1},{1,0},{2,3},{3,2},{4,5},{5,4},{6,7},{7,6},{8,9},{9,8},{10,11... | collective-permute-start | bytes 98312 | tf_op jit(solution)/shard_map/ppermute | solution.py:547
